TPU v7x, 32 devices: a whole 2x2x4 slice. The times are simulated.
32 devices in a mesh: groups: 2 (over x), section: 2 (over core), tensor: 8 (over z, y).
Axes of the slice: x: 2, y: 2, z: 4, core: 2. Of those that a mesh axis runs over, the one named last changes fastest.
Arguments:
- hidden: bfloat16 [16, 8192], P(('groups', 'section'), 'tensor'), parts along dimension 0, may hold values from -6 to 6
- w_query: bfloat16 [8192, 8192], P(None, 'tensor'), may hold values from -0.0625 to 0.0625
- w_output: bfloat16 [8192, 8192], P('tensor'), may hold values from -0.75 to 0.75
- cache: bfloat16 [16, 1024, 2048], P(('groups', 'section'), 'tensor'), parts along dimension 0
- fresh: bfloat16 [16, 512, 2048], P(('groups', 'section'), 'tensor'), parts along dimension 0, may hold values from -6 to 6
- cache_lengths: int32 [16], P(('groups', 'section')), parts along dimension 0, may hold values from 1 to 1024, 4097 in all
- new_lengths: int32 [16], P(('groups', 'section')), parts along dimension 0, may hold values from 1 to 512, 2049 in all
Outputs:
- attended: bfloat16 [16, 8192], P(('groups', 'section'), 'tensor'), parts along dimension 0
There are 2 independent parts, one for each index of `groups`. A program takes and returns all parts, laid end to end along the dimension named above; an argument that names none is the same for every part. Nothing has to cross between parts.
All inputs are finite; a program needn't handle non-finite values. No bound on the sum of `cache_lengths` or of `new_lengths` on one device may be relied on, other than what follows from the above.
Results may differ from a plain program's by a relative error of at most 0.035.
Values may be sent and summed in bfloat16 or wider, within the bound.
No kernel may reach another device: no remote copies, remote signals or barrier semaphores. Data moves between devices by JAX's collectives and lax.ppermute only.
A program may use at most 128 MiB of HBM per device.

v0:
```python
import jax
import jax.numpy as jnp
from jax import lax
from jax.sharding import PartitionSpec as P

HEADS = 64
KVH = 8
HD = 128


def combined_all(shard, axis, join):
    gathered = jax.tree.map(
        lambda a, kind: lax.all_gather(a.astype(kind), axis),
        shard,
        (jnp.bfloat16, jnp.bfloat16, jnp.bfloat16),
    )

    def take(source):
        return jax.tree.map(
            lambda a, own: lax.dynamic_index_in_dim(a, source, 0, False).astype(own.dtype),
            gathered,
            shard,
        )

    return lax.fori_loop(
        1, lax.axis_size(axis), lambda source, state: join(state, take(source)), take(0)
    )


def partial_scores(queries, block, valid):
    rows = block.shape[0]
    count = block.shape[1]
    width = KVH * HD
    keys = block[:, :, :width].reshape(rows, count, KVH, HD)
    scores = jnp.einsum(
        "rkgd,rtkd->rkgt", queries, keys, preferred_element_type=jnp.float32
    ) * HD ** (-0.5)
    return jnp.where(valid[:, None, None, :], scores, -1e30)


def partial_values(weights, block):
    rows = block.shape[0]
    count = block.shape[1]
    width = KVH * HD
    values = block[:, :, width:].reshape(rows, count, KVH, HD)
    return jnp.einsum(
        "rkgt,rtkd->rkgd", weights.astype(jnp.bfloat16), values, preferred_element_type=jnp.float32
    )


def combine_parts(first, second):
    num_a, top_a, sum_a = first
    num_b, top_b, sum_b = second
    top_new = jnp.maximum(top_a, top_b)
    scale_a = jnp.exp(top_a - top_new)
    scale_b = jnp.exp(top_b - top_new)
    return (
        num_a * scale_a[..., None] + num_b * scale_b[..., None],
        top_new,
        sum_a * scale_a + sum_b * scale_b,
    )


def body(hidden, w_query, w_output, cache, fresh, cache_lengths, new_lengths):
    rows = hidden.shape[0]
    group = HEADS // KVH
    local_heads = w_query.shape[1] // HD
    whole = lax.all_gather(hidden, "tensor", axis=1, tiled=True)
    query_own = jnp.dot(whole, w_query, preferred_element_type=jnp.float32).astype(jnp.bfloat16)
    queries = lax.all_gather(query_own, "tensor", axis=1, tiled=True).reshape(rows, KVH, group, HD)
    index = lax.axis_index("tensor")
    cache_count = cache.shape[1]
    fresh_count = fresh.shape[1]
    cache_pos = index * cache_count + jnp.arange(cache_count, dtype=jnp.int32)
    fresh_pos = index * fresh_count + jnp.arange(fresh_count, dtype=jnp.int32)
    cache_valid = cache_pos[None, :] < cache_lengths[:, None]
    fresh_valid = fresh_pos[None, :] < new_lengths[:, None]
    score_cache = partial_scores(queries, cache, cache_valid)
    score_fresh = partial_scores(queries, fresh, fresh_valid)
    top = jnp.maximum(jnp.max(score_cache, axis=3), jnp.max(score_fresh, axis=3))
    weight_cache = jnp.where(
        cache_valid[:, None, None, :], jnp.exp(score_cache - top[..., None]), 0.0
    )
    weight_fresh = jnp.where(
        fresh_valid[:, None, None, :], jnp.exp(score_fresh - top[..., None]), 0.0
    )
    summed = jnp.sum(weight_cache, axis=3) + jnp.sum(weight_fresh, axis=3)
    numerator = partial_values(weight_cache, cache) + partial_values(weight_fresh, fresh)
    numerator = numerator.reshape(rows, HEADS, HD)
    top = top.reshape(rows, HEADS)
    summed = summed.reshape(rows, HEADS)
    merged_num, merged_top, merged_sum = combined_all(
        (numerator, top, summed), "tensor", combine_parts
    )
    total_num = lax.dynamic_slice_in_dim(merged_num, index * local_heads, local_heads, 1)
    total_sum = lax.dynamic_slice_in_dim(merged_sum, index * local_heads, local_heads, 1)
    context = (
        (total_num / total_sum[..., None]).astype(jnp.bfloat16).reshape(rows, local_heads * HD)
    )
    terms = jnp.dot(context, w_output, preferred_element_type=jnp.float32)
    return lax.psum_scatter(terms, "tensor", scatter_dimension=1, tiled=True).astype(jnp.bfloat16)


def solution(mesh):
    return jax.shard_map(
        body,
        mesh=mesh,
        in_specs=(
            P(("groups", "section"), "tensor"),
            P(None, "tensor"),
            P("tensor", None),
            P(("groups", "section"), "tensor", None),
            P(("groups", "section"), "tensor", None),
            P(("groups", "section")),
            P(("groups", "section")),
        ),
        out_specs=P(("groups", "section"), "tensor"),
        check_vma=False,
    )
```

profile of v0, /device:TPU:0, one launch (start us, length us, event | category | flops | bytes accessed | tf_op | source)
XLA Modules:
  0.0 262.3 jit_solution(13336673880678129886)
XLA Ops:
  6.5 0.0 copy-start.1
  6.5 0.0 copy-start.2
  6.5 0.0 copy-start.3
  6.5 0.0 reduce-scatter.4.cloned.1.call-start
  6.5 0.0 copy-start
  6.6 32.6 %all_gather.18 = bf16[4,8192]{1,0:T(4,128)(2,1)S(1)} all-gather(bf16[4,1024]{1,0:T(4,128)(2,1)} %param.9), channel_id=1, replica_groups=mesh['groups'=2,'section'=2,'tensor'=8] {'tensor'}, dimensions={1}, use_global_device_ids=true | all-gather | bytes 73728 | tf_op jit(solution)/shard_map/all_gather | solution.py:68
  39.2 8.0 %convolution_convert_fusion = bf16[4,1024]{1,0:T(4,128)(2,1)S(1)} fusion(bf16[4,8192]{1,0:T(4,128)(2,1)S(1)} %all_gather.18, bf16[8192,1024]{1,0:T(8,128)(2,1)} %param.10), kind=kOutput, calls=%fused_computation.17 | convolution fusion | flops 67112960 | bytes 16850944 | tf_op jit(solution)/shard_map/dot_general | solution.py:69
  47.2 30.5 %all_gather.19 = bf16[4,8192]{1,0:T(4,128)(2,1)S(1)} all-gather(bf16[4,1024]{1,0:T(4,128)(2,1)S(1)} %convolution_convert_fusion), channel_id=1, replica_groups=mesh['groups'=2,'section'=2,'tensor'=8] {'tensor'}, dimensions={1}, use_global_device_ids=true | all-gather | bytes 73728 | tf_op jit(solution)/shard_map/all_gather | solution.py:70
  77.7 0.0 copy-done.1
  77.7 1.1 slice_bitcast_fusion
  78.8 0.0 copy-done
  78.8 0.2 fusion.38
  79.0 0.7 copy.24
  79.7 0.0 copy-done.2
  79.7 0.1 broadcast_compare_fusion
  79.8 0.0 copy-done.3
  79.8 0.1 broadcast_compare_fusion.1
  79.9 1.5 fusion.40
  81.4 0.5 fusion.39
  81.8 0.1 convert_element_type.119
  81.9 20.5 %all_gather.21 = bf16[8,4,64]{2,1,0:T(4,128)(2,1)S(1)} all-gather(bf16[1,4,64]{2,1,0:T(4,128)(2,1)S(1)} %convert_element_type.119), channel_id=1, replica_groups=mesh['groups'=2,'section'=2,'tensor'=8] {'tensor'}, dimensions={0}, use_global_device_ids=true | all-gather | bytes 4608 | tf_op jit(solution)/shard_map/all_gather | solution.py:13
  102.4 0.2 fusion.13
  102.6 0.2 fusion.11
  102.8 0.1 convert_element_type.123
  102.9 16.3 %all_gather.22 = bf16[8,4,64]{2,1,0:T(4,128)(2,1)S(1)} all-gather(bf16[1,4,64]{2,1,0:T(4,128)(2,1)S(1)} %convert_element_type.123), channel_id=1, replica_groups=mesh['groups'=2,'section'=2,'tensor'=8] {'tensor'}, dimensions={0}, use_global_device_ids=true | all-gather | bytes 4608 | tf_op jit(solution)/shard_map/all_gather | solution.py:13
  119.2 0.7 copy.25
  119.9 0.7 fusion.16
  120.6 1.4 fusion.6
  121.9 31.2 %all_gather.20 = bf16[8,4,64,128]{3,2,1,0:T(8,128)(2,1)S(1)} all-gather(bf16[1,4,64,128]{3,2,1,0:T(8,128)(2,1)S(1)} %fusion.6), channel_id=1, replica_groups=mesh['groups'=2,'section'=2,'tensor'=8] {'tensor'}, dimensions={0}, use_global_device_ids=true | all-gather | bytes 589824 | tf_op jit(solution)/shard_map/all_gather | solution.py:13
  153.1 1.5 while.19
  153.2 0.2 fusion.49
  153.4 0.2 fusion.49
  153.6 0.2 fusion.49
  153.8 0.2 fusion.49
  154.1 0.2 fusion.49
  154.3 0.2 fusion.49
  154.5 0.2 fusion.49
  154.7 0.1 constant_dynamic-slice_fusion.1
  154.8 0.1 fusion.31
  154.8 12.1 %convolution_bitcast_fusion = f32[8192,4]{1,0:T(8,128)} fusion(bf16[1024,8192]{1,0:T(8,128)(2,1)} %param.11, bf16[1,4,8,128]{3,2,1,0:T(8,128)(2,1)S(1)} %fusion.31), kind=kOutput, calls=%fused_computation.9 | convolution fusion | flops 67108864 | bytes 16916480
  166.9 0.0 reduce-scatter.4.cloned.1.call-update
  166.9 86.7 %reduce-scatter.4.cloned.1.call-done = f32[1024,4]{1,0:T(8,128)} async-done(((f32[8192,4]{1,0:T(8,128)}), f32[1024,4]{1,0:T(8,128)}) %reduce-scatter.4.cloned.1.call-update) | async-done | bytes 16400
  253.7 1.8 copy.23
  (14 shorter events, 0.2 us)
Async XLA Ops:
  6.5 71.2 %copy-start.1 = (bf16[4,64,2048]{2,1,0:T(8,128)(2,1)S(1)}, bf16[4,64,2048]{2,1,0:T(8,128)(2,1)}, u32[]{:S(2)}) copy-start(bf16[4,64,2048]{2,1,0:T(8,128)(2,1)} %param.13) | copy-start | bytes 3145732
  6.5 73.2 %copy-start.2 = (s32[4]{0:T(128)S(1)}, s32[4]{0:T(128)}, u32[]{:S(2)}) copy-start(s32[4]{0:T(128)} %param.15) | copy-start | bytes 52
  6.5 73.3 %copy-start.3 = (s32[4]{0:T(128)S(1)}, s32[4]{0:T(128)}, u32[]{:S(2)}) copy-start(s32[4]{0:T(128)} %param.14) | copy-start | bytes 52
  6.5 247.1 %reduce-scatter.4.cloned.1.call-start = ((), (), s32[]{:S(2)}) async-start(), calls=%async_computation.1 | async-start | bytes 4718592
  6.5 72.3 %copy-start = (bf16[4,128,2048]{2,1,0:T(8,128)(2,1)S(1)}, bf16[4,128,2048]{2,1,0:T(8,128)(2,1)}, u32[]{:S(2)}) copy-start(bf16[4,128,2048]{2,1,0:T(8,128)(2,1)} %param.12) | copy-start | bytes 6291460
Sparse Core Ops, SparseCore 0:
  167.0 86.5 reduce-scatter.3
where the time goes:
time: 263 us; the launch traced here: 262 us
  blocking collectives  131 us (50%)
  waiting for transfers between devices  86.8 us (33%)
  matrix products  24.1 us (9%)
  between operations  13.5 us (5%)
  local copies, waits for them, and re-layouts  4.71 us (2%)
    unnamed x2, waiting for transfers between devices  86.8 us
    all_gather x3, blocking collectives, combined_all(): lax.all_gather(a.astype(kind), axis)  67.9 us
    all_gather x1, blocking collectives, body(): whole = lax.all_gather(hidden, 'tensor', axis=1, tiled=True)  32.6 us
    all_gather x1, blocking collectives, body(): lax.all_gather(query_own, 'tensor', axis=1, tiled=True)  30.5 us
    unnamed x1, matrix products  12.1 us
    dot_general x1, matrix products, body(): jnp.dot(whole, w_query, preferred_element_type=jnp.float32)  8.04 us
  transfers between devices with their start and end apart: 1, of which 1 were waited for; matrix products, arithmetic and copies ran while one was open for 0% of the time, Pallas kernels for 0%

commit v1 on v0

v1 whole, which is shorter than its diff:
```python
import jax
import jax.numpy as jnp
from jax import lax
from jax.sharding import PartitionSpec as P

KVH = 8
HD = 128


def exchange(x, axis):
    return lax.all_to_all(x, axis, 0, 0, tiled=True)


def pieces(x, count):
    out = []
    for _ in range(count):
        part = x.astype(jnp.bfloat16)
        out.append(part)
        x = x - part.astype(jnp.float32)
    return out


def body(hidden, w_query, w_output, cache, fresh, cache_lengths, new_lengths):
    rows, feat = hidden.shape
    n = lax.axis_size("tensor")
    width = KVH * HD
    index = lax.axis_index("tensor")
    whole = exchange(jnp.broadcast_to(hidden[None], (n, rows, feat)), "tensor")
    whole = whole.transpose(1, 0, 2).reshape(rows, n * feat)
    own = jnp.dot(whole, w_query, preferred_element_type=jnp.float32).astype(jnp.bfloat16)
    cols = own.shape[1]
    q = exchange(jnp.broadcast_to(own[None], (n, rows, cols)), "tensor")
    q = q.transpose(1, 0, 2).reshape(rows, KVH, n * cols // width, HD)
    heads = KVH * q.shape[2]
    both = jnp.concatenate([cache, fresh], axis=1)
    cc, fc = cache.shape[1], fresh.shape[1]
    pos = jnp.concatenate([index * cc + jnp.arange(cc), index * fc + jnp.arange(fc)])
    limit = jnp.where(
        jnp.arange(cc + fc)[None, :] < cc, cache_lengths[:, None], new_lengths[:, None]
    )
    valid = (pos[None, :] < limit)[:, None, None, :]
    keys = both[:, :, :width].reshape(rows, cc + fc, KVH, HD)
    vals = both[:, :, width:].reshape(rows, cc + fc, KVH, HD)
    s = jnp.einsum("rkgd,rtkd->rkgt", q, keys, preferred_element_type=jnp.float32)
    s = jnp.where(valid, s * HD**-0.5, -1e30)
    top = jnp.max(s, axis=3, keepdims=True)
    w = jnp.where(valid, jnp.exp(s - top), 0.0)
    total = jnp.sum(w, axis=3, keepdims=True)
    num = jnp.einsum(
        "rkgt,rtkd->rkgd", w.astype(jnp.bfloat16), vals, preferred_element_type=jnp.float32
    )
    num = num.astype(jnp.bfloat16).reshape(rows, heads, HD)
    stats = jnp.concatenate(pieces(top, 3) + pieces(total, 2), axis=3).reshape(rows, heads, 5)
    stats = jnp.pad(stats, ((0, 0), (0, 0), (0, HD - 5)))
    pay = jnp.concatenate([num, stats], axis=2).reshape(rows, n, heads // n, 2 * HD)
    got = exchange(pay.transpose(1, 0, 2, 3), "tensor").astype(jnp.float32)
    tops = got[..., HD] + got[..., HD + 1] + got[..., HD + 2]
    sums = got[..., HD + 3] + got[..., HD + 4]
    scale = jnp.exp(tops - jnp.max(tops, axis=0))
    num = jnp.sum(got[..., :HD] * scale[..., None], axis=0)
    den = jnp.sum(sums * scale, axis=0)
    context = (num / den[..., None]).astype(jnp.bfloat16).reshape(rows, heads // n * HD)
    terms = jnp.dot(context, w_output, preferred_element_type=jnp.float32)
    terms = terms.astype(jnp.bfloat16).reshape(rows, n, -1).transpose(1, 0, 2)
    return jnp.sum(exchange(terms, "tensor").astype(jnp.float32), axis=0).astype(jnp.bfloat16)


def solution(mesh):
    return jax.shard_map(
        body,
        mesh=mesh,
        in_specs=(
            P(("groups", "section"), "tensor"),
            P(None, "tensor"),
            P("tensor", None),
            P(("groups", "section"), "tensor", None),
            P(("groups", "section"), "tensor", None),
            P(("groups", "section")),
            P(("groups", "section")),
        ),
        out_specs=P(("groups", "section"), "tensor"),
        check_vma=False,
    )
```

time: 263 us -> 67.3 us (0.26)
  blocking collectives: 131 us -> 19 us
  waiting for transfers between devices: 86.8 us -> 11 us
  between operations: 13.5 us -> 0.18 us
  starting transfers between devices: 0.01 us -> 10.6 us
  matrix products: 24.1 us -> 17.7 us
    all_gather x5 -> x0, blocking collectives: 131 us -> none  [the longest x3 67.9 us: combined_all(): lax.all_gather(a.astype(kind), axis)]
    unnamed x2 -> x0, waiting for transfers between devices: 86.8 us -> none
    all_to_all x0 -> x2, blocking collectives: none -> 19 us  [exchange(): return lax.all_to_all(x, axis, 0, 0, tiled=True)]
    unnamed x1 -> x0, matrix products: 12.1 us -> none
    all_to_all x0 -> x2, waiting for transfers between devices: none -> 11 us  [exchange(): return lax.all_to_all(x, axis, 0, 0, tiled=True)]
    all_to_all x0 -> x2, starting transfers between devices: none -> 10.6 us  [exchange(): return lax.all_to_all(x, axis, 0, 0, tiled=True)]
    dot_general x4 -> x3, matrix products: 4.02 us -> 9.6 us  [the longest x1 8.06 us: body(): terms = jnp.dot(context, w_output, preferred_element_type=jnp.float32)]
  transfers between devices with their start and end apart: 1 -> 2, of which waited for: 1 -> 2; matrix products, arithmetic and copies ran while one was open for 0% -> 4% of each run, Pallas kernels for 0% -> 0%
where the time goes in v1:
time: 67.3 us; the launch traced here: 66.8 us
  blocking collectives  19 us (28%)
  matrix products  17.7 us (26%)
  waiting for transfers between devices  11 us (16%)
  starting transfers between devices  10.6 us (16%)
  local copies, waits for them, and re-layouts  6.3 us (9%)
  other arithmetic  2.06 us (3%)
    all_to_all x2, blocking collectives, exchange(): return lax.all_to_all(x, axis, 0, 0, tiled=True)  19 us
    all_to_all x2, waiting for transfers between devices, exchange(): return lax.all_to_all(x, axis, 0, 0, tiled=True)  11 us
    all_to_all x2, starting transfers between devices, exchange(): return lax.all_to_all(x, axis, 0, 0, tiled=True)  10.6 us
    dot_general x1, matrix products, body(): jnp.dot(whole, w_query, preferred_element_type=jnp.float32)  8.06 us
    dot_general x1, matrix products, body(): terms = jnp.dot(context, w_output, preferred_element_type=jnp.float32)  8.06 us
    unnamed x9, local copies, waits for them, and re-layouts  2.67 us
    broadcast_in_dim x1, local copies, waits for them, and re-layouts, body(): whole = exchange(jnp.broadcast_to(hidden[None], (n, rows, feat)), 'tensor')  1.42 us
  transfers between devices with their start and end apart: 2, of which 2 were waited for; matrix products, arithmetic and copies ran while one was open for 4% of the time, Pallas kernels for 0%

profile of v1, /device:TPU:0, one launch (start us, length us, event | category | flops | bytes accessed | tf_op | source)
XLA Modules:
  0.0 66.8 jit_solution(531070036019862325)
XLA Ops:
  0.0 0.0 copy-start
  0.0 1.4 %broadcast_in_dim.68 = bf16[8,4,1024]{2,1,0:T(4,128)(2,1)} broadcast(bf16[4,1024]{1,0:T(4,128)(2,1)} %param.7), dimensions={1,2} | broadcast | bytes 73728 | tf_op jit(solution)/shard_map/broadcast_in_dim | solution.py:28
  1.4 7.3 %all-to-all-start = ((bf16[8,4,1024]{2,1,0:T(4,128)(2,1)}), bf16[8,4,1024]{2,1,0:T(4,128)(2,1)S(1)}, u32[]{:S(2)}, u32[]{:S(2)}) async-start(bf16[8,4,1024]{2,1,0:T(4,128)(2,1)} %broadcast_in_dim.68), calls=%async_computation | async-start | bytes 131072 | tf_op jit(solution)/shard_map/all_to_all | solution.py:11
  8.7 1.8 %constant_dynamic-update-slice_fusion.1 = bf16[4,192,2048]{2,1,0:T(8,128)(2,1)S(1)} fusion(bf16[4,128,2048]{2,1,0:T(8,128)(2,1)} %param.10), kind=kLoop, calls=%fused_computation.31 | loop fusion | bytes 4194304
  10.6 0.0 copy-done
  10.6 0.1 constant_dynamic-update-slice_fusion
  10.6 0.7 %slice_bitcast_fusion = (bf16[4,24,8,8,128]{4,3,2,1,0:T(8,128)(2,1)S(1)}, bf16[4,24,8,8,128]{4,3,2,1,0:T(8,128)(2,1)S(1)}) fusion(bf16[4,192,2048]{2,1,0:T(8,128)(2,1)S(1)} %constant_dynamic-update-slice_fusion), kind=kLoop, calls=%fused_computation.9 | loop fusion | bytes 6291456
  11.4 4.2 %all-to-all-done = bf16[8,4,1024]{2,1,0:T(4,128)(2,1)S(1)} async-done(((bf16[8,4,1024]{2,1,0:T(4,128)(2,1)}), bf16[8,4,1024]{2,1,0:T(4,128)(2,1)S(1)}, u32[]{:S(2)}, u32[]{:S(2)}) %all-to-all-start) | async-done | bytes 65568 | tf_op jit(solution)/shard_map/all_to_all | solution.py:11
  15.6 0.0 copy-start.1
  15.6 0.0 copy-start.2
  15.6 8.1 %convolution_convert_fusion.1 = bf16[4,1024]{1,0:T(4,128)(2,1)S(1)} fusion(bf16[4,8192]{1,0:T(4,128)(2,1)S(1)} %bitcast.53, bf16[8192,1024]{1,0:T(8,128)(2,1)} %param.8), kind=kOutput, calls=%fused_computation.14 | convolution fusion | flops 67112960 | bytes 16850944 | tf_op jit(solution)/shard_map/dot_general | solution.py:30
  23.7 0.6 broadcast_in_dim.69
  24.3 3.3 %all-to-all-start.1 = ((bf16[8,4,1024]{2,1,0:T(4,128)(2,1)}), bf16[8,4,1024]{2,1,0:T(4,128)(2,1)S(1)}, u32[]{:S(2)}, u32[]{:S(2)}) async-start(bf16[8,4,1024]{2,1,0:T(4,128)(2,1)} %broadcast_in_dim.69), calls=%async_computation.1 | async-start | bytes 131072 | tf_op jit(solution)/shard_map/all_to_all | solution.py:11
  27.7 0.0 copy-done.1
  27.7 0.0 copy-done.2
  27.7 0.1 select_compare_fusion
  27.8 6.7 %all-to-all-done.1 = bf16[8,4,1024]{2,1,0:T(4,128)(2,1)S(1)} async-done(((bf16[8,4,1024]{2,1,0:T(4,128)(2,1)}), bf16[8,4,1024]{2,1,0:T(4,128)(2,1)S(1)}, u32[]{:S(2)}, u32[]{:S(2)}) %all-to-all-start.1) | async-done | bytes 65568 | tf_op jit(solution)/shard_map/all_to_all | solution.py:11
  34.6 1.0 %fusion.33 = (f32[4,8,8]{2,1,0:T(8,128)S(1)}, f32[4,8,8,192]{3,2,1,0:T(8,128)S(1)}) fusion(bf16[4,24,8,8,128]{4,3,2,1,0:T(8,128)(2,1)S(1)} %get-tuple-element.8, bf16[4,8,8,128]{3,2,0,1:T(8,128)(2,1)S(1)} %reshape.185, pred[4,192]{1,0:T(4,128)(4,1)S(1)} %select_compare_fusion), kind=kOutput, calls=%fused_computation.55 | convolution fusion | flops 12730112 | bytes 1836800 | tf_op jit(solution)/shard_map/rkgd,rtkd->rkgt/dot_general | solution.py:44
  35.5 0.1 reduce_max.21
  35.7 0.2 fusion.16
  35.9 0.1 reduce_sum.42
  36.0 0.1 copy.50
  36.2 0.6 fusion.13
  36.8 9.7 %all_to_all.20 = bf16[8,4,8,256]{3,2,1,0:T(8,128)(2,1)S(1)} all-to-all(bf16[8,4,8,256]{3,2,1,0:T(8,128)(2,1)S(1)} %copy.45), channel_id=1, replica_groups=mesh['groups'=2,'section'=2,'tensor'=8] {'tensor'}, dimensions={0} | all-to-all | bytes 262144 | tf_op jit(solution)/shard_map/all_to_all | solution.py:11
  46.5 1.2 %copy.46 = bf16[8,4,8,256]{2,0,3,1:T(8,128)(2,1)S(1)} copy(bf16[8,4,8,256]{3,2,1,0:T(8,128)(2,1)S(1)} %all_to_all.20) | data formatting | bytes 262144 | tf_op jit(solution)/shard_map/all_to_all | solution.py:11
  47.7 0.3 convert_element_type.158
  48.1 0.6 fusion
  48.7 0.1 copy.47
  48.8 0.1 fusion.29
  48.9 8.1 %convolution_convert_fusion = bf16[4,8192]{1,0:T(4,128)(2,1)S(1)} fusion(bf16[1024,8192]{1,0:T(8,128)(2,1)} %param.9, bf16[1,4,8,128]{3,2,1,0:T(8,128)(2,1)S(1)} %fusion.29), kind=kOutput, calls=%fused_computation | convolution fusion | flops 67141632 | bytes 16850944 | tf_op jit(solution)/shard_map/dot_general | solution.py:63
  56.9 9.3 %all_to_all.21 = bf16[8,4,1024]{2,1,0:T(4,128)(2,1)S(1)} all-to-all(bf16[8,4,1024]{2,1,0:T(4,128)(2,1)S(1)} %bitcast.54), channel_id=1, replica_groups=mesh['groups'=2,'section'=2,'tensor'=8] {'tensor'}, dimensions={0} | all-to-all | bytes 131072 | tf_op jit(solution)/shard_map/all_to_all | solution.py:11
  66.2 0.6 reduce_sum.45
  (16 shorter events, 0.2 us)
Async XLA Ops:
  0.0 10.6 %copy-start = (bf16[4,64,2048]{2,1,0:T(8,128)(2,1)S(1)}, bf16[4,64,2048]{2,1,0:T(8,128)(2,1)}, u32[]{:S(2)}) copy-start(bf16[4,64,2048]{2,1,0:T(8,128)(2,1)} %param.11) | copy-start | bytes 3145732
  1.4 14.2 %all-to-all-start = ((bf16[8,4,1024]{2,1,0:T(4,128)(2,1)}), bf16[8,4,1024]{2,1,0:T(4,128)(2,1)S(1)}, u32[]{:S(2)}, u32[]{:S(2)}) async-start(bf16[8,4,1024]{2,1,0:T(4,128)(2,1)} %broadcast_in_dim.68), calls=%async_computation | async-start | bytes 131072 | tf_op jit(solution)/shard_map/all_to_all | solution.py:11
  15.6 12.1 %copy-start.1 = (s32[4]{0:T(128)S(1)}, s32[4]{0:T(128)}, u32[]{:S(2)}) copy-start(s32[4]{0:T(128)} %param.13) | copy-start | bytes 52
  15.6 12.1 %copy-start.2 = (s32[4]{0:T(128)S(1)}, s32[4]{0:T(128)}, u32[]{:S(2)}) copy-start(s32[4]{0:T(128)} %param.12) | copy-start | bytes 52
  24.3 10.2 %all-to-all-start.1 = ((bf16[8,4,1024]{2,1,0:T(4,128)(2,1)}), bf16[8,4,1024]{2,1,0:T(4,128)(2,1)S(1)}, u32[]{:S(2)}, u32[]{:S(2)}) async-start(bf16[8,4,1024]{2,1,0:T(4,128)(2,1)} %broadcast_in_dim.69), calls=%async_computation.1 | async-start | bytes 131072 | tf_op jit(solution)/shard_map/all_to_all | solution.py:11

commit v2 on v1

v2 whole, which is shorter than its diff:
```python
import functools

import jax
import jax.numpy as jnp
from jax import lax
from jax.experimental import pallas as pl
from jax.experimental.pallas import tpu as pltpu
from jax.sharding import PartitionSpec as P

KVH = 8
HD = 128
GROUP = 8
F32 = jnp.float32
BF16 = jnp.bfloat16
VMEM = pl.BlockSpec(memory_space=pltpu.VMEM)
SMEM = pl.BlockSpec(memory_space=pltpu.SMEM)


def exchange(x):
    return lax.all_to_all(x, "tensor", 0, 0, tiled=True)


def dot(a, b):
    return jnp.dot(a, b, preferred_element_type=F32)


def call(kernel, shape, dtype, *args, specs=None, scratch=(), limit=8, cost=pl.CostEstimate(flops=10**12, bytes_accessed=64 << 20, transcendentals=10**9)):
    return pl.pallas_call(
        kernel,
        in_specs=specs or [VMEM] * len(args),
        out_specs=VMEM,
        out_shape=jax.ShapeDtypeStruct(shape, dtype),
        scratch_shapes=scratch,
        cost_estimate=cost,
        compiler_params=pltpu.CompilerParams(vmem_limit_bytes=limit << 20),
    )(*args)


def spread_kernel(x_ref, o_ref):
    o_ref[...] = jnp.broadcast_to(x_ref[...][None], o_ref.shape)


def query_kernel(all_ref, w_ref, o_ref, heads_ref):
    n, rows, feat = all_ref.shape
    own = w_ref.shape[1] // HD
    acc = jnp.zeros((rows, own * HD), F32)
    for t in range(n):
        acc += dot(all_ref[t], w_ref[t * feat : (t + 1) * feat, :])
    for h in range(own):
        heads_ref[pl.ds(h, rows, stride=own), :] = acc[:, h * HD : (h + 1) * HD]
    o_ref[...] = jnp.broadcast_to(heads_ref[...].astype(BF16)[None], o_ref.shape)


def attend_kernel(place_ref, clen_ref, nlen_ref, q_ref, cache_ref, fresh_ref, o_ref):
    rows, cc, width = cache_ref.shape
    width = width // 2
    fc = fresh_ref.shape[1]
    place = place_ref[0]
    lane = lax.broadcasted_iota(jnp.int32, (2 * GROUP, HD), 1)
    zero = jnp.zeros((GROUP, HD), F32)

    def logits(q, ref, r, cols, start, length):
        keys = ref[r, :, cols]
        s = lax.dot_general(q, keys, (((1,), (1,)), ((), ())), preferred_element_type=F32)
        pos = start + lax.broadcasted_iota(jnp.int32, s.shape, 1)
        valid = pos < length
        return jnp.where(valid, s * HD**-0.5, -1e30), valid

    def attend(r, pair, q):
        cols = slice(2 * pair * HD, 2 * (pair + 1) * HD)
        vals = slice(width + 2 * pair * HD, width + 2 * (pair + 1) * HD)
        sc, okc = logits(q, cache_ref, r, cols, place * cc, clen_ref[r])
        sf, okf = logits(q, fresh_ref, r, cols, place * fc, nlen_ref[r])
        top = jnp.maximum(
            jnp.max(sc, axis=1, keepdims=True), jnp.max(sf, axis=1, keepdims=True)
        )
        wc = jnp.where(okc, jnp.exp(sc - top), 0.0)
        wf = jnp.where(okf, jnp.exp(sf - top), 0.0)
        total = jnp.sum(wc, axis=1, keepdims=True) + jnp.sum(wf, axis=1, keepdims=True)
        num = dot(wc.astype(BF16), cache_ref[r, :, vals])
        num += dot(wf.astype(BF16), fresh_ref[r, :, vals])
        stats = jnp.zeros((2 * GROUP, HD), F32)
        rest = top
        for i in range(3):
            piece = rest.astype(BF16).astype(F32)
            stats = jnp.where(lane == i, piece, stats)
            rest = rest - piece
        rest = total
        for i in range(3, 6):
            piece = rest.astype(BF16).astype(F32)
            stats = jnp.where(lane == i, piece, stats)
            rest = rest - piece
        return num, stats

    for pair in range(KVH // 2):
        for two in range(rows // 2):
            at = slice(two * 2 * GROUP, (two + 1) * 2 * GROUP)
            qa = q_ref[2 * pair, at, :].astype(F32)
            qb = q_ref[2 * pair + 1, at, :].astype(F32)
            out = []
            for i in range(2):
                half = slice(i * GROUP, (i + 1) * GROUP)
                q = jnp.concatenate(
                    [
                        jnp.concatenate([qa[half], zero], axis=1),
                        jnp.concatenate([zero, qb[half]], axis=1),
                    ],
                    axis=0,
                ).astype(BF16)
                out.append(attend(2 * two + i, pair, q))
            for j in range(2):
                half = slice(j * GROUP, (j + 1) * GROUP)
                cols = slice(j * HD, (j + 1) * HD)
                num = jnp.concatenate([o[0][half, cols] for o in out], axis=0)
                stats = jnp.concatenate([o[1][half] for o in out], axis=0)
                o_ref[2 * pair + j, at, 0:HD] = num.astype(BF16)
                o_ref[2 * pair + j, at, HD : 2 * HD] = stats.astype(BF16)


def project_kernel(own, got_ref, w_ref, o_ref, heads_ref):
    n, both, _ = got_ref.shape
    rows = both // own
    line = lax.broadcasted_iota(jnp.int32, (HD, 2 * HD), 0)
    column = lax.broadcasted_iota(jnp.int32, (HD, 2 * HD), 1)
    first = jnp.where(column < HD, 0, 3)
    pick = ((line >= first) & (line < first + 3)).astype(F32).astype(BF16)
    stats = [dot(got_ref[t, :, HD : 2 * HD], pick) for t in range(n)]
    top = functools.reduce(jnp.maximum, [s[:, :HD] for s in stats])
    num = jnp.zeros((both, HD), F32)
    den = jnp.zeros((both, HD), F32)
    for t in range(n):
        scale = jnp.exp(stats[t][:, :HD] - top)
        num += got_ref[t, :, 0:HD].astype(F32) * scale
        den += stats[t][:, HD:] * scale
    heads_ref[...] = num / den
    context = jnp.concatenate(
        [heads_ref[pl.ds(h, rows, stride=own), :] for h in range(own)], axis=1
    ).astype(BF16)
    wide = o_ref.shape[2]
    for t in range(n):
        o_ref[t] = dot(context, w_ref[:, t * wide : (t + 1) * wide]).astype(BF16)


def sum_kernel(x_ref, o_ref):
    o_ref[...] = jnp.sum(x_ref[...].astype(F32), axis=0).astype(BF16)


def body(hidden, w_query, w_output, cache, fresh, cache_lengths, new_lengths):
    rows, feat = hidden.shape
    n = lax.axis_size("tensor")
    own = w_query.shape[1] // HD
    place = lax.axis_index("tensor").astype(jnp.int32).reshape(1)
    wide = w_output.shape[1] // n
    w_query = pltpu.with_memory_space_constraint(w_query, pltpu.VMEM)
    w_output = pltpu.with_memory_space_constraint(w_output, pltpu.VMEM)
    cache = pltpu.with_memory_space_constraint(cache, pltpu.VMEM)
    fresh = pltpu.with_memory_space_constraint(fresh, pltpu.VMEM)

    long = pl.CostEstimate(flops=0, bytes_accessed=64 << 20, transcendentals=0)
    x = call(spread_kernel, (n, rows, feat), BF16, hidden)
    x = exchange(x)
    q = call(
        query_kernel,
        (n, rows * own, HD),
        BF16,
        x,
        w_query,
        scratch=[pltpu.VMEM((rows * own, HD), F32)],
    )
    q = exchange(q)
    if own != GROUP:
        q = q.reshape(KVH, GROUP, rows, HD).transpose(0, 2, 1, 3).reshape(KVH, rows * GROUP, HD)
    part = call(
        attend_kernel,
        (KVH, rows * GROUP, 2 * HD),
        BF16,
        place,
        cache_lengths,
        new_lengths,
        q,
        cache,
        fresh,
        specs=[SMEM] * 3 + [VMEM] * 3,
    )
    if own != GROUP:
        part = part.reshape(KVH, rows, GROUP, 2 * HD).transpose(0, 2, 1, 3)
        part = part.reshape(n, rows * own, 2 * HD)
    part = exchange(part)
    terms = call(
        functools.partial(project_kernel, own),
        (n, rows, wide),
        BF16,
        part,
        w_output,
        scratch=[pltpu.VMEM((rows * own, HD), F32)],
    )
    terms = exchange(terms)
    return call(sum_kernel, (rows, wide), BF16, terms)


def solution(mesh):
    return jax.shard_map(
        body,
        mesh=mesh,
        in_specs=(
            P(("groups", "section"), "tensor"),
            P(None, "tensor"),
            P("tensor", None),
            P(("groups", "section"), "tensor", None),
            P(("groups", "section"), "tensor", None),
            P(("groups", "section")),
            P(("groups", "section")),
        ),
        out_specs=P(("groups", "section"), "tensor"),
        check_vma=False,
    )
```

time: 67.3 us -> 55.2 us (0.82)
  matrix products: 17.7 us -> 0 us
  blocking collectives: 19 us -> 33.4 us
  Pallas kernels: 0 us -> 10.5 us
  starting transfers between devices: 10.6 us -> 3.35 us
  local copies, waits for them, and re-layouts: 6.3 us -> 0.72 us
  waiting for transfers between devices: 11 us -> 6.84 us
  other arithmetic: 2.06 us -> 0 us
    dot_general x4 -> x0, matrix products: 17.7 us -> none  [the longest x1 8.06 us: body(): jnp.dot(whole, w_query, preferred_element_type=jnp.float32)]
    all_to_all x2 -> x3, blocking collectives: 19 us -> 33.4 us  [exchange(): return lax.all_to_all(x, 'tensor', 0, 0, tiled=True)]
    pallas_call x0 -> x5, Pallas kernels: none -> 10.5 us  [call(): pl.pallas_call(kernel, in_specs=specs or [VMEM] * len(args), out_specs=VM...]
    all_to_all x2 -> x1, starting transfers between devices: 10.6 us -> 3.35 us  [exchange(): return lax.all_to_all(x, 'tensor', 0, 0, tiled=True)]
    all_to_all x2 -> x1, waiting for transfers between devices: 11 us -> 6.84 us  [exchange(): return lax.all_to_all(x, 'tensor', 0, 0, tiled=True)]
    broadcast_in_dim x2 -> x0, local copies, waits for them, and re-layouts: 2.07 us -> none  [the longest x1 1.42 us: body(): whole = exchange(jnp.broadcast_to(hidden[None], (n, rows, feat)), 'tensor')]
    unnamed x9 -> x14, local copies, waits for them, and re-layouts: 2.67 us -> 0.72 us
    reduce_sum x4 -> x0, other arithmetic: 1.49 us -> none  [the longest x1 0.64 us: body(): jnp.sum(exchange(terms, 'tensor').astype(jnp.float32), axis=0)]
  transfers between devices with their start and end apart: 2 -> 1, of which waited for: 2 -> 1; matrix products, arithmetic and copies ran while one was open for 4% -> 0% of each run, Pallas kernels for 0% -> 0%
where the time goes in v2:
time: 55.2 us; the launch traced here: 54.8 us
  blocking collectives  33.4 us (61%)
  Pallas kernels  10.5 us (19%)
  waiting for transfers between devices  6.84 us (12%)
  starting transfers between devices  3.35 us (6%)
  local copies, waits for them, and re-layouts  0.72 us (1%)
    all_to_all x3, blocking collectives, exchange(): return lax.all_to_all(x, 'tensor', 0, 0, tiled=True)  33.4 us
    pallas_call x5, Pallas kernels, call(): pl.pallas_call(kernel, in_specs=specs or [VMEM] * len(args), out_specs=VM...  10.5 us
    all_to_all x1, waiting for transfers between devices, exchange(): return lax.all_to_all(x, 'tensor', 0, 0, tiled=True)  6.84 us
    all_to_all x1, starting transfers between devices, exchange(): return lax.all_to_all(x, 'tensor', 0, 0, tiled=True)  3.35 us
  transfers between devices with their start and end apart: 1, of which 1 were waited for; matrix products, arithmetic and copies ran while one was open for 0% of the time, Pallas kernels for 0%

profile of v2, /device:TPU:0, one launch (start us, length us, event | category | flops | bytes accessed | tf_op | source)
XLA Modules:
  0.0 54.8 jit_solution(453224176194849626)
XLA Ops:
  0.0 0.0 copy-start.4
  0.0 0.7 %copy-done.4 = bf16[4,1024]{1,0:T(4,128)(2,1)S(1)} copy-done((bf16[4,1024]{1,0:T(4,128)(2,1)S(1)}, bf16[4,1024]{1,0:T(4,128)(2,1)}, u32[]{:S(2)}) %copy-start.4) | copy-done | bytes 8216
  0.7 0.0 copy-start
  0.7 14.2 %all_to_all.20.all_ref = bf16[8,4,1024]{2,1,0:T(4,128)(2,1)S(1)} all-to-all(bf16[8,4,1024]{2,1,0:T(4,128)(2,1)S(1)} %shard_map.73), channel_id=1, replica_groups=mesh['groups'=2,'section'=2,'tensor'=8] {'tensor'}, dimensions={0} | all-to-all | bytes 131072 | tf_op jit(solution)/shard_map/all_to_all | solution.py:20
  14.9 0.0 copy-done
  15.0 0.0 copy-start.2
  15.0 0.0 copy-start.3
  15.0 0.0 copy-start.5
  15.0 0.0 copy-start.6
  15.0 2.9 %shard_map.74 = bf16[8,32,128]{2,1,0:T(8,128)(2,1)} custom-call(bf16[8,4,1024]{2,1,0:T(4,128)(2,1)S(1)} %all_to_all.20.all_ref, bf16[8192,1024]{1,0:T(8,128)(2,1)S(1)} %copy-done), custom_call_target="tpu_custom_call" | custom-call | flops 999999995904 | bytes 67108864 | tf_op jit(solution)/shard_map/pallas_call | solution.py:28
  17.9 3.3 %all-to-all-start.1 = ((bf16[8,32,128]{2,1,0:T(8,128)(2,1)}), bf16[8,32,128]{2,1,0:T(8,128)(2,1)S(1)}, u32[]{:S(2)}, u32[]{:S(2)}) async-start(bf16[8,32,128]{2,1,0:T(8,128)(2,1)} %shard_map.74), calls=%async_computation.1 | async-start | bytes 131072 | tf_op jit(solution)/shard_map/all_to_all | solution.py:20
  21.3 6.8 %all-to-all-done.1.q_ref = bf16[8,32,128]{2,1,0:T(8,128)(2,1)S(1)} async-done(((bf16[8,32,128]{2,1,0:T(8,128)(2,1)}), bf16[8,32,128]{2,1,0:T(8,128)(2,1)S(1)}, u32[]{:S(2)}, u32[]{:S(2)}) %all-to-all-start.1) | async-done | bytes 65568 | tf_op jit(solution)/shard_map/all_to_all | solution.py:20
  28.1 0.0 copy-done.2
  28.1 0.0 copy-done.3
  28.1 0.0 copy-done.5
  28.1 0.0 copy-done.6
  28.1 0.0 copy-start.1
  28.1 4.5 %shard_map.75 = bf16[8,32,256]{2,1,0:T(8,128)(2,1)S(1)} custom-call(s32[1]{0:T(128)} %bitcast.place_ref, s32[4]{0:T(128)S(1)} %copy-done.5, s32[4]{0:T(128)S(1)} %copy-done.6, bf16[8,32,128]{2,1,0:T(8,128)(2,1)S(1)} %all-to-all-done.1.q_ref, bf16[4,128,2048]{2,1,0:T(8,128)(2,1)S(1)} %copy-done.2, bf16[4,64,2048]{2,1,0:T(8,128)(2,1)S(1)} %copy-done.3), custom_call_target="tpu_custom_call" | custom-call | flops 999999995904 | bytes 67108864 | tf_op jit(solution)/shard_map/pallas_call | solution.py:28
  32.6 9.9 %all_to_all.21.got_ref = bf16[8,32,256]{2,1,0:T(8,128)(2,1)S(1)} all-to-all(bf16[8,32,256]{2,1,0:T(8,128)(2,1)S(1)} %shard_map.75), channel_id=1, replica_groups=mesh['groups'=2,'section'=2,'tensor'=8] {'tensor'}, dimensions={0} | all-to-all | bytes 262144 | tf_op jit(solution)/shard_map/all_to_all | solution.py:20
  42.5 0.0 copy-done.1
  42.5 2.5 %shard_map.76 = bf16[8,4,1024]{2,1,0:T(4,128)(2,1)S(1)} custom-call(bf16[8,32,256]{2,1,0:T(8,128)(2,1)S(1)} %all_to_all.21.got_ref, bf16[1024,8192]{1,0:T(8,128)(2,1)S(1)} %copy-done.1), custom_call_target="tpu_custom_call" | custom-call | flops 999999995904 | bytes 67108864 | tf_op jit(solution)/shard_map/pallas_call | solution.py:28
  44.9 9.3 %all_to_all.22.x_ref = bf16[8,4,1024]{2,1,0:T(4,128)(2,1)S(1)} all-to-all(bf16[8,4,1024]{2,1,0:T(4,128)(2,1)S(1)} %shard_map.76), channel_id=1, replica_groups=mesh['groups'=2,'section'=2,'tensor'=8] {'tensor'}, dimensions={0} | all-to-all | bytes 131072 | tf_op jit(solution)/shard_map/all_to_all | solution.py:20
  54.2 0.6 %shard_map.77 = bf16[4,1024]{1,0:T(4,128)(2,1)} custom-call(bf16[8,4,1024]{2,1,0:T(4,128)(2,1)S(1)} %all_to_all.22.x_ref), custom_call_target="tpu_custom_call" | custom-call | flops 999999995904 | bytes 67108864 | tf_op jit(solution)/shard_map/pallas_call | solution.py:28
  (1 shorter events, 0.0 us)
Async XLA Ops:
  0.0 0.7 %copy-start.4 = (bf16[4,1024]{1,0:T(4,128)(2,1)S(1)}, bf16[4,1024]{1,0:T(4,128)(2,1)}, u32[]{:S(2)}) copy-start(bf16[4,1024]{1,0:T(4,128)(2,1)} %x_ref.1) | copy-start | bytes 24580
  0.7 14.3 %copy-start = (bf16[8192,1024]{1,0:T(8,128)(2,1)S(1)}, bf16[8192,1024]{1,0:T(8,128)(2,1)}, u32[]{:S(2)}) copy-start(bf16[8192,1024]{1,0:T(8,128)(2,1)} %w_ref.2) | copy-start | bytes 50331652
  15.0 13.1 %copy-start.2 = (bf16[4,128,2048]{2,1,0:T(8,128)(2,1)S(1)}, bf16[4,128,2048]{2,1,0:T(8,128)(2,1)}, u32[]{:S(2)}) copy-start(bf16[4,128,2048]{2,1,0:T(8,128)(2,1)} %cache_ref.1) | copy-start | bytes 6291460
  15.0 13.1 %copy-start.3 = (bf16[4,64,2048]{2,1,0:T(8,128)(2,1)S(1)}, bf16[4,64,2048]{2,1,0:T(8,128)(2,1)}, u32[]{:S(2)}) copy-start(bf16[4,64,2048]{2,1,0:T(8,128)(2,1)} %fresh_ref.1) | copy-start | bytes 3145732
  15.0 13.1 %copy-start.5 = (s32[4]{0:T(128)S(1)}, s32[4]{0:T(128)}, u32[]{:S(2)}) copy-start(s32[4]{0:T(128)} %clen_ref.1) | copy-start | bytes 52
  15.0 13.1 %copy-start.6 = (s32[4]{0:T(128)S(1)}, s32[4]{0:T(128)}, u32[]{:S(2)}) copy-start(s32[4]{0:T(128)} %nlen_ref.1) | copy-start | bytes 52
  17.9 10.2 %all-to-all-start.1 = ((bf16[8,32,128]{2,1,0:T(8,128)(2,1)}), bf16[8,32,128]{2,1,0:T(8,128)(2,1)S(1)}, u32[]{:S(2)}, u32[]{:S(2)}) async-start(bf16[8,32,128]{2,1,0:T(8,128)(2,1)} %shard_map.74), calls=%async_computation.1 | async-start | bytes 131072 | tf_op jit(solution)/shard_map/all_to_all | solution.py:20
  28.1 14.4 %copy-start.1 = (bf16[1024,8192]{1,0:T(8,128)(2,1)S(1)}, bf16[1024,8192]{1,0:T(8,128)(2,1)}, u32[]{:S(2)}) copy-start(bf16[1024,8192]{1,0:T(8,128)(2,1)} %w_ref.3) | copy-start | bytes 50331652

commit v3 on v2

--- a/solution.py
+++ b/solution.py
@@ -51,70 +51,62 @@
     o_ref[...] = jnp.broadcast_to(heads_ref[...].astype(BF16)[None], o_ref.shape)
 
 
-def attend_kernel(place_ref, clen_ref, nlen_ref, q_ref, cache_ref, fresh_ref, o_ref):
+def attend_kernel(clen_ref, nlen_ref, q_ref, cache_ref, fresh_ref, o_ref):
     rows, cc, width = cache_ref.shape
     width = width // 2
     fc = fresh_ref.shape[1]
-    place = place_ref[0]
-    lane = lax.broadcasted_iota(jnp.int32, (2 * GROUP, HD), 1)
-    zero = jnp.zeros((GROUP, HD), F32)
-
-    def logits(q, ref, r, cols, start, length):
-        keys = ref[r, :, cols]
-        s = lax.dot_general(q, keys, (((1,), (1,)), ((), ())), preferred_element_type=F32)
-        pos = start + lax.broadcasted_iota(jnp.int32, s.shape, 1)
-        valid = pos < length
+    heads = KVH * GROUP
+    place = lax.axis_index("tensor")
+    head_of = lax.broadcasted_iota(jnp.int32, (heads, width), 0) // GROUP
+    diagonal = head_of == lax.broadcasted_iota(jnp.int32, (heads, width), 1) // HD
+
+    def logits(ref, r, wide, start, length):
+        s = lax.dot_general(
+            ref[r, :, 0:width], wide, (((1,), (1,)), ((), ())), preferred_element_type=F32
+        )
+        valid = start + lax.broadcasted_iota(jnp.int32, s.shape, 0) < length
         return jnp.where(valid, s * HD**-0.5, -1e30), valid
 
-    def attend(r, pair, q):
-        cols = slice(2 * pair * HD, 2 * (pair + 1) * HD)
-        vals = slice(width + 2 * pair * HD, width + 2 * (pair + 1) * HD)
-        sc, okc = logits(q, cache_ref, r, cols, place * cc, clen_ref[r])
-        sf, okf = logits(q, fresh_ref, r, cols, place * fc, nlen_ref[r])
+    def attend(r, q):
+        wide = jnp.where(diagonal, jnp.concatenate([q] * KVH, axis=1), 0.0).astype(BF16)
+        sc, okc = logits(cache_ref, r, wide, place * cc, clen_ref[r])
+        sf, okf = logits(fresh_ref, r, wide, place * fc, nlen_ref[r])
         top = jnp.maximum(
-            jnp.max(sc, axis=1, keepdims=True), jnp.max(sf, axis=1, keepdims=True)
+            jnp.max(sc, axis=0, keepdims=True), jnp.max(sf, axis=0, keepdims=True)
         )
         wc = jnp.where(okc, jnp.exp(sc - top), 0.0)
         wf = jnp.where(okf, jnp.exp(sf - top), 0.0)
-        total = jnp.sum(wc, axis=1, keepdims=True) + jnp.sum(wf, axis=1, keepdims=True)
-        num = dot(wc.astype(BF16), cache_ref[r, :, vals])
-        num += dot(wf.astype(BF16), fresh_ref[r, :, vals])
-        stats = jnp.zeros((2 * GROUP, HD), F32)
-        rest = top
-        for i in range(3):
-            piece = rest.astype(BF16).astype(F32)
-            stats = jnp.where(lane == i, piece, stats)
-            rest = rest - piece
-        rest = total
-        for i in range(3, 6):
-            piece = rest.astype(BF16).astype(F32)
-            stats = jnp.where(lane == i, piece, stats)
-            rest = rest - piece
-        return num, stats
-
-    for pair in range(KVH // 2):
-        for two in range(rows // 2):
-            at = slice(two * 2 * GROUP, (two + 1) * 2 * GROUP)
-            qa = q_ref[2 * pair, at, :].astype(F32)
-            qb = q_ref[2 * pair + 1, at, :].astype(F32)
-            out = []
-            for i in range(2):
-                half = slice(i * GROUP, (i + 1) * GROUP)
-                q = jnp.concatenate(
-                    [
-                        jnp.concatenate([qa[half], zero], axis=1),
-                        jnp.concatenate([zero, qb[half]], axis=1),
-                    ],
-                    axis=0,
-                ).astype(BF16)
-                out.append(attend(2 * two + i, pair, q))
-            for j in range(2):
-                half = slice(j * GROUP, (j + 1) * GROUP)
-                cols = slice(j * HD, (j + 1) * HD)
-                num = jnp.concatenate([o[0][half, cols] for o in out], axis=0)
-                stats = jnp.concatenate([o[1][half] for o in out], axis=0)
-                o_ref[2 * pair + j, at, 0:HD] = num.astype(BF16)
-                o_ref[2 * pair + j, at, HD : 2 * HD] = stats.astype(BF16)
+        total = jnp.sum(wc, axis=0, keepdims=True) + jnp.sum(wf, axis=0, keepdims=True)
+        stats = []
+        for rest in (top, total):
+            for _ in range(3):
+                piece = rest.astype(BF16).astype(F32)
+                stats.append(piece)
+                rest = rest - piece
+        stats = jnp.concatenate(stats + [jnp.zeros((HD - 6, heads), F32)], axis=0)
+        pc = wc.T.astype(BF16)
+        pf = wf.T.astype(BF16)
+        nums = []
+        for pair in range(KVH // 2):
+            at = slice(2 * pair * GROUP, 2 * (pair + 1) * GROUP)
+            vals = slice(width + 2 * pair * HD, width + 2 * (pair + 1) * HD)
+            num = dot(pc[at], cache_ref[r, :, vals]) + dot(pf[at], fresh_ref[r, :, vals])
+            nums += [num[:GROUP, :HD], num[GROUP:, HD:]]
+        return nums, stats.T
+
+    for two in range(rows // 2):
+        at = slice(two * 2 * GROUP, (two + 1) * 2 * GROUP)
+        both = [q_ref[g, at, :].astype(F32) for g in range(KVH)]
+        out = []
+        for i in range(2):
+            half = slice(i * GROUP, (i + 1) * GROUP)
+            out.append(attend(2 * two + i, jnp.concatenate([q[half] for q in both], axis=0)))
+        for g in range(KVH):
+            half = slice(g * GROUP, (g + 1) * GROUP)
+            num = jnp.concatenate([o[0][g] for o in out], axis=0)
+            stats = jnp.concatenate([o[1][half] for o in out], axis=0)
+            o_ref[g, at, 0:HD] = num.astype(BF16)
+            o_ref[g, at, HD : 2 * HD] = stats.astype(BF16)
 
 
 def project_kernel(own, got_ref, w_ref, o_ref, heads_ref):
@@ -149,7 +141,6 @@
     rows, feat = hidden.shape
     n = lax.axis_size("tensor")
     own = w_query.shape[1] // HD
-    place = lax.axis_index("tensor").astype(jnp.int32).reshape(1)
     wide = w_output.shape[1] // n
     w_query = pltpu.with_memory_space_constraint(w_query, pltpu.VMEM)
     w_output = pltpu.with_memory_space_constraint(w_output, pltpu.VMEM)
@@ -174,13 +165,12 @@
         attend_kernel,
         (KVH, rows * GROUP, 2 * HD),
         BF16,
-        place,
         cache_lengths,
         new_lengths,
         q,
         cache,
         fresh,
-        specs=[SMEM] * 3 + [VMEM] * 3,
+        specs=[SMEM] * 2 + [VMEM] * 3,
     )
     if own != GROUP:
         part = part.reshape(KVH, rows, GROUP, 2 * HD).transpose(0, 2, 1, 3)

time: 55.2 us -> 51.9 us (0.940)
  blocking collectives: 33.4 us -> 43.1 us
  waiting for transfers between devices: 6.84 us -> 0 us
  starting transfers between devices: 3.35 us -> 0 us
  Pallas kernels: 10.5 us -> 7.76 us
    all_to_all x3 -> x4, blocking collectives: 33.4 us -> 43.1 us  [exchange(): return lax.all_to_all(x, 'tensor', 0, 0, tiled=True)]
    all_to_all x1 -> x0, waiting for transfers between devices: 6.84 us -> none  [exchange(): return lax.all_to_all(x, 'tensor', 0, 0, tiled=True)]
    all_to_all x1 -> x0, starting transfers between devices: 3.35 us -> none  [exchange(): return lax.all_to_all(x, 'tensor', 0, 0, tiled=True)]
    pallas_call x5, Pallas kernels: 10.5 us -> 7.76 us  [call(): pl.pallas_call(kernel, in_specs=specs or [VMEM] * len(args), out_specs=VM...]
  transfers between devices with their start and end apart: 1 -> 0, of which waited for: 1 -> 0; matrix products, arithmetic and copies ran while one was open for 0% -> 0% of each run, Pallas kernels for 0% -> 0%
where the time goes in v3:
time: 51.9 us; the launch traced here: 51.6 us
  blocking collectives  43.1 us (83%)
  Pallas kernels  7.76 us (15%)
  local copies, waits for them, and re-layouts  0.72 us (1%)
    all_to_all x4, blocking collectives, exchange(): return lax.all_to_all(x, 'tensor', 0, 0, tiled=True)  43.1 us
    pallas_call x5, Pallas kernels, call(): pl.pallas_call(kernel, in_specs=specs or [VMEM] * len(args), out_specs=VM...  7.76 us

profile of v3, /device:TPU:0, one launch (start us, length us, event | category | flops | bytes accessed | tf_op | source)
XLA Modules:
  0.0 51.6 jit_solution(12253471722976208926)
XLA Ops:
  0.0 0.0 copy-start.4
  0.0 0.7 %copy-done.4 = bf16[4,1024]{1,0:T(4,128)(2,1)S(1)} copy-done((bf16[4,1024]{1,0:T(4,128)(2,1)S(1)}, bf16[4,1024]{1,0:T(4,128)(2,1)}, u32[]{:S(2)}) %copy-start.4) | copy-done | bytes 8216
  0.7 0.0 copy-start
  0.7 14.2 %all_to_all.20.all_ref = bf16[8,4,1024]{2,1,0:T(4,128)(2,1)S(1)} all-to-all(bf16[8,4,1024]{2,1,0:T(4,128)(2,1)S(1)} %shard_map.73), channel_id=1, replica_groups=mesh['groups'=2,'section'=2,'tensor'=8] {'tensor'}, dimensions={0} | all-to-all | bytes 131072 | tf_op jit(solution)/shard_map/all_to_all | solution.py:20
  14.9 0.0 copy-done
  15.0 0.0 copy-start.2
  15.0 0.0 copy-start.3
  15.0 0.0 copy-start.5
  15.0 0.0 copy-start.6
  15.0 2.3 %shard_map.74 = bf16[8,32,128]{2,1,0:T(8,128)(2,1)S(1)} custom-call(bf16[8,4,1024]{2,1,0:T(4,128)(2,1)S(1)} %all_to_all.20.all_ref, bf16[8192,1024]{1,0:T(8,128)(2,1)S(1)} %copy-done), custom_call_target="tpu_custom_call" | custom-call | flops 999999995904 | bytes 67108864 | tf_op jit(solution)/shard_map/pallas_call | solution.py:28
  17.2 9.3 %all_to_all.21.q_ref = bf16[8,32,128]{2,1,0:T(8,128)(2,1)S(1)} all-to-all(bf16[8,32,128]{2,1,0:T(8,128)(2,1)S(1)} %shard_map.74), channel_id=1, replica_groups=mesh['groups'=2,'section'=2,'tensor'=8] {'tensor'}, dimensions={0} | all-to-all | bytes 131072 | tf_op jit(solution)/shard_map/all_to_all | solution.py:20
  26.5 0.0 copy-done.2
  26.5 0.0 copy-done.3
  26.5 0.0 copy-done.5
  26.5 0.0 copy-done.6
  26.6 0.0 copy-start.1
  26.6 2.4 %shard_map.75 = bf16[8,32,256]{2,1,0:T(8,128)(2,1)S(1)} custom-call(s32[4]{0:T(128)S(1)} %copy-done.5, s32[4]{0:T(128)S(1)} %copy-done.6, bf16[8,32,128]{2,1,0:T(8,128)(2,1)S(1)} %all_to_all.21.q_ref, bf16[4,128,2048]{2,1,0:T(8,128)(2,1)S(1)} %copy-done.2, bf16[4,64,2048]{2,1,0:T(8,128)(2,1)S(1)} %copy-done.3), custom_call_target="tpu_custom_call" | custom-call | flops 999999995904 | bytes 67108864 | tf_op jit(solution)/shard_map/pallas_call | solution.py:28
  29.0 10.3 %all_to_all.22.got_ref = bf16[8,32,256]{2,1,0:T(8,128)(2,1)S(1)} all-to-all(bf16[8,32,256]{2,1,0:T(8,128)(2,1)S(1)} %shard_map.75), channel_id=1, replica_groups=mesh['groups'=2,'section'=2,'tensor'=8] {'tensor'}, dimensions={0} | all-to-all | bytes 262144 | tf_op jit(solution)/shard_map/all_to_all | solution.py:20
  39.2 0.0 copy-done.1
  39.2 2.5 %shard_map.76 = bf16[8,4,1024]{2,1,0:T(4,128)(2,1)S(1)} custom-call(bf16[8,32,256]{2,1,0:T(8,128)(2,1)S(1)} %all_to_all.22.got_ref, bf16[1024,8192]{1,0:T(8,128)(2,1)S(1)} %copy-done.1), custom_call_target="tpu_custom_call" | custom-call | flops 999999995904 | bytes 67108864 | tf_op jit(solution)/shard_map/pallas_call | solution.py:28
  41.7 9.3 %all_to_all.23.x_ref = bf16[8,4,1024]{2,1,0:T(4,128)(2,1)S(1)} all-to-all(bf16[8,4,1024]{2,1,0:T(4,128)(2,1)S(1)} %shard_map.76), channel_id=1, replica_groups=mesh['groups'=2,'section'=2,'tensor'=8] {'tensor'}, dimensions={0} | all-to-all | bytes 131072 | tf_op jit(solution)/shard_map/all_to_all | solution.py:20
  51.0 0.6 %shard_map.77 = bf16[4,1024]{1,0:T(4,128)(2,1)} custom-call(bf16[8,4,1024]{2,1,0:T(4,128)(2,1)S(1)} %all_to_all.23.x_ref), custom_call_target="tpu_custom_call" | custom-call | flops 999999995904 | bytes 67108864 | tf_op jit(solution)/shard_map/pallas_call | solution.py:28
  (1 shorter events, 0.0 us)
Async XLA Ops:
  0.0 0.7 %copy-start.4 = (bf16[4,1024]{1,0:T(4,128)(2,1)S(1)}, bf16[4,1024]{1,0:T(4,128)(2,1)}, u32[]{:S(2)}) copy-start(bf16[4,1024]{1,0:T(4,128)(2,1)} %x_ref.1) | copy-start | bytes 24580
  0.7 14.3 %copy-start = (bf16[8192,1024]{1,0:T(8,128)(2,1)S(1)}, bf16[8192,1024]{1,0:T(8,128)(2,1)}, u32[]{:S(2)}) copy-start(bf16[8192,1024]{1,0:T(8,128)(2,1)} %w_ref.2) | copy-start | bytes 50331652
  15.0 11.6 %copy-start.2 = (bf16[4,128,2048]{2,1,0:T(8,128)(2,1)S(1)}, bf16[4,128,2048]{2,1,0:T(8,128)(2,1)}, u32[]{:S(2)}) copy-start(bf16[4,128,2048]{2,1,0:T(8,128)(2,1)} %cache_ref.1) | copy-start | bytes 6291460
  15.0 11.6 %copy-start.3 = (bf16[4,64,2048]{2,1,0:T(8,128)(2,1)S(1)}, bf16[4,64,2048]{2,1,0:T(8,128)(2,1)}, u32[]{:S(2)}) copy-start(bf16[4,64,2048]{2,1,0:T(8,128)(2,1)} %fresh_ref.1) | copy-start | bytes 3145732
  15.0 11.6 %copy-start.5 = (s32[4]{0:T(128)S(1)}, s32[4]{0:T(128)}, u32[]{:S(2)}) copy-start(s32[4]{0:T(128)} %clen_ref.1) | copy-start | bytes 52
  15.0 11.6 %copy-start.6 = (s32[4]{0:T(128)S(1)}, s32[4]{0:T(128)}, u32[]{:S(2)}) copy-start(s32[4]{0:T(128)} %nlen_ref.1) | copy-start | bytes 52
  26.6 12.7 %copy-start.1 = (bf16[1024,8192]{1,0:T(8,128)(2,1)S(1)}, bf16[1024,8192]{1,0:T(8,128)(2,1)}, u32[]{:S(2)}) copy-start(bf16[1024,8192]{1,0:T(8,128)(2,1)} %w_ref.3) | copy-start | bytes 50331652

commit v4 on v3

v4 whole, which is shorter than its diff:
```python
import functools

import jax
import jax.numpy as jnp
from jax import lax
from jax.experimental import pallas as pl
from jax.experimental.pallas import tpu as pltpu
from jax.sharding import PartitionSpec as P

KVH = 8
HD = 128
GROUP = 8
HEADS = KVH * GROUP
STATS = 8
F32 = jnp.float32
BF16 = jnp.bfloat16
VMEM = pl.BlockSpec(memory_space=pltpu.VMEM)
SMEM = pl.BlockSpec(memory_space=pltpu.SMEM)
BOTH = ("section", "tensor")
SPLIT_OUTPUT = False
ORDER = (4, 6, 2)
LONG = 10**12
FIRST = 0
ATTEND = 10**12


def exchange(x, shared):
    return lax.all_to_all(x, BOTH if shared > 1 else "tensor", 0, 0, tiled=True)


def dot(a, b):
    return jnp.dot(a, b, preferred_element_type=F32)


def swap(x, apart):
    n = lax.axis_size("tensor")
    return lax.ppermute(x, "tensor", [(i, i ^ apart) for i in range(n)])


def call(kernel, shape, dtype, *args, specs=None, scratch=(), flops=0):
    return pl.pallas_call(
        kernel,
        in_specs=specs or [VMEM] * len(args),
        out_specs=VMEM,
        out_shape=jax.ShapeDtypeStruct(shape, dtype),
        scratch_shapes=scratch,
        cost_estimate=pl.CostEstimate(flops=flops, bytes_accessed=0, transcendentals=0),
        compiler_params=pltpu.CompilerParams(vmem_limit_bytes=8 << 20),
    )(*args)


def spread_kernel(x_ref, o_ref):
    o_ref[...] = jnp.broadcast_to(x_ref[...][None], o_ref.shape)


def copy_kernel(x_ref, o_ref):
    o_ref[...] = x_ref[...]


def stack_kernel(x_ref, y_ref, o_ref):
    o_ref[0] = x_ref[...]
    o_ref[1] = y_ref[...]


def write_queries(acc, o_ref, heads_ref):
    rows = acc.shape[0]
    own = acc.shape[1] // HD
    for h in range(own):
        heads_ref[pl.ds(h, rows, stride=own), :] = acc[:, h * HD : (h + 1) * HD]
    o_ref[...] = jnp.broadcast_to(heads_ref[...].astype(BF16)[None], o_ref.shape)


def query_kernel(all_ref, w_ref, o_ref, heads_ref):
    n, rows, feat = all_ref.shape
    acc = jnp.zeros((rows, w_ref.shape[1]), F32)
    for t in range(n):
        acc += dot(all_ref[t], w_ref[t * feat : (t + 1) * feat, :])
    write_queries(acc, o_ref, heads_ref)


def pair_product(apart, x_ref, w_ref):
    feat = x_ref.shape[2]
    me = lax.axis_index("tensor")
    acc = jnp.zeros((x_ref.shape[1], w_ref.shape[1]), F32)
    for i in range(2):
        at = pl.multiple_of((me ^ (apart + i)) * feat, feat)
        acc += dot(x_ref[i], w_ref[pl.ds(at, feat), :])
    return acc


def first_kernel(x_ref, w_ref, acc_ref):
    acc_ref[...] = pair_product(0, x_ref, w_ref)


def next_kernel(apart, x_ref, w_ref, old_ref, acc_ref):
    acc_ref[...] = old_ref[...] + pair_product(apart, x_ref, w_ref)


def last_kernel(apart, x_ref, w_ref, old_ref, o_ref, heads_ref):
    write_queries(old_ref[...] + pair_product(apart, x_ref, w_ref), o_ref, heads_ref)


def attend_kernel(clen_ref, nlen_ref, q_ref, cache_ref, fresh_ref, o_ref):
    rows, cc, width = cache_ref.shape
    width = width // 2
    fc = fresh_ref.shape[1]
    shares = q_ref.shape[0] // KVH
    part = GROUP // shares
    place = lax.axis_index("tensor")
    head_of = lax.broadcasted_iota(jnp.int32, (HEADS, width), 0) // GROUP
    diagonal = head_of == lax.broadcasted_iota(jnp.int32, (HEADS, width), 1) // HD

    def logits(ref, r, wide, start, length):
        s = lax.dot_general(
            ref[r, :, 0:width], wide, (((1,), (1,)), ((), ())), preferred_element_type=F32
        )
        valid = start + lax.broadcasted_iota(jnp.int32, s.shape, 0) < length
        return jnp.where(valid, s * HD**-0.5, -1e30), valid

    def attend(r, q):
        wide = jnp.where(diagonal, jnp.concatenate([q] * KVH, axis=1), 0.0).astype(BF16)
        sc, okc = logits(cache_ref, r, wide, place * cc, clen_ref[r])
        sf, okf = logits(fresh_ref, r, wide, place * fc, nlen_ref[r])
        top = jnp.maximum(
            jnp.max(sc, axis=0, keepdims=True), jnp.max(sf, axis=0, keepdims=True)
        )
        wc = jnp.where(okc, jnp.exp(sc - top), 0.0)
        wf = jnp.where(okf, jnp.exp(sf - top), 0.0)
        total = jnp.sum(wc, axis=0, keepdims=True) + jnp.sum(wf, axis=0, keepdims=True)
        some = total > 0.0
        total = jnp.where(some, total, 1.0)
        inverse = 1.0 / total
        pc = (wc * inverse).T.astype(BF16)
        pf = (wf * inverse).T.astype(BF16)
        nums = []
        for pair in range(KVH // 2):
            at = slice(2 * pair * GROUP, 2 * (pair + 1) * GROUP)
            vals = slice(width + 2 * pair * HD, width + 2 * (pair + 1) * HD)
            num = dot(pc[at], cache_ref[r, :, vals]) + dot(pf[at], fresh_ref[r, :, vals])
            nums += [num[:GROUP, :HD], num[GROUP:, HD:]]
        return nums, jnp.where(some, top + jnp.log(total), -1e30)

    stats = []
    for two in range(rows // 2):
        out = []
        for r in (2 * two, 2 * two + 1):
            at = slice(r * part, (r + 1) * part)
            at16 = slice(2 * two * part, 2 * (two + 1) * part)
            half = slice((r % 2) * part, (r % 2 + 1) * part)
            q = [
                q_ref[s * KVH + g, at16, :].astype(F32)[half]
                for g in range(KVH)
                for s in range(shares)
            ]
            out.append(attend(r, jnp.concatenate(q, axis=0)))
        at = slice(two * 2 * GROUP, (two + 1) * 2 * GROUP)
        for d in range(o_ref.shape[0]):
            g = d % KVH
            o_ref[d, at, :] = jnp.concatenate([o[0][g] for o in out], axis=0).astype(BF16)
        rest = jnp.concatenate([o[1] for o in out], axis=1)
        for _ in range(3):
            piece = rest.astype(BF16).astype(F32)
            stats.append(piece)
            rest = rest - piece
        stats.append(jnp.zeros_like(rest))
    stats = jnp.concatenate(stats, axis=0).astype(BF16)
    for d in range(o_ref.shape[0]):
        o_ref[d, rows * GROUP :, :] = stats


def project_kernel(shared, own, got_ref, w_ref, o_ref, heads_ref):
    total, both, _ = got_ref.shape
    both -= STATS
    n = total // shared
    rows = both // own
    wide = o_ref.shape[2]
    me = lax.axis_index("tensor")
    line = lax.broadcasted_iota(jnp.int32, (both, HD), 0)
    column = lax.broadcasted_iota(jnp.int32, (both, HD), 1)
    mine = column == (line // own % 2) * HEADS + me * own + line % own
    mine = mine.astype(F32).astype(BF16)
    line = lax.broadcasted_iota(jnp.int32, (both, n * STATS), 0)
    column = lax.broadcasted_iota(jnp.int32, (both, n * STATS), 1)
    pair = (column % STATS) // (STATS // 2) == line // own // 2
    context = []
    for s in range(shared):
        stats = [got_ref[s * n + t, both:, :].astype(F32) for t in range(n)]
        stats = jnp.concatenate(stats, axis=0).astype(BF16)
        pieces = lax.dot_general(
            mine, stats, (((1,), (1,)), ((), ())), preferred_element_type=F32
        )
        pieces = jnp.where(pair, pieces, 0.0)
        logs = [
            jnp.sum(jnp.where(column // STATS == t, pieces, 0.0), axis=1, keepdims=True)
            for t in range(n)
        ]
        top = functools.reduce(jnp.maximum, logs)
        scales = [jnp.exp(x - top) for x in logs]
        inverse = 1.0 / functools.reduce(jnp.add, scales)
        heads_ref[...] = functools.reduce(
            jnp.add,
            [
                got_ref[s * n + t, 0:both, :].astype(F32) * (scales[t] * inverse)
                for t in range(n)
            ],
        )
        context.append(
            jnp.concatenate(
                [heads_ref[pl.ds(h, rows, stride=own), :] for h in range(own)], axis=1
            )
        )
    context = jnp.concatenate(context, axis=0).astype(BF16)
    offset = 0
    if shared > 1:
        offset = lax.axis_index("section") * wide
    for t in range(n):
        at = t * shared * wide + offset
        if shared > 1:
            at = pl.multiple_of(at, HD)
        terms = dot(context, w_ref[:, pl.ds(at, wide)])
        for s in range(shared):
            o_ref[s * n + t] = terms[s * rows : (s + 1) * rows].astype(BF16)


def sum_kernel(x_ref, o_ref):
    total, _, wide = x_ref.shape
    shared = o_ref.shape[1] // wide
    n = total // shared
    for s in range(shared):
        x = x_ref[s * n : (s + 1) * n].astype(F32)
        o_ref[:, s * wide : (s + 1) * wide] = jnp.sum(x, axis=0).astype(BF16)


def body(hidden, w_query, w_output, cache, fresh, cache_lengths, new_lengths):
    rows, feat = hidden.shape
    n = lax.axis_size("tensor")
    cores = lax.axis_size("section")
    own = w_query.shape[1] // HD
    wide = w_output.shape[1] // n
    usual = own == GROUP
    o_shared = cores if usual and SPLIT_OUTPUT else 1
    w_query = pltpu.with_memory_space_constraint(w_query, pltpu.VMEM)
    w_output = pltpu.with_memory_space_constraint(w_output, pltpu.VMEM)
    cache = pltpu.with_memory_space_constraint(cache, pltpu.VMEM)
    fresh = pltpu.with_memory_space_constraint(fresh, pltpu.VMEM)

    scratch = [pltpu.VMEM((rows * own, HD), F32)]
    if n == 8:
        mine = call(copy_kernel, (rows, feat), BF16, hidden, flops=LONG)
        near = swap(mine, 1)
        pair = call(stack_kernel, (2, rows, feat), BF16, mine, near)
        acc = call(first_kernel, (rows, own * HD), F32, pair, w_query, flops=FIRST)
        got = [swap(pair, apart) for apart in ORDER]
        for apart, x in zip(ORDER[:2], got):
            step = functools.partial(next_kernel, apart)
            acc = call(step, (rows, own * HD), F32, x, w_query, acc)
        step = functools.partial(last_kernel, ORDER[2])
        q = call(step, (n, rows * own, HD), BF16, got[2], w_query, acc, scratch=scratch)
    else:
        x = call(spread_kernel, (n, rows, feat), BF16, hidden, flops=LONG)
        x = exchange(x, 1)
        q = call(query_kernel, (n, rows * own, HD), BF16, x, w_query, scratch=scratch)
    q = exchange(q, 1)
    if not usual:
        q = q.reshape(KVH, GROUP, rows, HD).transpose(0, 2, 1, 3).reshape(KVH, rows * GROUP, HD)
    part = call(
        attend_kernel,
        (o_shared * KVH, rows * GROUP + STATS, HD),
        BF16,
        cache_lengths,
        new_lengths,
        q,
        cache,
        fresh,
        flops=ATTEND,
        specs=[SMEM] * 2 + [VMEM] * 3,
    )
    if not usual:
        stats = jnp.broadcast_to(part[:1, rows * GROUP :], (n, STATS, HD))
        part = part[:, : rows * GROUP].reshape(KVH, rows, GROUP, HD).transpose(0, 2, 1, 3)
        part = jnp.concatenate([part.reshape(n, rows * own, HD), stats], axis=1)
    part = exchange(part, o_shared)
    terms = call(
        functools.partial(project_kernel, o_shared, own),
        (o_shared * n, rows, wide // o_shared),
        BF16,
        part,
        w_output,
        scratch=[pltpu.VMEM((rows * own, HD), F32)],
    )
    terms = exchange(terms, o_shared)
    return call(sum_kernel, (rows, wide), BF16, terms)


def solution(mesh):
    return jax.shard_map(
        body,
        mesh=mesh,
        in_specs=(
            P(("groups", "section"), "tensor"),
            P(None, "tensor"),
            P("tensor", None),
            P(("groups", "section"), "tensor", None),
            P(("groups", "section"), "tensor", None),
            P(("groups", "section")),
            P(("groups", "section")),
        ),
        out_specs=P(("groups", "section"), "tensor"),
        check_vma=False,
    )
```

time: 51.9 us -> 50.7 us (0.977)
  blocking collectives: 43.1 us -> 29.4 us
  starting transfers between devices: 0 us -> 7.64 us
  waiting for transfers between devices: 0 us -> 4.24 us
  Pallas kernels: 7.76 us -> 8.34 us
    all_to_all x4 -> x3, blocking collectives: 43.1 us -> 29.4 us  [exchange(): return lax.all_to_all(x, BOTH if shared > 1 else 'tensor', 0, 0, tiled=True)]
    ppermute x0 -> x4, starting transfers between devices: none -> 7.64 us  [swap(): return lax.ppermute(x, 'tensor', [(i, i ^ apart) for i in range(n)])]
    ppermute x0 -> x4, waiting for transfers between devices: none -> 4.24 us  [swap(): return lax.ppermute(x, 'tensor', [(i, i ^ apart) for i in range(n)])]
    pallas_call x5 -> x9, Pallas kernels: 7.76 us -> 8.34 us  [call(): pl.pallas_call(kernel, in_specs=specs or [VMEM] * len(args), out_specs=VM...]
  transfers between devices with their start and end apart: 0 -> 4, of which waited for: 0 -> 2; matrix products, arithmetic and copies ran while one was open for 0% -> 0% of each run, Pallas kernels for 0% -> 4%
where the time goes in v4:
time: 50.7 us; the launch traced here: 50.4 us
  blocking collectives  29.4 us (58%)
  Pallas kernels  8.34 us (16%)
  starting transfers between devices  7.64 us (15%)
  waiting for transfers between devices  4.24 us (8%)
  local copies, waits for them, and re-layouts  0.72 us (1%)
    all_to_all x3, blocking collectives, exchange(): return lax.all_to_all(x, BOTH if shared > 1 else 'tensor', 0, 0, tiled=True)  29.4 us
    pallas_call x9, Pallas kernels, call(): pl.pallas_call(kernel, in_specs=specs or [VMEM] * len(args), out_specs=VM...  8.34 us
    ppermute x4, starting transfers between devices, swap(): return lax.ppermute(x, 'tensor', [(i, i ^ apart) for i in range(n)])  7.64 us
    ppermute x4, waiting for transfers between devices, swap(): return lax.ppermute(x, 'tensor', [(i, i ^ apart) for i in range(n)])  4.24 us
  transfers between devices with their start and end apart: 4, of which 2 were waited for; matrix products, arithmetic and copies ran while one was open for 0% of the time, Pallas kernels for 4%

profile of v4, /device:TPU:0, one launch (start us, length us, event | category | flops | bytes accessed | tf_op | source)
XLA Modules:
  0.0 50.4 jit_solution(2472777918907893632)
XLA Ops:
  0.0 0.0 copy-start.4
  0.0 0.7 %copy-done.4 = bf16[4,1024]{1,0:T(4,128)(2,1)S(1)} copy-done((bf16[4,1024]{1,0:T(4,128)(2,1)S(1)}, bf16[4,1024]{1,0:T(4,128)(2,1)}, u32[]{:S(2)}) %copy-start.4) | copy-done | bytes 8216
  0.7 0.0 copy-start
  0.7 3.0 %collective-permute-start = (bf16[4,1024]{1,0:T(4,128)(2,1)S(1)}, bf16[4,1024]{1,0:T(4,128)(2,1)S(1)}, u32[]{:S(2)}, u32[]{:S(2)}) collective-permute-start(bf16[4,1024]{1,0:T(4,128)(2,1)S(1)} %shard_map.73.x_ref), channel_id=1, source_target_pairs={{0,1},{1,0},{2,3},{3,2},{4,5},{5,4},{6,7},{7,6},{8,9},{9,8},{10,11... | collective-permute-start | bytes 24584 | tf_op jit(solution)/shard_map/ppermute | solution.py:37
  3.7 1.6 %collective-permute-done.y_ref = bf16[4,1024]{1,0:T(4,128)(2,1)S(1)} collective-permute-done((bf16[4,1024]{1,0:T(4,128)(2,1)S(1)}, bf16[4,1024]{1,0:T(4,128)(2,1)S(1)}, u32[]{:S(2)}, u32[]{:S(2)}) %collective-permute-start) | collective-permute-done | bytes 8224 | tf_op jit(solution)/shard_map/ppermute | solution.py:37
  5.3 3.1 %collective-permute-start.3 = (bf16[2,4,1024]{2,1,0:T(4,128)(2,1)S(1)}, bf16[2,4,1024]{2,1,0:T(4,128)(2,1)S(1)}, u32[]{:S(2)}, u32[]{:S(2)}) collective-permute-start(bf16[2,4,1024]{2,1,0:T(4,128)(2,1)S(1)} %shard_map.74.x_ref), channel_id=1, source_target_pairs={{0,4},{1,5},{2,6},{3,7},{4,0},{5,1},{6,2},{7,3},{8,12},{9,13},{10,... | collective-permute-start | bytes 49160 | tf_op jit(solution)/shard_map/ppermute | solution.py:37
  8.4 1.3 %collective-permute-start.2 = (bf16[2,4,1024]{2,1,0:T(4,128)(2,1)S(1)}, bf16[2,4,1024]{2,1,0:T(4,128)(2,1)S(1)}, u32[]{:S(2)}, u32[]{:S(2)}) collective-permute-start(bf16[2,4,1024]{2,1,0:T(4,128)(2,1)S(1)} %shard_map.74.x_ref), channel_id=1, source_target_pairs={{0,6},{1,7},{2,4},{3,5},{4,2},{5,3},{6,0},{7,1},{8,14},{9,15},{10,... | collective-permute-start | bytes 49160 | tf_op jit(solution)/shard_map/ppermute | solution.py:37
  9.7 0.2 collective-permute-start.1
  10.0 0.0 copy-done
  10.0 0.6 %shard_map.75.old_ref = f32[4,1024]{1,0:T(4,128)S(1)} custom-call(bf16[2,4,1024]{2,1,0:T(4,128)(2,1)S(1)} %shard_map.74.x_ref, bf16[8192,1024]{1,0:T(8,128)(2,1)S(1)} %copy-done), custom_call_target="tpu_custom_call" | custom-call | tf_op jit(solution)/shard_map/pallas_call | solution.py:41
  10.6 0.0 collective-permute-done.3.x_ref
  10.6 0.7 %shard_map.76.old_ref = f32[4,1024]{1,0:T(4,128)S(1)} custom-call(bf16[2,4,1024]{2,1,0:T(4,128)(2,1)S(1)} %collective-permute-done.3.x_ref, bf16[8192,1024]{1,0:T(8,128)(2,1)S(1)} %copy-done, f32[4,1024]{1,0:T(4,128)S(1)} %shard_map.75.old_ref), custom_call_target="tpu_custom_call" | custom-call | tf_op jit(solution)/shard_map/pallas_call | solution.py:41
  11.3 0.0 copy-start.2
  11.3 0.0 copy-start.3
  11.3 0.0 copy-start.5
  11.3 0.0 copy-start.6
  11.3 2.6 %collective-permute-done.2.x_ref = bf16[2,4,1024]{2,1,0:T(4,128)(2,1)S(1)} collective-permute-done((bf16[2,4,1024]{2,1,0:T(4,128)(2,1)S(1)}, bf16[2,4,1024]{2,1,0:T(4,128)(2,1)S(1)}, u32[]{:S(2)}, u32[]{:S(2)}) %collective-permute-start.2) | collective-permute-done | bytes 16416 | tf_op jit(solution)/shard_map/ppermute | solution.py:37
  13.9 0.7 %shard_map.77.old_ref = f32[4,1024]{1,0:T(4,128)S(1)} custom-call(bf16[2,4,1024]{2,1,0:T(4,128)(2,1)S(1)} %collective-permute-done.2.x_ref, bf16[8192,1024]{1,0:T(8,128)(2,1)S(1)} %copy-done, f32[4,1024]{1,0:T(4,128)S(1)} %shard_map.76.old_ref), custom_call_target="tpu_custom_call" | custom-call | tf_op jit(solution)/shard_map/pallas_call | solution.py:41
  14.6 0.0 collective-permute-done.1.x_ref
  14.6 0.7 %shard_map.78 = bf16[8,32,128]{2,1,0:T(8,128)(2,1)S(1)} custom-call(bf16[2,4,1024]{2,1,0:T(4,128)(2,1)S(1)} %collective-permute-done.1.x_ref, bf16[8192,1024]{1,0:T(8,128)(2,1)S(1)} %copy-done, f32[4,1024]{1,0:T(4,128)S(1)} %shard_map.77.old_ref), custom_call_target="tpu_custom_call" | custom-call | tf_op jit(solution)/shard_map/pallas_call | solution.py:41
  15.3 10.3 %all_to_all.15.q_ref = bf16[8,32,128]{2,1,0:T(8,128)(2,1)S(1)} all-to-all(bf16[8,32,128]{2,1,0:T(8,128)(2,1)S(1)} %shard_map.78), channel_id=1, replica_groups=mesh['groups'=2,'section'=2,'tensor'=8] {'tensor'}, dimensions={0} | all-to-all | bytes 131072 | tf_op jit(solution)/shard_map/all_to_all | solution.py:28
  25.6 0.0 copy-done.2
  25.6 0.0 copy-done.3
  25.6 0.0 copy-done.5
  25.6 0.0 copy-done.6
  25.6 0.0 copy-start.1
  25.6 2.5 %shard_map.79 = bf16[8,40,128]{2,1,0:T(8,128)(2,1)S(1)} custom-call(s32[4]{0:T(128)S(1)} %copy-done.5, s32[4]{0:T(128)S(1)} %copy-done.6, bf16[8,32,128]{2,1,0:T(8,128)(2,1)S(1)} %all_to_all.15.q_ref, bf16[4,128,2048]{2,1,0:T(8,128)(2,1)S(1)} %copy-done.2, bf16[4,64,2048]{2,1,0:T(8,128)(2,1)S(1)} %copy-done.3), custom_call_target="tpu_custom_call" | custom-call | flops 999999995904 | tf_op jit(solution)/shard_map/pallas_call | solution.py:41
  28.1 9.8 %all_to_all.16.got_ref = bf16[8,40,128]{2,1,0:T(8,128)(2,1)S(1)} all-to-all(bf16[8,40,128]{2,1,0:T(8,128)(2,1)S(1)} %shard_map.79), channel_id=1, replica_groups=mesh['groups'=2,'section'=2,'tensor'=8] {'tensor'}, dimensions={0} | all-to-all | bytes 163840 | tf_op jit(solution)/shard_map/all_to_all | solution.py:28
  37.9 0.0 copy-done.1
  37.9 2.5 %shard_map.80 = bf16[8,4,1024]{2,1,0:T(4,128)(2,1)S(1)} custom-call(bf16[8,40,128]{2,1,0:T(8,128)(2,1)S(1)} %all_to_all.16.got_ref, bf16[1024,8192]{1,0:T(8,128)(2,1)S(1)} %copy-done.1), custom_call_target="tpu_custom_call" | custom-call | tf_op jit(solution)/shard_map/pallas_call | solution.py:41
  40.4 9.3 %all_to_all.17.x_ref = bf16[8,4,1024]{2,1,0:T(4,128)(2,1)S(1)} all-to-all(bf16[8,4,1024]{2,1,0:T(4,128)(2,1)S(1)} %shard_map.80), channel_id=1, replica_groups=mesh['groups'=2,'section'=2,'tensor'=8] {'tensor'}, dimensions={0} | all-to-all | bytes 131072 | tf_op jit(solution)/shard_map/all_to_all | solution.py:28
  49.7 0.6 %shard_map.81 = bf16[4,1024]{1,0:T(4,128)(2,1)} custom-call(bf16[8,4,1024]{2,1,0:T(4,128)(2,1)S(1)} %all_to_all.17.x_ref), custom_call_target="tpu_custom_call" | custom-call | tf_op jit(solution)/shard_map/pallas_call | solution.py:41
  (2 shorter events, 0.0 us)
Async XLA Ops:
  0.0 0.7 %copy-start.4 = (bf16[4,1024]{1,0:T(4,128)(2,1)S(1)}, bf16[4,1024]{1,0:T(4,128)(2,1)}, u32[]{:S(2)}) copy-start(bf16[4,1024]{1,0:T(4,128)(2,1)} %x_ref.1) | copy-start | bytes 24580
  0.7 9.3 %copy-start = (bf16[8192,1024]{1,0:T(8,128)(2,1)S(1)}, bf16[8192,1024]{1,0:T(8,128)(2,1)}, u32[]{:S(2)}) copy-start(bf16[8192,1024]{1,0:T(8,128)(2,1)} %w_ref.8) | copy-start | bytes 50331652
  0.7 4.6 %collective-permute-start = (bf16[4,1024]{1,0:T(4,128)(2,1)S(1)}, bf16[4,1024]{1,0:T(4,128)(2,1)S(1)}, u32[]{:S(2)}, u32[]{:S(2)}) collective-permute-start(bf16[4,1024]{1,0:T(4,128)(2,1)S(1)} %shard_map.73.x_ref), channel_id=1, source_target_pairs={{0,1},{1,0},{2,3},{3,2},{4,5},{5,4},{6,7},{7,6},{8,9},{9,8},{10,11... | collective-permute-start | bytes 24584 | tf_op jit(solution)/shard_map/ppermute | solution.py:37
  5.3 5.3 %collective-permute-start.3 = (bf16[2,4,1024]{2,1,0:T(4,128)(2,1)S(1)}, bf16[2,4,1024]{2,1,0:T(4,128)(2,1)S(1)}, u32[]{:S(2)}, u32[]{:S(2)}) collective-permute-start(bf16[2,4,1024]{2,1,0:T(4,128)(2,1)S(1)} %shard_map.74.x_ref), channel_id=1, source_target_pairs={{0,4},{1,5},{2,6},{3,7},{4,0},{5,1},{6,2},{7,3},{8,12},{9,13},{10,... | collective-permute-start | bytes 49160 | tf_op jit(solution)/shard_map/ppermute | solution.py:37
  8.4 5.5 %collective-permute-start.2 = (bf16[2,4,1024]{2,1,0:T(4,128)(2,1)S(1)}, bf16[2,4,1024]{2,1,0:T(4,128)(2,1)S(1)}, u32[]{:S(2)}, u32[]{:S(2)}) collective-permute-start(bf16[2,4,1024]{2,1,0:T(4,128)(2,1)S(1)} %shard_map.74.x_ref), channel_id=1, source_target_pairs={{0,6},{1,7},{2,4},{3,5},{4,2},{5,3},{6,0},{7,1},{8,14},{9,15},{10,... | collective-permute-start | bytes 49160 | tf_op jit(solution)/shard_map/ppermute | solution.py:37
  9.7 4.8 %collective-permute-start.1 = (bf16[2,4,1024]{2,1,0:T(4,128)(2,1)S(1)}, bf16[2,4,1024]{2,1,0:T(4,128)(2,1)S(1)}, u32[]{:S(2)}, u32[]{:S(2)}) collective-permute-start(bf16[2,4,1024]{2,1,0:T(4,128)(2,1)S(1)} %shard_map.74.x_ref), channel_id=1, source_target_pairs={{0,2},{1,3},{2,0},{3,1},{4,6},{5,7},{6,4},{7,5},{8,10},{9,11},{10,... | collective-permute-start | bytes 49160 | tf_op jit(solution)/shard_map/ppermute | solution.py:37
  11.3 14.3 %copy-start.2 = (bf16[4,128,2048]{2,1,0:T(8,128)(2,1)S(1)}, bf16[4,128,2048]{2,1,0:T(8,128)(2,1)}, u32[]{:S(2)}) copy-start(bf16[4,128,2048]{2,1,0:T(8,128)(2,1)} %cache_ref.1) | copy-start | bytes 6291460
  11.3 14.3 %copy-start.3 = (bf16[4,64,2048]{2,1,0:T(8,128)(2,1)S(1)}, bf16[4,64,2048]{2,1,0:T(8,128)(2,1)}, u32[]{:S(2)}) copy-start(bf16[4,64,2048]{2,1,0:T(8,128)(2,1)} %fresh_ref.1) | copy-start | bytes 3145732
  11.3 14.3 %copy-start.5 = (s32[4]{0:T(128)S(1)}, s32[4]{0:T(128)}, u32[]{:S(2)}) copy-start(s32[4]{0:T(128)} %clen_ref.1) | copy-start | bytes 52
  11.3 14.3 %copy-start.6 = (s32[4]{0:T(128)S(1)}, s32[4]{0:T(128)}, u32[]{:S(2)}) copy-start(s32[4]{0:T(128)} %nlen_ref.1) | copy-start | bytes 52
  25.6 12.3 %copy-start.1 = (bf16[1024,8192]{1,0:T(8,128)(2,1)S(1)}, bf16[1024,8192]{1,0:T(8,128)(2,1)}, u32[]{:S(2)}) copy-start(bf16[1024,8192]{1,0:T(8,128)(2,1)} %w_ref.9) | copy-start | bytes 50331652

commit v5 on v4

--- a/solution.py
+++ b/solution.py
@@ -109,18 +109,43 @@
     place = lax.axis_index("tensor")
     head_of = lax.broadcasted_iota(jnp.int32, (HEADS, width), 0) // GROUP
     diagonal = head_of == lax.broadcasted_iota(jnp.int32, (HEADS, width), 1) // HD
-
-    def logits(ref, r, wide, start, length):
-        s = lax.dot_general(
-            ref[r, :, 0:width], wide, (((1,), (1,)), ((), ())), preferred_element_type=F32
-        )
+    none = jnp.zeros((HEADS, width), BF16)
+
+    def logits(ref, r, wide, start, length_ref):
+        s = [
+            lax.dot_general(
+                ref[r + i, :, 0:width],
+                wide[i],
+                (((1,), (1,)), ((), ())),
+                preferred_element_type=F32,
+            )
+            for i in range(2)
+        ]
+        s = s[0] + s[1]
+        second = lax.broadcasted_iota(jnp.int32, s.shape, 1) >= HEADS
+        length = jnp.where(second, length_ref[r + 1], length_ref[r])
         valid = start + lax.broadcasted_iota(jnp.int32, s.shape, 0) < length
         return jnp.where(valid, s * HD**-0.5, -1e30), valid
 
-    def attend(r, q):
-        wide = jnp.where(diagonal, jnp.concatenate([q] * KVH, axis=1), 0.0).astype(BF16)
-        sc, okc = logits(cache_ref, r, wide, place * cc, clen_ref[r])
-        sf, okf = logits(fresh_ref, r, wide, place * fc, nlen_ref[r])
+    scores = []
+    for r in range(0, rows, 2):
+        at = slice(r * part, (r + 2) * part)
+        both = [
+            q_ref[s * KVH + g, at, :].astype(F32) for g in range(KVH) for s in range(shares)
+        ]
+        wide = []
+        for i in range(2):
+            q = jnp.concatenate([x[i * part : (i + 1) * part] for x in both], axis=0)
+            q = jnp.where(diagonal, jnp.concatenate([q] * KVH, axis=1), 0.0).astype(BF16)
+            wide.append(jnp.concatenate([q, none] if i == 0 else [none, q], axis=0))
+        scores.append(
+            (
+                logits(cache_ref, r, wide, place * cc, clen_ref),
+                logits(fresh_ref, r, wide, place * fc, nlen_ref),
+            )
+        )
+    stats, weights = [], []
+    for (sc, okc), (sf, okf) in scores:
         top = jnp.maximum(
             jnp.max(sc, axis=0, keepdims=True), jnp.max(sf, axis=0, keepdims=True)
         )
@@ -130,39 +155,29 @@
         some = total > 0.0
         total = jnp.where(some, total, 1.0)
         inverse = 1.0 / total
-        pc = (wc * inverse).T.astype(BF16)
-        pf = (wf * inverse).T.astype(BF16)
-        nums = []
-        for pair in range(KVH // 2):
-            at = slice(2 * pair * GROUP, 2 * (pair + 1) * GROUP)
-            vals = slice(width + 2 * pair * HD, width + 2 * (pair + 1) * HD)
-            num = dot(pc[at], cache_ref[r, :, vals]) + dot(pf[at], fresh_ref[r, :, vals])
-            nums += [num[:GROUP, :HD], num[GROUP:, HD:]]
-        return nums, jnp.where(some, top + jnp.log(total), -1e30)
-
-    stats = []
-    for two in range(rows // 2):
-        out = []
-        for r in (2 * two, 2 * two + 1):
-            at = slice(r * part, (r + 1) * part)
-            at16 = slice(2 * two * part, 2 * (two + 1) * part)
-            half = slice((r % 2) * part, (r % 2 + 1) * part)
-            q = [
-                q_ref[s * KVH + g, at16, :].astype(F32)[half]
-                for g in range(KVH)
-                for s in range(shares)
-            ]
-            out.append(attend(r, jnp.concatenate(q, axis=0)))
-        at = slice(two * 2 * GROUP, (two + 1) * 2 * GROUP)
-        for d in range(o_ref.shape[0]):
-            g = d % KVH
-            o_ref[d, at, :] = jnp.concatenate([o[0][g] for o in out], axis=0).astype(BF16)
-        rest = jnp.concatenate([o[1] for o in out], axis=1)
+        weights.append(((wc * inverse).T.astype(BF16), (wf * inverse).T.astype(BF16)))
+        rest = jnp.where(some, top + jnp.log(total), -1e30)
         for _ in range(3):
             piece = rest.astype(BF16).astype(F32)
             stats.append(piece)
             rest = rest - piece
         stats.append(jnp.zeros_like(rest))
+    for two, (pc, pf) in enumerate(weights):
+        for pair in range(KVH // 2):
+            vals = slice(width + 2 * pair * HD, width + 2 * (pair + 1) * HD)
+            nums = []
+            for i in range(2):
+                at = slice(i * HEADS + 2 * pair * GROUP, i * HEADS + 2 * (pair + 1) * GROUP)
+                nums.append(
+                    dot(pc[at], cache_ref[2 * two + i, :, vals])
+                    + dot(pf[at], fresh_ref[2 * two + i, :, vals])
+                )
+            at = slice(two * 2 * GROUP, (two + 1) * 2 * GROUP)
+            for j in range(2):
+                num = [x[j * GROUP : (j + 1) * GROUP, j * HD : (j + 1) * HD] for x in nums]
+                num = jnp.concatenate(num, axis=0).astype(BF16)
+                for d in range(2 * pair + j, o_ref.shape[0], KVH):
+                    o_ref[d, at, :] = num
     stats = jnp.concatenate(stats, axis=0).astype(BF16)
     for d in range(o_ref.shape[0]):
         o_ref[d, rows * GROUP :, :] = stats

time: 50.7 us -> 49.8 us (0.982)
  Pallas kernels: 8.34 us -> 7.37 us
    pallas_call x9, Pallas kernels: 8.34 us -> 7.37 us  [call(): pl.pallas_call(kernel, in_specs=specs or [VMEM] * len(args), out_specs=VM...]
where the time goes in v5:
time: 49.8 us; the launch traced here: 49.5 us
  blocking collectives  29.5 us (59%)
  starting transfers between devices  7.64 us (15%)
  Pallas kernels  7.37 us (15%)
  waiting for transfers between devices  4.24 us (9%)
  local copies, waits for them, and re-layouts  0.72 us (1%)
    all_to_all x3, blocking collectives, exchange(): return lax.all_to_all(x, BOTH if shared > 1 else 'tensor', 0, 0, tiled=True)  29.5 us
    ppermute x4, starting transfers between devices, swap(): return lax.ppermute(x, 'tensor', [(i, i ^ apart) for i in range(n)])  7.64 us
    pallas_call x9, Pallas kernels, call(): pl.pallas_call(kernel, in_specs=specs or [VMEM] * len(args), out_specs=VM...  7.37 us
    ppermute x4, waiting for transfers between devices, swap(): return lax.ppermute(x, 'tensor', [(i, i ^ apart) for i in range(n)])  4.24 us
  transfers between devices with their start and end apart: 4, of which 2 were waited for; matrix products, arithmetic and copies ran while one was open for 0% of the time, Pallas kernels for 4%

profile of v5, /device:TPU:0, one launch (start us, length us, event | category | flops | bytes accessed | tf_op | source)
XLA Modules:
  0.0 49.5 jit_solution(12191652726774548610)
XLA Ops:
  0.0 0.0 copy-start.4
  0.0 0.7 %copy-done.4 = bf16[4,1024]{1,0:T(4,128)(2,1)S(1)} copy-done((bf16[4,1024]{1,0:T(4,128)(2,1)S(1)}, bf16[4,1024]{1,0:T(4,128)(2,1)}, u32[]{:S(2)}) %copy-start.4) | copy-done | bytes 8216
  0.7 0.0 copy-start
  0.7 3.0 %collective-permute-start = (bf16[4,1024]{1,0:T(4,128)(2,1)S(1)}, bf16[4,1024]{1,0:T(4,128)(2,1)S(1)}, u32[]{:S(2)}, u32[]{:S(2)}) collective-permute-start(bf16[4,1024]{1,0:T(4,128)(2,1)S(1)} %shard_map.73.x_ref), channel_id=1, source_target_pairs={{0,1},{1,0},{2,3},{3,2},{4,5},{5,4},{6,7},{7,6},{8,9},{9,8},{10,11... | collective-permute-start | bytes 24584 | tf_op jit(solution)/shard_map/ppermute | solution.py:37
  3.7 1.6 %collective-permute-done.y_ref = bf16[4,1024]{1,0:T(4,128)(2,1)S(1)} collective-permute-done((bf16[4,1024]{1,0:T(4,128)(2,1)S(1)}, bf16[4,1024]{1,0:T(4,128)(2,1)S(1)}, u32[]{:S(2)}, u32[]{:S(2)}) %collective-permute-start) | collective-permute-done | bytes 8224 | tf_op jit(solution)/shard_map/ppermute | solution.py:37
  5.3 3.1 %collective-permute-start.3 = (bf16[2,4,1024]{2,1,0:T(4,128)(2,1)S(1)}, bf16[2,4,1024]{2,1,0:T(4,128)(2,1)S(1)}, u32[]{:S(2)}, u32[]{:S(2)}) collective-permute-start(bf16[2,4,1024]{2,1,0:T(4,128)(2,1)S(1)} %shard_map.74.x_ref), channel_id=1, source_target_pairs={{0,4},{1,5},{2,6},{3,7},{4,0},{5,1},{6,2},{7,3},{8,12},{9,13},{10,... | collective-permute-start | bytes 49160 | tf_op jit(solution)/shard_map/ppermute | solution.py:37
  8.4 1.3 %collective-permute-start.2 = (bf16[2,4,1024]{2,1,0:T(4,128)(2,1)S(1)}, bf16[2,4,1024]{2,1,0:T(4,128)(2,1)S(1)}, u32[]{:S(2)}, u32[]{:S(2)}) collective-permute-start(bf16[2,4,1024]{2,1,0:T(4,128)(2,1)S(1)} %shard_map.74.x_ref), channel_id=1, source_target_pairs={{0,6},{1,7},{2,4},{3,5},{4,2},{5,3},{6,0},{7,1},{8,14},{9,15},{10,... | collective-permute-start | bytes 49160 | tf_op jit(solution)/shard_map/ppermute | solution.py:37
  9.7 0.2 collective-permute-start.1
  10.0 0.0 copy-done
  10.0 0.6 %shard_map.75.old_ref = f32[4,1024]{1,0:T(4,128)S(1)} custom-call(bf16[2,4,1024]{2,1,0:T(4,128)(2,1)S(1)} %shard_map.74.x_ref, bf16[8192,1024]{1,0:T(8,128)(2,1)S(1)} %copy-done), custom_call_target="tpu_custom_call" | custom-call | tf_op jit(solution)/shard_map/pallas_call | solution.py:41
  10.6 0.0 collective-permute-done.3.x_ref
  10.6 0.7 %shard_map.76.old_ref = f32[4,1024]{1,0:T(4,128)S(1)} custom-call(bf16[2,4,1024]{2,1,0:T(4,128)(2,1)S(1)} %collective-permute-done.3.x_ref, bf16[8192,1024]{1,0:T(8,128)(2,1)S(1)} %copy-done, f32[4,1024]{1,0:T(4,128)S(1)} %shard_map.75.old_ref), custom_call_target="tpu_custom_call" | custom-call | tf_op jit(solution)/shard_map/pallas_call | solution.py:41
  11.3 0.0 copy-start.2
  11.3 0.0 copy-start.3
  11.3 0.0 copy-start.5
  11.3 0.0 copy-start.6
  11.3 2.6 %collective-permute-done.2.x_ref = bf16[2,4,1024]{2,1,0:T(4,128)(2,1)S(1)} collective-permute-done((bf16[2,4,1024]{2,1,0:T(4,128)(2,1)S(1)}, bf16[2,4,1024]{2,1,0:T(4,128)(2,1)S(1)}, u32[]{:S(2)}, u32[]{:S(2)}) %collective-permute-start.2) | collective-permute-done | bytes 16416 | tf_op jit(solution)/shard_map/ppermute | solution.py:37
  13.9 0.7 %shard_map.77.old_ref = f32[4,1024]{1,0:T(4,128)S(1)} custom-call(bf16[2,4,1024]{2,1,0:T(4,128)(2,1)S(1)} %collective-permute-done.2.x_ref, bf16[8192,1024]{1,0:T(8,128)(2,1)S(1)} %copy-done, f32[4,1024]{1,0:T(4,128)S(1)} %shard_map.76.old_ref), custom_call_target="tpu_custom_call" | custom-call | tf_op jit(solution)/shard_map/pallas_call | solution.py:41
  14.6 0.0 collective-permute-done.1.x_ref
  14.6 0.7 %shard_map.78 = bf16[8,32,128]{2,1,0:T(8,128)(2,1)S(1)} custom-call(bf16[2,4,1024]{2,1,0:T(4,128)(2,1)S(1)} %collective-permute-done.1.x_ref, bf16[8192,1024]{1,0:T(8,128)(2,1)S(1)} %copy-done, f32[4,1024]{1,0:T(4,128)S(1)} %shard_map.77.old_ref), custom_call_target="tpu_custom_call" | custom-call | tf_op jit(solution)/shard_map/pallas_call | solution.py:41
  15.3 10.3 %all_to_all.15.q_ref = bf16[8,32,128]{2,1,0:T(8,128)(2,1)S(1)} all-to-all(bf16[8,32,128]{2,1,0:T(8,128)(2,1)S(1)} %shard_map.78), channel_id=1, replica_groups=mesh['groups'=2,'section'=2,'tensor'=8] {'tensor'}, dimensions={0} | all-to-all | bytes 131072 | tf_op jit(solution)/shard_map/all_to_all | solution.py:28
  25.6 0.0 copy-done.2
  25.6 0.0 copy-done.3
  25.6 0.0 copy-done.5
  25.6 0.0 copy-done.6
  25.6 0.0 copy-start.1
  25.6 1.5 %shard_map.79 = bf16[8,40,128]{2,1,0:T(8,128)(2,1)S(1)} custom-call(s32[4]{0:T(128)S(1)} %copy-done.5, s32[4]{0:T(128)S(1)} %copy-done.6, bf16[8,32,128]{2,1,0:T(8,128)(2,1)S(1)} %all_to_all.15.q_ref, bf16[4,128,2048]{2,1,0:T(8,128)(2,1)S(1)} %copy-done.2, bf16[4,64,2048]{2,1,0:T(8,128)(2,1)S(1)} %copy-done.3), custom_call_target="tpu_custom_call" | custom-call | flops 999999995904 | tf_op jit(solution)/shard_map/pallas_call | solution.py:41
  27.1 9.9 %all_to_all.16.got_ref = bf16[8,40,128]{2,1,0:T(8,128)(2,1)S(1)} all-to-all(bf16[8,40,128]{2,1,0:T(8,128)(2,1)S(1)} %shard_map.79), channel_id=1, replica_groups=mesh['groups'=2,'section'=2,'tensor'=8] {'tensor'}, dimensions={0} | all-to-all | bytes 163840 | tf_op jit(solution)/shard_map/all_to_all | solution.py:28
  37.1 0.0 copy-done.1
  37.1 2.5 %shard_map.80 = bf16[8,4,1024]{2,1,0:T(4,128)(2,1)S(1)} custom-call(bf16[8,40,128]{2,1,0:T(8,128)(2,1)S(1)} %all_to_all.16.got_ref, bf16[1024,8192]{1,0:T(8,128)(2,1)S(1)} %copy-done.1), custom_call_target="tpu_custom_call" | custom-call | tf_op jit(solution)/shard_map/pallas_call | solution.py:41
  39.6 9.3 %all_to_all.17.x_ref = bf16[8,4,1024]{2,1,0:T(4,128)(2,1)S(1)} all-to-all(bf16[8,4,1024]{2,1,0:T(4,128)(2,1)S(1)} %shard_map.80), channel_id=1, replica_groups=mesh['groups'=2,'section'=2,'tensor'=8] {'tensor'}, dimensions={0} | all-to-all | bytes 131072 | tf_op jit(solution)/shard_map/all_to_all | solution.py:28
  48.9 0.6 %shard_map.81 = bf16[4,1024]{1,0:T(4,128)(2,1)} custom-call(bf16[8,4,1024]{2,1,0:T(4,128)(2,1)S(1)} %all_to_all.17.x_ref), custom_call_target="tpu_custom_call" | custom-call | tf_op jit(solution)/shard_map/pallas_call | solution.py:41
  (2 shorter events, 0.0 us)
Async XLA Ops:
  0.0 0.7 %copy-start.4 = (bf16[4,1024]{1,0:T(4,128)(2,1)S(1)}, bf16[4,1024]{1,0:T(4,128)(2,1)}, u32[]{:S(2)}) copy-start(bf16[4,1024]{1,0:T(4,128)(2,1)} %x_ref.1) | copy-start | bytes 24580
  0.7 9.3 %copy-start = (bf16[8192,1024]{1,0:T(8,128)(2,1)S(1)}, bf16[8192,1024]{1,0:T(8,128)(2,1)}, u32[]{:S(2)}) copy-start(bf16[8192,1024]{1,0:T(8,128)(2,1)} %w_ref.8) | copy-start | bytes 50331652
  0.7 4.6 %collective-permute-start = (bf16[4,1024]{1,0:T(4,128)(2,1)S(1)}, bf16[4,1024]{1,0:T(4,128)(2,1)S(1)}, u32[]{:S(2)}, u32[]{:S(2)}) collective-permute-start(bf16[4,1024]{1,0:T(4,128)(2,1)S(1)} %shard_map.73.x_ref), channel_id=1, source_target_pairs={{0,1},{1,0},{2,3},{3,2},{4,5},{5,4},{6,7},{7,6},{8,9},{9,8},{10,11... | collective-permute-start | bytes 24584 | tf_op jit(solution)/shard_map/ppermute | solution.py:37
  5.3 5.3 %collective-permute-start.3 = (bf16[2,4,1024]{2,1,0:T(4,128)(2,1)S(1)}, bf16[2,4,1024]{2,1,0:T(4,128)(2,1)S(1)}, u32[]{:S(2)}, u32[]{:S(2)}) collective-permute-start(bf16[2,4,1024]{2,1,0:T(4,128)(2,1)S(1)} %shard_map.74.x_ref), channel_id=1, source_target_pairs={{0,4},{1,5},{2,6},{3,7},{4,0},{5,1},{6,2},{7,3},{8,12},{9,13},{10,... | collective-permute-start | bytes 49160 | tf_op jit(solution)/shard_map/ppermute | solution.py:37
  8.4 5.5 %collective-permute-start.2 = (bf16[2,4,1024]{2,1,0:T(4,128)(2,1)S(1)}, bf16[2,4,1024]{2,1,0:T(4,128)(2,1)S(1)}, u32[]{:S(2)}, u32[]{:S(2)}) collective-permute-start(bf16[2,4,1024]{2,1,0:T(4,128)(2,1)S(1)} %shard_map.74.x_ref), channel_id=1, source_target_pairs={{0,6},{1,7},{2,4},{3,5},{4,2},{5,3},{6,0},{7,1},{8,14},{9,15},{10,... | collective-permute-start | bytes 49160 | tf_op jit(solution)/shard_map/ppermute | solution.py:37
  9.7 4.8 %collective-permute-start.1 = (bf16[2,4,1024]{2,1,0:T(4,128)(2,1)S(1)}, bf16[2,4,1024]{2,1,0:T(4,128)(2,1)S(1)}, u32[]{:S(2)}, u32[]{:S(2)}) collective-permute-start(bf16[2,4,1024]{2,1,0:T(4,128)(2,1)S(1)} %shard_map.74.x_ref), channel_id=1, source_target_pairs={{0,2},{1,3},{2,0},{3,1},{4,6},{5,7},{6,4},{7,5},{8,10},{9,11},{10,... | collective-permute-start | bytes 49160 | tf_op jit(solution)/shard_map/ppermute | solution.py:37
  11.3 14.3 %copy-start.2 = (bf16[4,128,2048]{2,1,0:T(8,128)(2,1)S(1)}, bf16[4,128,2048]{2,1,0:T(8,128)(2,1)}, u32[]{:S(2)}) copy-start(bf16[4,128,2048]{2,1,0:T(8,128)(2,1)} %cache_ref.1) | copy-start | bytes 6291460
  11.3 14.3 %copy-start.3 = (bf16[4,64,2048]{2,1,0:T(8,128)(2,1)S(1)}, bf16[4,64,2048]{2,1,0:T(8,128)(2,1)}, u32[]{:S(2)}) copy-start(bf16[4,64,2048]{2,1,0:T(8,128)(2,1)} %fresh_ref.1) | copy-start | bytes 3145732
  11.3 14.3 %copy-start.5 = (s32[4]{0:T(128)S(1)}, s32[4]{0:T(128)}, u32[]{:S(2)}) copy-start(s32[4]{0:T(128)} %clen_ref.1) | copy-start | bytes 52
  11.3 14.3 %copy-start.6 = (s32[4]{0:T(128)S(1)}, s32[4]{0:T(128)}, u32[]{:S(2)}) copy-start(s32[4]{0:T(128)} %nlen_ref.1) | copy-start | bytes 52
  25.6 11.5 %copy-start.1 = (bf16[1024,8192]{1,0:T(8,128)(2,1)S(1)}, bf16[1024,8192]{1,0:T(8,128)(2,1)}, u32[]{:S(2)}) copy-start(bf16[1024,8192]{1,0:T(8,128)(2,1)} %w_ref.9) | copy-start | bytes 50331652

commit v6 on v5

--- a/solution.py
+++ b/solution.py
@@ -21,7 +21,7 @@
 ORDER = (4, 6, 2)
 LONG = 10**12
 FIRST = 0
-ATTEND = 10**12
+ATTEND = 0
 
 
 def exchange(x, shared):
@@ -107,18 +107,11 @@
     shares = q_ref.shape[0] // KVH
     part = GROUP // shares
     place = lax.axis_index("tensor")
-    head_of = lax.broadcasted_iota(jnp.int32, (HEADS, width), 0) // GROUP
-    diagonal = head_of == lax.broadcasted_iota(jnp.int32, (HEADS, width), 1) // HD
-    none = jnp.zeros((HEADS, width), BF16)
+    lane = lax.broadcasted_iota(jnp.int32, (HD, 2 * HEADS), 1)
 
     def logits(ref, r, wide, start, length_ref):
         s = [
-            lax.dot_general(
-                ref[r + i, :, 0:width],
-                wide[i],
-                (((1,), (1,)), ((), ())),
-                preferred_element_type=F32,
-            )
+            dot(ref[r + i, :, 0:width], wide[i])
             for i in range(2)
         ]
         s = s[0] + s[1]
@@ -133,11 +126,15 @@
         both = [
             q_ref[s * KVH + g, at, :].astype(F32) for g in range(KVH) for s in range(shares)
         ]
+        q = [x[i * part : (i + 1) * part] for i in range(2) for x in both]
+        q = jnp.concatenate(q, axis=0).T
         wide = []
         for i in range(2):
-            q = jnp.concatenate([x[i * part : (i + 1) * part] for x in both], axis=0)
-            q = jnp.where(diagonal, jnp.concatenate([q] * KVH, axis=1), 0.0).astype(BF16)
-            wide.append(jnp.concatenate([q, none] if i == 0 else [none, q], axis=0))
+            blocks = []
+            for g in range(KVH):
+                first = i * HEADS + g * GROUP
+                blocks.append(jnp.where((lane >= first) & (lane < first + GROUP), q, 0.0))
+            wide.append(jnp.concatenate(blocks, axis=0).astype(BF16))
         scores.append(
             (
                 logits(cache_ref, r, wide, place * cc, clen_ref),
@@ -268,7 +265,7 @@
         got = [swap(pair, apart) for apart in ORDER]
         for apart, x in zip(ORDER[:2], got):
             step = functools.partial(next_kernel, apart)
-            acc = call(step, (rows, own * HD), F32, x, w_query, acc)
+            acc = call(step, (rows, own * HD), F32, x, w_query, acc, flops=10**10 if apart == ORDER[0] else 0)
         step = functools.partial(last_kernel, ORDER[2])
         q = call(step, (n, rows * own, HD), BF16, got[2], w_query, acc, scratch=scratch)
     else:

time: 49.8 us -> 49.6 us (level)
  no operation moved by 1% of the time
where the time goes in v6:
time: 49.6 us; the launch traced here: 49.3 us
  blocking collectives  29.2 us (59%)
  starting transfers between devices  7.64 us (15%)
  Pallas kernels  7.34 us (15%)
  waiting for transfers between devices  4.22 us (9%)
  local copies, waits for them, and re-layouts  0.74 us (1%)
    all_to_all x3, blocking collectives, exchange(): return lax.all_to_all(x, BOTH if shared > 1 else 'tensor', 0, 0, tiled=True)  29.2 us
    ppermute x4, starting transfers between devices, swap(): return lax.ppermute(x, 'tensor', [(i, i ^ apart) for i in range(n)])  7.64 us
    pallas_call x9, Pallas kernels, call(): pl.pallas_call(kernel, in_specs=specs or [VMEM] * len(args), out_specs=VM...  7.34 us
    ppermute x4, waiting for transfers between devices, swap(): return lax.ppermute(x, 'tensor', [(i, i ^ apart) for i in range(n)])  4.22 us
  transfers between devices with their start and end apart: 4, of which 2 were waited for; matrix products, arithmetic and copies ran while one was open for 0% of the time, Pallas kernels for 4%

profile of v6, /device:TPU:0, one launch (start us, length us, event | category | flops | bytes accessed | tf_op | source)
XLA Modules:
  0.0 49.3 jit_solution(1633596221033703554)
XLA Ops:
  0.0 0.0 copy-start.5
  0.0 0.7 %copy-done.5 = bf16[4,1024]{1,0:T(4,128)(2,1)S(1)} copy-done((bf16[4,1024]{1,0:T(4,128)(2,1)S(1)}, bf16[4,1024]{1,0:T(4,128)(2,1)}, u32[]{:S(2)}) %copy-start.5) | copy-done | bytes 8216
  0.7 0.0 copy-start
  0.7 3.0 %collective-permute-start = (bf16[4,1024]{1,0:T(4,128)(2,1)S(1)}, bf16[4,1024]{1,0:T(4,128)(2,1)S(1)}, u32[]{:S(2)}, u32[]{:S(2)}) collective-permute-start(bf16[4,1024]{1,0:T(4,128)(2,1)S(1)} %shard_map.73.x_ref), channel_id=1, source_target_pairs={{0,1},{1,0},{2,3},{3,2},{4,5},{5,4},{6,7},{7,6},{8,9},{9,8},{10,11... | collective-permute-start | bytes 24584 | tf_op jit(solution)/shard_map/ppermute | solution.py:37
  3.7 1.6 %collective-permute-done.y_ref = bf16[4,1024]{1,0:T(4,128)(2,1)S(1)} collective-permute-done((bf16[4,1024]{1,0:T(4,128)(2,1)S(1)}, bf16[4,1024]{1,0:T(4,128)(2,1)S(1)}, u32[]{:S(2)}, u32[]{:S(2)}) %collective-permute-start) | collective-permute-done | bytes 8224 | tf_op jit(solution)/shard_map/ppermute | solution.py:37
  5.3 3.1 %collective-permute-start.3 = (bf16[2,4,1024]{2,1,0:T(4,128)(2,1)S(1)}, bf16[2,4,1024]{2,1,0:T(4,128)(2,1)S(1)}, u32[]{:S(2)}, u32[]{:S(2)}) collective-permute-start(bf16[2,4,1024]{2,1,0:T(4,128)(2,1)S(1)} %shard_map.74.x_ref), channel_id=1, source_target_pairs={{0,4},{1,5},{2,6},{3,7},{4,0},{5,1},{6,2},{7,3},{8,12},{9,13},{10,... | collective-permute-start | bytes 49160 | tf_op jit(solution)/shard_map/ppermute | solution.py:37
  8.4 1.3 %collective-permute-start.2 = (bf16[2,4,1024]{2,1,0:T(4,128)(2,1)S(1)}, bf16[2,4,1024]{2,1,0:T(4,128)(2,1)S(1)}, u32[]{:S(2)}, u32[]{:S(2)}) collective-permute-start(bf16[2,4,1024]{2,1,0:T(4,128)(2,1)S(1)} %shard_map.74.x_ref), channel_id=1, source_target_pairs={{0,6},{1,7},{2,4},{3,5},{4,2},{5,3},{6,0},{7,1},{8,14},{9,15},{10,... | collective-permute-start | bytes 49160 | tf_op jit(solution)/shard_map/ppermute | solution.py:37
  9.7 0.2 collective-permute-start.1
  10.0 0.0 copy-done
  10.0 0.6 %shard_map.75.old_ref = f32[4,1024]{1,0:T(4,128)S(1)} custom-call(bf16[2,4,1024]{2,1,0:T(4,128)(2,1)S(1)} %shard_map.74.x_ref, bf16[8192,1024]{1,0:T(8,128)(2,1)S(1)} %copy-done), custom_call_target="tpu_custom_call" | custom-call | tf_op jit(solution)/shard_map/pallas_call | solution.py:41
  10.6 0.0 collective-permute-done.3.x_ref
  10.6 0.7 %shard_map.76.old_ref = f32[4,1024]{1,0:T(4,128)S(1)} custom-call(bf16[2,4,1024]{2,1,0:T(4,128)(2,1)S(1)} %collective-permute-done.3.x_ref, bf16[8192,1024]{1,0:T(8,128)(2,1)S(1)} %copy-done, f32[4,1024]{1,0:T(4,128)S(1)} %shard_map.75.old_ref), custom_call_target="tpu_custom_call" | custom-call | flops 10000000000 | tf_op jit(solution)/shard_map/pallas_call | solution.py:41
  11.3 0.0 copy-start.1
  11.3 0.0 copy-start.2
  11.3 0.0 copy-start.3
  11.3 0.0 copy-start.4
  11.3 0.0 slice-start
  11.3 0.0 slice-start.1
  11.3 2.6 %collective-permute-done.2.x_ref = bf16[2,4,1024]{2,1,0:T(4,128)(2,1)S(1)} collective-permute-done((bf16[2,4,1024]{2,1,0:T(4,128)(2,1)S(1)}, bf16[2,4,1024]{2,1,0:T(4,128)(2,1)S(1)}, u32[]{:S(2)}, u32[]{:S(2)}) %collective-permute-start.2) | collective-permute-done | bytes 16416 | tf_op jit(solution)/shard_map/ppermute | solution.py:37
  13.9 0.7 %shard_map.77.old_ref = f32[4,1024]{1,0:T(4,128)S(1)} custom-call(bf16[2,4,1024]{2,1,0:T(4,128)(2,1)S(1)} %collective-permute-done.2.x_ref, bf16[8192,1024]{1,0:T(8,128)(2,1)S(1)} %copy-done, f32[4,1024]{1,0:T(4,128)S(1)} %shard_map.76.old_ref), custom_call_target="tpu_custom_call" | custom-call | tf_op jit(solution)/shard_map/pallas_call | solution.py:41
  14.6 0.0 slice-start.2
  14.6 0.0 slice-start.3
  14.6 0.0 collective-permute-done.1.x_ref
  14.6 0.7 %shard_map.78 = bf16[8,32,128]{2,1,0:T(8,128)(2,1)S(1)} custom-call(bf16[2,4,1024]{2,1,0:T(4,128)(2,1)S(1)} %collective-permute-done.1.x_ref, bf16[8192,1024]{1,0:T(8,128)(2,1)S(1)} %copy-done, f32[4,1024]{1,0:T(4,128)S(1)} %shard_map.77.old_ref), custom_call_target="tpu_custom_call" | custom-call | tf_op jit(solution)/shard_map/pallas_call | solution.py:41
  15.3 10.5 %all_to_all.15.q_ref = bf16[8,32,128]{2,1,0:T(8,128)(2,1)S(1)} all-to-all(bf16[8,32,128]{2,1,0:T(8,128)(2,1)S(1)} %shard_map.78), channel_id=1, replica_groups=mesh['groups'=2,'section'=2,'tensor'=8] {'tensor'}, dimensions={0} | all-to-all | bytes 131072 | tf_op jit(solution)/shard_map/all_to_all | solution.py:28
  25.8 0.0 copy-done.1
  25.8 0.0 copy-done.2
  25.8 0.0 copy-done.3
  25.8 0.0 copy-done.4
  25.8 1.5 %shard_map.79 = bf16[8,40,128]{2,1,0:T(8,128)(2,1)S(1)} custom-call(s32[4]{0:T(128)S(1)} %copy-done.3, s32[4]{0:T(128)S(1)} %copy-done.4, bf16[8,32,128]{2,1,0:T(8,128)(2,1)S(1)} %all_to_all.15.q_ref, bf16[4,128,2048]{2,1,0:T(8,128)(2,1)S(1)} %copy-done.1, bf16[4,64,2048]{2,1,0:T(8,128)(2,1)S(1)} %copy-done.2), custom_call_target="tpu_custom_call" | custom-call | tf_op jit(solution)/shard_map/pallas_call | solution.py:41
  27.4 9.4 %all_to_all.16.got_ref = bf16[8,40,128]{2,1,0:T(8,128)(2,1)S(1)} all-to-all(bf16[8,40,128]{2,1,0:T(8,128)(2,1)S(1)} %shard_map.79), channel_id=1, replica_groups=mesh['groups'=2,'section'=2,'tensor'=8] {'tensor'}, dimensions={0} | all-to-all | bytes 163840 | tf_op jit(solution)/shard_map/all_to_all | solution.py:28
  36.8 0.0 slice-done
  36.8 0.0 slice-done.1
  36.8 0.0 slice-done.2
  36.8 0.0 slice-done.3
  36.8 2.5 %shard_map.80 = bf16[8,4,1024]{2,1,0:T(4,128)(2,1)S(1)} custom-call(bf16[8,40,128]{2,1,0:T(8,128)(2,1)S(1)} %all_to_all.16.got_ref, bf16[1024,8192]{1,0:T(8,128)(2,1)S(1)} %bitcast.1), custom_call_target="tpu_custom_call" | custom-call | tf_op jit(solution)/shard_map/pallas_call | solution.py:41
  39.4 9.3 %all_to_all.17.x_ref = bf16[8,4,1024]{2,1,0:T(4,128)(2,1)S(1)} all-to-all(bf16[8,4,1024]{2,1,0:T(4,128)(2,1)S(1)} %shard_map.80), channel_id=1, replica_groups=mesh['groups'=2,'section'=2,'tensor'=8] {'tensor'}, dimensions={0} | all-to-all | bytes 131072 | tf_op jit(solution)/shard_map/all_to_all | solution.py:28
  48.6 0.6 %shard_map.81 = bf16[4,1024]{1,0:T(4,128)(2,1)} custom-call(bf16[8,4,1024]{2,1,0:T(4,128)(2,1)S(1)} %all_to_all.17.x_ref), custom_call_target="tpu_custom_call" | custom-call | tf_op jit(solution)/shard_map/pallas_call | solution.py:41
  (3 shorter events, 0.0 us)
Async XLA Ops:
  0.0 0.7 %copy-start.5 = (bf16[4,1024]{1,0:T(4,128)(2,1)S(1)}, bf16[4,1024]{1,0:T(4,128)(2,1)}, u32[]{:S(2)}) copy-start(bf16[4,1024]{1,0:T(4,128)(2,1)} %x_ref.1) | copy-start | bytes 24580
  0.7 9.3 %copy-start = (bf16[8192,1024]{1,0:T(8,128)(2,1)S(1)}, bf16[8192,1024]{1,0:T(8,128)(2,1)}, u32[]{:S(2)}) copy-start(bf16[8192,1024]{1,0:T(8,128)(2,1)} %w_ref.8) | copy-start | bytes 50331652
  0.7 4.6 %collective-permute-start = (bf16[4,1024]{1,0:T(4,128)(2,1)S(1)}, bf16[4,1024]{1,0:T(4,128)(2,1)S(1)}, u32[]{:S(2)}, u32[]{:S(2)}) collective-permute-start(bf16[4,1024]{1,0:T(4,128)(2,1)S(1)} %shard_map.73.x_ref), channel_id=1, source_target_pairs={{0,1},{1,0},{2,3},{3,2},{4,5},{5,4},{6,7},{7,6},{8,9},{9,8},{10,11... | collective-permute-start | bytes 24584 | tf_op jit(solution)/shard_map/ppermute | solution.py:37
  5.3 5.3 %collective-permute-start.3 = (bf16[2,4,1024]{2,1,0:T(4,128)(2,1)S(1)}, bf16[2,4,1024]{2,1,0:T(4,128)(2,1)S(1)}, u32[]{:S(2)}, u32[]{:S(2)}) collective-permute-start(bf16[2,4,1024]{2,1,0:T(4,128)(2,1)S(1)} %shard_map.74.x_ref), channel_id=1, source_target_pairs={{0,4},{1,5},{2,6},{3,7},{4,0},{5,1},{6,2},{7,3},{8,12},{9,13},{10,... | collective-permute-start | bytes 49160 | tf_op jit(solution)/shard_map/ppermute | solution.py:37
  8.4 5.5 %collective-permute-start.2 = (bf16[2,4,1024]{2,1,0:T(4,128)(2,1)S(1)}, bf16[2,4,1024]{2,1,0:T(4,128)(2,1)S(1)}, u32[]{:S(2)}, u32[]{:S(2)}) collective-permute-start(bf16[2,4,1024]{2,1,0:T(4,128)(2,1)S(1)} %shard_map.74.x_ref), channel_id=1, source_target_pairs={{0,6},{1,7},{2,4},{3,5},{4,2},{5,3},{6,0},{7,1},{8,14},{9,15},{10,... | collective-permute-start | bytes 49160 | tf_op jit(solution)/shard_map/ppermute | solution.py:37
  9.7 4.9 %collective-permute-start.1 = (bf16[2,4,1024]{2,1,0:T(4,128)(2,1)S(1)}, bf16[2,4,1024]{2,1,0:T(4,128)(2,1)S(1)}, u32[]{:S(2)}, u32[]{:S(2)}) collective-permute-start(bf16[2,4,1024]{2,1,0:T(4,128)(2,1)S(1)} %shard_map.74.x_ref), channel_id=1, source_target_pairs={{0,2},{1,3},{2,0},{3,1},{4,6},{5,7},{6,4},{7,5},{8,10},{9,11},{10,... | collective-permute-start | bytes 49160 | tf_op jit(solution)/shard_map/ppermute | solution.py:37
  11.3 14.5 %copy-start.1 = (bf16[4,128,2048]{2,1,0:T(8,128)(2,1)S(1)}, bf16[4,128,2048]{2,1,0:T(8,128)(2,1)}, u32[]{:S(2)}) copy-start(bf16[4,128,2048]{2,1,0:T(8,128)(2,1)} %cache_ref.1) | copy-start | bytes 6291460
  11.3 14.5 %copy-start.2 = (bf16[4,64,2048]{2,1,0:T(8,128)(2,1)S(1)}, bf16[4,64,2048]{2,1,0:T(8,128)(2,1)}, u32[]{:S(2)}) copy-start(bf16[4,64,2048]{2,1,0:T(8,128)(2,1)} %fresh_ref.1) | copy-start | bytes 3145732
  11.3 14.5 %copy-start.3 = (s32[4]{0:T(128)S(1)}, s32[4]{0:T(128)}, u32[]{:S(2)}) copy-start(s32[4]{0:T(128)} %clen_ref.1) | copy-start | bytes 52
  11.3 14.5 %copy-start.4 = (s32[4]{0:T(128)S(1)}, s32[4]{0:T(128)}, u32[]{:S(2)}) copy-start(s32[4]{0:T(128)} %nlen_ref.1) | copy-start | bytes 52
  11.3 25.5 %slice-start = ((s8[16777216]{0:T(1024)(128)(4,1)}), s8[4194304]{0:T(1024)(128)(4,1)S(1)}, s32[]{:S(2)}) async-start(s8[16777216]{0:T(1024)(128)(4,1)} %bitcast), calls=%async_computation.3 | async-start | bytes 8388608
  11.3 25.5 %slice-start.1 = ((s8[16777216]{0:T(1024)(128)(4,1)}), s8[4194304]{0:T(1024)(128)(4,1)S(1)}, s32[]{:S(2)}) async-start(s8[16777216]{0:T(1024)(128)(4,1)} %bitcast), calls=%async_computation.4 | async-start | bytes 8388608
  14.6 22.2 %slice-start.2 = ((s8[16777216]{0:T(1024)(128)(4,1)}), s8[4194304]{0:T(1024)(128)(4,1)S(1)}, s32[]{:S(2)}) async-start(s8[16777216]{0:T(1024)(128)(4,1)} %bitcast), calls=%async_computation.5 | async-start | bytes 8388608
  14.6 22.2 %slice-start.3 = ((s8[16777216]{0:T(1024)(128)(4,1)}), s8[4194304]{0:T(1024)(128)(4,1)S(1)}, s32[]{:S(2)}) async-start(s8[16777216]{0:T(1024)(128)(4,1)} %bitcast), calls=%async_computation.6 | async-start | bytes 8388608

commit v7 on v6

--- a/solution.py
+++ b/solution.py
@@ -35,6 +35,11 @@
 def swap(x, apart):
     n = lax.axis_size("tensor")
     return lax.ppermute(x, "tensor", [(i, i ^ apart) for i in range(n)])
+
+
+def flip(x, apart):
+    n = lax.axis_size("tensor")
+    return lax.ppermute(x, BOTH, [(i, ((i // n) ^ 1) * n + (i % n ^ apart)) for i in range(2 * n)])
 
 
 def call(kernel, shape, dtype, *args, specs=None, scratch=(), flops=0):
@@ -259,10 +264,10 @@
     scratch = [pltpu.VMEM((rows * own, HD), F32)]
     if n == 8:
         mine = call(copy_kernel, (rows, feat), BF16, hidden, flops=LONG)
-        near = swap(mine, 1)
-        pair = call(stack_kernel, (2, rows, feat), BF16, mine, near)
-        acc = call(first_kernel, (rows, own * HD), F32, pair, w_query, flops=FIRST)
-        got = [swap(pair, apart) for apart in ORDER]
+        near = flip(mine, 1)
+        pair = call(stack_kernel, (2, rows, feat), BF16, flip(mine, 0), near)
+        acc = call(first_kernel, (rows, own * HD), F32, flip(pair, 0), w_query, flops=FIRST)
+        got = [flip(pair, apart) for apart in ORDER]
         for apart, x in zip(ORDER[:2], got):
             step = functools.partial(next_kernel, apart)
             acc = call(step, (rows, own * HD), F32, x, w_query, acc, flops=10**10 if apart == ORDER[0] else 0)

time: 49.6 us -> 48.6 us (0.980)
  waiting for transfers between devices: 4.22 us -> 3.12 us
    ppermute x4 -> x6, waiting for transfers between devices: 4.22 us -> 3.12 us  [flip(): lax.ppermute(x, BOTH, [(i, (i // n ^ 1) * n + (i % n ^ apart)) for i in r...]
    ppermute x4 -> x6, starting transfers between devices: 7.64 us -> 7.75 us  [flip(): lax.ppermute(x, BOTH, [(i, (i // n ^ 1) * n + (i % n ^ apart)) for i in r...]
  transfers between devices with their start and end apart: 4 -> 6, of which waited for: 2 -> 3; matrix products, arithmetic and copies ran while one was open for 0% -> 0% of each run, Pallas kernels for 4% -> 4%
where the time goes in v7:
time: 48.6 us; the launch traced here: 48.3 us
  blocking collectives  29.3 us (60%)
  starting transfers between devices  7.75 us (16%)
  Pallas kernels  7.35 us (15%)
  waiting for transfers between devices  3.12 us (6%)
  local copies, waits for them, and re-layouts  0.74 us (2%)
    all_to_all x3, blocking collectives, exchange(): return lax.all_to_all(x, BOTH if shared > 1 else 'tensor', 0, 0, tiled=True)  29.3 us
    ppermute x6, starting transfers between devices, flip(): lax.ppermute(x, BOTH, [(i, (i // n ^ 1) * n + (i % n ^ apart)) for i in r...  7.75 us
    pallas_call x9, Pallas kernels, call(): pl.pallas_call(kernel, in_specs=specs or [VMEM] * len(args), out_specs=VM...  7.35 us
    ppermute x6, waiting for transfers between devices, flip(): lax.ppermute(x, BOTH, [(i, (i // n ^ 1) * n + (i % n ^ apart)) for i in r...  3.12 us
  transfers between devices with their start and end apart: 6, of which 3 were waited for; matrix products, arithmetic and copies ran while one was open for 0% of the time, Pallas kernels for 4%

profile of v7, /device:TPU:0, one launch (start us, length us, event | category | flops | bytes accessed | tf_op | source)
XLA Modules:
  0.0 48.3 jit_solution(14332363573140820631)
XLA Ops:
  0.0 0.0 copy-start.5
  0.0 0.7 %copy-done.5 = bf16[4,1024]{1,0:T(4,128)(2,1)S(1)} copy-done((bf16[4,1024]{1,0:T(4,128)(2,1)S(1)}, bf16[4,1024]{1,0:T(4,128)(2,1)}, u32[]{:S(2)}) %copy-start.5) | copy-done | bytes 8216
  0.7 0.0 copy-start
  0.7 2.4 %collective-permute-start.1 = (bf16[4,1024]{1,0:T(4,128)(2,1)S(1)}, bf16[4,1024]{1,0:T(4,128)(2,1)S(1)}, u32[]{:S(2)}, u32[]{:S(2)}) collective-permute-start(bf16[4,1024]{1,0:T(4,128)(2,1)S(1)} %shard_map.73), channel_id=1, source_target_pairs={{0,9},{1,8},{2,11},{3,10},{4,13},{5,12},{6,15},{7,14},{8,1},{9,0},... | collective-permute-start | bytes 24584 | tf_op jit(solution)/shard_map/ppermute | solution.py:42
  3.1 0.7 %collective-permute-start = (bf16[4,1024]{1,0:T(4,128)(2,1)S(1)}, bf16[4,1024]{1,0:T(4,128)(2,1)S(1)}, u32[]{:S(2)}, u32[]{:S(2)}) collective-permute-start(bf16[4,1024]{1,0:T(4,128)(2,1)S(1)} %shard_map.73), channel_id=1, source_target_pairs={{0,8},{1,9},{2,10},{3,11},{4,12},{5,13},{6,14},{7,15},{8,0},{9,1},... | collective-permute-start | bytes 24584 | tf_op jit(solution)/shard_map/ppermute | solution.py:42
  3.8 0.7 %collective-permute-done.1.y_ref = bf16[4,1024]{1,0:T(4,128)(2,1)S(1)} collective-permute-done((bf16[4,1024]{1,0:T(4,128)(2,1)S(1)}, bf16[4,1024]{1,0:T(4,128)(2,1)S(1)}, u32[]{:S(2)}, u32[]{:S(2)}) %collective-permute-start.1) | collective-permute-done | bytes 8224 | tf_op jit(solution)/shard_map/ppermute | solution.py:42
  4.5 0.1 collective-permute-done.x_ref
  4.6 0.5 %collective-permute-start.5 = (bf16[2,4,1024]{2,1,0:T(4,128)(2,1)S(1)}, bf16[2,4,1024]{2,1,0:T(4,128)(2,1)S(1)}, u32[]{:S(2)}, u32[]{:S(2)}) collective-permute-start(bf16[2,4,1024]{2,1,0:T(4,128)(2,1)S(1)} %shard_map.74), channel_id=1, source_target_pairs={{0,8},{1,9},{2,10},{3,11},{4,12},{5,13},{6,14},{7,15},{8,0},{9,1},... | collective-permute-start | bytes 49160 | tf_op jit(solution)/shard_map/ppermute | solution.py:42
  5.1 2.8 %collective-permute-start.4 = (bf16[2,4,1024]{2,1,0:T(4,128)(2,1)S(1)}, bf16[2,4,1024]{2,1,0:T(4,128)(2,1)S(1)}, u32[]{:S(2)}, u32[]{:S(2)}) collective-permute-start(bf16[2,4,1024]{2,1,0:T(4,128)(2,1)S(1)} %shard_map.74), channel_id=1, source_target_pairs={{0,12},{1,13},{2,14},{3,15},{4,8},{5,9},{6,10},{7,11},{8,4},{9,5},... | collective-permute-start | bytes 49160 | tf_op jit(solution)/shard_map/ppermute | solution.py:42
  8.0 1.1 %collective-permute-start.3 = (bf16[2,4,1024]{2,1,0:T(4,128)(2,1)S(1)}, bf16[2,4,1024]{2,1,0:T(4,128)(2,1)S(1)}, u32[]{:S(2)}, u32[]{:S(2)}) collective-permute-start(bf16[2,4,1024]{2,1,0:T(4,128)(2,1)S(1)} %shard_map.74), channel_id=1, source_target_pairs={{0,14},{1,15},{2,12},{3,13},{4,10},{5,11},{6,8},{7,9},{8,6},{9,7},... | collective-permute-start | bytes 49160 | tf_op jit(solution)/shard_map/ppermute | solution.py:42
  9.1 0.2 collective-permute-start.2
  9.3 0.0 collective-permute-done.5.x_ref
  9.3 0.0 copy-done
  9.3 0.7 %shard_map.75.old_ref = f32[4,1024]{1,0:T(4,128)S(1)} custom-call(bf16[2,4,1024]{2,1,0:T(4,128)(2,1)S(1)} %collective-permute-done.5.x_ref, bf16[8192,1024]{1,0:T(8,128)(2,1)S(1)} %copy-done), custom_call_target="tpu_custom_call" | custom-call | tf_op jit(solution)/shard_map/pallas_call | solution.py:46
  9.9 0.0 collective-permute-done.4.x_ref
  9.9 0.7 %shard_map.76.old_ref = f32[4,1024]{1,0:T(4,128)S(1)} custom-call(bf16[2,4,1024]{2,1,0:T(4,128)(2,1)S(1)} %collective-permute-done.4.x_ref, bf16[8192,1024]{1,0:T(8,128)(2,1)S(1)} %copy-done, f32[4,1024]{1,0:T(4,128)S(1)} %shard_map.75.old_ref), custom_call_target="tpu_custom_call" | custom-call | flops 10000000000 | tf_op jit(solution)/shard_map/pallas_call | solution.py:46
  10.6 0.0 copy-start.1
  10.6 0.0 copy-start.2
  10.6 0.0 copy-start.3
  10.6 0.0 copy-start.4
  10.6 0.0 slice-start
  10.7 0.0 slice-start.1
  10.7 2.3 %collective-permute-done.3.x_ref = bf16[2,4,1024]{2,1,0:T(4,128)(2,1)S(1)} collective-permute-done((bf16[2,4,1024]{2,1,0:T(4,128)(2,1)S(1)}, bf16[2,4,1024]{2,1,0:T(4,128)(2,1)S(1)}, u32[]{:S(2)}, u32[]{:S(2)}) %collective-permute-start.3) | collective-permute-done | bytes 16416 | tf_op jit(solution)/shard_map/ppermute | solution.py:42
  12.9 0.7 %shard_map.77.old_ref = f32[4,1024]{1,0:T(4,128)S(1)} custom-call(bf16[2,4,1024]{2,1,0:T(4,128)(2,1)S(1)} %collective-permute-done.3.x_ref, bf16[8192,1024]{1,0:T(8,128)(2,1)S(1)} %copy-done, f32[4,1024]{1,0:T(4,128)S(1)} %shard_map.76.old_ref), custom_call_target="tpu_custom_call" | custom-call | tf_op jit(solution)/shard_map/pallas_call | solution.py:46
  13.6 0.0 slice-start.2
  13.6 0.0 slice-start.3
  13.6 0.0 collective-permute-done.2.x_ref
  13.6 0.7 %shard_map.78 = bf16[8,32,128]{2,1,0:T(8,128)(2,1)S(1)} custom-call(bf16[2,4,1024]{2,1,0:T(4,128)(2,1)S(1)} %collective-permute-done.2.x_ref, bf16[8192,1024]{1,0:T(8,128)(2,1)S(1)} %copy-done, f32[4,1024]{1,0:T(4,128)S(1)} %shard_map.77.old_ref), custom_call_target="tpu_custom_call" | custom-call | tf_op jit(solution)/shard_map/pallas_call | solution.py:46
  14.3 10.6 %all_to_all.15.q_ref = bf16[8,32,128]{2,1,0:T(8,128)(2,1)S(1)} all-to-all(bf16[8,32,128]{2,1,0:T(8,128)(2,1)S(1)} %shard_map.78), channel_id=1, replica_groups=mesh['groups'=2,'section'=2,'tensor'=8] {'tensor'}, dimensions={0} | all-to-all | bytes 131072 | tf_op jit(solution)/shard_map/all_to_all | solution.py:28
  24.9 0.0 copy-done.1
  24.9 0.0 copy-done.2
  24.9 0.0 copy-done.3
  24.9 0.0 copy-done.4
  24.9 1.5 %shard_map.79 = bf16[8,40,128]{2,1,0:T(8,128)(2,1)S(1)} custom-call(s32[4]{0:T(128)S(1)} %copy-done.3, s32[4]{0:T(128)S(1)} %copy-done.4, bf16[8,32,128]{2,1,0:T(8,128)(2,1)S(1)} %all_to_all.15.q_ref, bf16[4,128,2048]{2,1,0:T(8,128)(2,1)S(1)} %copy-done.1, bf16[4,64,2048]{2,1,0:T(8,128)(2,1)S(1)} %copy-done.2), custom_call_target="tpu_custom_call" | custom-call | tf_op jit(solution)/shard_map/pallas_call | solution.py:46
  26.4 9.4 %all_to_all.16.got_ref = bf16[8,40,128]{2,1,0:T(8,128)(2,1)S(1)} all-to-all(bf16[8,40,128]{2,1,0:T(8,128)(2,1)S(1)} %shard_map.79), channel_id=1, replica_groups=mesh['groups'=2,'section'=2,'tensor'=8] {'tensor'}, dimensions={0} | all-to-all | bytes 163840 | tf_op jit(solution)/shard_map/all_to_all | solution.py:28
  35.8 0.0 slice-done
  35.8 0.0 slice-done.1
  35.8 0.0 slice-done.2
  35.8 0.0 slice-done.3
  35.9 2.5 %shard_map.80 = bf16[8,4,1024]{2,1,0:T(4,128)(2,1)S(1)} custom-call(bf16[8,40,128]{2,1,0:T(8,128)(2,1)S(1)} %all_to_all.16.got_ref, bf16[1024,8192]{1,0:T(8,128)(2,1)S(1)} %bitcast.1), custom_call_target="tpu_custom_call" | custom-call | tf_op jit(solution)/shard_map/pallas_call | solution.py:46
  38.4 9.3 %all_to_all.17.x_ref = bf16[8,4,1024]{2,1,0:T(4,128)(2,1)S(1)} all-to-all(bf16[8,4,1024]{2,1,0:T(4,128)(2,1)S(1)} %shard_map.80), channel_id=1, replica_groups=mesh['groups'=2,'section'=2,'tensor'=8] {'tensor'}, dimensions={0} | all-to-all | bytes 131072 | tf_op jit(solution)/shard_map/all_to_all | solution.py:28
  47.7 0.6 %shard_map.81 = bf16[4,1024]{1,0:T(4,128)(2,1)} custom-call(bf16[8,4,1024]{2,1,0:T(4,128)(2,1)S(1)} %all_to_all.17.x_ref), custom_call_target="tpu_custom_call" | custom-call | tf_op jit(solution)/shard_map/pallas_call | solution.py:46
  (3 shorter events, 0.0 us)
Async XLA Ops:
  0.0 0.7 %copy-start.5 = (bf16[4,1024]{1,0:T(4,128)(2,1)S(1)}, bf16[4,1024]{1,0:T(4,128)(2,1)}, u32[]{:S(2)}) copy-start(bf16[4,1024]{1,0:T(4,128)(2,1)} %x_ref.1) | copy-start | bytes 24580
  0.7 8.6 %copy-start = (bf16[8192,1024]{1,0:T(8,128)(2,1)S(1)}, bf16[8192,1024]{1,0:T(8,128)(2,1)}, u32[]{:S(2)}) copy-start(bf16[8192,1024]{1,0:T(8,128)(2,1)} %w_ref.8) | copy-start | bytes 50331652
  0.7 3.8 %collective-permute-start.1 = (bf16[4,1024]{1,0:T(4,128)(2,1)S(1)}, bf16[4,1024]{1,0:T(4,128)(2,1)S(1)}, u32[]{:S(2)}, u32[]{:S(2)}) collective-permute-start(bf16[4,1024]{1,0:T(4,128)(2,1)S(1)} %shard_map.73), channel_id=1, source_target_pairs={{0,9},{1,8},{2,11},{3,10},{4,13},{5,12},{6,15},{7,14},{8,1},{9,0},... | collective-permute-start | bytes 24584 | tf_op jit(solution)/shard_map/ppermute | solution.py:42
  3.1 1.5 %collective-permute-start = (bf16[4,1024]{1,0:T(4,128)(2,1)S(1)}, bf16[4,1024]{1,0:T(4,128)(2,1)S(1)}, u32[]{:S(2)}, u32[]{:S(2)}) collective-permute-start(bf16[4,1024]{1,0:T(4,128)(2,1)S(1)} %shard_map.73), channel_id=1, source_target_pairs={{0,8},{1,9},{2,10},{3,11},{4,12},{5,13},{6,14},{7,15},{8,0},{9,1},... | collective-permute-start | bytes 24584 | tf_op jit(solution)/shard_map/ppermute | solution.py:42
  4.6 4.7 %collective-permute-start.5 = (bf16[2,4,1024]{2,1,0:T(4,128)(2,1)S(1)}, bf16[2,4,1024]{2,1,0:T(4,128)(2,1)S(1)}, u32[]{:S(2)}, u32[]{:S(2)}) collective-permute-start(bf16[2,4,1024]{2,1,0:T(4,128)(2,1)S(1)} %shard_map.74), channel_id=1, source_target_pairs={{0,8},{1,9},{2,10},{3,11},{4,12},{5,13},{6,14},{7,15},{8,0},{9,1},... | collective-permute-start | bytes 49160 | tf_op jit(solution)/shard_map/ppermute | solution.py:42
  5.1 4.8 %collective-permute-start.4 = (bf16[2,4,1024]{2,1,0:T(4,128)(2,1)S(1)}, bf16[2,4,1024]{2,1,0:T(4,128)(2,1)S(1)}, u32[]{:S(2)}, u32[]{:S(2)}) collective-permute-start(bf16[2,4,1024]{2,1,0:T(4,128)(2,1)S(1)} %shard_map.74), channel_id=1, source_target_pairs={{0,12},{1,13},{2,14},{3,15},{4,8},{5,9},{6,10},{7,11},{8,4},{9,5},... | collective-permute-start | bytes 49160 | tf_op jit(solution)/shard_map/ppermute | solution.py:42
  8.0 5.0 %collective-permute-start.3 = (bf16[2,4,1024]{2,1,0:T(4,128)(2,1)S(1)}, bf16[2,4,1024]{2,1,0:T(4,128)(2,1)S(1)}, u32[]{:S(2)}, u32[]{:S(2)}) collective-permute-start(bf16[2,4,1024]{2,1,0:T(4,128)(2,1)S(1)} %shard_map.74), channel_id=1, source_target_pairs={{0,14},{1,15},{2,12},{3,13},{4,10},{5,11},{6,8},{7,9},{8,6},{9,7},... | collective-permute-start | bytes 49160 | tf_op jit(solution)/shard_map/ppermute | solution.py:42
  9.1 4.6 %collective-permute-start.2 = (bf16[2,4,1024]{2,1,0:T(4,128)(2,1)S(1)}, bf16[2,4,1024]{2,1,0:T(4,128)(2,1)S(1)}, u32[]{:S(2)}, u32[]{:S(2)}) collective-permute-start(bf16[2,4,1024]{2,1,0:T(4,128)(2,1)S(1)} %shard_map.74), channel_id=1, source_target_pairs={{0,10},{1,11},{2,8},{3,9},{4,14},{5,15},{6,12},{7,13},{8,2},{9,3},... | collective-permute-start | bytes 49160 | tf_op jit(solution)/shard_map/ppermute | solution.py:42
  10.6 14.3 %copy-start.1 = (bf16[4,128,2048]{2,1,0:T(8,128)(2,1)S(1)}, bf16[4,128,2048]{2,1,0:T(8,128)(2,1)}, u32[]{:S(2)}) copy-start(bf16[4,128,2048]{2,1,0:T(8,128)(2,1)} %cache_ref.1) | copy-start | bytes 6291460
  10.6 14.3 %copy-start.2 = (bf16[4,64,2048]{2,1,0:T(8,128)(2,1)S(1)}, bf16[4,64,2048]{2,1,0:T(8,128)(2,1)}, u32[]{:S(2)}) copy-start(bf16[4,64,2048]{2,1,0:T(8,128)(2,1)} %fresh_ref.1) | copy-start | bytes 3145732
  10.6 14.3 %copy-start.3 = (s32[4]{0:T(128)S(1)}, s32[4]{0:T(128)}, u32[]{:S(2)}) copy-start(s32[4]{0:T(128)} %clen_ref.1) | copy-start | bytes 52
  10.6 14.2 %copy-start.4 = (s32[4]{0:T(128)S(1)}, s32[4]{0:T(128)}, u32[]{:S(2)}) copy-start(s32[4]{0:T(128)} %nlen_ref.1) | copy-start | bytes 52
  10.6 25.2 %slice-start = ((s8[16777216]{0:T(1024)(128)(4,1)}), s8[4194304]{0:T(1024)(128)(4,1)S(1)}, s32[]{:S(2)}) async-start(s8[16777216]{0:T(1024)(128)(4,1)} %bitcast), calls=%async_computation.3 | async-start | bytes 8388608
  10.7 25.2 %slice-start.1 = ((s8[16777216]{0:T(1024)(128)(4,1)}), s8[4194304]{0:T(1024)(128)(4,1)S(1)}, s32[]{:S(2)}) async-start(s8[16777216]{0:T(1024)(128)(4,1)} %bitcast), calls=%async_computation.4 | async-start | bytes 8388608
  13.6 22.2 %slice-start.2 = ((s8[16777216]{0:T(1024)(128)(4,1)}), s8[4194304]{0:T(1024)(128)(4,1)S(1)}, s32[]{:S(2)}) async-start(s8[16777216]{0:T(1024)(128)(4,1)} %bitcast), calls=%async_computation.5 | async-start | bytes 8388608
  13.6 22.2 %slice-start.3 = ((s8[16777216]{0:T(1024)(128)(4,1)}), s8[4194304]{0:T(1024)(128)(4,1)S(1)}, s32[]{:S(2)}) async-start(s8[16777216]{0:T(1024)(128)(4,1)} %bitcast), calls=%async_computation.6 | async-start | bytes 8388608

commit v8 on v7

--- a/solution.py
+++ b/solution.py
@@ -19,6 +19,9 @@
 BOTH = ("section", "tensor")
 SPLIT_OUTPUT = False
 ORDER = (4, 6, 2)
+BACK = (4, 6, 2)
+ADD = 23000000
+PIECE = 11500000
 LONG = 10**12
 FIRST = 0
 ATTEND = 0
@@ -43,11 +46,16 @@
 
 
 def call(kernel, shape, dtype, *args, specs=None, scratch=(), flops=0):
+    if isinstance(shape, list):
+        out = [jax.ShapeDtypeStruct(*x) for x in zip(shape, dtype)]
+        outs = [VMEM] * len(out)
+    else:
+        out, outs = jax.ShapeDtypeStruct(shape, dtype), VMEM
     return pl.pallas_call(
         kernel,
         in_specs=specs or [VMEM] * len(args),
-        out_specs=VMEM,
-        out_shape=jax.ShapeDtypeStruct(shape, dtype),
+        out_specs=outs,
+        out_shape=out,
         scratch_shapes=scratch,
         cost_estimate=pl.CostEstimate(flops=flops, bytes_accessed=0, transcendentals=0),
         compiler_params=pltpu.CompilerParams(vmem_limit_bytes=8 << 20),
@@ -185,12 +193,11 @@
         o_ref[d, rows * GROUP :, :] = stats
 
 
-def project_kernel(shared, own, got_ref, w_ref, o_ref, heads_ref):
+def combine(shared, own, got_ref, heads_ref):
     total, both, _ = got_ref.shape
     both -= STATS
     n = total // shared
     rows = both // own
-    wide = o_ref.shape[2]
     me = lax.axis_index("tensor")
     line = lax.broadcasted_iota(jnp.int32, (both, HD), 0)
     column = lax.broadcasted_iota(jnp.int32, (both, HD), 1)
@@ -226,7 +233,13 @@
                 [heads_ref[pl.ds(h, rows, stride=own), :] for h in range(own)], axis=1
             )
         )
-    context = jnp.concatenate(context, axis=0).astype(BF16)
+    return jnp.concatenate(context, axis=0).astype(BF16)
+
+
+def project_kernel(shared, own, got_ref, w_ref, o_ref, heads_ref):
+    context = combine(shared, own, got_ref, heads_ref)
+    total, rows, wide = o_ref.shape
+    n = total // shared
     offset = 0
     if shared > 1:
         offset = lax.axis_index("section") * wide
@@ -237,6 +250,42 @@
         terms = dot(context, w_ref[:, pl.ds(at, wide)])
         for s in range(shared):
             o_ref[s * n + t] = terms[s * rows : (s + 1) * rows].astype(BF16)
+
+
+def pair_terms(apart, context, w_ref, o_ref):
+    wide = o_ref.shape[2]
+    me = lax.axis_index("tensor")
+    for i in range(2):
+        at = pl.multiple_of((me ^ (apart + i)) * wide, wide)
+        o_ref[i] = dot(context, w_ref[:, pl.ds(at, wide)]).astype(o_ref.dtype)
+
+
+def begin_kernel(apart, own, got_ref, w_ref, o_ref, context_ref, heads_ref):
+    context = combine(1, own, got_ref, heads_ref)
+    context_ref[...] = context
+    pair_terms(apart, context, w_ref, o_ref)
+
+
+def terms_kernel(apart, context_ref, w_ref, o_ref):
+    pair_terms(apart, context_ref[...], w_ref, o_ref)
+
+
+def widen_kernel(x_ref, o_ref):
+    o_ref[...] = x_ref[...].astype(F32)
+
+
+def merge_kernel(x_ref, y_ref, o_ref):
+    o_ref[...] = x_ref[...].astype(F32) + y_ref[...].astype(F32)
+
+
+def finish_kernel(x_ref, y_ref, mine_ref, far_ref):
+    out = x_ref[...] + y_ref[...].astype(F32)
+    mine_ref[...] = out[0]
+    far_ref[...] = out[1].astype(BF16)
+
+
+def add_kernel(x_ref, y_ref, o_ref):
+    o_ref[...] = (x_ref[...] + y_ref[...].astype(F32)).astype(BF16)
 
 
 def sum_kernel(x_ref, o_ref):
@@ -297,13 +346,36 @@
         part = part[:, : rows * GROUP].reshape(KVH, rows, GROUP, HD).transpose(0, 2, 1, 3)
         part = jnp.concatenate([part.reshape(n, rows * own, HD), stats], axis=1)
     part = exchange(part, o_shared)
+    scratch = [pltpu.VMEM((rows * own, HD), F32)]
+    if n == 8:
+        two = (2, rows, wide)
+        step = functools.partial(begin_kernel, BACK[0], own)
+        shapes = [two, (rows, own * HD)]
+        out, context = call(
+            step, shapes, [BF16, BF16], part, w_output, scratch=scratch, flops=PIECE
+        )
+        got = [flip(out, BACK[0])]
+        for apart in BACK[1:]:
+            step = functools.partial(terms_kernel, apart)
+            out = call(step, two, BF16, context, w_output, flops=PIECE)
+            got.append(flip(out, apart))
+        own_terms = call(
+            functools.partial(terms_kernel, 0), two, BF16, context, w_output, flops=PIECE
+        )
+        out = call(widen_kernel, two, F32, got[0], flops=ADD)
+        out = call(merge_kernel, two, F32, out, got[1], flops=ADD)
+        out = call(merge_kernel, two, F32, out, got[2], flops=ADD)
+        mine, far = call(
+            finish_kernel, [(rows, wide)] * 2, [F32, BF16], out, flip(own_terms, 0), flops=ADD
+        )
+        return call(add_kernel, (rows, wide), BF16, flip(mine, 0), flip(far, 1))
     terms = call(
         functools.partial(project_kernel, o_shared, own),
         (o_shared * n, rows, wide // o_shared),
         BF16,
         part,
         w_output,
-        scratch=[pltpu.VMEM((rows * own, HD), F32)],
+        scratch=scratch,
     )
     terms = exchange(terms, o_shared)
     return call(sum_kernel, (rows, wide), BF16, terms)

time: 48.6 us -> 47.6 us (0.979)
  blocking collectives: 29.3 us -> 20 us
  starting transfers between devices: 7.75 us -> 12.4 us
  waiting for transfers between devices: 3.12 us -> 6.4 us
    all_to_all x3 -> x2, blocking collectives: 29.3 us -> 20 us  [exchange(): return lax.all_to_all(x, BOTH if shared > 1 else 'tensor', 0, 0, tiled=True)]
    ppermute x6 -> x12, starting transfers between devices: 7.75 us -> 12.4 us  [flip(): lax.ppermute(x, BOTH, [(i, (i // n ^ 1) * n + (i % n ^ apart)) for i in r...]
    ppermute x6 -> x12, waiting for transfers between devices: 3.12 us -> 6.4 us  [flip(): lax.ppermute(x, BOTH, [(i, (i // n ^ 1) * n + (i % n ^ apart)) for i in r...]
    pallas_call x9 -> x16, Pallas kernels: 7.35 us -> 7.7 us  [call(): pl.pallas_call(kernel, in_specs=specs or [VMEM] * len(args), out_specs=ou...]
  transfers between devices with their start and end apart: 6 -> 12, of which waited for: 3 -> 6; matrix products, arithmetic and copies ran while one was open for 0% -> 0% of each run, Pallas kernels for 4% -> 8%
where the time goes in v8:
time: 47.6 us; the launch traced here: 47.4 us
  blocking collectives  20 us (42%)
  starting transfers between devices  12.4 us (26%)
  Pallas kernels  7.7 us (16%)
  waiting for transfers between devices  6.4 us (13%)
  local copies, waits for them, and re-layouts  0.74 us (2%)
    all_to_all x2, blocking collectives, exchange(): return lax.all_to_all(x, BOTH if shared > 1 else 'tensor', 0, 0, tiled=True)  20 us
    ppermute x12, starting transfers between devices, flip(): lax.ppermute(x, BOTH, [(i, (i // n ^ 1) * n + (i % n ^ apart)) for i in r...  12.4 us
    pallas_call x16, Pallas kernels, call(): pl.pallas_call(kernel, in_specs=specs or [VMEM] * len(args), out_specs=ou...  7.7 us
    ppermute x12, waiting for transfers between devices, flip(): lax.ppermute(x, BOTH, [(i, (i // n ^ 1) * n + (i % n ^ apart)) for i in r...  6.4 us
  transfers between devices with their start and end apart: 12, of which 6 were waited for; matrix products, arithmetic and copies ran while one was open for 0% of the time, Pallas kernels for 8%

profile of v8, /device:TPU:0, one launch (start us, length us, event | category | flops | bytes accessed | tf_op | source)
XLA Modules:
  0.0 47.4 jit_solution(1534031649436967517)
XLA Ops:
  0.0 0.0 copy-start.5
  0.0 0.7 %copy-done.5 = bf16[4,1024]{1,0:T(4,128)(2,1)S(1)} copy-done((bf16[4,1024]{1,0:T(4,128)(2,1)S(1)}, bf16[4,1024]{1,0:T(4,128)(2,1)}, u32[]{:S(2)}) %copy-start.5) | copy-done | bytes 8216
  0.7 0.0 copy-start
  0.7 2.4 %collective-permute-start.1 = (bf16[4,1024]{1,0:T(4,128)(2,1)S(1)}, bf16[4,1024]{1,0:T(4,128)(2,1)S(1)}, u32[]{:S(2)}, u32[]{:S(2)}) collective-permute-start(bf16[4,1024]{1,0:T(4,128)(2,1)S(1)} %shard_map.73), channel_id=1, source_target_pairs={{0,9},{1,8},{2,11},{3,10},{4,13},{5,12},{6,15},{7,14},{8,1},{9,0},... | collective-permute-start | bytes 24584 | tf_op jit(solution)/shard_map/ppermute | solution.py:45
  3.1 0.7 %collective-permute-start = (bf16[4,1024]{1,0:T(4,128)(2,1)S(1)}, bf16[4,1024]{1,0:T(4,128)(2,1)S(1)}, u32[]{:S(2)}, u32[]{:S(2)}) collective-permute-start(bf16[4,1024]{1,0:T(4,128)(2,1)S(1)} %shard_map.73), channel_id=1, source_target_pairs={{0,8},{1,9},{2,10},{3,11},{4,12},{5,13},{6,14},{7,15},{8,0},{9,1},... | collective-permute-start | bytes 24584 | tf_op jit(solution)/shard_map/ppermute | solution.py:45
  3.8 0.7 %collective-permute-done.1.y_ref = bf16[4,1024]{1,0:T(4,128)(2,1)S(1)} collective-permute-done((bf16[4,1024]{1,0:T(4,128)(2,1)S(1)}, bf16[4,1024]{1,0:T(4,128)(2,1)S(1)}, u32[]{:S(2)}, u32[]{:S(2)}) %collective-permute-start.1) | collective-permute-done | bytes 8224 | tf_op jit(solution)/shard_map/ppermute | solution.py:45
  4.5 0.1 collective-permute-done.x_ref
  4.6 0.5 %collective-permute-start.5 = (bf16[2,4,1024]{2,1,0:T(4,128)(2,1)S(1)}, bf16[2,4,1024]{2,1,0:T(4,128)(2,1)S(1)}, u32[]{:S(2)}, u32[]{:S(2)}) collective-permute-start(bf16[2,4,1024]{2,1,0:T(4,128)(2,1)S(1)} %shard_map.74), channel_id=1, source_target_pairs={{0,8},{1,9},{2,10},{3,11},{4,12},{5,13},{6,14},{7,15},{8,0},{9,1},... | collective-permute-start | bytes 49160 | tf_op jit(solution)/shard_map/ppermute | solution.py:45
  5.1 2.8 %collective-permute-start.4 = (bf16[2,4,1024]{2,1,0:T(4,128)(2,1)S(1)}, bf16[2,4,1024]{2,1,0:T(4,128)(2,1)S(1)}, u32[]{:S(2)}, u32[]{:S(2)}) collective-permute-start(bf16[2,4,1024]{2,1,0:T(4,128)(2,1)S(1)} %shard_map.74), channel_id=1, source_target_pairs={{0,12},{1,13},{2,14},{3,15},{4,8},{5,9},{6,10},{7,11},{8,4},{9,5},... | collective-permute-start | bytes 49160 | tf_op jit(solution)/shard_map/ppermute | solution.py:45
  8.0 1.1 %collective-permute-start.3 = (bf16[2,4,1024]{2,1,0:T(4,128)(2,1)S(1)}, bf16[2,4,1024]{2,1,0:T(4,128)(2,1)S(1)}, u32[]{:S(2)}, u32[]{:S(2)}) collective-permute-start(bf16[2,4,1024]{2,1,0:T(4,128)(2,1)S(1)} %shard_map.74), channel_id=1, source_target_pairs={{0,14},{1,15},{2,12},{3,13},{4,10},{5,11},{6,8},{7,9},{8,6},{9,7},... | collective-permute-start | bytes 49160 | tf_op jit(solution)/shard_map/ppermute | solution.py:45
  9.1 0.2 collective-permute-start.2
  9.3 0.0 collective-permute-done.5.x_ref
  9.3 0.0 copy-done
  9.3 0.7 %shard_map.75.old_ref = f32[4,1024]{1,0:T(4,128)S(1)} custom-call(bf16[2,4,1024]{2,1,0:T(4,128)(2,1)S(1)} %collective-permute-done.5.x_ref, bf16[8192,1024]{1,0:T(8,128)(2,1)S(1)} %copy-done), custom_call_target="tpu_custom_call" | custom-call | tf_op jit(solution)/shard_map/pallas_call | solution.py:54
  9.9 0.0 collective-permute-done.4.x_ref
  9.9 0.7 %shard_map.76.old_ref = f32[4,1024]{1,0:T(4,128)S(1)} custom-call(bf16[2,4,1024]{2,1,0:T(4,128)(2,1)S(1)} %collective-permute-done.4.x_ref, bf16[8192,1024]{1,0:T(8,128)(2,1)S(1)} %copy-done, f32[4,1024]{1,0:T(4,128)S(1)} %shard_map.75.old_ref), custom_call_target="tpu_custom_call" | custom-call | flops 10000000000 | tf_op jit(solution)/shard_map/pallas_call | solution.py:54
  10.6 0.0 copy-start.1
  10.6 0.0 copy-start.2
  10.6 0.0 copy-start.3
  10.6 0.0 copy-start.4
  10.6 0.0 slice-start
  10.7 0.0 slice-start.1
  10.7 2.3 %collective-permute-done.3.x_ref = bf16[2,4,1024]{2,1,0:T(4,128)(2,1)S(1)} collective-permute-done((bf16[2,4,1024]{2,1,0:T(4,128)(2,1)S(1)}, bf16[2,4,1024]{2,1,0:T(4,128)(2,1)S(1)}, u32[]{:S(2)}, u32[]{:S(2)}) %collective-permute-start.3) | collective-permute-done | bytes 16416 | tf_op jit(solution)/shard_map/ppermute | solution.py:45
  12.9 0.7 %shard_map.77.old_ref = f32[4,1024]{1,0:T(4,128)S(1)} custom-call(bf16[2,4,1024]{2,1,0:T(4,128)(2,1)S(1)} %collective-permute-done.3.x_ref, bf16[8192,1024]{1,0:T(8,128)(2,1)S(1)} %copy-done, f32[4,1024]{1,0:T(4,128)S(1)} %shard_map.76.old_ref), custom_call_target="tpu_custom_call" | custom-call | tf_op jit(solution)/shard_map/pallas_call | solution.py:54
  13.6 0.0 slice-start.2
  13.6 0.0 slice-start.3
  13.6 0.0 collective-permute-done.2.x_ref
  13.6 0.7 %shard_map.78 = bf16[8,32,128]{2,1,0:T(8,128)(2,1)S(1)} custom-call(bf16[2,4,1024]{2,1,0:T(4,128)(2,1)S(1)} %collective-permute-done.2.x_ref, bf16[8192,1024]{1,0:T(8,128)(2,1)S(1)} %copy-done, f32[4,1024]{1,0:T(4,128)S(1)} %shard_map.77.old_ref), custom_call_target="tpu_custom_call" | custom-call | tf_op jit(solution)/shard_map/pallas_call | solution.py:54
  14.3 10.6 %all_to_all.10.q_ref = bf16[8,32,128]{2,1,0:T(8,128)(2,1)S(1)} all-to-all(bf16[8,32,128]{2,1,0:T(8,128)(2,1)S(1)} %shard_map.78), channel_id=1, replica_groups=mesh['groups'=2,'section'=2,'tensor'=8] {'tensor'}, dimensions={0} | all-to-all | bytes 131072 | tf_op jit(solution)/shard_map/all_to_all | solution.py:31
  24.9 0.0 copy-done.1
  24.9 0.0 copy-done.2
  24.9 0.0 copy-done.3
  24.9 0.0 copy-done.4
  24.9 1.5 %shard_map.79 = bf16[8,40,128]{2,1,0:T(8,128)(2,1)S(1)} custom-call(s32[4]{0:T(128)S(1)} %copy-done.3, s32[4]{0:T(128)S(1)} %copy-done.4, bf16[8,32,128]{2,1,0:T(8,128)(2,1)S(1)} %all_to_all.10.q_ref, bf16[4,128,2048]{2,1,0:T(8,128)(2,1)S(1)} %copy-done.1, bf16[4,64,2048]{2,1,0:T(8,128)(2,1)S(1)} %copy-done.2), custom_call_target="tpu_custom_call" | custom-call | tf_op jit(solution)/shard_map/pallas_call | solution.py:54
  26.4 9.4 %all_to_all.11.got_ref = bf16[8,40,128]{2,1,0:T(8,128)(2,1)S(1)} all-to-all(bf16[8,40,128]{2,1,0:T(8,128)(2,1)S(1)} %shard_map.79), channel_id=1, replica_groups=mesh['groups'=2,'section'=2,'tensor'=8] {'tensor'}, dimensions={0} | all-to-all | bytes 163840 | tf_op jit(solution)/shard_map/all_to_all | solution.py:31
  35.8 0.0 slice-done
  35.8 0.0 slice-done.1
  35.8 0.0 slice-done.2
  35.8 0.0 slice-done.3
  35.9 0.9 %shard_map.80 = (bf16[2,4,1024]{2,1,0:T(4,128)(2,1)S(1)}, bf16[4,1024]{1,0:T(4,128)(2,1)S(1)}) custom-call(bf16[8,40,128]{2,1,0:T(8,128)(2,1)S(1)} %all_to_all.11.got_ref, bf16[1024,8192]{1,0:T(8,128)(2,1)S(1)} %bitcast.1), custom_call_target="tpu_custom_call" | custom-call | flops 11500000 | tf_op jit(solution)/shard_map/pallas_call | solution.py:54
  36.8 0.0 collective-permute-start.6
  36.8 0.7 %shard_map.82 = bf16[2,4,1024]{2,1,0:T(4,128)(2,1)S(1)} custom-call(bf16[4,1024]{1,0:T(4,128)(2,1)S(1)} %get-tuple-element.10.context_ref, bf16[1024,8192]{1,0:T(8,128)(2,1)S(1)} %bitcast.1), custom_call_target="tpu_custom_call" | custom-call | flops 11500000 | tf_op jit(solution)/shard_map/pallas_call | solution.py:54
  37.4 2.2 %collective-permute-start.7 = (bf16[2,4,1024]{2,1,0:T(4,128)(2,1)S(1)}, bf16[2,4,1024]{2,1,0:T(4,128)(2,1)S(1)}, u32[]{:S(2)}, u32[]{:S(2)}) collective-permute-start(bf16[2,4,1024]{2,1,0:T(4,128)(2,1)S(1)} %shard_map.82), channel_id=1, source_target_pairs={{0,14},{1,15},{2,12},{3,13},{4,10},{5,11},{6,8},{7,9},{8,6},{9,7},... | collective-permute-start | bytes 49160 | tf_op jit(solution)/shard_map/ppermute | solution.py:45
  39.7 0.7 %shard_map.84 = bf16[2,4,1024]{2,1,0:T(4,128)(2,1)S(1)} custom-call(bf16[4,1024]{1,0:T(4,128)(2,1)S(1)} %get-tuple-element.10.context_ref, bf16[1024,8192]{1,0:T(8,128)(2,1)S(1)} %bitcast.1), custom_call_target="tpu_custom_call" | custom-call | flops 11500000 | tf_op jit(solution)/shard_map/pallas_call | solution.py:54
  40.3 0.0 collective-permute-start.8
  40.3 0.7 %shard_map.86 = bf16[2,4,1024]{2,1,0:T(4,128)(2,1)S(1)} custom-call(bf16[4,1024]{1,0:T(4,128)(2,1)S(1)} %get-tuple-element.10.context_ref, bf16[1024,8192]{1,0:T(8,128)(2,1)S(1)} %bitcast.1), custom_call_target="tpu_custom_call" | custom-call | flops 11500000 | tf_op jit(solution)/shard_map/pallas_call | solution.py:54
  41.0 1.1 %collective-permute-start.9 = (bf16[2,4,1024]{2,1,0:T(4,128)(2,1)S(1)}, bf16[2,4,1024]{2,1,0:T(4,128)(2,1)S(1)}, u32[]{:S(2)}, u32[]{:S(2)}) collective-permute-start(bf16[2,4,1024]{2,1,0:T(4,128)(2,1)S(1)} %shard_map.86), channel_id=1, source_target_pairs={{0,8},{1,9},{2,10},{3,11},{4,12},{5,13},{6,14},{7,15},{8,0},{9,1},... | collective-permute-start | bytes 49160 | tf_op jit(solution)/shard_map/ppermute | solution.py:45
  42.1 0.0 collective-permute-done.6.x_ref
  42.1 0.3 collective-permute-done.7.y_ref
  42.4 1.1 %collective-permute-done.8.y_ref = bf16[2,4,1024]{2,1,0:T(4,128)(2,1)S(1)} collective-permute-done((bf16[2,4,1024]{2,1,0:T(4,128)(2,1)S(1)}, bf16[2,4,1024]{2,1,0:T(4,128)(2,1)S(1)}, u32[]{:S(2)}, u32[]{:S(2)}) %collective-permute-start.8) | collective-permute-done | bytes 16416 | tf_op jit(solution)/shard_map/ppermute | solution.py:45
  43.5 0.0 collective-permute-done.9.y_ref
  43.5 0.1 collective-permute-start.10
  43.6 1.2 %collective-permute-start.11 = (bf16[4,1024]{1,0:T(4,128)(2,1)S(1)}, bf16[4,1024]{1,0:T(4,128)(2,1)S(1)}, u32[]{:S(2)}, u32[]{:S(2)}) collective-permute-start(bf16[4,1024]{1,0:T(4,128)(2,1)S(1)} %get-tuple-element.12), channel_id=1, source_target_pairs={{0,9},{1,8},{2,11},{3,10},{4,13},{5,12},{6,15},{7,14},{8,1},{9,0},... | collective-permute-start | bytes 24584 | tf_op jit(solution)/shard_map/ppermute | solution.py:45
  44.8 1.9 %collective-permute-done.11.y_ref = bf16[4,1024]{1,0:T(4,128)(2,1)S(1)} collective-permute-done((bf16[4,1024]{1,0:T(4,128)(2,1)S(1)}, bf16[4,1024]{1,0:T(4,128)(2,1)S(1)}, u32[]{:S(2)}, u32[]{:S(2)}) %collective-permute-start.11) | collective-permute-done | bytes 8224 | tf_op jit(solution)/shard_map/ppermute | solution.py:45
  46.7 0.0 collective-permute-done.10.x_ref
  46.7 0.6 %shard_map.88 = bf16[4,1024]{1,0:T(4,128)(2,1)} custom-call(f32[4,1024]{1,0:T(4,128)S(1)} %collective-permute-done.10.x_ref, bf16[4,1024]{1,0:T(4,128)(2,1)S(1)} %collective-permute-done.11.y_ref), custom_call_target="tpu_custom_call" | custom-call | tf_op jit(solution)/shard_map/pallas_call | solution.py:54
  (7 shorter events, 0.0 us)
Async XLA Ops:
  0.0 0.7 %copy-start.5 = (bf16[4,1024]{1,0:T(4,128)(2,1)S(1)}, bf16[4,1024]{1,0:T(4,128)(2,1)}, u32[]{:S(2)}) copy-start(bf16[4,1024]{1,0:T(4,128)(2,1)} %x_ref.1) | copy-start | bytes 24580
  0.7 8.6 %copy-start = (bf16[8192,1024]{1,0:T(8,128)(2,1)S(1)}, bf16[8192,1024]{1,0:T(8,128)(2,1)}, u32[]{:S(2)}) copy-start(bf16[8192,1024]{1,0:T(8,128)(2,1)} %w_ref.11) | copy-start | bytes 50331652
  0.7 3.8 %collective-permute-start.1 = (bf16[4,1024]{1,0:T(4,128)(2,1)S(1)}, bf16[4,1024]{1,0:T(4,128)(2,1)S(1)}, u32[]{:S(2)}, u32[]{:S(2)}) collective-permute-start(bf16[4,1024]{1,0:T(4,128)(2,1)S(1)} %shard_map.73), channel_id=1, source_target_pairs={{0,9},{1,8},{2,11},{3,10},{4,13},{5,12},{6,15},{7,14},{8,1},{9,0},... | collective-permute-start | bytes 24584 | tf_op jit(solution)/shard_map/ppermute | solution.py:45
  3.1 1.5 %collective-permute-start = (bf16[4,1024]{1,0:T(4,128)(2,1)S(1)}, bf16[4,1024]{1,0:T(4,128)(2,1)S(1)}, u32[]{:S(2)}, u32[]{:S(2)}) collective-permute-start(bf16[4,1024]{1,0:T(4,128)(2,1)S(1)} %shard_map.73), channel_id=1, source_target_pairs={{0,8},{1,9},{2,10},{3,11},{4,12},{5,13},{6,14},{7,15},{8,0},{9,1},... | collective-permute-start | bytes 24584 | tf_op jit(solution)/shard_map/ppermute | solution.py:45
  4.6 4.7 %collective-permute-start.5 = (bf16[2,4,1024]{2,1,0:T(4,128)(2,1)S(1)}, bf16[2,4,1024]{2,1,0:T(4,128)(2,1)S(1)}, u32[]{:S(2)}, u32[]{:S(2)}) collective-permute-start(bf16[2,4,1024]{2,1,0:T(4,128)(2,1)S(1)} %shard_map.74), channel_id=1, source_target_pairs={{0,8},{1,9},{2,10},{3,11},{4,12},{5,13},{6,14},{7,15},{8,0},{9,1},... | collective-permute-start | bytes 49160 | tf_op jit(solution)/shard_map/ppermute | solution.py:45
  5.1 4.8 %collective-permute-start.4 = (bf16[2,4,1024]{2,1,0:T(4,128)(2,1)S(1)}, bf16[2,4,1024]{2,1,0:T(4,128)(2,1)S(1)}, u32[]{:S(2)}, u32[]{:S(2)}) collective-permute-start(bf16[2,4,1024]{2,1,0:T(4,128)(2,1)S(1)} %shard_map.74), channel_id=1, source_target_pairs={{0,12},{1,13},{2,14},{3,15},{4,8},{5,9},{6,10},{7,11},{8,4},{9,5},... | collective-permute-start | bytes 49160 | tf_op jit(solution)/shard_map/ppermute | solution.py:45
  8.0 5.0 %collective-permute-start.3 = (bf16[2,4,1024]{2,1,0:T(4,128)(2,1)S(1)}, bf16[2,4,1024]{2,1,0:T(4,128)(2,1)S(1)}, u32[]{:S(2)}, u32[]{:S(2)}) collective-permute-start(bf16[2,4,1024]{2,1,0:T(4,128)(2,1)S(1)} %shard_map.74), channel_id=1, source_target_pairs={{0,14},{1,15},{2,12},{3,13},{4,10},{5,11},{6,8},{7,9},{8,6},{9,7},... | collective-permute-start | bytes 49160 | tf_op jit(solution)/shard_map/ppermute | solution.py:45
  9.1 4.6 %collective-permute-start.2 = (bf16[2,4,1024]{2,1,0:T(4,128)(2,1)S(1)}, bf16[2,4,1024]{2,1,0:T(4,128)(2,1)S(1)}, u32[]{:S(2)}, u32[]{:S(2)}) collective-permute-start(bf16[2,4,1024]{2,1,0:T(4,128)(2,1)S(1)} %shard_map.74), channel_id=1, source_target_pairs={{0,10},{1,11},{2,8},{3,9},{4,14},{5,15},{6,12},{7,13},{8,2},{9,3},... | collective-permute-start | bytes 49160 | tf_op jit(solution)/shard_map/ppermute | solution.py:45
  10.6 14.3 %copy-start.1 = (bf16[4,128,2048]{2,1,0:T(8,128)(2,1)S(1)}, bf16[4,128,2048]{2,1,0:T(8,128)(2,1)}, u32[]{:S(2)}) copy-start(bf16[4,128,2048]{2,1,0:T(8,128)(2,1)} %cache_ref.1) | copy-start | bytes 6291460
  10.6 14.3 %copy-start.2 = (bf16[4,64,2048]{2,1,0:T(8,128)(2,1)S(1)}, bf16[4,64,2048]{2,1,0:T(8,128)(2,1)}, u32[]{:S(2)}) copy-start(bf16[4,64,2048]{2,1,0:T(8,128)(2,1)} %fresh_ref.1) | copy-start | bytes 3145732
  10.6 14.3 %copy-start.3 = (s32[4]{0:T(128)S(1)}, s32[4]{0:T(128)}, u32[]{:S(2)}) copy-start(s32[4]{0:T(128)} %clen_ref.1) | copy-start | bytes 52
  10.6 14.2 %copy-start.4 = (s32[4]{0:T(128)S(1)}, s32[4]{0:T(128)}, u32[]{:S(2)}) copy-start(s32[4]{0:T(128)} %nlen_ref.1) | copy-start | bytes 52
  10.6 25.2 %slice-start = ((s8[16777216]{0:T(1024)(128)(4,1)}), s8[4194304]{0:T(1024)(128)(4,1)S(1)}, s32[]{:S(2)}) async-start(s8[16777216]{0:T(1024)(128)(4,1)} %bitcast), calls=%async_computation.2 | async-start | bytes 8388608
  10.7 25.2 %slice-start.1 = ((s8[16777216]{0:T(1024)(128)(4,1)}), s8[4194304]{0:T(1024)(128)(4,1)S(1)}, s32[]{:S(2)}) async-start(s8[16777216]{0:T(1024)(128)(4,1)} %bitcast), calls=%async_computation.3 | async-start | bytes 8388608
  13.6 22.2 %slice-start.2 = ((s8[16777216]{0:T(1024)(128)(4,1)}), s8[4194304]{0:T(1024)(128)(4,1)S(1)}, s32[]{:S(2)}) async-start(s8[16777216]{0:T(1024)(128)(4,1)} %bitcast), calls=%async_computation.4 | async-start | bytes 8388608
  13.6 22.2 %slice-start.3 = ((s8[16777216]{0:T(1024)(128)(4,1)}), s8[4194304]{0:T(1024)(128)(4,1)S(1)}, s32[]{:S(2)}) async-start(s8[16777216]{0:T(1024)(128)(4,1)} %bitcast), calls=%async_computation.5 | async-start | bytes 8388608
  36.8 5.3 %collective-permute-start.6 = (bf16[2,4,1024]{2,1,0:T(4,128)(2,1)S(1)}, bf16[2,4,1024]{2,1,0:T(4,128)(2,1)S(1)}, u32[]{:S(2)}, u32[]{:S(2)}) collective-permute-start(bf16[2,4,1024]{2,1,0:T(4,128)(2,1)S(1)} %get-tuple-element.9), channel_id=1, source_target_pairs={{0,12},{1,13},{2,14},{3,15},{4,8},{5,9},{6,10},{7,11},{8,4},{9,5},... | collective-permute-start | bytes 49160 | tf_op jit(solution)/shard_map/ppermute | solution.py:45
  37.4 5.0 %collective-permute-start.7 = (bf16[2,4,1024]{2,1,0:T(4,128)(2,1)S(1)}, bf16[2,4,1024]{2,1,0:T(4,128)(2,1)S(1)}, u32[]{:S(2)}, u32[]{:S(2)}) collective-permute-start(bf16[2,4,1024]{2,1,0:T(4,128)(2,1)S(1)} %shard_map.82), channel_id=1, source_target_pairs={{0,14},{1,15},{2,12},{3,13},{4,10},{5,11},{6,8},{7,9},{8,6},{9,7},... | collective-permute-start | bytes 49160 | tf_op jit(solution)/shard_map/ppermute | solution.py:45
  40.3 3.2 %collective-permute-start.8 = (bf16[2,4,1024]{2,1,0:T(4,128)(2,1)S(1)}, bf16[2,4,1024]{2,1,0:T(4,128)(2,1)S(1)}, u32[]{:S(2)}, u32[]{:S(2)}) collective-permute-start(bf16[2,4,1024]{2,1,0:T(4,128)(2,1)S(1)} %shard_map.84), channel_id=1, source_target_pairs={{0,10},{1,11},{2,8},{3,9},{4,14},{5,15},{6,12},{7,13},{8,2},{9,3},... | collective-permute-start | bytes 49160 | tf_op jit(solution)/shard_map/ppermute | solution.py:45
  41.0 2.5 %collective-permute-start.9 = (bf16[2,4,1024]{2,1,0:T(4,128)(2,1)S(1)}, bf16[2,4,1024]{2,1,0:T(4,128)(2,1)S(1)}, u32[]{:S(2)}, u32[]{:S(2)}) collective-permute-start(bf16[2,4,1024]{2,1,0:T(4,128)(2,1)S(1)} %shard_map.86), channel_id=1, source_target_pairs={{0,8},{1,9},{2,10},{3,11},{4,12},{5,13},{6,14},{7,15},{8,0},{9,1},... | collective-permute-start | bytes 49160 | tf_op jit(solution)/shard_map/ppermute | solution.py:45
  43.5 3.2 %collective-permute-start.10 = (f32[4,1024]{1,0:T(4,128)S(1)}, f32[4,1024]{1,0:T(4,128)S(1)}, u32[]{:S(2)}, u32[]{:S(2)}) collective-permute-start(f32[4,1024]{1,0:T(4,128)S(1)} %get-tuple-element.11), channel_id=1, source_target_pairs={{0,8},{1,9},{2,10},{3,11},{4,12},{5,13},{6,14},{7,15},{8,0},{9,1},... | collective-permute-start | bytes 49160 | tf_op jit(solution)/shard_map/ppermute | solution.py:45
  43.6 3.1 %collective-permute-start.11 = (bf16[4,1024]{1,0:T(4,128)(2,1)S(1)}, bf16[4,1024]{1,0:T(4,128)(2,1)S(1)}, u32[]{:S(2)}, u32[]{:S(2)}) collective-permute-start(bf16[4,1024]{1,0:T(4,128)(2,1)S(1)} %get-tuple-element.12), channel_id=1, source_target_pairs={{0,9},{1,8},{2,11},{3,10},{4,13},{5,12},{6,15},{7,14},{8,1},{9,0},... | collective-permute-start | bytes 24584 | tf_op jit(solution)/shard_map/ppermute | solution.py:45

commit v9 on v8

--- a/solution.py
+++ b/solution.py
@@ -19,6 +19,7 @@
 BOTH = ("section", "tensor")
 SPLIT_OUTPUT = False
 ORDER = (4, 6, 2)
+MIDDLE = (4, 6, 2)
 BACK = (4, 6, 2)
 ADD = 23000000
 PIECE = 11500000
@@ -80,7 +81,8 @@
     own = acc.shape[1] // HD
     for h in range(own):
         heads_ref[pl.ds(h, rows, stride=own), :] = acc[:, h * HD : (h + 1) * HD]
-    o_ref[...] = jnp.broadcast_to(heads_ref[...].astype(BF16)[None], o_ref.shape)
+    q = heads_ref[...].astype(BF16)
+    o_ref[...] = q if len(o_ref.shape) == 2 else jnp.broadcast_to(q[None], o_ref.shape)
 
 
 def query_kernel(all_ref, w_ref, o_ref, heads_ref):
@@ -193,6 +195,110 @@
         o_ref[d, rows * GROUP :, :] = stats
 
 
+def order_kernel(x_ref, y_ref, o_ref):
+    odd = lax.axis_index("tensor") % 2
+    o_ref[odd] = x_ref[...]
+    o_ref[1 - odd] = y_ref[...]
+
+
+def pair_attend_kernel(apart, clen_ref, nlen_ref, q_ref, cache_ref, fresh_ref, o_ref):
+    rows, cc, width = cache_ref.shape
+    width = width // 2
+    fc = fresh_ref.shape[1]
+    both = 2 * GROUP
+    place = lax.axis_index("tensor")
+    at = (place ^ apart) // 2 * (2 * HD)
+    keys = pl.ds(pl.multiple_of(at, 2 * HD), 2 * HD)
+    vals = pl.ds(pl.multiple_of(width + at, 2 * HD), 2 * HD)
+    lane = lax.broadcasted_iota(jnp.int32, (HD, rows * both), 1)
+    heads = [q_ref[i].astype(F32) for i in range(2)]
+    q = [heads[i][r * GROUP : (r + 1) * GROUP] for r in range(rows) for i in range(2)]
+    q = jnp.concatenate(q, axis=0).T
+    wide = []
+    for r in range(rows):
+        blocks = []
+        for i in range(2):
+            first = r * both + i * GROUP
+            blocks.append(jnp.where((lane >= first) & (lane < first + GROUP), q, 0.0))
+        wide.append(jnp.concatenate(blocks, axis=0).astype(BF16))
+
+    def logits(ref, start, length_ref):
+        s = functools.reduce(jnp.add, [dot(ref[r, :, keys], wide[r]) for r in range(rows)])
+        request = lax.broadcasted_iota(jnp.int32, s.shape, 1) // both
+        length = jnp.full(s.shape, length_ref[0], jnp.int32)
+        for r in range(1, rows):
+            length = jnp.where(request == r, length_ref[r], length)
+        valid = start + lax.broadcasted_iota(jnp.int32, s.shape, 0) < length
+        return jnp.where(valid, s * HD**-0.5, -1e30), valid
+
+    sc, okc = logits(cache_ref, place * cc, clen_ref)
+    sf, okf = logits(fresh_ref, place * fc, nlen_ref)
+    top = jnp.maximum(jnp.max(sc, axis=0, keepdims=True), jnp.max(sf, axis=0, keepdims=True))
+    wc = jnp.where(okc, jnp.exp(sc - top), 0.0)
+    wf = jnp.where(okf, jnp.exp(sf - top), 0.0)
+    total = jnp.sum(wc, axis=0, keepdims=True) + jnp.sum(wf, axis=0, keepdims=True)
+    some = total > 0.0
+    total = jnp.where(some, total, 1.0)
+    inverse = 1.0 / total
+    pc = (wc * inverse).T.astype(BF16)
+    pf = (wf * inverse).T.astype(BF16)
+    nums = []
+    for r in range(rows):
+        mine = slice(r * both, (r + 1) * both)
+        nums.append(dot(pc[mine], cache_ref[r, :, vals]) + dot(pf[mine], fresh_ref[r, :, vals]))
+    for i in range(2):
+        for r in range(0, rows, 2):
+            num = [x[i * GROUP : (i + 1) * GROUP, i * HD : (i + 1) * HD] for x in nums[r : r + 2]]
+            o_ref[i, r * GROUP : (r + 2) * GROUP, :] = jnp.concatenate(num, axis=0).astype(BF16)
+    rest = jnp.where(some, top + jnp.log(total), -1e30)
+    stats = []
+    for _ in range(3):
+        piece = rest.astype(BF16).astype(F32)
+        stats.append(piece)
+        rest = rest - piece
+    stats.append(jnp.zeros((STATS - 3, rows * both), F32))
+    stats = jnp.concatenate(stats, axis=0)
+    stats = jnp.concatenate([stats, jnp.zeros((STATS, HD - rows * both), F32)], axis=1)
+    for i in range(2):
+        o_ref[i, rows * GROUP :, :] = stats.astype(BF16)
+
+
+def part_kernel(a_ref, b_ref, c_ref, d_ref, mine_ref, far_ref):
+    odd = lax.axis_index("tensor") % 2
+    for i, ref in enumerate((a_ref, b_ref, c_ref, d_ref)):
+        mine_ref[i] = ref[odd]
+        far_ref[i] = ref[1 - odd]
+
+
+def combine_pair(a_ref, b_ref, heads_ref):
+    n = 2 * a_ref.shape[0]
+    both = a_ref.shape[1] - STATS
+    rows = both // GROUP
+    odd = lax.axis_index("tensor") % 2
+    line = lax.broadcasted_iota(jnp.int32, (both, HD), 0)
+    column = lax.broadcasted_iota(jnp.int32, (both, HD), 1)
+    mine = column == (line // GROUP) * 2 * GROUP + odd * GROUP + line % GROUP
+    mine = mine.astype(F32).astype(BF16)
+    column = lax.broadcasted_iota(jnp.int32, (both, n * STATS), 1)
+    parts = [ref.at[i] for ref in (a_ref, b_ref) for i in range(n // 2)]
+    stats = [x[both:, :].astype(F32) for x in parts]
+    stats = jnp.concatenate(stats, axis=0).astype(BF16)
+    pieces = lax.dot_general(mine, stats, (((1,), (1,)), ((), ())), preferred_element_type=F32)
+    logs = [
+        jnp.sum(jnp.where(column // STATS == t, pieces, 0.0), axis=1, keepdims=True)
+        for t in range(n)
+    ]
+    top = functools.reduce(jnp.maximum, logs)
+    scales = [jnp.exp(x - top) for x in logs]
+    inverse = 1.0 / functools.reduce(jnp.add, scales)
+    heads_ref[...] = functools.reduce(
+        jnp.add,
+        [x[0:both, :].astype(F32) * (scale * inverse) for x, scale in zip(parts, scales)],
+    )
+    context = [heads_ref[pl.ds(h, rows, stride=GROUP), :] for h in range(GROUP)]
+    return jnp.concatenate(context, axis=1).astype(BF16)
+
+
 def combine(shared, own, got_ref, heads_ref):
     total, both, _ = got_ref.shape
     both -= STATS
@@ -260,8 +366,8 @@
         o_ref[i] = dot(context, w_ref[:, pl.ds(at, wide)]).astype(o_ref.dtype)
 
 
-def begin_kernel(apart, own, got_ref, w_ref, o_ref, context_ref, heads_ref):
-    context = combine(1, own, got_ref, heads_ref)
+def begin_kernel(apart, a_ref, b_ref, w_ref, o_ref, context_ref, heads_ref):
+    context = combine_pair(a_ref, b_ref, heads_ref)
     context_ref[...] = context
     pair_terms(apart, context, w_ref, o_ref)
 
@@ -321,38 +427,61 @@
             step = functools.partial(next_kernel, apart)
             acc = call(step, (rows, own * HD), F32, x, w_query, acc, flops=10**10 if apart == ORDER[0] else 0)
         step = functools.partial(last_kernel, ORDER[2])
-        q = call(step, (n, rows * own, HD), BF16, got[2], w_query, acc, scratch=scratch)
+        q = call(step, (rows * own, HD), BF16, got[2], w_query, acc, scratch=scratch)
     else:
         x = call(spread_kernel, (n, rows, feat), BF16, hidden, flops=LONG)
         x = exchange(x, 1)
         q = call(query_kernel, (n, rows * own, HD), BF16, x, w_query, scratch=scratch)
-    q = exchange(q, 1)
-    if not usual:
-        q = q.reshape(KVH, GROUP, rows, HD).transpose(0, 2, 1, 3).reshape(KVH, rows * GROUP, HD)
-    part = call(
-        attend_kernel,
-        (o_shared * KVH, rows * GROUP + STATS, HD),
-        BF16,
-        cache_lengths,
-        new_lengths,
-        q,
-        cache,
-        fresh,
-        flops=ATTEND,
-        specs=[SMEM] * 2 + [VMEM] * 3,
-    )
-    if not usual:
-        stats = jnp.broadcast_to(part[:1, rows * GROUP :], (n, STATS, HD))
-        part = part[:, : rows * GROUP].reshape(KVH, rows, GROUP, HD).transpose(0, 2, 1, 3)
-        part = jnp.concatenate([part.reshape(n, rows * own, HD), stats], axis=1)
-    part = exchange(part, o_shared)
+    if n == 8:
+        near = flip(q, 1)
+        pair = call(order_kernel, (2, rows * own, HD), BF16, flip(q, 0), near)
+
+        def attend(apart):
+            return call(
+                functools.partial(pair_attend_kernel, apart),
+                (2, rows * GROUP + STATS, HD),
+                BF16,
+                cache_lengths,
+                new_lengths,
+                flip(pair, apart),
+                cache,
+                fresh,
+                specs=[SMEM] * 2 + [VMEM] * 3,
+                flops=PIECE,
+            )
+
+        parts = [flip(attend(apart), apart) for apart in (0,) + MIDDLE]
+        shape = (4, rows * GROUP + STATS, HD)
+        mine, far = call(part_kernel, [shape] * 2, [BF16, BF16], *parts, flops=ADD)
+        parts = flip(mine, 0), flip(far, 1)
+    else:
+        q = exchange(q, 1)
+        if not usual:
+            q = q.reshape(KVH, GROUP, rows, HD).transpose(0, 2, 1, 3).reshape(KVH, rows * GROUP, HD)
+        part = call(
+            attend_kernel,
+            (o_shared * KVH, rows * GROUP + STATS, HD),
+            BF16,
+            cache_lengths,
+            new_lengths,
+            q,
+            cache,
+            fresh,
+            flops=ATTEND,
+            specs=[SMEM] * 2 + [VMEM] * 3,
+        )
+        if not usual:
+            stats = jnp.broadcast_to(part[:1, rows * GROUP :], (n, STATS, HD))
+            part = part[:, : rows * GROUP].reshape(KVH, rows, GROUP, HD).transpose(0, 2, 1, 3)
+            part = jnp.concatenate([part.reshape(n, rows * own, HD), stats], axis=1)
+        part = exchange(part, o_shared)
     scratch = [pltpu.VMEM((rows * own, HD), F32)]
     if n == 8:
         two = (2, rows, wide)
-        step = functools.partial(begin_kernel, BACK[0], own)
+        step = functools.partial(begin_kernel, BACK[0])
         shapes = [two, (rows, own * HD)]
         out, context = call(
-            step, shapes, [BF16, BF16], part, w_output, scratch=scratch, flops=PIECE
+            step, shapes, [BF16, BF16], *parts, w_output, scratch=scratch, flops=PIECE
         )
         got = [flip(out, BACK[0])]
         for apart in BACK[1:]:

time: 47.6 us -> 48 us (level)
  blocking collectives: 20 us -> 0 us
  starting transfers between devices: 12.4 us -> 23.3 us
  waiting for transfers between devices: 6.4 us -> 12.8 us
  Pallas kernels: 7.7 us -> 10.8 us
    all_to_all x2 -> x0, blocking collectives: 20 us -> none  [exchange(): return lax.all_to_all(x, BOTH if shared > 1 else 'tensor', 0, 0, tiled=True)]
    ppermute x12 -> x24, starting transfers between devices: 12.4 us -> 23.3 us  [flip(): lax.ppermute(x, BOTH, [(i, (i // n ^ 1) * n + (i % n ^ apart)) for i in r...]
    ppermute x12 -> x24, waiting for transfers between devices: 6.4 us -> 12.8 us  [flip(): lax.ppermute(x, BOTH, [(i, (i // n ^ 1) * n + (i % n ^ apart)) for i in r...]
    pallas_call x16 -> x21, Pallas kernels: 7.7 us -> 10.8 us  [call(): pl.pallas_call(kernel, in_specs=specs or [VMEM] * len(args), out_specs=ou...]
  transfers between devices with their start and end apart: 12 -> 24, of which waited for: 6 -> 10; matrix products, arithmetic and copies ran while one was open for 0% -> 0% of each run, Pallas kernels for 8% -> 18%
where the time goes in v9:
time: 48 us; the launch traced here: 47.8 us
  starting transfers between devices  23.3 us (49%)
  waiting for transfers between devices  12.8 us (27%)
  Pallas kernels  10.8 us (22%)
  local copies, waits for them, and re-layouts  0.73 us (2%)
    ppermute x24, starting transfers between devices, flip(): lax.ppermute(x, BOTH, [(i, (i // n ^ 1) * n + (i % n ^ apart)) for i in r...  23.3 us
    ppermute x24, waiting for transfers between devices, flip(): lax.ppermute(x, BOTH, [(i, (i // n ^ 1) * n + (i % n ^ apart)) for i in r...  12.8 us
    pallas_call x21, Pallas kernels, call(): pl.pallas_call(kernel, in_specs=specs or [VMEM] * len(args), out_specs=ou...  10.8 us
  transfers between devices with their start and end apart: 24, of which 10 were waited for; matrix products, arithmetic and copies ran while one was open for 0% of the time, Pallas kernels for 18%

profile of v9, /device:TPU:0, one launch (start us, length us, event | category | flops | bytes accessed | tf_op | source)
XLA Modules:
  0.0 47.8 jit_solution(8525200314775241270)
XLA Ops:
  0.0 0.7 %copy-done.5 = bf16[4,1024]{1,0:T(4,128)(2,1)S(1)} copy-done((bf16[4,1024]{1,0:T(4,128)(2,1)S(1)}, bf16[4,1024]{1,0:T(4,128)(2,1)}, u32[]{:S(2)}) %copy-start.5) | copy-done | bytes 8216
  0.7 2.4 %collective-permute-start.1 = (bf16[4,1024]{1,0:T(4,128)(2,1)S(1)}, bf16[4,1024]{1,0:T(4,128)(2,1)S(1)}, u32[]{:S(2)}, u32[]{:S(2)}) collective-permute-start(bf16[4,1024]{1,0:T(4,128)(2,1)S(1)} %shard_map.73), channel_id=1, source_target_pairs={{0,9},{1,8},{2,11},{3,10},{4,13},{5,12},{6,15},{7,14},{8,1},{9,0},... | collective-permute-start | bytes 24584 | tf_op jit(solution)/shard_map/ppermute | solution.py:46
  3.1 0.7 %collective-permute-start = (bf16[4,1024]{1,0:T(4,128)(2,1)S(1)}, bf16[4,1024]{1,0:T(4,128)(2,1)S(1)}, u32[]{:S(2)}, u32[]{:S(2)}) collective-permute-start(bf16[4,1024]{1,0:T(4,128)(2,1)S(1)} %shard_map.73), channel_id=1, source_target_pairs={{0,8},{1,9},{2,10},{3,11},{4,12},{5,13},{6,14},{7,15},{8,0},{9,1},... | collective-permute-start | bytes 24584 | tf_op jit(solution)/shard_map/ppermute | solution.py:46
  3.8 0.7 %collective-permute-done.1.y_ref = bf16[4,1024]{1,0:T(4,128)(2,1)S(1)} collective-permute-done((bf16[4,1024]{1,0:T(4,128)(2,1)S(1)}, bf16[4,1024]{1,0:T(4,128)(2,1)S(1)}, u32[]{:S(2)}, u32[]{:S(2)}) %collective-permute-start.1) | collective-permute-done | bytes 8224 | tf_op jit(solution)/shard_map/ppermute | solution.py:46
  4.5 0.1 collective-permute-done.x_ref
  4.6 0.5 %collective-permute-start.5 = (bf16[2,4,1024]{2,1,0:T(4,128)(2,1)S(1)}, bf16[2,4,1024]{2,1,0:T(4,128)(2,1)S(1)}, u32[]{:S(2)}, u32[]{:S(2)}) collective-permute-start(bf16[2,4,1024]{2,1,0:T(4,128)(2,1)S(1)} %shard_map.74), channel_id=1, source_target_pairs={{0,8},{1,9},{2,10},{3,11},{4,12},{5,13},{6,14},{7,15},{8,0},{9,1},... | collective-permute-start | bytes 49160 | tf_op jit(solution)/shard_map/ppermute | solution.py:46
  5.1 2.8 %collective-permute-start.4 = (bf16[2,4,1024]{2,1,0:T(4,128)(2,1)S(1)}, bf16[2,4,1024]{2,1,0:T(4,128)(2,1)S(1)}, u32[]{:S(2)}, u32[]{:S(2)}) collective-permute-start(bf16[2,4,1024]{2,1,0:T(4,128)(2,1)S(1)} %shard_map.74), channel_id=1, source_target_pairs={{0,12},{1,13},{2,14},{3,15},{4,8},{5,9},{6,10},{7,11},{8,4},{9,5},... | collective-permute-start | bytes 49160 | tf_op jit(solution)/shard_map/ppermute | solution.py:46
  8.0 1.1 %collective-permute-start.3 = (bf16[2,4,1024]{2,1,0:T(4,128)(2,1)S(1)}, bf16[2,4,1024]{2,1,0:T(4,128)(2,1)S(1)}, u32[]{:S(2)}, u32[]{:S(2)}) collective-permute-start(bf16[2,4,1024]{2,1,0:T(4,128)(2,1)S(1)} %shard_map.74), channel_id=1, source_target_pairs={{0,14},{1,15},{2,12},{3,13},{4,10},{5,11},{6,8},{7,9},{8,6},{9,7},... | collective-permute-start | bytes 49160 | tf_op jit(solution)/shard_map/ppermute | solution.py:46
  9.1 0.2 collective-permute-start.2
  9.3 0.0 collective-permute-done.5.x_ref
  9.3 0.7 %shard_map.75.old_ref = f32[4,1024]{1,0:T(4,128)S(1)} custom-call(bf16[2,4,1024]{2,1,0:T(4,128)(2,1)S(1)} %collective-permute-done.5.x_ref, bf16[8192,1024]{1,0:T(8,128)(2,1)S(1)} %copy-done), custom_call_target="tpu_custom_call" | custom-call | tf_op jit(solution)/shard_map/pallas_call | solution.py:55
  9.9 0.0 collective-permute-done.4.x_ref
  9.9 0.7 %shard_map.76.old_ref = f32[4,1024]{1,0:T(4,128)S(1)} custom-call(bf16[2,4,1024]{2,1,0:T(4,128)(2,1)S(1)} %collective-permute-done.4.x_ref, bf16[8192,1024]{1,0:T(8,128)(2,1)S(1)} %copy-done, f32[4,1024]{1,0:T(4,128)S(1)} %shard_map.75.old_ref), custom_call_target="tpu_custom_call" | custom-call | flops 10000000000 | tf_op jit(solution)/shard_map/pallas_call | solution.py:55
  10.6 0.0 copy-start.4
  10.6 2.3 %collective-permute-done.3.x_ref = bf16[2,4,1024]{2,1,0:T(4,128)(2,1)S(1)} collective-permute-done((bf16[2,4,1024]{2,1,0:T(4,128)(2,1)S(1)}, bf16[2,4,1024]{2,1,0:T(4,128)(2,1)S(1)}, u32[]{:S(2)}, u32[]{:S(2)}) %collective-permute-start.3) | collective-permute-done | bytes 16416 | tf_op jit(solution)/shard_map/ppermute | solution.py:46
  12.9 0.7 %shard_map.77.old_ref = f32[4,1024]{1,0:T(4,128)S(1)} custom-call(bf16[2,4,1024]{2,1,0:T(4,128)(2,1)S(1)} %collective-permute-done.3.x_ref, bf16[8192,1024]{1,0:T(8,128)(2,1)S(1)} %copy-done, f32[4,1024]{1,0:T(4,128)S(1)} %shard_map.76.old_ref), custom_call_target="tpu_custom_call" | custom-call | tf_op jit(solution)/shard_map/pallas_call | solution.py:55
  13.6 0.0 collective-permute-done.2.x_ref
  13.6 0.7 %shard_map.78 = bf16[32,128]{1,0:T(8,128)(2,1)S(1)} custom-call(bf16[2,4,1024]{2,1,0:T(4,128)(2,1)S(1)} %collective-permute-done.2.x_ref, bf16[8192,1024]{1,0:T(8,128)(2,1)S(1)} %copy-done, f32[4,1024]{1,0:T(4,128)S(1)} %shard_map.77.old_ref), custom_call_target="tpu_custom_call" | custom-call | tf_op jit(solution)/shard_map/pallas_call | solution.py:55
  14.3 1.4 %collective-permute-start.7 = (bf16[32,128]{1,0:T(8,128)(2,1)S(1)}, bf16[32,128]{1,0:T(8,128)(2,1)S(1)}, u32[]{:S(2)}, u32[]{:S(2)}) collective-permute-start(bf16[32,128]{1,0:T(8,128)(2,1)S(1)} %shard_map.78), channel_id=1, source_target_pairs={{0,9},{1,8},{2,11},{3,10},{4,13},{5,12},{6,15},{7,14},{8,1},{9,0},... | collective-permute-start | bytes 24584 | tf_op jit(solution)/shard_map/ppermute | solution.py:46
  15.7 0.3 collective-permute-start.6
  16.0 1.4 %collective-permute-done.7.y_ref = bf16[32,128]{1,0:T(8,128)(2,1)S(1)} collective-permute-done((bf16[32,128]{1,0:T(8,128)(2,1)S(1)}, bf16[32,128]{1,0:T(8,128)(2,1)S(1)}, u32[]{:S(2)}, u32[]{:S(2)}) %collective-permute-start.7) | collective-permute-done | bytes 8224 | tf_op jit(solution)/shard_map/ppermute | solution.py:46
  17.4 0.0 collective-permute-done.6.x_ref
  17.4 0.2 collective-permute-start.8
  17.6 0.4 collective-permute-start.10
  18.1 1.4 %collective-permute-start.12 = (bf16[2,32,128]{2,1,0:T(8,128)(2,1)S(1)}, bf16[2,32,128]{2,1,0:T(8,128)(2,1)S(1)}, u32[]{:S(2)}, u32[]{:S(2)}) collective-permute-start(bf16[2,32,128]{2,1,0:T(8,128)(2,1)S(1)} %shard_map.79), channel_id=1, source_target_pairs={{0,14},{1,15},{2,12},{3,13},{4,10},{5,11},{6,8},{7,9},{8,6},{9,7},... | collective-permute-start | bytes 49160 | tf_op jit(solution)/shard_map/ppermute | solution.py:46
  19.5 1.3 %collective-permute-start.14 = (bf16[2,32,128]{2,1,0:T(8,128)(2,1)S(1)}, bf16[2,32,128]{2,1,0:T(8,128)(2,1)S(1)}, u32[]{:S(2)}, u32[]{:S(2)}) collective-permute-start(bf16[2,32,128]{2,1,0:T(8,128)(2,1)S(1)} %shard_map.79), channel_id=1, source_target_pairs={{0,10},{1,11},{2,8},{3,9},{4,14},{5,15},{6,12},{7,13},{8,2},{9,3},... | collective-permute-start | bytes 49160 | tf_op jit(solution)/shard_map/ppermute | solution.py:46
  20.8 0.0 collective-permute-done.8.q_ref
  20.8 0.0 copy-done.1
  20.8 1.1 %shard_map.80 = bf16[2,40,128]{2,1,0:T(8,128)(2,1)S(1)} custom-call(s32[4]{0:T(128)S(1)} %copy-done.3, s32[4]{0:T(128)S(1)} %copy-done.4, bf16[2,32,128]{2,1,0:T(8,128)(2,1)S(1)} %collective-permute-done.8.q_ref, bf16[4,128,2048]{2,1,0:T(8,128)(2,1)S(1)} %copy-done.1, bf16[4,64,2048]{2,1,0:T(8,128)(2,1)S(1)} %copy-done.2), custom_call_target="tpu_custom_call" | custom-call | flops 11500000 | tf_op jit(solution)/shard_map/pallas_call | solution.py:55
  22.0 0.2 collective-permute-start.9
  22.2 0.0 collective-permute-done.10.q_ref
  22.2 1.1 %shard_map.81 = bf16[2,40,128]{2,1,0:T(8,128)(2,1)S(1)} custom-call(s32[4]{0:T(128)S(1)} %copy-done.3, s32[4]{0:T(128)S(1)} %copy-done.4, bf16[2,32,128]{2,1,0:T(8,128)(2,1)S(1)} %collective-permute-done.10.q_ref, bf16[4,128,2048]{2,1,0:T(8,128)(2,1)S(1)} %copy-done.1, bf16[4,64,2048]{2,1,0:T(8,128)(2,1)S(1)} %copy-done.2), custom_call_target="tpu_custom_call" | custom-call | flops 11500000 | tf_op jit(solution)/shard_map/pallas_call | solution.py:55
  23.4 1.4 %collective-permute-start.11 = (bf16[2,40,128]{2,1,0:T(8,128)(2,1)S(1)}, bf16[2,40,128]{2,1,0:T(8,128)(2,1)S(1)}, u32[]{:S(2)}, u32[]{:S(2)}) collective-permute-start(bf16[2,40,128]{2,1,0:T(8,128)(2,1)S(1)} %shard_map.81), channel_id=1, source_target_pairs={{0,12},{1,13},{2,14},{3,15},{4,8},{5,9},{6,10},{7,11},{8,4},{9,5},... | collective-permute-start | bytes 61448 | tf_op jit(solution)/shard_map/ppermute | solution.py:46
  24.8 0.0 collective-permute-done.12.q_ref
  24.8 1.1 %shard_map.82 = bf16[2,40,128]{2,1,0:T(8,128)(2,1)S(1)} custom-call(s32[4]{0:T(128)S(1)} %copy-done.3, s32[4]{0:T(128)S(1)} %copy-done.4, bf16[2,32,128]{2,1,0:T(8,128)(2,1)S(1)} %collective-permute-done.12.q_ref, bf16[4,128,2048]{2,1,0:T(8,128)(2,1)S(1)} %copy-done.1, bf16[4,64,2048]{2,1,0:T(8,128)(2,1)S(1)} %copy-done.2), custom_call_target="tpu_custom_call" | custom-call | flops 11500000 | tf_op jit(solution)/shard_map/pallas_call | solution.py:55
  25.9 1.5 %collective-permute-start.13 = (bf16[2,40,128]{2,1,0:T(8,128)(2,1)S(1)}, bf16[2,40,128]{2,1,0:T(8,128)(2,1)S(1)}, u32[]{:S(2)}, u32[]{:S(2)}) collective-permute-start(bf16[2,40,128]{2,1,0:T(8,128)(2,1)S(1)} %shard_map.82), channel_id=1, source_target_pairs={{0,14},{1,15},{2,12},{3,13},{4,10},{5,11},{6,8},{7,9},{8,6},{9,7},... | collective-permute-start | bytes 61448 | tf_op jit(solution)/shard_map/ppermute | solution.py:46
  27.4 0.0 collective-permute-done.14.q_ref
  27.4 1.1 %shard_map.83 = bf16[2,40,128]{2,1,0:T(8,128)(2,1)S(1)} custom-call(s32[4]{0:T(128)S(1)} %copy-done.3, s32[4]{0:T(128)S(1)} %copy-done.4, bf16[2,32,128]{2,1,0:T(8,128)(2,1)S(1)} %collective-permute-done.14.q_ref, bf16[4,128,2048]{2,1,0:T(8,128)(2,1)S(1)} %copy-done.1, bf16[4,64,2048]{2,1,0:T(8,128)(2,1)S(1)} %copy-done.2), custom_call_target="tpu_custom_call" | custom-call | flops 11500000 | tf_op jit(solution)/shard_map/pallas_call | solution.py:55
  28.5 0.5 collective-permute-start.15
  29.0 0.0 collective-permute-done.9.a_ref
  29.0 0.0 collective-permute-done.11.b_ref
  29.0 2.0 %collective-permute-done.13.c_ref = bf16[2,40,128]{2,1,0:T(8,128)(2,1)S(1)} collective-permute-done((bf16[2,40,128]{2,1,0:T(8,128)(2,1)S(1)}, bf16[2,40,128]{2,1,0:T(8,128)(2,1)S(1)}, u32[]{:S(2)}, u32[]{:S(2)}) %collective-permute-start.13) | collective-permute-done | bytes 20512 | tf_op jit(solution)/shard_map/ppermute | solution.py:46
  31.0 0.8 %collective-permute-done.15.d_ref = bf16[2,40,128]{2,1,0:T(8,128)(2,1)S(1)} collective-permute-done((bf16[2,40,128]{2,1,0:T(8,128)(2,1)S(1)}, bf16[2,40,128]{2,1,0:T(8,128)(2,1)S(1)}, u32[]{:S(2)}, u32[]{:S(2)}) %collective-permute-start.15) | collective-permute-done | bytes 20512 | tf_op jit(solution)/shard_map/ppermute | solution.py:46
  31.8 0.4 collective-permute-start.16
  32.2 1.4 %collective-permute-start.17 = (bf16[4,40,128]{2,1,0:T(8,128)(2,1)S(1)}, bf16[4,40,128]{2,1,0:T(8,128)(2,1)S(1)}, u32[]{:S(2)}, u32[]{:S(2)}) collective-permute-start(bf16[4,40,128]{2,1,0:T(8,128)(2,1)S(1)} %get-tuple-element.12), channel_id=1, source_target_pairs={{0,9},{1,8},{2,11},{3,10},{4,13},{5,12},{6,15},{7,14},{8,1},{9,0},... | collective-permute-start | bytes 122888 | tf_op jit(solution)/shard_map/ppermute | solution.py:46
  33.6 0.0 collective-permute-done.16.a_ref
  33.6 2.2 %collective-permute-done.17.b_ref = bf16[4,40,128]{2,1,0:T(8,128)(2,1)S(1)} collective-permute-done((bf16[4,40,128]{2,1,0:T(8,128)(2,1)S(1)}, bf16[4,40,128]{2,1,0:T(8,128)(2,1)S(1)}, u32[]{:S(2)}, u32[]{:S(2)}) %collective-permute-start.17) | collective-permute-done | bytes 40992 | tf_op jit(solution)/shard_map/ppermute | solution.py:46
  35.8 0.9 %shard_map.85 = (bf16[2,4,1024]{2,1,0:T(4,128)(2,1)S(1)}, bf16[4,1024]{1,0:T(4,128)(2,1)S(1)}) custom-call(bf16[4,40,128]{2,1,0:T(8,128)(2,1)S(1)} %collective-permute-done.16.a_ref, bf16[4,40,128]{2,1,0:T(8,128)(2,1)S(1)} %collective-permute-done.17.b_ref, bf16[1024,8192]{1,0:T(8,128)(2,1)S(1)} %bitcast.1), custom_call_target="tpu_custom_call" | custom-call | flops 11500000 | tf_op jit(solution)/shard_map/pallas_call | solution.py:55
  36.7 0.6 %collective-permute-start.18 = (bf16[2,4,1024]{2,1,0:T(4,128)(2,1)S(1)}, bf16[2,4,1024]{2,1,0:T(4,128)(2,1)S(1)}, u32[]{:S(2)}, u32[]{:S(2)}) collective-permute-start(bf16[2,4,1024]{2,1,0:T(4,128)(2,1)S(1)} %get-tuple-element.13), channel_id=1, source_target_pairs={{0,12},{1,13},{2,14},{3,15},{4,8},{5,9},{6,10},{7,11},{8,4},{9,5},... | collective-permute-start | bytes 49160 | tf_op jit(solution)/shard_map/ppermute | solution.py:46
  37.4 0.7 %shard_map.87 = bf16[2,4,1024]{2,1,0:T(4,128)(2,1)S(1)} custom-call(bf16[4,1024]{1,0:T(4,128)(2,1)S(1)} %get-tuple-element.14.context_ref, bf16[1024,8192]{1,0:T(8,128)(2,1)S(1)} %bitcast.1), custom_call_target="tpu_custom_call" | custom-call | flops 11500000 | tf_op jit(solution)/shard_map/pallas_call | solution.py:55
  38.0 2.0 %collective-permute-start.19 = (bf16[2,4,1024]{2,1,0:T(4,128)(2,1)S(1)}, bf16[2,4,1024]{2,1,0:T(4,128)(2,1)S(1)}, u32[]{:S(2)}, u32[]{:S(2)}) collective-permute-start(bf16[2,4,1024]{2,1,0:T(4,128)(2,1)S(1)} %shard_map.87), channel_id=1, source_target_pairs={{0,14},{1,15},{2,12},{3,13},{4,10},{5,11},{6,8},{7,9},{8,6},{9,7},... | collective-permute-start | bytes 49160 | tf_op jit(solution)/shard_map/ppermute | solution.py:46
  40.0 0.7 %shard_map.89 = bf16[2,4,1024]{2,1,0:T(4,128)(2,1)S(1)} custom-call(bf16[4,1024]{1,0:T(4,128)(2,1)S(1)} %get-tuple-element.14.context_ref, bf16[1024,8192]{1,0:T(8,128)(2,1)S(1)} %bitcast.1), custom_call_target="tpu_custom_call" | custom-call | flops 11500000 | tf_op jit(solution)/shard_map/pallas_call | solution.py:55
  40.7 0.4 collective-permute-start.20
  41.0 0.7 %shard_map.91 = bf16[2,4,1024]{2,1,0:T(4,128)(2,1)S(1)} custom-call(bf16[4,1024]{1,0:T(4,128)(2,1)S(1)} %get-tuple-element.14.context_ref, bf16[1024,8192]{1,0:T(8,128)(2,1)S(1)} %bitcast.1), custom_call_target="tpu_custom_call" | custom-call | flops 11500000 | tf_op jit(solution)/shard_map/pallas_call | solution.py:55
  41.7 0.4 collective-permute-start.21
  42.1 0.0 collective-permute-done.18.x_ref
  42.1 0.9 %collective-permute-done.19.y_ref = bf16[2,4,1024]{2,1,0:T(4,128)(2,1)S(1)} collective-permute-done((bf16[2,4,1024]{2,1,0:T(4,128)(2,1)S(1)}, bf16[2,4,1024]{2,1,0:T(4,128)(2,1)S(1)}, u32[]{:S(2)}, u32[]{:S(2)}) %collective-permute-start.19) | collective-permute-done | bytes 16416 | tf_op jit(solution)/shard_map/ppermute | solution.py:46
  43.0 0.8 %collective-permute-done.20.y_ref = bf16[2,4,1024]{2,1,0:T(4,128)(2,1)S(1)} collective-permute-done((bf16[2,4,1024]{2,1,0:T(4,128)(2,1)S(1)}, bf16[2,4,1024]{2,1,0:T(4,128)(2,1)S(1)}, u32[]{:S(2)}, u32[]{:S(2)}) %collective-permute-start.20) | collective-permute-done | bytes 16416 | tf_op jit(solution)/shard_map/ppermute | solution.py:46
  43.9 0.0 collective-permute-done.21.y_ref
  43.9 0.2 collective-permute-start.22
  44.1 1.5 %collective-permute-start.23 = (bf16[4,1024]{1,0:T(4,128)(2,1)S(1)}, bf16[4,1024]{1,0:T(4,128)(2,1)S(1)}, u32[]{:S(2)}, u32[]{:S(2)}) collective-permute-start(bf16[4,1024]{1,0:T(4,128)(2,1)S(1)} %get-tuple-element.16), channel_id=1, source_target_pairs={{0,9},{1,8},{2,11},{3,10},{4,13},{5,12},{6,15},{7,14},{8,1},{9,0},... | collective-permute-start | bytes 24584 | tf_op jit(solution)/shard_map/ppermute | solution.py:46
  45.6 1.6 %collective-permute-done.23.y_ref = bf16[4,1024]{1,0:T(4,128)(2,1)S(1)} collective-permute-done((bf16[4,1024]{1,0:T(4,128)(2,1)S(1)}, bf16[4,1024]{1,0:T(4,128)(2,1)S(1)}, u32[]{:S(2)}, u32[]{:S(2)}) %collective-permute-start.23) | collective-permute-done | bytes 8224 | tf_op jit(solution)/shard_map/ppermute | solution.py:46
  47.2 0.0 collective-permute-done.22.x_ref
  47.2 0.6 %shard_map.93 = bf16[4,1024]{1,0:T(4,128)(2,1)} custom-call(f32[4,1024]{1,0:T(4,128)S(1)} %collective-permute-done.22.x_ref, bf16[4,1024]{1,0:T(4,128)(2,1)S(1)} %collective-permute-done.23.y_ref), custom_call_target="tpu_custom_call" | custom-call | tf_op jit(solution)/shard_map/pallas_call | solution.py:55
  (26 shorter events, 0.1 us)
Async XLA Ops:
  0.0 0.7 %copy-start.5 = (bf16[4,1024]{1,0:T(4,128)(2,1)S(1)}, bf16[4,1024]{1,0:T(4,128)(2,1)}, u32[]{:S(2)}) copy-start(bf16[4,1024]{1,0:T(4,128)(2,1)} %x_ref.1) | copy-start | bytes 24580
  0.7 8.6 %copy-start = (bf16[8192,1024]{1,0:T(8,128)(2,1)S(1)}, bf16[8192,1024]{1,0:T(8,128)(2,1)}, u32[]{:S(2)}) copy-start(bf16[8192,1024]{1,0:T(8,128)(2,1)} %w_ref.11) | copy-start | bytes 50331652
  0.7 3.8 %collective-permute-start.1 = (bf16[4,1024]{1,0:T(4,128)(2,1)S(1)}, bf16[4,1024]{1,0:T(4,128)(2,1)S(1)}, u32[]{:S(2)}, u32[]{:S(2)}) collective-permute-start(bf16[4,1024]{1,0:T(4,128)(2,1)S(1)} %shard_map.73), channel_id=1, source_target_pairs={{0,9},{1,8},{2,11},{3,10},{4,13},{5,12},{6,15},{7,14},{8,1},{9,0},... | collective-permute-start | bytes 24584 | tf_op jit(solution)/shard_map/ppermute | solution.py:46
  3.1 1.5 %collective-permute-start = (bf16[4,1024]{1,0:T(4,128)(2,1)S(1)}, bf16[4,1024]{1,0:T(4,128)(2,1)S(1)}, u32[]{:S(2)}, u32[]{:S(2)}) collective-permute-start(bf16[4,1024]{1,0:T(4,128)(2,1)S(1)} %shard_map.73), channel_id=1, source_target_pairs={{0,8},{1,9},{2,10},{3,11},{4,12},{5,13},{6,14},{7,15},{8,0},{9,1},... | collective-permute-start | bytes 24584 | tf_op jit(solution)/shard_map/ppermute | solution.py:46
  4.6 4.7 %collective-permute-start.5 = (bf16[2,4,1024]{2,1,0:T(4,128)(2,1)S(1)}, bf16[2,4,1024]{2,1,0:T(4,128)(2,1)S(1)}, u32[]{:S(2)}, u32[]{:S(2)}) collective-permute-start(bf16[2,4,1024]{2,1,0:T(4,128)(2,1)S(1)} %shard_map.74), channel_id=1, source_target_pairs={{0,8},{1,9},{2,10},{3,11},{4,12},{5,13},{6,14},{7,15},{8,0},{9,1},... | collective-permute-start | bytes 49160 | tf_op jit(solution)/shard_map/ppermute | solution.py:46
  5.1 4.8 %collective-permute-start.4 = (bf16[2,4,1024]{2,1,0:T(4,128)(2,1)S(1)}, bf16[2,4,1024]{2,1,0:T(4,128)(2,1)S(1)}, u32[]{:S(2)}, u32[]{:S(2)}) collective-permute-start(bf16[2,4,1024]{2,1,0:T(4,128)(2,1)S(1)} %shard_map.74), channel_id=1, source_target_pairs={{0,12},{1,13},{2,14},{3,15},{4,8},{5,9},{6,10},{7,11},{8,4},{9,5},... | collective-permute-start | bytes 49160 | tf_op jit(solution)/shard_map/ppermute | solution.py:46
  8.0 5.0 %collective-permute-start.3 = (bf16[2,4,1024]{2,1,0:T(4,128)(2,1)S(1)}, bf16[2,4,1024]{2,1,0:T(4,128)(2,1)S(1)}, u32[]{:S(2)}, u32[]{:S(2)}) collective-permute-start(bf16[2,4,1024]{2,1,0:T(4,128)(2,1)S(1)} %shard_map.74), channel_id=1, source_target_pairs={{0,14},{1,15},{2,12},{3,13},{4,10},{5,11},{6,8},{7,9},{8,6},{9,7},... | collective-permute-start | bytes 49160 | tf_op jit(solution)/shard_map/ppermute | solution.py:46
  9.1 4.5 %collective-permute-start.2 = (bf16[2,4,1024]{2,1,0:T(4,128)(2,1)S(1)}, bf16[2,4,1024]{2,1,0:T(4,128)(2,1)S(1)}, u32[]{:S(2)}, u32[]{:S(2)}) collective-permute-start(bf16[2,4,1024]{2,1,0:T(4,128)(2,1)S(1)} %shard_map.74), channel_id=1, source_target_pairs={{0,10},{1,11},{2,8},{3,9},{4,14},{5,15},{6,12},{7,13},{8,2},{9,3},... | collective-permute-start | bytes 49160 | tf_op jit(solution)/shard_map/ppermute | solution.py:46
  10.6 10.2 %copy-start.1 = (bf16[4,128,2048]{2,1,0:T(8,128)(2,1)S(1)}, bf16[4,128,2048]{2,1,0:T(8,128)(2,1)}, u32[]{:S(2)}) copy-start(bf16[4,128,2048]{2,1,0:T(8,128)(2,1)} %cache_ref.7) | copy-start | bytes 6291460
  10.6 10.2 %copy-start.2 = (bf16[4,64,2048]{2,1,0:T(8,128)(2,1)S(1)}, bf16[4,64,2048]{2,1,0:T(8,128)(2,1)}, u32[]{:S(2)}) copy-start(bf16[4,64,2048]{2,1,0:T(8,128)(2,1)} %fresh_ref.7) | copy-start | bytes 3145732
  10.6 10.2 %copy-start.3 = (s32[4]{0:T(128)S(1)}, s32[4]{0:T(128)}, u32[]{:S(2)}) copy-start(s32[4]{0:T(128)} %clen_ref.7) | copy-start | bytes 52
  10.6 10.2 %copy-start.4 = (s32[4]{0:T(128)S(1)}, s32[4]{0:T(128)}, u32[]{:S(2)}) copy-start(s32[4]{0:T(128)} %nlen_ref.7) | copy-start | bytes 52
  12.9 22.9 %slice-start = ((s8[16777216]{0:T(1024)(128)(4,1)}), s8[4194304]{0:T(1024)(128)(4,1)S(1)}, s32[]{:S(2)}) async-start(s8[16777216]{0:T(1024)(128)(4,1)} %bitcast), calls=%async_computation | async-start | bytes 8388608
  12.9 22.9 %slice-start.1 = ((s8[16777216]{0:T(1024)(128)(4,1)}), s8[4194304]{0:T(1024)(128)(4,1)S(1)}, s32[]{:S(2)}) async-start(s8[16777216]{0:T(1024)(128)(4,1)} %bitcast), calls=%async_computation.1 | async-start | bytes 8388608
  13.6 22.2 %slice-start.2 = ((s8[16777216]{0:T(1024)(128)(4,1)}), s8[4194304]{0:T(1024)(128)(4,1)S(1)}, s32[]{:S(2)}) async-start(s8[16777216]{0:T(1024)(128)(4,1)} %bitcast), calls=%async_computation.2 | async-start | bytes 8388608
  14.3 3.1 %collective-permute-start.7 = (bf16[32,128]{1,0:T(8,128)(2,1)S(1)}, bf16[32,128]{1,0:T(8,128)(2,1)S(1)}, u32[]{:S(2)}, u32[]{:S(2)}) collective-permute-start(bf16[32,128]{1,0:T(8,128)(2,1)S(1)} %shard_map.78), channel_id=1, source_target_pairs={{0,9},{1,8},{2,11},{3,10},{4,13},{5,12},{6,15},{7,14},{8,1},{9,0},... | collective-permute-start | bytes 24584 | tf_op jit(solution)/shard_map/ppermute | solution.py:46
  15.7 1.7 %collective-permute-start.6 = (bf16[32,128]{1,0:T(8,128)(2,1)S(1)}, bf16[32,128]{1,0:T(8,128)(2,1)S(1)}, u32[]{:S(2)}, u32[]{:S(2)}) collective-permute-start(bf16[32,128]{1,0:T(8,128)(2,1)S(1)} %shard_map.78), channel_id=1, source_target_pairs={{0,8},{1,9},{2,10},{3,11},{4,12},{5,13},{6,14},{7,15},{8,0},{9,1},... | collective-permute-start | bytes 24584 | tf_op jit(solution)/shard_map/ppermute | solution.py:46
  17.4 18.4 %slice-start.3 = ((s8[16777216]{0:T(1024)(128)(4,1)}), s8[4194304]{0:T(1024)(128)(4,1)S(1)}, s32[]{:S(2)}) async-start(s8[16777216]{0:T(1024)(128)(4,1)} %bitcast), calls=%async_computation.3 | async-start | bytes 8388608
  17.4 3.4 %collective-permute-start.8 = (bf16[2,32,128]{2,1,0:T(8,128)(2,1)S(1)}, bf16[2,32,128]{2,1,0:T(8,128)(2,1)S(1)}, u32[]{:S(2)}, u32[]{:S(2)}) collective-permute-start(bf16[2,32,128]{2,1,0:T(8,128)(2,1)S(1)} %shard_map.79), channel_id=1, source_target_pairs={{0,8},{1,9},{2,10},{3,11},{4,12},{5,13},{6,14},{7,15},{8,0},{9,1},... | collective-permute-start | bytes 49160 | tf_op jit(solution)/shard_map/ppermute | solution.py:46
  17.6 4.6 %collective-permute-start.10 = (bf16[2,32,128]{2,1,0:T(8,128)(2,1)S(1)}, bf16[2,32,128]{2,1,0:T(8,128)(2,1)S(1)}, u32[]{:S(2)}, u32[]{:S(2)}) collective-permute-start(bf16[2,32,128]{2,1,0:T(8,128)(2,1)S(1)} %shard_map.79), channel_id=1, source_target_pairs={{0,12},{1,13},{2,14},{3,15},{4,8},{5,9},{6,10},{7,11},{8,4},{9,5},... | collective-permute-start | bytes 49160 | tf_op jit(solution)/shard_map/ppermute | solution.py:46
  18.1 6.7 %collective-permute-start.12 = (bf16[2,32,128]{2,1,0:T(8,128)(2,1)S(1)}, bf16[2,32,128]{2,1,0:T(8,128)(2,1)S(1)}, u32[]{:S(2)}, u32[]{:S(2)}) collective-permute-start(bf16[2,32,128]{2,1,0:T(8,128)(2,1)S(1)} %shard_map.79), channel_id=1, source_target_pairs={{0,14},{1,15},{2,12},{3,13},{4,10},{5,11},{6,8},{7,9},{8,6},{9,7},... | collective-permute-start | bytes 49160 | tf_op jit(solution)/shard_map/ppermute | solution.py:46
  19.5 7.9 %collective-permute-start.14 = (bf16[2,32,128]{2,1,0:T(8,128)(2,1)S(1)}, bf16[2,32,128]{2,1,0:T(8,128)(2,1)S(1)}, u32[]{:S(2)}, u32[]{:S(2)}) collective-permute-start(bf16[2,32,128]{2,1,0:T(8,128)(2,1)S(1)} %shard_map.79), channel_id=1, source_target_pairs={{0,10},{1,11},{2,8},{3,9},{4,14},{5,15},{6,12},{7,13},{8,2},{9,3},... | collective-permute-start | bytes 49160 | tf_op jit(solution)/shard_map/ppermute | solution.py:46
  22.0 7.1 %collective-permute-start.9 = (bf16[2,40,128]{2,1,0:T(8,128)(2,1)S(1)}, bf16[2,40,128]{2,1,0:T(8,128)(2,1)S(1)}, u32[]{:S(2)}, u32[]{:S(2)}) collective-permute-start(bf16[2,40,128]{2,1,0:T(8,128)(2,1)S(1)} %shard_map.80), channel_id=1, source_target_pairs={{0,8},{1,9},{2,10},{3,11},{4,12},{5,13},{6,14},{7,15},{8,0},{9,1},... | collective-permute-start | bytes 61448 | tf_op jit(solution)/shard_map/ppermute | solution.py:46
  23.4 5.7 %collective-permute-start.11 = (bf16[2,40,128]{2,1,0:T(8,128)(2,1)S(1)}, bf16[2,40,128]{2,1,0:T(8,128)(2,1)S(1)}, u32[]{:S(2)}, u32[]{:S(2)}) collective-permute-start(bf16[2,40,128]{2,1,0:T(8,128)(2,1)S(1)} %shard_map.81), channel_id=1, source_target_pairs={{0,12},{1,13},{2,14},{3,15},{4,8},{5,9},{6,10},{7,11},{8,4},{9,5},... | collective-permute-start | bytes 61448 | tf_op jit(solution)/shard_map/ppermute | solution.py:46
  25.9 5.1 %collective-permute-start.13 = (bf16[2,40,128]{2,1,0:T(8,128)(2,1)S(1)}, bf16[2,40,128]{2,1,0:T(8,128)(2,1)S(1)}, u32[]{:S(2)}, u32[]{:S(2)}) collective-permute-start(bf16[2,40,128]{2,1,0:T(8,128)(2,1)S(1)} %shard_map.82), channel_id=1, source_target_pairs={{0,14},{1,15},{2,12},{3,13},{4,10},{5,11},{6,8},{7,9},{8,6},{9,7},... | collective-permute-start | bytes 61448 | tf_op jit(solution)/shard_map/ppermute | solution.py:46
  28.5 3.3 %collective-permute-start.15 = (bf16[2,40,128]{2,1,0:T(8,128)(2,1)S(1)}, bf16[2,40,128]{2,1,0:T(8,128)(2,1)S(1)}, u32[]{:S(2)}, u32[]{:S(2)}) collective-permute-start(bf16[2,40,128]{2,1,0:T(8,128)(2,1)S(1)} %shard_map.83), channel_id=1, source_target_pairs={{0,10},{1,11},{2,8},{3,9},{4,14},{5,15},{6,12},{7,13},{8,2},{9,3},... | collective-permute-start | bytes 61448 | tf_op jit(solution)/shard_map/ppermute | solution.py:46
  31.8 1.8 %collective-permute-start.16 = (bf16[4,40,128]{2,1,0:T(8,128)(2,1)S(1)}, bf16[4,40,128]{2,1,0:T(8,128)(2,1)S(1)}, u32[]{:S(2)}, u32[]{:S(2)}) collective-permute-start(bf16[4,40,128]{2,1,0:T(8,128)(2,1)S(1)} %get-tuple-element.11), channel_id=1, source_target_pairs={{0,8},{1,9},{2,10},{3,11},{4,12},{5,13},{6,14},{7,15},{8,0},{9,1},... | collective-permute-start | bytes 122888 | tf_op jit(solution)/shard_map/ppermute | solution.py:46
  32.2 3.6 %collective-permute-start.17 = (bf16[4,40,128]{2,1,0:T(8,128)(2,1)S(1)}, bf16[4,40,128]{2,1,0:T(8,128)(2,1)S(1)}, u32[]{:S(2)}, u32[]{:S(2)}) collective-permute-start(bf16[4,40,128]{2,1,0:T(8,128)(2,1)S(1)} %get-tuple-element.12), channel_id=1, source_target_pairs={{0,9},{1,8},{2,11},{3,10},{4,13},{5,12},{6,15},{7,14},{8,1},{9,0},... | collective-permute-start | bytes 122888 | tf_op jit(solution)/shard_map/ppermute | solution.py:46
  36.7 5.4 %collective-permute-start.18 = (bf16[2,4,1024]{2,1,0:T(4,128)(2,1)S(1)}, bf16[2,4,1024]{2,1,0:T(4,128)(2,1)S(1)}, u32[]{:S(2)}, u32[]{:S(2)}) collective-permute-start(bf16[2,4,1024]{2,1,0:T(4,128)(2,1)S(1)} %get-tuple-element.13), channel_id=1, source_target_pairs={{0,12},{1,13},{2,14},{3,15},{4,8},{5,9},{6,10},{7,11},{8,4},{9,5},... | collective-permute-start | bytes 49160 | tf_op jit(solution)/shard_map/ppermute | solution.py:46
  38.0 5.0 %collective-permute-start.19 = (bf16[2,4,1024]{2,1,0:T(4,128)(2,1)S(1)}, bf16[2,4,1024]{2,1,0:T(4,128)(2,1)S(1)}, u32[]{:S(2)}, u32[]{:S(2)}) collective-permute-start(bf16[2,4,1024]{2,1,0:T(4,128)(2,1)S(1)} %shard_map.87), channel_id=1, source_target_pairs={{0,14},{1,15},{2,12},{3,13},{4,10},{5,11},{6,8},{7,9},{8,6},{9,7},... | collective-permute-start | bytes 49160 | tf_op jit(solution)/shard_map/ppermute | solution.py:46
  40.7 3.2 %collective-permute-start.20 = (bf16[2,4,1024]{2,1,0:T(4,128)(2,1)S(1)}, bf16[2,4,1024]{2,1,0:T(4,128)(2,1)S(1)}, u32[]{:S(2)}, u32[]{:S(2)}) collective-permute-start(bf16[2,4,1024]{2,1,0:T(4,128)(2,1)S(1)} %shard_map.89), channel_id=1, source_target_pairs={{0,10},{1,11},{2,8},{3,9},{4,14},{5,15},{6,12},{7,13},{8,2},{9,3},... | collective-permute-start | bytes 49160 | tf_op jit(solution)/shard_map/ppermute | solution.py:46
  41.7 2.2 %collective-permute-start.21 = (bf16[2,4,1024]{2,1,0:T(4,128)(2,1)S(1)}, bf16[2,4,1024]{2,1,0:T(4,128)(2,1)S(1)}, u32[]{:S(2)}, u32[]{:S(2)}) collective-permute-start(bf16[2,4,1024]{2,1,0:T(4,128)(2,1)S(1)} %shard_map.91), channel_id=1, source_target_pairs={{0,8},{1,9},{2,10},{3,11},{4,12},{5,13},{6,14},{7,15},{8,0},{9,1},... | collective-permute-start | bytes 49160 | tf_op jit(solution)/shard_map/ppermute | solution.py:46
  43.9 3.3 %collective-permute-start.22 = (f32[4,1024]{1,0:T(4,128)S(1)}, f32[4,1024]{1,0:T(4,128)S(1)}, u32[]{:S(2)}, u32[]{:S(2)}) collective-permute-start(f32[4,1024]{1,0:T(4,128)S(1)} %get-tuple-element.15), channel_id=1, source_target_pairs={{0,8},{1,9},{2,10},{3,11},{4,12},{5,13},{6,14},{7,15},{8,0},{9,1},... | collective-permute-start | bytes 49160 | tf_op jit(solution)/shard_map/ppermute | solution.py:46
  44.1 3.1 %collective-permute-start.23 = (bf16[4,1024]{1,0:T(4,128)(2,1)S(1)}, bf16[4,1024]{1,0:T(4,128)(2,1)S(1)}, u32[]{:S(2)}, u32[]{:S(2)}) collective-permute-start(bf16[4,1024]{1,0:T(4,128)(2,1)S(1)} %get-tuple-element.16), channel_id=1, source_target_pairs={{0,9},{1,8},{2,11},{3,10},{4,13},{5,12},{6,15},{7,14},{8,1},{9,0},... | collective-permute-start | bytes 24584 | tf_op jit(solution)/shard_map/ppermute | solution.py:46

commit v10 on v9

--- a/solution.py
+++ b/solution.py
@@ -103,7 +103,8 @@
     return acc
 
 
-def first_kernel(x_ref, w_ref, acc_ref):
+def first_kernel(cc, fc, clen_ref, nlen_ref, x_ref, w_ref, acc_ref, limit_ref):
+    limit_kernel(cc, fc, clen_ref, nlen_ref, limit_ref)
     acc_ref[...] = pair_product(0, x_ref, w_ref)
 
 
@@ -201,10 +202,19 @@
     o_ref[1 - odd] = y_ref[...]
 
 
-def pair_attend_kernel(apart, clen_ref, nlen_ref, q_ref, cache_ref, fresh_ref, o_ref):
-    rows, cc, width = cache_ref.shape
+def limit_kernel(cc, fc, clen_ref, nlen_ref, o_ref):
+    place = lax.axis_index("tensor")
+    request = lax.broadcasted_iota(jnp.int32, (1, o_ref.shape[1]), 1) // (2 * GROUP)
+    for i, (ref, count) in enumerate(((clen_ref, cc), (nlen_ref, fc))):
+        limit = jnp.full(request.shape, ref[0] - place * count, jnp.int32)
+        for r in range(1, ref.shape[0]):
+            limit = jnp.where(request == r, ref[r] - place * count, limit)
+        o_ref[i : i + 1, :] = limit
+
+
+def pair_attend_kernel(apart, limit_ref, q_ref, cache_ref, fresh_ref, o_ref):
+    rows, _, width = cache_ref.shape
     width = width // 2
-    fc = fresh_ref.shape[1]
     both = 2 * GROUP
     place = lax.axis_index("tensor")
     at = (place ^ apart) // 2 * (2 * HD)
@@ -222,17 +232,13 @@
             blocks.append(jnp.where((lane >= first) & (lane < first + GROUP), q, 0.0))
         wide.append(jnp.concatenate(blocks, axis=0).astype(BF16))
 
-    def logits(ref, start, length_ref):
+    def logits(ref, limit):
         s = functools.reduce(jnp.add, [dot(ref[r, :, keys], wide[r]) for r in range(rows)])
-        request = lax.broadcasted_iota(jnp.int32, s.shape, 1) // both
-        length = jnp.full(s.shape, length_ref[0], jnp.int32)
-        for r in range(1, rows):
-            length = jnp.where(request == r, length_ref[r], length)
-        valid = start + lax.broadcasted_iota(jnp.int32, s.shape, 0) < length
+        valid = lax.broadcasted_iota(jnp.int32, s.shape, 0) < limit
         return jnp.where(valid, s * HD**-0.5, -1e30), valid
 
-    sc, okc = logits(cache_ref, place * cc, clen_ref)
-    sf, okf = logits(fresh_ref, place * fc, nlen_ref)
+    sc, okc = logits(cache_ref, limit_ref[0:1, :])
+    sf, okf = logits(fresh_ref, limit_ref[1:2, :])
     top = jnp.maximum(jnp.max(sc, axis=0, keepdims=True), jnp.max(sf, axis=0, keepdims=True))
     wc = jnp.where(okc, jnp.exp(sc - top), 0.0)
     wf = jnp.where(okf, jnp.exp(sf - top), 0.0)
@@ -421,7 +427,17 @@
         mine = call(copy_kernel, (rows, feat), BF16, hidden, flops=LONG)
         near = flip(mine, 1)
         pair = call(stack_kernel, (2, rows, feat), BF16, flip(mine, 0), near)
-        acc = call(first_kernel, (rows, own * HD), F32, flip(pair, 0), w_query, flops=FIRST)
+        acc, limits = call(
+            functools.partial(first_kernel, cache.shape[1], fresh.shape[1]),
+            [(rows, own * HD), (2, rows * 2 * GROUP)],
+            [F32, jnp.int32],
+            cache_lengths,
+            new_lengths,
+            flip(pair, 0),
+            w_query,
+            specs=[SMEM] * 2 + [VMEM] * 2,
+            flops=FIRST,
+        )
         got = [flip(pair, apart) for apart in ORDER]
         for apart, x in zip(ORDER[:2], got):
             step = functools.partial(next_kernel, apart)
@@ -441,12 +457,10 @@
                 functools.partial(pair_attend_kernel, apart),
                 (2, rows * GROUP + STATS, HD),
                 BF16,
-                cache_lengths,
-                new_lengths,
+                limits,
                 flip(pair, apart),
                 cache,
                 fresh,
-                specs=[SMEM] * 2 + [VMEM] * 3,
                 flops=PIECE,
             )
 

time: 48 us -> 46 us (0.958)
  Pallas kernels: 10.8 us -> 9.15 us
    pallas_call x21, Pallas kernels: 10.8 us -> 9.15 us  [call(): pl.pallas_call(kernel, in_specs=specs or [VMEM] * len(args), out_specs=ou...]
  transfers between devices with their start and end apart: 24 -> 24, of which waited for: 10 -> 11; matrix products, arithmetic and copies ran while one was open for 0% -> 0% of each run, Pallas kernels for 18% -> 15%
where the time goes in v10:
time: 46 us; the launch traced here: 45.8 us
  starting transfers between devices  23.2 us (50%)
  waiting for transfers between devices  12.7 us (28%)
  Pallas kernels  9.15 us (20%)
  local copies, waits for them, and re-layouts  0.73 us (2%)
    ppermute x24, starting transfers between devices, flip(): lax.ppermute(x, BOTH, [(i, (i // n ^ 1) * n + (i % n ^ apart)) for i in r...  23.2 us
    ppermute x24, waiting for transfers between devices, flip(): lax.ppermute(x, BOTH, [(i, (i // n ^ 1) * n + (i % n ^ apart)) for i in r...  12.7 us
    pallas_call x21, Pallas kernels, call(): pl.pallas_call(kernel, in_specs=specs or [VMEM] * len(args), out_specs=ou...  9.15 us
  transfers between devices with their start and end apart: 24, of which 11 were waited for; matrix products, arithmetic and copies ran while one was open for 0% of the time, Pallas kernels for 15%

profile of v10, /device:TPU:0, one launch (start us, length us, event | category | flops | bytes accessed | tf_op | source)
XLA Modules:
  0.0 45.8 jit_solution(15372686161072527788)
XLA Ops:
  0.0 0.7 %copy-done.5 = bf16[4,1024]{1,0:T(4,128)(2,1)S(1)} copy-done((bf16[4,1024]{1,0:T(4,128)(2,1)S(1)}, bf16[4,1024]{1,0:T(4,128)(2,1)}, u32[]{:S(2)}) %copy-start.5) | copy-done | bytes 8216
  0.7 2.5 %collective-permute-start.1 = (bf16[4,1024]{1,0:T(4,128)(2,1)S(1)}, bf16[4,1024]{1,0:T(4,128)(2,1)S(1)}, u32[]{:S(2)}, u32[]{:S(2)}) collective-permute-start(bf16[4,1024]{1,0:T(4,128)(2,1)S(1)} %shard_map.73), channel_id=1, source_target_pairs={{0,9},{1,8},{2,11},{3,10},{4,13},{5,12},{6,15},{7,14},{8,1},{9,0},... | collective-permute-start | bytes 24584 | tf_op jit(solution)/shard_map/ppermute | solution.py:46
  3.2 0.7 %collective-permute-start = (bf16[4,1024]{1,0:T(4,128)(2,1)S(1)}, bf16[4,1024]{1,0:T(4,128)(2,1)S(1)}, u32[]{:S(2)}, u32[]{:S(2)}) collective-permute-start(bf16[4,1024]{1,0:T(4,128)(2,1)S(1)} %shard_map.73), channel_id=1, source_target_pairs={{0,8},{1,9},{2,10},{3,11},{4,12},{5,13},{6,14},{7,15},{8,0},{9,1},... | collective-permute-start | bytes 24584 | tf_op jit(solution)/shard_map/ppermute | solution.py:46
  3.9 0.7 %collective-permute-done.1.y_ref = bf16[4,1024]{1,0:T(4,128)(2,1)S(1)} collective-permute-done((bf16[4,1024]{1,0:T(4,128)(2,1)S(1)}, bf16[4,1024]{1,0:T(4,128)(2,1)S(1)}, u32[]{:S(2)}, u32[]{:S(2)}) %collective-permute-start.1) | collective-permute-done | bytes 8224 | tf_op jit(solution)/shard_map/ppermute | solution.py:46
  4.5 0.1 collective-permute-done.x_ref
  4.7 0.5 %collective-permute-start.2 = (bf16[2,4,1024]{2,1,0:T(4,128)(2,1)S(1)}, bf16[2,4,1024]{2,1,0:T(4,128)(2,1)S(1)}, u32[]{:S(2)}, u32[]{:S(2)}) collective-permute-start(bf16[2,4,1024]{2,1,0:T(4,128)(2,1)S(1)} %shard_map.74), channel_id=1, source_target_pairs={{0,8},{1,9},{2,10},{3,11},{4,12},{5,13},{6,14},{7,15},{8,0},{9,1},... | collective-permute-start | bytes 49160 | tf_op jit(solution)/shard_map/ppermute | solution.py:46
  5.2 2.8 %collective-permute-start.5 = (bf16[2,4,1024]{2,1,0:T(4,128)(2,1)S(1)}, bf16[2,4,1024]{2,1,0:T(4,128)(2,1)S(1)}, u32[]{:S(2)}, u32[]{:S(2)}) collective-permute-start(bf16[2,4,1024]{2,1,0:T(4,128)(2,1)S(1)} %shard_map.74), channel_id=1, source_target_pairs={{0,12},{1,13},{2,14},{3,15},{4,8},{5,9},{6,10},{7,11},{8,4},{9,5},... | collective-permute-start | bytes 49160 | tf_op jit(solution)/shard_map/ppermute | solution.py:46
  8.0 1.1 %collective-permute-start.4 = (bf16[2,4,1024]{2,1,0:T(4,128)(2,1)S(1)}, bf16[2,4,1024]{2,1,0:T(4,128)(2,1)S(1)}, u32[]{:S(2)}, u32[]{:S(2)}) collective-permute-start(bf16[2,4,1024]{2,1,0:T(4,128)(2,1)S(1)} %shard_map.74), channel_id=1, source_target_pairs={{0,14},{1,15},{2,12},{3,13},{4,10},{5,11},{6,8},{7,9},{8,6},{9,7},... | collective-permute-start | bytes 49160 | tf_op jit(solution)/shard_map/ppermute | solution.py:46
  9.1 0.2 collective-permute-start.3
  9.4 0.0 collective-permute-done.2.x_ref
  9.4 0.0 copy-done
  9.4 1.2 %shard_map.75 = (f32[4,1024]{1,0:T(4,128)S(1)}, s32[2,64]{1,0:T(2,128)S(1)}) custom-call(s32[4]{0:T(128)S(1)} %copy-done.3, s32[4]{0:T(128)S(1)} %copy-done.4, bf16[2,4,1024]{2,1,0:T(4,128)(2,1)S(1)} %collective-permute-done.2.x_ref, bf16[8192,1024]{1,0:T(8,128)(2,1)S(1)} %copy-done), custom_call_target="tpu_custom_call" | custom-call | tf_op jit(solution)/shard_map/pallas_call | solution.py:55
  10.6 0.0 collective-permute-done.5.x_ref
  10.6 0.7 %shard_map.76.old_ref = f32[4,1024]{1,0:T(4,128)S(1)} custom-call(bf16[2,4,1024]{2,1,0:T(4,128)(2,1)S(1)} %collective-permute-done.5.x_ref, bf16[8192,1024]{1,0:T(8,128)(2,1)S(1)} %copy-done, f32[4,1024]{1,0:T(4,128)S(1)} %get-tuple-element.14.old_ref), custom_call_target="tpu_custom_call" | custom-call | flops 10000000000 | tf_op jit(solution)/shard_map/pallas_call | solution.py:55
  11.2 1.8 %collective-permute-done.4.x_ref = bf16[2,4,1024]{2,1,0:T(4,128)(2,1)S(1)} collective-permute-done((bf16[2,4,1024]{2,1,0:T(4,128)(2,1)S(1)}, bf16[2,4,1024]{2,1,0:T(4,128)(2,1)S(1)}, u32[]{:S(2)}, u32[]{:S(2)}) %collective-permute-start.4) | collective-permute-done | bytes 16416 | tf_op jit(solution)/shard_map/ppermute | solution.py:46
  13.0 0.7 %shard_map.77.old_ref = f32[4,1024]{1,0:T(4,128)S(1)} custom-call(bf16[2,4,1024]{2,1,0:T(4,128)(2,1)S(1)} %collective-permute-done.4.x_ref, bf16[8192,1024]{1,0:T(8,128)(2,1)S(1)} %copy-done, f32[4,1024]{1,0:T(4,128)S(1)} %shard_map.76.old_ref), custom_call_target="tpu_custom_call" | custom-call | tf_op jit(solution)/shard_map/pallas_call | solution.py:55
  13.7 0.0 collective-permute-done.3.x_ref
  13.7 0.7 %shard_map.78 = bf16[32,128]{1,0:T(8,128)(2,1)S(1)} custom-call(bf16[2,4,1024]{2,1,0:T(4,128)(2,1)S(1)} %collective-permute-done.3.x_ref, bf16[8192,1024]{1,0:T(8,128)(2,1)S(1)} %copy-done, f32[4,1024]{1,0:T(4,128)S(1)} %shard_map.77.old_ref), custom_call_target="tpu_custom_call" | custom-call | tf_op jit(solution)/shard_map/pallas_call | solution.py:55
  14.3 1.4 %collective-permute-start.7 = (bf16[32,128]{1,0:T(8,128)(2,1)S(1)}, bf16[32,128]{1,0:T(8,128)(2,1)S(1)}, u32[]{:S(2)}, u32[]{:S(2)}) collective-permute-start(bf16[32,128]{1,0:T(8,128)(2,1)S(1)} %shard_map.78), channel_id=1, source_target_pairs={{0,9},{1,8},{2,11},{3,10},{4,13},{5,12},{6,15},{7,14},{8,1},{9,0},... | collective-permute-start | bytes 24584 | tf_op jit(solution)/shard_map/ppermute | solution.py:46
  15.7 0.3 collective-permute-start.6
  16.1 1.4 %collective-permute-done.7.y_ref = bf16[32,128]{1,0:T(8,128)(2,1)S(1)} collective-permute-done((bf16[32,128]{1,0:T(8,128)(2,1)S(1)}, bf16[32,128]{1,0:T(8,128)(2,1)S(1)}, u32[]{:S(2)}, u32[]{:S(2)}) %collective-permute-start.7) | collective-permute-done | bytes 8224 | tf_op jit(solution)/shard_map/ppermute | solution.py:46
  17.4 0.0 collective-permute-done.6.x_ref
  17.4 0.2 collective-permute-start.8
  17.6 1.0 %collective-permute-start.10 = (bf16[2,32,128]{2,1,0:T(8,128)(2,1)S(1)}, bf16[2,32,128]{2,1,0:T(8,128)(2,1)S(1)}, u32[]{:S(2)}, u32[]{:S(2)}) collective-permute-start(bf16[2,32,128]{2,1,0:T(8,128)(2,1)S(1)} %shard_map.79), channel_id=1, source_target_pairs={{0,12},{1,13},{2,14},{3,15},{4,8},{5,9},{6,10},{7,11},{8,4},{9,5},... | collective-permute-start | bytes 49160 | tf_op jit(solution)/shard_map/ppermute | solution.py:46
  18.6 1.1 %collective-permute-start.12 = (bf16[2,32,128]{2,1,0:T(8,128)(2,1)S(1)}, bf16[2,32,128]{2,1,0:T(8,128)(2,1)S(1)}, u32[]{:S(2)}, u32[]{:S(2)}) collective-permute-start(bf16[2,32,128]{2,1,0:T(8,128)(2,1)S(1)} %shard_map.79), channel_id=1, source_target_pairs={{0,14},{1,15},{2,12},{3,13},{4,10},{5,11},{6,8},{7,9},{8,6},{9,7},... | collective-permute-start | bytes 49160 | tf_op jit(solution)/shard_map/ppermute | solution.py:46
  19.7 1.0 %collective-permute-start.14 = (bf16[2,32,128]{2,1,0:T(8,128)(2,1)S(1)}, bf16[2,32,128]{2,1,0:T(8,128)(2,1)S(1)}, u32[]{:S(2)}, u32[]{:S(2)}) collective-permute-start(bf16[2,32,128]{2,1,0:T(8,128)(2,1)S(1)} %shard_map.79), channel_id=1, source_target_pairs={{0,10},{1,11},{2,8},{3,9},{4,14},{5,15},{6,12},{7,13},{8,2},{9,3},... | collective-permute-start | bytes 49160 | tf_op jit(solution)/shard_map/ppermute | solution.py:46
  20.8 0.0 collective-permute-done.8.q_ref
  20.8 0.0 slice-start.3
  20.8 0.6 %shard_map.80 = bf16[2,40,128]{2,1,0:T(8,128)(2,1)S(1)} custom-call(s32[2,64]{1,0:T(2,128)S(1)} %get-tuple-element.13.limit_ref, bf16[2,32,128]{2,1,0:T(8,128)(2,1)S(1)} %collective-permute-done.8.q_ref, bf16[4,128,2048]{2,1,0:T(8,128)(2,1)S(1)} %copy-done.1, bf16[4,64,2048]{2,1,0:T(8,128)(2,1)S(1)} %copy-done.2), custom_call_target="tpu_custom_call" | custom-call | flops 11500000 | tf_op jit(solution)/shard_map/pallas_call | solution.py:55
  21.4 0.3 collective-permute-start.9
  21.7 0.2 collective-permute-done.10.q_ref
  21.9 0.6 %shard_map.81 = bf16[2,40,128]{2,1,0:T(8,128)(2,1)S(1)} custom-call(s32[2,64]{1,0:T(2,128)S(1)} %get-tuple-element.13.limit_ref, bf16[2,32,128]{2,1,0:T(8,128)(2,1)S(1)} %collective-permute-done.10.q_ref, bf16[4,128,2048]{2,1,0:T(8,128)(2,1)S(1)} %copy-done.1, bf16[4,64,2048]{2,1,0:T(8,128)(2,1)S(1)} %copy-done.2), custom_call_target="tpu_custom_call" | custom-call | flops 11500000 | tf_op jit(solution)/shard_map/pallas_call | solution.py:55
  22.5 1.8 %collective-permute-start.11 = (bf16[2,40,128]{2,1,0:T(8,128)(2,1)S(1)}, bf16[2,40,128]{2,1,0:T(8,128)(2,1)S(1)}, u32[]{:S(2)}, u32[]{:S(2)}) collective-permute-start(bf16[2,40,128]{2,1,0:T(8,128)(2,1)S(1)} %shard_map.81), channel_id=1, source_target_pairs={{0,12},{1,13},{2,14},{3,15},{4,8},{5,9},{6,10},{7,11},{8,4},{9,5},... | collective-permute-start | bytes 61448 | tf_op jit(solution)/shard_map/ppermute | solution.py:46
  24.2 0.0 collective-permute-done.12.q_ref
  24.2 0.6 %shard_map.82 = bf16[2,40,128]{2,1,0:T(8,128)(2,1)S(1)} custom-call(s32[2,64]{1,0:T(2,128)S(1)} %get-tuple-element.13.limit_ref, bf16[2,32,128]{2,1,0:T(8,128)(2,1)S(1)} %collective-permute-done.12.q_ref, bf16[4,128,2048]{2,1,0:T(8,128)(2,1)S(1)} %copy-done.1, bf16[4,64,2048]{2,1,0:T(8,128)(2,1)S(1)} %copy-done.2), custom_call_target="tpu_custom_call" | custom-call | flops 11500000 | tf_op jit(solution)/shard_map/pallas_call | solution.py:55
  24.8 1.2 %collective-permute-start.13 = (bf16[2,40,128]{2,1,0:T(8,128)(2,1)S(1)}, bf16[2,40,128]{2,1,0:T(8,128)(2,1)S(1)}, u32[]{:S(2)}, u32[]{:S(2)}) collective-permute-start(bf16[2,40,128]{2,1,0:T(8,128)(2,1)S(1)} %shard_map.82), channel_id=1, source_target_pairs={{0,14},{1,15},{2,12},{3,13},{4,10},{5,11},{6,8},{7,9},{8,6},{9,7},... | collective-permute-start | bytes 61448 | tf_op jit(solution)/shard_map/ppermute | solution.py:46
  26.0 0.0 collective-permute-done.14.q_ref
  26.0 0.6 %shard_map.83 = bf16[2,40,128]{2,1,0:T(8,128)(2,1)S(1)} custom-call(s32[2,64]{1,0:T(2,128)S(1)} %get-tuple-element.13.limit_ref, bf16[2,32,128]{2,1,0:T(8,128)(2,1)S(1)} %collective-permute-done.14.q_ref, bf16[4,128,2048]{2,1,0:T(8,128)(2,1)S(1)} %copy-done.1, bf16[4,64,2048]{2,1,0:T(8,128)(2,1)S(1)} %copy-done.2), custom_call_target="tpu_custom_call" | custom-call | flops 11500000 | tf_op jit(solution)/shard_map/pallas_call | solution.py:55
  26.6 0.3 collective-permute-start.15
  26.9 0.0 collective-permute-done.9.a_ref
  26.9 0.0 collective-permute-done.11.b_ref
  26.9 3.0 %collective-permute-done.13.c_ref = bf16[2,40,128]{2,1,0:T(8,128)(2,1)S(1)} collective-permute-done((bf16[2,40,128]{2,1,0:T(8,128)(2,1)S(1)}, bf16[2,40,128]{2,1,0:T(8,128)(2,1)S(1)}, u32[]{:S(2)}, u32[]{:S(2)}) %collective-permute-start.13) | collective-permute-done | bytes 20512 | tf_op jit(solution)/shard_map/ppermute | solution.py:46
  29.9 0.5 %collective-permute-done.15.d_ref = bf16[2,40,128]{2,1,0:T(8,128)(2,1)S(1)} collective-permute-done((bf16[2,40,128]{2,1,0:T(8,128)(2,1)S(1)}, bf16[2,40,128]{2,1,0:T(8,128)(2,1)S(1)}, u32[]{:S(2)}, u32[]{:S(2)}) %collective-permute-start.15) | collective-permute-done | bytes 20512 | tf_op jit(solution)/shard_map/ppermute | solution.py:46
  30.4 0.2 collective-permute-start.16
  30.6 1.6 %collective-permute-start.17 = (bf16[4,40,128]{2,1,0:T(8,128)(2,1)S(1)}, bf16[4,40,128]{2,1,0:T(8,128)(2,1)S(1)}, u32[]{:S(2)}, u32[]{:S(2)}) collective-permute-start(bf16[4,40,128]{2,1,0:T(8,128)(2,1)S(1)} %get-tuple-element.16), channel_id=1, source_target_pairs={{0,9},{1,8},{2,11},{3,10},{4,13},{5,12},{6,15},{7,14},{8,1},{9,0},... | collective-permute-start | bytes 122888 | tf_op jit(solution)/shard_map/ppermute | solution.py:46
  32.2 0.0 collective-permute-done.16.a_ref
  32.2 1.9 %collective-permute-done.17.b_ref = bf16[4,40,128]{2,1,0:T(8,128)(2,1)S(1)} collective-permute-done((bf16[4,40,128]{2,1,0:T(8,128)(2,1)S(1)}, bf16[4,40,128]{2,1,0:T(8,128)(2,1)S(1)}, u32[]{:S(2)}, u32[]{:S(2)}) %collective-permute-start.17) | collective-permute-done | bytes 40992 | tf_op jit(solution)/shard_map/ppermute | solution.py:46
  34.1 0.9 %shard_map.85 = (bf16[2,4,1024]{2,1,0:T(4,128)(2,1)S(1)}, bf16[4,1024]{1,0:T(4,128)(2,1)S(1)}) custom-call(bf16[4,40,128]{2,1,0:T(8,128)(2,1)S(1)} %collective-permute-done.16.a_ref, bf16[4,40,128]{2,1,0:T(8,128)(2,1)S(1)} %collective-permute-done.17.b_ref, bf16[1024,8192]{1,0:T(8,128)(2,1)S(1)} %bitcast.1), custom_call_target="tpu_custom_call" | custom-call | flops 11500000 | tf_op jit(solution)/shard_map/pallas_call | solution.py:55
  35.0 0.7 %collective-permute-start.18 = (bf16[2,4,1024]{2,1,0:T(4,128)(2,1)S(1)}, bf16[2,4,1024]{2,1,0:T(4,128)(2,1)S(1)}, u32[]{:S(2)}, u32[]{:S(2)}) collective-permute-start(bf16[2,4,1024]{2,1,0:T(4,128)(2,1)S(1)} %get-tuple-element.17), channel_id=1, source_target_pairs={{0,12},{1,13},{2,14},{3,15},{4,8},{5,9},{6,10},{7,11},{8,4},{9,5},... | collective-permute-start | bytes 49160 | tf_op jit(solution)/shard_map/ppermute | solution.py:46
  35.7 0.7 %shard_map.87 = bf16[2,4,1024]{2,1,0:T(4,128)(2,1)S(1)} custom-call(bf16[4,1024]{1,0:T(4,128)(2,1)S(1)} %get-tuple-element.18.context_ref, bf16[1024,8192]{1,0:T(8,128)(2,1)S(1)} %bitcast.1), custom_call_target="tpu_custom_call" | custom-call | flops 11500000 | tf_op jit(solution)/shard_map/pallas_call | solution.py:55
  36.4 1.4 %collective-permute-start.19 = (bf16[2,4,1024]{2,1,0:T(4,128)(2,1)S(1)}, bf16[2,4,1024]{2,1,0:T(4,128)(2,1)S(1)}, u32[]{:S(2)}, u32[]{:S(2)}) collective-permute-start(bf16[2,4,1024]{2,1,0:T(4,128)(2,1)S(1)} %shard_map.87), channel_id=1, source_target_pairs={{0,14},{1,15},{2,12},{3,13},{4,10},{5,11},{6,8},{7,9},{8,6},{9,7},... | collective-permute-start | bytes 49160 | tf_op jit(solution)/shard_map/ppermute | solution.py:46
  37.8 0.7 %shard_map.89 = bf16[2,4,1024]{2,1,0:T(4,128)(2,1)S(1)} custom-call(bf16[4,1024]{1,0:T(4,128)(2,1)S(1)} %get-tuple-element.18.context_ref, bf16[1024,8192]{1,0:T(8,128)(2,1)S(1)} %bitcast.1), custom_call_target="tpu_custom_call" | custom-call | flops 11500000 | tf_op jit(solution)/shard_map/pallas_call | solution.py:55
  38.4 1.1 %collective-permute-start.20 = (bf16[2,4,1024]{2,1,0:T(4,128)(2,1)S(1)}, bf16[2,4,1024]{2,1,0:T(4,128)(2,1)S(1)}, u32[]{:S(2)}, u32[]{:S(2)}) collective-permute-start(bf16[2,4,1024]{2,1,0:T(4,128)(2,1)S(1)} %shard_map.89), channel_id=1, source_target_pairs={{0,10},{1,11},{2,8},{3,9},{4,14},{5,15},{6,12},{7,13},{8,2},{9,3},... | collective-permute-start | bytes 49160 | tf_op jit(solution)/shard_map/ppermute | solution.py:46
  39.5 0.7 %shard_map.91 = bf16[2,4,1024]{2,1,0:T(4,128)(2,1)S(1)} custom-call(bf16[4,1024]{1,0:T(4,128)(2,1)S(1)} %get-tuple-element.18.context_ref, bf16[1024,8192]{1,0:T(8,128)(2,1)S(1)} %bitcast.1), custom_call_target="tpu_custom_call" | custom-call | flops 11500000 | tf_op jit(solution)/shard_map/pallas_call | solution.py:55
  40.2 0.2 collective-permute-start.21
  40.4 0.0 collective-permute-done.18.x_ref
  40.4 1.0 %collective-permute-done.19.y_ref = bf16[2,4,1024]{2,1,0:T(4,128)(2,1)S(1)} collective-permute-done((bf16[2,4,1024]{2,1,0:T(4,128)(2,1)S(1)}, bf16[2,4,1024]{2,1,0:T(4,128)(2,1)S(1)}, u32[]{:S(2)}, u32[]{:S(2)}) %collective-permute-start.19) | collective-permute-done | bytes 16416 | tf_op jit(solution)/shard_map/ppermute | solution.py:46
  41.4 0.2 collective-permute-done.20.y_ref
  41.6 0.0 collective-permute-done.21.y_ref
  41.6 0.5 %collective-permute-start.22 = (f32[4,1024]{1,0:T(4,128)S(1)}, f32[4,1024]{1,0:T(4,128)S(1)}, u32[]{:S(2)}, u32[]{:S(2)}) collective-permute-start(f32[4,1024]{1,0:T(4,128)S(1)} %get-tuple-element.19), channel_id=1, source_target_pairs={{0,8},{1,9},{2,10},{3,11},{4,12},{5,13},{6,14},{7,15},{8,0},{9,1},... | collective-permute-start | bytes 49160 | tf_op jit(solution)/shard_map/ppermute | solution.py:46
  42.1 1.2 %collective-permute-start.23 = (bf16[4,1024]{1,0:T(4,128)(2,1)S(1)}, bf16[4,1024]{1,0:T(4,128)(2,1)S(1)}, u32[]{:S(2)}, u32[]{:S(2)}) collective-permute-start(bf16[4,1024]{1,0:T(4,128)(2,1)S(1)} %get-tuple-element.20), channel_id=1, source_target_pairs={{0,9},{1,8},{2,11},{3,10},{4,13},{5,12},{6,15},{7,14},{8,1},{9,0},... | collective-permute-start | bytes 24584 | tf_op jit(solution)/shard_map/ppermute | solution.py:46
  43.4 1.8 %collective-permute-done.23.y_ref = bf16[4,1024]{1,0:T(4,128)(2,1)S(1)} collective-permute-done((bf16[4,1024]{1,0:T(4,128)(2,1)S(1)}, bf16[4,1024]{1,0:T(4,128)(2,1)S(1)}, u32[]{:S(2)}, u32[]{:S(2)}) %collective-permute-start.23) | collective-permute-done | bytes 8224 | tf_op jit(solution)/shard_map/ppermute | solution.py:46
  45.2 0.0 collective-permute-done.22.x_ref
  45.2 0.6 %shard_map.93 = bf16[4,1024]{1,0:T(4,128)(2,1)} custom-call(f32[4,1024]{1,0:T(4,128)S(1)} %collective-permute-done.22.x_ref, bf16[4,1024]{1,0:T(4,128)(2,1)S(1)} %collective-permute-done.23.y_ref), custom_call_target="tpu_custom_call" | custom-call | tf_op jit(solution)/shard_map/pallas_call | solution.py:55
  (26 shorter events, 0.1 us)
Async XLA Ops:
  0.0 0.7 %copy-start.5 = (bf16[4,1024]{1,0:T(4,128)(2,1)S(1)}, bf16[4,1024]{1,0:T(4,128)(2,1)}, u32[]{:S(2)}) copy-start(bf16[4,1024]{1,0:T(4,128)(2,1)} %x_ref.1) | copy-start | bytes 24580
  0.7 8.7 %copy-start = (bf16[8192,1024]{1,0:T(8,128)(2,1)S(1)}, bf16[8192,1024]{1,0:T(8,128)(2,1)}, u32[]{:S(2)}) copy-start(bf16[8192,1024]{1,0:T(8,128)(2,1)} %w_ref.11) | copy-start | bytes 50331652
  0.7 8.7 %copy-start.3 = (s32[4]{0:T(128)S(1)}, s32[4]{0:T(128)}, u32[]{:S(2)}) copy-start(s32[4]{0:T(128)} %clen_ref.1) | copy-start | bytes 52
  0.7 8.7 %copy-start.4 = (s32[4]{0:T(128)S(1)}, s32[4]{0:T(128)}, u32[]{:S(2)}) copy-start(s32[4]{0:T(128)} %nlen_ref.1) | copy-start | bytes 52
  0.7 3.8 %collective-permute-start.1 = (bf16[4,1024]{1,0:T(4,128)(2,1)S(1)}, bf16[4,1024]{1,0:T(4,128)(2,1)S(1)}, u32[]{:S(2)}, u32[]{:S(2)}) collective-permute-start(bf16[4,1024]{1,0:T(4,128)(2,1)S(1)} %shard_map.73), channel_id=1, source_target_pairs={{0,9},{1,8},{2,11},{3,10},{4,13},{5,12},{6,15},{7,14},{8,1},{9,0},... | collective-permute-start | bytes 24584 | tf_op jit(solution)/shard_map/ppermute | solution.py:46
  3.2 1.5 %collective-permute-start = (bf16[4,1024]{1,0:T(4,128)(2,1)S(1)}, bf16[4,1024]{1,0:T(4,128)(2,1)S(1)}, u32[]{:S(2)}, u32[]{:S(2)}) collective-permute-start(bf16[4,1024]{1,0:T(4,128)(2,1)S(1)} %shard_map.73), channel_id=1, source_target_pairs={{0,8},{1,9},{2,10},{3,11},{4,12},{5,13},{6,14},{7,15},{8,0},{9,1},... | collective-permute-start | bytes 24584 | tf_op jit(solution)/shard_map/ppermute | solution.py:46
  4.7 4.7 %collective-permute-start.2 = (bf16[2,4,1024]{2,1,0:T(4,128)(2,1)S(1)}, bf16[2,4,1024]{2,1,0:T(4,128)(2,1)S(1)}, u32[]{:S(2)}, u32[]{:S(2)}) collective-permute-start(bf16[2,4,1024]{2,1,0:T(4,128)(2,1)S(1)} %shard_map.74), channel_id=1, source_target_pairs={{0,8},{1,9},{2,10},{3,11},{4,12},{5,13},{6,14},{7,15},{8,0},{9,1},... | collective-permute-start | bytes 49160 | tf_op jit(solution)/shard_map/ppermute | solution.py:46
  5.2 5.4 %collective-permute-start.5 = (bf16[2,4,1024]{2,1,0:T(4,128)(2,1)S(1)}, bf16[2,4,1024]{2,1,0:T(4,128)(2,1)S(1)}, u32[]{:S(2)}, u32[]{:S(2)}) collective-permute-start(bf16[2,4,1024]{2,1,0:T(4,128)(2,1)S(1)} %shard_map.74), channel_id=1, source_target_pairs={{0,12},{1,13},{2,14},{3,15},{4,8},{5,9},{6,10},{7,11},{8,4},{9,5},... | collective-permute-start | bytes 49160 | tf_op jit(solution)/shard_map/ppermute | solution.py:46
  8.0 5.0 %collective-permute-start.4 = (bf16[2,4,1024]{2,1,0:T(4,128)(2,1)S(1)}, bf16[2,4,1024]{2,1,0:T(4,128)(2,1)S(1)}, u32[]{:S(2)}, u32[]{:S(2)}) collective-permute-start(bf16[2,4,1024]{2,1,0:T(4,128)(2,1)S(1)} %shard_map.74), channel_id=1, source_target_pairs={{0,14},{1,15},{2,12},{3,13},{4,10},{5,11},{6,8},{7,9},{8,6},{9,7},... | collective-permute-start | bytes 49160 | tf_op jit(solution)/shard_map/ppermute | solution.py:46
  9.1 4.5 %collective-permute-start.3 = (bf16[2,4,1024]{2,1,0:T(4,128)(2,1)S(1)}, bf16[2,4,1024]{2,1,0:T(4,128)(2,1)S(1)}, u32[]{:S(2)}, u32[]{:S(2)}) collective-permute-start(bf16[2,4,1024]{2,1,0:T(4,128)(2,1)S(1)} %shard_map.74), channel_id=1, source_target_pairs={{0,10},{1,11},{2,8},{3,9},{4,14},{5,15},{6,12},{7,13},{8,2},{9,3},... | collective-permute-start | bytes 49160 | tf_op jit(solution)/shard_map/ppermute | solution.py:46
  11.2 9.5 %copy-start.1 = (bf16[4,128,2048]{2,1,0:T(8,128)(2,1)S(1)}, bf16[4,128,2048]{2,1,0:T(8,128)(2,1)}, u32[]{:S(2)}) copy-start(bf16[4,128,2048]{2,1,0:T(8,128)(2,1)} %cache_ref.7) | copy-start | bytes 6291460
  11.2 9.5 %copy-start.2 = (bf16[4,64,2048]{2,1,0:T(8,128)(2,1)S(1)}, bf16[4,64,2048]{2,1,0:T(8,128)(2,1)}, u32[]{:S(2)}) copy-start(bf16[4,64,2048]{2,1,0:T(8,128)(2,1)} %fresh_ref.7) | copy-start | bytes 3145732
  13.0 21.1 %slice-start = ((s8[16777216]{0:T(1024)(128)(4,1)}), s8[4194304]{0:T(1024)(128)(4,1)S(1)}, s32[]{:S(2)}) async-start(s8[16777216]{0:T(1024)(128)(4,1)} %bitcast), calls=%async_computation | async-start | bytes 8388608
  13.0 21.1 %slice-start.1 = ((s8[16777216]{0:T(1024)(128)(4,1)}), s8[4194304]{0:T(1024)(128)(4,1)S(1)}, s32[]{:S(2)}) async-start(s8[16777216]{0:T(1024)(128)(4,1)} %bitcast), calls=%async_computation.1 | async-start | bytes 8388608
  13.7 20.4 %slice-start.2 = ((s8[16777216]{0:T(1024)(128)(4,1)}), s8[4194304]{0:T(1024)(128)(4,1)S(1)}, s32[]{:S(2)}) async-start(s8[16777216]{0:T(1024)(128)(4,1)} %bitcast), calls=%async_computation.2 | async-start | bytes 8388608
  14.3 3.1 %collective-permute-start.7 = (bf16[32,128]{1,0:T(8,128)(2,1)S(1)}, bf16[32,128]{1,0:T(8,128)(2,1)S(1)}, u32[]{:S(2)}, u32[]{:S(2)}) collective-permute-start(bf16[32,128]{1,0:T(8,128)(2,1)S(1)} %shard_map.78), channel_id=1, source_target_pairs={{0,9},{1,8},{2,11},{3,10},{4,13},{5,12},{6,15},{7,14},{8,1},{9,0},... | collective-permute-start | bytes 24584 | tf_op jit(solution)/shard_map/ppermute | solution.py:46
  15.7 1.7 %collective-permute-start.6 = (bf16[32,128]{1,0:T(8,128)(2,1)S(1)}, bf16[32,128]{1,0:T(8,128)(2,1)S(1)}, u32[]{:S(2)}, u32[]{:S(2)}) collective-permute-start(bf16[32,128]{1,0:T(8,128)(2,1)S(1)} %shard_map.78), channel_id=1, source_target_pairs={{0,8},{1,9},{2,10},{3,11},{4,12},{5,13},{6,14},{7,15},{8,0},{9,1},... | collective-permute-start | bytes 24584 | tf_op jit(solution)/shard_map/ppermute | solution.py:46
  17.4 3.3 %collective-permute-start.8 = (bf16[2,32,128]{2,1,0:T(8,128)(2,1)S(1)}, bf16[2,32,128]{2,1,0:T(8,128)(2,1)S(1)}, u32[]{:S(2)}, u32[]{:S(2)}) collective-permute-start(bf16[2,32,128]{2,1,0:T(8,128)(2,1)S(1)} %shard_map.79), channel_id=1, source_target_pairs={{0,8},{1,9},{2,10},{3,11},{4,12},{5,13},{6,14},{7,15},{8,0},{9,1},... | collective-permute-start | bytes 49160 | tf_op jit(solution)/shard_map/ppermute | solution.py:46
  17.6 4.2 %collective-permute-start.10 = (bf16[2,32,128]{2,1,0:T(8,128)(2,1)S(1)}, bf16[2,32,128]{2,1,0:T(8,128)(2,1)S(1)}, u32[]{:S(2)}, u32[]{:S(2)}) collective-permute-start(bf16[2,32,128]{2,1,0:T(8,128)(2,1)S(1)} %shard_map.79), channel_id=1, source_target_pairs={{0,12},{1,13},{2,14},{3,15},{4,8},{5,9},{6,10},{7,11},{8,4},{9,5},... | collective-permute-start | bytes 49160 | tf_op jit(solution)/shard_map/ppermute | solution.py:46
  18.6 5.6 %collective-permute-start.12 = (bf16[2,32,128]{2,1,0:T(8,128)(2,1)S(1)}, bf16[2,32,128]{2,1,0:T(8,128)(2,1)S(1)}, u32[]{:S(2)}, u32[]{:S(2)}) collective-permute-start(bf16[2,32,128]{2,1,0:T(8,128)(2,1)S(1)} %shard_map.79), channel_id=1, source_target_pairs={{0,14},{1,15},{2,12},{3,13},{4,10},{5,11},{6,8},{7,9},{8,6},{9,7},... | collective-permute-start | bytes 49160 | tf_op jit(solution)/shard_map/ppermute | solution.py:46
  19.7 6.3 %collective-permute-start.14 = (bf16[2,32,128]{2,1,0:T(8,128)(2,1)S(1)}, bf16[2,32,128]{2,1,0:T(8,128)(2,1)S(1)}, u32[]{:S(2)}, u32[]{:S(2)}) collective-permute-start(bf16[2,32,128]{2,1,0:T(8,128)(2,1)S(1)} %shard_map.79), channel_id=1, source_target_pairs={{0,10},{1,11},{2,8},{3,9},{4,14},{5,15},{6,12},{7,13},{8,2},{9,3},... | collective-permute-start | bytes 49160 | tf_op jit(solution)/shard_map/ppermute | solution.py:46
  20.8 13.3 %slice-start.3 = ((s8[16777216]{0:T(1024)(128)(4,1)}), s8[4194304]{0:T(1024)(128)(4,1)S(1)}, s32[]{:S(2)}) async-start(s8[16777216]{0:T(1024)(128)(4,1)} %bitcast), calls=%async_computation.3 | async-start | bytes 8388608
  21.4 5.5 %collective-permute-start.9 = (bf16[2,40,128]{2,1,0:T(8,128)(2,1)S(1)}, bf16[2,40,128]{2,1,0:T(8,128)(2,1)S(1)}, u32[]{:S(2)}, u32[]{:S(2)}) collective-permute-start(bf16[2,40,128]{2,1,0:T(8,128)(2,1)S(1)} %shard_map.80), channel_id=1, source_target_pairs={{0,8},{1,9},{2,10},{3,11},{4,12},{5,13},{6,14},{7,15},{8,0},{9,1},... | collective-permute-start | bytes 61448 | tf_op jit(solution)/shard_map/ppermute | solution.py:46
  22.5 4.4 %collective-permute-start.11 = (bf16[2,40,128]{2,1,0:T(8,128)(2,1)S(1)}, bf16[2,40,128]{2,1,0:T(8,128)(2,1)S(1)}, u32[]{:S(2)}, u32[]{:S(2)}) collective-permute-start(bf16[2,40,128]{2,1,0:T(8,128)(2,1)S(1)} %shard_map.81), channel_id=1, source_target_pairs={{0,12},{1,13},{2,14},{3,15},{4,8},{5,9},{6,10},{7,11},{8,4},{9,5},... | collective-permute-start | bytes 61448 | tf_op jit(solution)/shard_map/ppermute | solution.py:46
  24.8 5.1 %collective-permute-start.13 = (bf16[2,40,128]{2,1,0:T(8,128)(2,1)S(1)}, bf16[2,40,128]{2,1,0:T(8,128)(2,1)S(1)}, u32[]{:S(2)}, u32[]{:S(2)}) collective-permute-start(bf16[2,40,128]{2,1,0:T(8,128)(2,1)S(1)} %shard_map.82), channel_id=1, source_target_pairs={{0,14},{1,15},{2,12},{3,13},{4,10},{5,11},{6,8},{7,9},{8,6},{9,7},... | collective-permute-start | bytes 61448 | tf_op jit(solution)/shard_map/ppermute | solution.py:46
  26.6 3.8 %collective-permute-start.15 = (bf16[2,40,128]{2,1,0:T(8,128)(2,1)S(1)}, bf16[2,40,128]{2,1,0:T(8,128)(2,1)S(1)}, u32[]{:S(2)}, u32[]{:S(2)}) collective-permute-start(bf16[2,40,128]{2,1,0:T(8,128)(2,1)S(1)} %shard_map.83), channel_id=1, source_target_pairs={{0,10},{1,11},{2,8},{3,9},{4,14},{5,15},{6,12},{7,13},{8,2},{9,3},... | collective-permute-start | bytes 61448 | tf_op jit(solution)/shard_map/ppermute | solution.py:46
  30.4 1.8 %collective-permute-start.16 = (bf16[4,40,128]{2,1,0:T(8,128)(2,1)S(1)}, bf16[4,40,128]{2,1,0:T(8,128)(2,1)S(1)}, u32[]{:S(2)}, u32[]{:S(2)}) collective-permute-start(bf16[4,40,128]{2,1,0:T(8,128)(2,1)S(1)} %get-tuple-element.15), channel_id=1, source_target_pairs={{0,8},{1,9},{2,10},{3,11},{4,12},{5,13},{6,14},{7,15},{8,0},{9,1},... | collective-permute-start | bytes 122888 | tf_op jit(solution)/shard_map/ppermute | solution.py:46
  30.6 3.5 %collective-permute-start.17 = (bf16[4,40,128]{2,1,0:T(8,128)(2,1)S(1)}, bf16[4,40,128]{2,1,0:T(8,128)(2,1)S(1)}, u32[]{:S(2)}, u32[]{:S(2)}) collective-permute-start(bf16[4,40,128]{2,1,0:T(8,128)(2,1)S(1)} %get-tuple-element.16), channel_id=1, source_target_pairs={{0,9},{1,8},{2,11},{3,10},{4,13},{5,12},{6,15},{7,14},{8,1},{9,0},... | collective-permute-start | bytes 122888 | tf_op jit(solution)/shard_map/ppermute | solution.py:46
  35.0 5.4 %collective-permute-start.18 = (bf16[2,4,1024]{2,1,0:T(4,128)(2,1)S(1)}, bf16[2,4,1024]{2,1,0:T(4,128)(2,1)S(1)}, u32[]{:S(2)}, u32[]{:S(2)}) collective-permute-start(bf16[2,4,1024]{2,1,0:T(4,128)(2,1)S(1)} %get-tuple-element.17), channel_id=1, source_target_pairs={{0,12},{1,13},{2,14},{3,15},{4,8},{5,9},{6,10},{7,11},{8,4},{9,5},... | collective-permute-start | bytes 49160 | tf_op jit(solution)/shard_map/ppermute | solution.py:46
  36.4 5.0 %collective-permute-start.19 = (bf16[2,4,1024]{2,1,0:T(4,128)(2,1)S(1)}, bf16[2,4,1024]{2,1,0:T(4,128)(2,1)S(1)}, u32[]{:S(2)}, u32[]{:S(2)}) collective-permute-start(bf16[2,4,1024]{2,1,0:T(4,128)(2,1)S(1)} %shard_map.87), channel_id=1, source_target_pairs={{0,14},{1,15},{2,12},{3,13},{4,10},{5,11},{6,8},{7,9},{8,6},{9,7},... | collective-permute-start | bytes 49160 | tf_op jit(solution)/shard_map/ppermute | solution.py:46
  38.4 3.2 %collective-permute-start.20 = (bf16[2,4,1024]{2,1,0:T(4,128)(2,1)S(1)}, bf16[2,4,1024]{2,1,0:T(4,128)(2,1)S(1)}, u32[]{:S(2)}, u32[]{:S(2)}) collective-permute-start(bf16[2,4,1024]{2,1,0:T(4,128)(2,1)S(1)} %shard_map.89), channel_id=1, source_target_pairs={{0,10},{1,11},{2,8},{3,9},{4,14},{5,15},{6,12},{7,13},{8,2},{9,3},... | collective-permute-start | bytes 49160 | tf_op jit(solution)/shard_map/ppermute | solution.py:46
  40.2 1.4 %collective-permute-start.21 = (bf16[2,4,1024]{2,1,0:T(4,128)(2,1)S(1)}, bf16[2,4,1024]{2,1,0:T(4,128)(2,1)S(1)}, u32[]{:S(2)}, u32[]{:S(2)}) collective-permute-start(bf16[2,4,1024]{2,1,0:T(4,128)(2,1)S(1)} %shard_map.91), channel_id=1, source_target_pairs={{0,8},{1,9},{2,10},{3,11},{4,12},{5,13},{6,14},{7,15},{8,0},{9,1},... | collective-permute-start | bytes 49160 | tf_op jit(solution)/shard_map/ppermute | solution.py:46
  41.6 3.6 %collective-permute-start.22 = (f32[4,1024]{1,0:T(4,128)S(1)}, f32[4,1024]{1,0:T(4,128)S(1)}, u32[]{:S(2)}, u32[]{:S(2)}) collective-permute-start(f32[4,1024]{1,0:T(4,128)S(1)} %get-tuple-element.19), channel_id=1, source_target_pairs={{0,8},{1,9},{2,10},{3,11},{4,12},{5,13},{6,14},{7,15},{8,0},{9,1},... | collective-permute-start | bytes 49160 | tf_op jit(solution)/shard_map/ppermute | solution.py:46
  42.1 3.1 %collective-permute-start.23 = (bf16[4,1024]{1,0:T(4,128)(2,1)S(1)}, bf16[4,1024]{1,0:T(4,128)(2,1)S(1)}, u32[]{:S(2)}, u32[]{:S(2)}) collective-permute-start(bf16[4,1024]{1,0:T(4,128)(2,1)S(1)} %get-tuple-element.20), channel_id=1, source_target_pairs={{0,9},{1,8},{2,11},{3,10},{4,13},{5,12},{6,15},{7,14},{8,1},{9,0},... | collective-permute-start | bytes 24584 | tf_op jit(solution)/shard_map/ppermute | solution.py:46

commit v11 on v10

--- a/solution.py
+++ b/solution.py
@@ -20,6 +20,7 @@
 SPLIT_OUTPUT = False
 ORDER = (4, 6, 2)
 MIDDLE = (4, 6, 2)
+LIMIT = 10**7
 BACK = (4, 6, 2)
 ADD = 23000000
 PIECE = 11500000
@@ -71,7 +72,7 @@
     o_ref[...] = x_ref[...]
 
 
-def stack_kernel(x_ref, y_ref, o_ref):
+def stack_kernel(x_ref, y_ref, _, o_ref):
     o_ref[0] = x_ref[...]
     o_ref[1] = y_ref[...]
 
@@ -103,8 +104,7 @@
     return acc
 
 
-def first_kernel(cc, fc, clen_ref, nlen_ref, x_ref, w_ref, acc_ref, limit_ref):
-    limit_kernel(cc, fc, clen_ref, nlen_ref, limit_ref)
+def first_kernel(x_ref, w_ref, acc_ref):
     acc_ref[...] = pair_product(0, x_ref, w_ref)
 
 
@@ -426,18 +426,17 @@
     if n == 8:
         mine = call(copy_kernel, (rows, feat), BF16, hidden, flops=LONG)
         near = flip(mine, 1)
-        pair = call(stack_kernel, (2, rows, feat), BF16, flip(mine, 0), near)
-        acc, limits = call(
-            functools.partial(first_kernel, cache.shape[1], fresh.shape[1]),
-            [(rows, own * HD), (2, rows * 2 * GROUP)],
-            [F32, jnp.int32],
+        limits = call(
+            functools.partial(limit_kernel, cache.shape[1], fresh.shape[1]),
+            (2, rows * 2 * GROUP),
+            jnp.int32,
             cache_lengths,
             new_lengths,
-            flip(pair, 0),
-            w_query,
-            specs=[SMEM] * 2 + [VMEM] * 2,
-            flops=FIRST,
-        )
+            specs=[SMEM] * 2,
+            flops=LIMIT,
+        )
+        pair = call(stack_kernel, (2, rows, feat), BF16, flip(mine, 0), near, limits)
+        acc = call(first_kernel, (rows, own * HD), F32, flip(pair, 0), w_query, flops=FIRST)
         got = [flip(pair, apart) for apart in ORDER]
         for apart, x in zip(ORDER[:2], got):
             step = functools.partial(next_kernel, apart)
@@ -464,7 +463,7 @@
                 flops=PIECE,
             )
 
-        parts = [flip(attend(apart), apart) for apart in (0,) + MIDDLE]
+        parts = [flip(attend(apart), apart) for apart in MIDDLE + (0,)]
         shape = (4, rows * GROUP + STATS, HD)
         mine, far = call(part_kernel, [shape] * 2, [BF16, BF16], *parts, flops=ADD)
         parts = flip(mine, 0), flip(far, 1)

time: 46 us -> 45.7 us (level)
  waiting for transfers between devices: 12.7 us -> 11.9 us
    ppermute x24, waiting for transfers between devices: 12.7 us -> 11.9 us  [flip(): lax.ppermute(x, BOTH, [(i, (i // n ^ 1) * n + (i % n ^ apart)) for i in r...]
    pallas_call x21 -> x22, Pallas kernels: 9.15 us -> 9.15 us  [call(): pl.pallas_call(kernel, in_specs=specs or [VMEM] * len(args), out_specs=ou...]
  transfers between devices with their start and end apart: 24 -> 24, of which waited for: 11 -> 12; matrix products, arithmetic and copies ran while one was open for 0% -> 0% of each run, Pallas kernels for 15% -> 15%
where the time goes in v11:
time: 45.7 us; the launch traced here: 45.5 us
  starting transfers between devices  23.6 us (52%)
  waiting for transfers between devices  11.9 us (26%)
  Pallas kernels  9.15 us (20%)
  local copies, waits for them, and re-layouts  0.73 us (2%)
    ppermute x24, starting transfers between devices, flip(): lax.ppermute(x, BOTH, [(i, (i // n ^ 1) * n + (i % n ^ apart)) for i in r...  23.6 us
    ppermute x24, waiting for transfers between devices, flip(): lax.ppermute(x, BOTH, [(i, (i // n ^ 1) * n + (i % n ^ apart)) for i in r...  11.9 us
    pallas_call x22, Pallas kernels, call(): pl.pallas_call(kernel, in_specs=specs or [VMEM] * len(args), out_specs=ou...  9.15 us
  transfers between devices with their start and end apart: 24, of which 12 were waited for; matrix products, arithmetic and copies ran while one was open for 0% of the time, Pallas kernels for 15%

profile of v11, /device:TPU:0, one launch (start us, length us, event | category | flops | bytes accessed | tf_op | source)
XLA Modules:
  0.0 45.5 jit_solution(4729740731402322446)
XLA Ops:
  0.0 0.7 %copy-done.3 = bf16[4,1024]{1,0:T(4,128)(2,1)S(1)} copy-done((bf16[4,1024]{1,0:T(4,128)(2,1)S(1)}, bf16[4,1024]{1,0:T(4,128)(2,1)}, u32[]{:S(2)}) %copy-start.3) | copy-done | bytes 8216
  0.7 2.5 %collective-permute-start.1 = (bf16[4,1024]{1,0:T(4,128)(2,1)S(1)}, bf16[4,1024]{1,0:T(4,128)(2,1)S(1)}, u32[]{:S(2)}, u32[]{:S(2)}) collective-permute-start(bf16[4,1024]{1,0:T(4,128)(2,1)S(1)} %shard_map.74), channel_id=1, source_target_pairs={{0,9},{1,8},{2,11},{3,10},{4,13},{5,12},{6,15},{7,14},{8,1},{9,0},... | collective-permute-start | bytes 24584 | tf_op jit(solution)/shard_map/ppermute | solution.py:47
  3.2 0.7 %collective-permute-start = (bf16[4,1024]{1,0:T(4,128)(2,1)S(1)}, bf16[4,1024]{1,0:T(4,128)(2,1)S(1)}, u32[]{:S(2)}, u32[]{:S(2)}) collective-permute-start(bf16[4,1024]{1,0:T(4,128)(2,1)S(1)} %shard_map.74), channel_id=1, source_target_pairs={{0,8},{1,9},{2,10},{3,11},{4,12},{5,13},{6,14},{7,15},{8,0},{9,1},... | collective-permute-start | bytes 24584 | tf_op jit(solution)/shard_map/ppermute | solution.py:47
  3.9 0.0 copy-done.5
  3.9 0.6 %shard_map.73._.limit_ref = s32[2,64]{1,0:T(2,128)S(1)} custom-call(s32[4]{0:T(128)S(1)} %copy-done.4, s32[4]{0:T(128)S(1)} %copy-done.5), custom_call_target="tpu_custom_call" | custom-call | flops 10000000 | tf_op jit(solution)/shard_map/pallas_call | solution.py:56
  4.4 0.1 collective-permute-done.1.y_ref
  4.5 0.1 collective-permute-done.x_ref
  4.7 0.5 %collective-permute-start.5 = (bf16[2,4,1024]{2,1,0:T(4,128)(2,1)S(1)}, bf16[2,4,1024]{2,1,0:T(4,128)(2,1)S(1)}, u32[]{:S(2)}, u32[]{:S(2)}) collective-permute-start(bf16[2,4,1024]{2,1,0:T(4,128)(2,1)S(1)} %shard_map.75), channel_id=1, source_target_pairs={{0,8},{1,9},{2,10},{3,11},{4,12},{5,13},{6,14},{7,15},{8,0},{9,1},... | collective-permute-start | bytes 49160 | tf_op jit(solution)/shard_map/ppermute | solution.py:47
  5.2 2.8 %collective-permute-start.4 = (bf16[2,4,1024]{2,1,0:T(4,128)(2,1)S(1)}, bf16[2,4,1024]{2,1,0:T(4,128)(2,1)S(1)}, u32[]{:S(2)}, u32[]{:S(2)}) collective-permute-start(bf16[2,4,1024]{2,1,0:T(4,128)(2,1)S(1)} %shard_map.75), channel_id=1, source_target_pairs={{0,12},{1,13},{2,14},{3,15},{4,8},{5,9},{6,10},{7,11},{8,4},{9,5},... | collective-permute-start | bytes 49160 | tf_op jit(solution)/shard_map/ppermute | solution.py:47
  8.0 1.1 %collective-permute-start.3 = (bf16[2,4,1024]{2,1,0:T(4,128)(2,1)S(1)}, bf16[2,4,1024]{2,1,0:T(4,128)(2,1)S(1)}, u32[]{:S(2)}, u32[]{:S(2)}) collective-permute-start(bf16[2,4,1024]{2,1,0:T(4,128)(2,1)S(1)} %shard_map.75), channel_id=1, source_target_pairs={{0,14},{1,15},{2,12},{3,13},{4,10},{5,11},{6,8},{7,9},{8,6},{9,7},... | collective-permute-start | bytes 49160 | tf_op jit(solution)/shard_map/ppermute | solution.py:47
  9.1 0.2 collective-permute-start.2
  9.4 0.0 collective-permute-done.5.x_ref
  9.4 0.7 %shard_map.76.old_ref = f32[4,1024]{1,0:T(4,128)S(1)} custom-call(bf16[2,4,1024]{2,1,0:T(4,128)(2,1)S(1)} %collective-permute-done.5.x_ref, bf16[8192,1024]{1,0:T(8,128)(2,1)S(1)} %copy-done), custom_call_target="tpu_custom_call" | custom-call | tf_op jit(solution)/shard_map/pallas_call | solution.py:56
  10.0 0.0 collective-permute-done.4.x_ref
  10.0 0.7 %shard_map.77.old_ref = f32[4,1024]{1,0:T(4,128)S(1)} custom-call(bf16[2,4,1024]{2,1,0:T(4,128)(2,1)S(1)} %collective-permute-done.4.x_ref, bf16[8192,1024]{1,0:T(8,128)(2,1)S(1)} %copy-done, f32[4,1024]{1,0:T(4,128)S(1)} %shard_map.76.old_ref), custom_call_target="tpu_custom_call" | custom-call | flops 10000000000 | tf_op jit(solution)/shard_map/pallas_call | solution.py:56
  10.7 2.3 %collective-permute-done.3.x_ref = bf16[2,4,1024]{2,1,0:T(4,128)(2,1)S(1)} collective-permute-done((bf16[2,4,1024]{2,1,0:T(4,128)(2,1)S(1)}, bf16[2,4,1024]{2,1,0:T(4,128)(2,1)S(1)}, u32[]{:S(2)}, u32[]{:S(2)}) %collective-permute-start.3) | collective-permute-done | bytes 16416 | tf_op jit(solution)/shard_map/ppermute | solution.py:47
  13.0 0.7 %shard_map.78.old_ref = f32[4,1024]{1,0:T(4,128)S(1)} custom-call(bf16[2,4,1024]{2,1,0:T(4,128)(2,1)S(1)} %collective-permute-done.3.x_ref, bf16[8192,1024]{1,0:T(8,128)(2,1)S(1)} %copy-done, f32[4,1024]{1,0:T(4,128)S(1)} %shard_map.77.old_ref), custom_call_target="tpu_custom_call" | custom-call | tf_op jit(solution)/shard_map/pallas_call | solution.py:56
  13.7 0.0 collective-permute-done.2.x_ref
  13.7 0.7 %shard_map.79 = bf16[32,128]{1,0:T(8,128)(2,1)S(1)} custom-call(bf16[2,4,1024]{2,1,0:T(4,128)(2,1)S(1)} %collective-permute-done.2.x_ref, bf16[8192,1024]{1,0:T(8,128)(2,1)S(1)} %copy-done, f32[4,1024]{1,0:T(4,128)S(1)} %shard_map.78.old_ref), custom_call_target="tpu_custom_call" | custom-call | tf_op jit(solution)/shard_map/pallas_call | solution.py:56
  14.3 1.4 %collective-permute-start.7 = (bf16[32,128]{1,0:T(8,128)(2,1)S(1)}, bf16[32,128]{1,0:T(8,128)(2,1)S(1)}, u32[]{:S(2)}, u32[]{:S(2)}) collective-permute-start(bf16[32,128]{1,0:T(8,128)(2,1)S(1)} %shard_map.79), channel_id=1, source_target_pairs={{0,9},{1,8},{2,11},{3,10},{4,13},{5,12},{6,15},{7,14},{8,1},{9,0},... | collective-permute-start | bytes 24584 | tf_op jit(solution)/shard_map/ppermute | solution.py:47
  15.7 0.3 collective-permute-start.6
  16.1 1.4 %collective-permute-done.7.y_ref = bf16[32,128]{1,0:T(8,128)(2,1)S(1)} collective-permute-done((bf16[32,128]{1,0:T(8,128)(2,1)S(1)}, bf16[32,128]{1,0:T(8,128)(2,1)S(1)}, u32[]{:S(2)}, u32[]{:S(2)}) %collective-permute-start.7) | collective-permute-done | bytes 8224 | tf_op jit(solution)/shard_map/ppermute | solution.py:47
  17.4 0.0 collective-permute-done.6.x_ref
  17.4 0.3 collective-permute-start.8
  17.8 1.6 %collective-permute-start.10 = (bf16[2,32,128]{2,1,0:T(8,128)(2,1)S(1)}, bf16[2,32,128]{2,1,0:T(8,128)(2,1)S(1)}, u32[]{:S(2)}, u32[]{:S(2)}) collective-permute-start(bf16[2,32,128]{2,1,0:T(8,128)(2,1)S(1)} %shard_map.80), channel_id=1, source_target_pairs={{0,14},{1,15},{2,12},{3,13},{4,10},{5,11},{6,8},{7,9},{8,6},{9,7},... | collective-permute-start | bytes 49160 | tf_op jit(solution)/shard_map/ppermute | solution.py:47
  19.4 1.2 %collective-permute-start.12 = (bf16[2,32,128]{2,1,0:T(8,128)(2,1)S(1)}, bf16[2,32,128]{2,1,0:T(8,128)(2,1)S(1)}, u32[]{:S(2)}, u32[]{:S(2)}) collective-permute-start(bf16[2,32,128]{2,1,0:T(8,128)(2,1)S(1)} %shard_map.80), channel_id=1, source_target_pairs={{0,10},{1,11},{2,8},{3,9},{4,14},{5,15},{6,12},{7,13},{8,2},{9,3},... | collective-permute-start | bytes 49160 | tf_op jit(solution)/shard_map/ppermute | solution.py:47
  20.5 0.3 collective-permute-start.14
  20.8 0.7 %collective-permute-done.8.q_ref = bf16[2,32,128]{2,1,0:T(8,128)(2,1)S(1)} collective-permute-done((bf16[2,32,128]{2,1,0:T(8,128)(2,1)S(1)}, bf16[2,32,128]{2,1,0:T(8,128)(2,1)S(1)}, u32[]{:S(2)}, u32[]{:S(2)}) %collective-permute-start.8) | collective-permute-done | bytes 16416 | tf_op jit(solution)/shard_map/ppermute | solution.py:47
  21.6 0.6 %shard_map.81 = bf16[2,40,128]{2,1,0:T(8,128)(2,1)S(1)} custom-call(s32[2,64]{1,0:T(2,128)S(1)} %shard_map.73._.limit_ref, bf16[2,32,128]{2,1,0:T(8,128)(2,1)S(1)} %collective-permute-done.8.q_ref, bf16[4,128,2048]{2,1,0:T(8,128)(2,1)S(1)} %copy-done.1, bf16[4,64,2048]{2,1,0:T(8,128)(2,1)S(1)} %copy-done.2), custom_call_target="tpu_custom_call" | custom-call | flops 11500000 | tf_op jit(solution)/shard_map/pallas_call | solution.py:56
  22.2 0.5 %collective-permute-start.9 = (bf16[2,40,128]{2,1,0:T(8,128)(2,1)S(1)}, bf16[2,40,128]{2,1,0:T(8,128)(2,1)S(1)}, u32[]{:S(2)}, u32[]{:S(2)}) collective-permute-start(bf16[2,40,128]{2,1,0:T(8,128)(2,1)S(1)} %shard_map.81), channel_id=1, source_target_pairs={{0,12},{1,13},{2,14},{3,15},{4,8},{5,9},{6,10},{7,11},{8,4},{9,5},... | collective-permute-start | bytes 61448 | tf_op jit(solution)/shard_map/ppermute | solution.py:47
  22.7 0.1 collective-permute-done.10.q_ref
  22.7 0.6 %shard_map.82 = bf16[2,40,128]{2,1,0:T(8,128)(2,1)S(1)} custom-call(s32[2,64]{1,0:T(2,128)S(1)} %shard_map.73._.limit_ref, bf16[2,32,128]{2,1,0:T(8,128)(2,1)S(1)} %collective-permute-done.10.q_ref, bf16[4,128,2048]{2,1,0:T(8,128)(2,1)S(1)} %copy-done.1, bf16[4,64,2048]{2,1,0:T(8,128)(2,1)S(1)} %copy-done.2), custom_call_target="tpu_custom_call" | custom-call | flops 11500000 | tf_op jit(solution)/shard_map/pallas_call | solution.py:56
  23.4 1.7 %collective-permute-start.11 = (bf16[2,40,128]{2,1,0:T(8,128)(2,1)S(1)}, bf16[2,40,128]{2,1,0:T(8,128)(2,1)S(1)}, u32[]{:S(2)}, u32[]{:S(2)}) collective-permute-start(bf16[2,40,128]{2,1,0:T(8,128)(2,1)S(1)} %shard_map.82), channel_id=1, source_target_pairs={{0,14},{1,15},{2,12},{3,13},{4,10},{5,11},{6,8},{7,9},{8,6},{9,7},... | collective-permute-start | bytes 61448 | tf_op jit(solution)/shard_map/ppermute | solution.py:47
  25.0 0.0 collective-permute-done.12.q_ref
  25.0 0.6 %shard_map.83 = bf16[2,40,128]{2,1,0:T(8,128)(2,1)S(1)} custom-call(s32[2,64]{1,0:T(2,128)S(1)} %shard_map.73._.limit_ref, bf16[2,32,128]{2,1,0:T(8,128)(2,1)S(1)} %collective-permute-done.12.q_ref, bf16[4,128,2048]{2,1,0:T(8,128)(2,1)S(1)} %copy-done.1, bf16[4,64,2048]{2,1,0:T(8,128)(2,1)S(1)} %copy-done.2), custom_call_target="tpu_custom_call" | custom-call | flops 11500000 | tf_op jit(solution)/shard_map/pallas_call | solution.py:56
  25.6 1.2 %collective-permute-start.13 = (bf16[2,40,128]{2,1,0:T(8,128)(2,1)S(1)}, bf16[2,40,128]{2,1,0:T(8,128)(2,1)S(1)}, u32[]{:S(2)}, u32[]{:S(2)}) collective-permute-start(bf16[2,40,128]{2,1,0:T(8,128)(2,1)S(1)} %shard_map.83), channel_id=1, source_target_pairs={{0,10},{1,11},{2,8},{3,9},{4,14},{5,15},{6,12},{7,13},{8,2},{9,3},... | collective-permute-start | bytes 61448 | tf_op jit(solution)/shard_map/ppermute | solution.py:47
  26.8 0.0 collective-permute-done.14.q_ref
  26.8 0.6 %shard_map.84 = bf16[2,40,128]{2,1,0:T(8,128)(2,1)S(1)} custom-call(s32[2,64]{1,0:T(2,128)S(1)} %shard_map.73._.limit_ref, bf16[2,32,128]{2,1,0:T(8,128)(2,1)S(1)} %collective-permute-done.14.q_ref, bf16[4,128,2048]{2,1,0:T(8,128)(2,1)S(1)} %copy-done.1, bf16[4,64,2048]{2,1,0:T(8,128)(2,1)S(1)} %copy-done.2), custom_call_target="tpu_custom_call" | custom-call | flops 11500000 | tf_op jit(solution)/shard_map/pallas_call | solution.py:56
  27.4 0.2 collective-permute-start.15
  27.6 0.0 collective-permute-done.9.a_ref
  27.6 0.8 %collective-permute-done.11.b_ref = bf16[2,40,128]{2,1,0:T(8,128)(2,1)S(1)} collective-permute-done((bf16[2,40,128]{2,1,0:T(8,128)(2,1)S(1)}, bf16[2,40,128]{2,1,0:T(8,128)(2,1)S(1)}, u32[]{:S(2)}, u32[]{:S(2)}) %collective-permute-start.11) | collective-permute-done | bytes 20512 | tf_op jit(solution)/shard_map/ppermute | solution.py:47
  28.4 0.5 %collective-permute-done.13.c_ref = bf16[2,40,128]{2,1,0:T(8,128)(2,1)S(1)} collective-permute-done((bf16[2,40,128]{2,1,0:T(8,128)(2,1)S(1)}, bf16[2,40,128]{2,1,0:T(8,128)(2,1)S(1)}, u32[]{:S(2)}, u32[]{:S(2)}) %collective-permute-start.13) | collective-permute-done | bytes 20512 | tf_op jit(solution)/shard_map/ppermute | solution.py:47
  28.9 0.0 collective-permute-done.15.d_ref
  28.9 0.3 collective-permute-start.16
  29.2 1.4 %collective-permute-start.17 = (bf16[4,40,128]{2,1,0:T(8,128)(2,1)S(1)}, bf16[4,40,128]{2,1,0:T(8,128)(2,1)S(1)}, u32[]{:S(2)}, u32[]{:S(2)}) collective-permute-start(bf16[4,40,128]{2,1,0:T(8,128)(2,1)S(1)} %get-tuple-element.12), channel_id=1, source_target_pairs={{0,9},{1,8},{2,11},{3,10},{4,13},{5,12},{6,15},{7,14},{8,1},{9,0},... | collective-permute-start | bytes 122888 | tf_op jit(solution)/shard_map/ppermute | solution.py:47
  30.7 0.0 collective-permute-done.16.a_ref
  30.7 2.0 %collective-permute-done.17.b_ref = bf16[4,40,128]{2,1,0:T(8,128)(2,1)S(1)} collective-permute-done((bf16[4,40,128]{2,1,0:T(8,128)(2,1)S(1)}, bf16[4,40,128]{2,1,0:T(8,128)(2,1)S(1)}, u32[]{:S(2)}, u32[]{:S(2)}) %collective-permute-start.17) | collective-permute-done | bytes 40992 | tf_op jit(solution)/shard_map/ppermute | solution.py:47
  32.7 0.9 %shard_map.86 = (bf16[2,4,1024]{2,1,0:T(4,128)(2,1)S(1)}, bf16[4,1024]{1,0:T(4,128)(2,1)S(1)}) custom-call(bf16[4,40,128]{2,1,0:T(8,128)(2,1)S(1)} %collective-permute-done.16.a_ref, bf16[4,40,128]{2,1,0:T(8,128)(2,1)S(1)} %collective-permute-done.17.b_ref, bf16[1024,8192]{1,0:T(8,128)(2,1)S(1)} %bitcast.1), custom_call_target="tpu_custom_call" | custom-call | flops 11500000 | tf_op jit(solution)/shard_map/pallas_call | solution.py:56
  33.6 1.2 %collective-permute-start.18 = (bf16[2,4,1024]{2,1,0:T(4,128)(2,1)S(1)}, bf16[2,4,1024]{2,1,0:T(4,128)(2,1)S(1)}, u32[]{:S(2)}, u32[]{:S(2)}) collective-permute-start(bf16[2,4,1024]{2,1,0:T(4,128)(2,1)S(1)} %get-tuple-element.13), channel_id=1, source_target_pairs={{0,12},{1,13},{2,14},{3,15},{4,8},{5,9},{6,10},{7,11},{8,4},{9,5},... | collective-permute-start | bytes 49160 | tf_op jit(solution)/shard_map/ppermute | solution.py:47
  34.8 0.7 %shard_map.88 = bf16[2,4,1024]{2,1,0:T(4,128)(2,1)S(1)} custom-call(bf16[4,1024]{1,0:T(4,128)(2,1)S(1)} %get-tuple-element.14.context_ref, bf16[1024,8192]{1,0:T(8,128)(2,1)S(1)} %bitcast.1), custom_call_target="tpu_custom_call" | custom-call | flops 11500000 | tf_op jit(solution)/shard_map/pallas_call | solution.py:56
  35.5 2.2 %collective-permute-start.19 = (bf16[2,4,1024]{2,1,0:T(4,128)(2,1)S(1)}, bf16[2,4,1024]{2,1,0:T(4,128)(2,1)S(1)}, u32[]{:S(2)}, u32[]{:S(2)}) collective-permute-start(bf16[2,4,1024]{2,1,0:T(4,128)(2,1)S(1)} %shard_map.88), channel_id=1, source_target_pairs={{0,14},{1,15},{2,12},{3,13},{4,10},{5,11},{6,8},{7,9},{8,6},{9,7},... | collective-permute-start | bytes 49160 | tf_op jit(solution)/shard_map/ppermute | solution.py:47
  37.7 0.7 %shard_map.90 = bf16[2,4,1024]{2,1,0:T(4,128)(2,1)S(1)} custom-call(bf16[4,1024]{1,0:T(4,128)(2,1)S(1)} %get-tuple-element.14.context_ref, bf16[1024,8192]{1,0:T(8,128)(2,1)S(1)} %bitcast.1), custom_call_target="tpu_custom_call" | custom-call | flops 11500000 | tf_op jit(solution)/shard_map/pallas_call | solution.py:56
  38.4 0.0 collective-permute-start.20
  38.4 0.7 %shard_map.92 = bf16[2,4,1024]{2,1,0:T(4,128)(2,1)S(1)} custom-call(bf16[4,1024]{1,0:T(4,128)(2,1)S(1)} %get-tuple-element.14.context_ref, bf16[1024,8192]{1,0:T(8,128)(2,1)S(1)} %bitcast.1), custom_call_target="tpu_custom_call" | custom-call | flops 11500000 | tf_op jit(solution)/shard_map/pallas_call | solution.py:56
  39.0 0.2 collective-permute-start.21
  39.2 0.0 collective-permute-done.18.x_ref
  39.2 1.3 %collective-permute-done.19.y_ref = bf16[2,4,1024]{2,1,0:T(4,128)(2,1)S(1)} collective-permute-done((bf16[2,4,1024]{2,1,0:T(4,128)(2,1)S(1)}, bf16[2,4,1024]{2,1,0:T(4,128)(2,1)S(1)}, u32[]{:S(2)}, u32[]{:S(2)}) %collective-permute-start.19) | collective-permute-done | bytes 16416 | tf_op jit(solution)/shard_map/ppermute | solution.py:47
  40.5 1.0 %collective-permute-done.20.y_ref = bf16[2,4,1024]{2,1,0:T(4,128)(2,1)S(1)} collective-permute-done((bf16[2,4,1024]{2,1,0:T(4,128)(2,1)S(1)}, bf16[2,4,1024]{2,1,0:T(4,128)(2,1)S(1)}, u32[]{:S(2)}, u32[]{:S(2)}) %collective-permute-start.20) | collective-permute-done | bytes 16416 | tf_op jit(solution)/shard_map/ppermute | solution.py:47
  41.5 0.0 collective-permute-done.21.y_ref
  41.6 0.2 collective-permute-start.22
  41.8 1.5 %collective-permute-start.23 = (bf16[4,1024]{1,0:T(4,128)(2,1)S(1)}, bf16[4,1024]{1,0:T(4,128)(2,1)S(1)}, u32[]{:S(2)}, u32[]{:S(2)}) collective-permute-start(bf16[4,1024]{1,0:T(4,128)(2,1)S(1)} %get-tuple-element.16), channel_id=1, source_target_pairs={{0,9},{1,8},{2,11},{3,10},{4,13},{5,12},{6,15},{7,14},{8,1},{9,0},... | collective-permute-start | bytes 24584 | tf_op jit(solution)/shard_map/ppermute | solution.py:47
  43.3 1.5 %collective-permute-done.23.y_ref = bf16[4,1024]{1,0:T(4,128)(2,1)S(1)} collective-permute-done((bf16[4,1024]{1,0:T(4,128)(2,1)S(1)}, bf16[4,1024]{1,0:T(4,128)(2,1)S(1)}, u32[]{:S(2)}, u32[]{:S(2)}) %collective-permute-start.23) | collective-permute-done | bytes 8224 | tf_op jit(solution)/shard_map/ppermute | solution.py:47
  44.9 0.0 collective-permute-done.22.x_ref
  44.9 0.6 %shard_map.94 = bf16[4,1024]{1,0:T(4,128)(2,1)} custom-call(f32[4,1024]{1,0:T(4,128)S(1)} %collective-permute-done.22.x_ref, bf16[4,1024]{1,0:T(4,128)(2,1)S(1)} %collective-permute-done.23.y_ref), custom_call_target="tpu_custom_call" | custom-call | tf_op jit(solution)/shard_map/pallas_call | solution.py:56
  (27 shorter events, 0.1 us)
Async XLA Ops:
  0.0 0.7 %copy-start.3 = (bf16[4,1024]{1,0:T(4,128)(2,1)S(1)}, bf16[4,1024]{1,0:T(4,128)(2,1)}, u32[]{:S(2)}) copy-start(bf16[4,1024]{1,0:T(4,128)(2,1)} %x_ref.1) | copy-start | bytes 24580
  0.7 3.2 %copy-start.4 = (s32[4]{0:T(128)S(1)}, s32[4]{0:T(128)}, u32[]{:S(2)}) copy-start(s32[4]{0:T(128)} %clen_ref.1) | copy-start | bytes 52
  0.7 3.2 %copy-start.5 = (s32[4]{0:T(128)S(1)}, s32[4]{0:T(128)}, u32[]{:S(2)}) copy-start(s32[4]{0:T(128)} %nlen_ref.1) | copy-start | bytes 52
  0.7 8.7 %copy-start = (bf16[8192,1024]{1,0:T(8,128)(2,1)S(1)}, bf16[8192,1024]{1,0:T(8,128)(2,1)}, u32[]{:S(2)}) copy-start(bf16[8192,1024]{1,0:T(8,128)(2,1)} %w_ref.11) | copy-start | bytes 50331652
  0.7 3.8 %collective-permute-start.1 = (bf16[4,1024]{1,0:T(4,128)(2,1)S(1)}, bf16[4,1024]{1,0:T(4,128)(2,1)S(1)}, u32[]{:S(2)}, u32[]{:S(2)}) collective-permute-start(bf16[4,1024]{1,0:T(4,128)(2,1)S(1)} %shard_map.74), channel_id=1, source_target_pairs={{0,9},{1,8},{2,11},{3,10},{4,13},{5,12},{6,15},{7,14},{8,1},{9,0},... | collective-permute-start | bytes 24584 | tf_op jit(solution)/shard_map/ppermute | solution.py:47
  3.2 1.5 %collective-permute-start = (bf16[4,1024]{1,0:T(4,128)(2,1)S(1)}, bf16[4,1024]{1,0:T(4,128)(2,1)S(1)}, u32[]{:S(2)}, u32[]{:S(2)}) collective-permute-start(bf16[4,1024]{1,0:T(4,128)(2,1)S(1)} %shard_map.74), channel_id=1, source_target_pairs={{0,8},{1,9},{2,10},{3,11},{4,12},{5,13},{6,14},{7,15},{8,0},{9,1},... | collective-permute-start | bytes 24584 | tf_op jit(solution)/shard_map/ppermute | solution.py:47
  4.7 4.7 %collective-permute-start.5 = (bf16[2,4,1024]{2,1,0:T(4,128)(2,1)S(1)}, bf16[2,4,1024]{2,1,0:T(4,128)(2,1)S(1)}, u32[]{:S(2)}, u32[]{:S(2)}) collective-permute-start(bf16[2,4,1024]{2,1,0:T(4,128)(2,1)S(1)} %shard_map.75), channel_id=1, source_target_pairs={{0,8},{1,9},{2,10},{3,11},{4,12},{5,13},{6,14},{7,15},{8,0},{9,1},... | collective-permute-start | bytes 49160 | tf_op jit(solution)/shard_map/ppermute | solution.py:47
  5.2 4.8 %collective-permute-start.4 = (bf16[2,4,1024]{2,1,0:T(4,128)(2,1)S(1)}, bf16[2,4,1024]{2,1,0:T(4,128)(2,1)S(1)}, u32[]{:S(2)}, u32[]{:S(2)}) collective-permute-start(bf16[2,4,1024]{2,1,0:T(4,128)(2,1)S(1)} %shard_map.75), channel_id=1, source_target_pairs={{0,12},{1,13},{2,14},{3,15},{4,8},{5,9},{6,10},{7,11},{8,4},{9,5},... | collective-permute-start | bytes 49160 | tf_op jit(solution)/shard_map/ppermute | solution.py:47
  8.0 5.0 %collective-permute-start.3 = (bf16[2,4,1024]{2,1,0:T(4,128)(2,1)S(1)}, bf16[2,4,1024]{2,1,0:T(4,128)(2,1)S(1)}, u32[]{:S(2)}, u32[]{:S(2)}) collective-permute-start(bf16[2,4,1024]{2,1,0:T(4,128)(2,1)S(1)} %shard_map.75), channel_id=1, source_target_pairs={{0,14},{1,15},{2,12},{3,13},{4,10},{5,11},{6,8},{7,9},{8,6},{9,7},... | collective-permute-start | bytes 49160 | tf_op jit(solution)/shard_map/ppermute | solution.py:47
  9.1 4.5 %collective-permute-start.2 = (bf16[2,4,1024]{2,1,0:T(4,128)(2,1)S(1)}, bf16[2,4,1024]{2,1,0:T(4,128)(2,1)S(1)}, u32[]{:S(2)}, u32[]{:S(2)}) collective-permute-start(bf16[2,4,1024]{2,1,0:T(4,128)(2,1)S(1)} %shard_map.75), channel_id=1, source_target_pairs={{0,10},{1,11},{2,8},{3,9},{4,14},{5,15},{6,12},{7,13},{8,2},{9,3},... | collective-permute-start | bytes 49160 | tf_op jit(solution)/shard_map/ppermute | solution.py:47
  10.7 10.9 %copy-start.1 = (bf16[4,128,2048]{2,1,0:T(8,128)(2,1)S(1)}, bf16[4,128,2048]{2,1,0:T(8,128)(2,1)}, u32[]{:S(2)}) copy-start(bf16[4,128,2048]{2,1,0:T(8,128)(2,1)} %cache_ref.7) | copy-start | bytes 6291460
  10.7 10.9 %copy-start.2 = (bf16[4,64,2048]{2,1,0:T(8,128)(2,1)S(1)}, bf16[4,64,2048]{2,1,0:T(8,128)(2,1)}, u32[]{:S(2)}) copy-start(bf16[4,64,2048]{2,1,0:T(8,128)(2,1)} %fresh_ref.7) | copy-start | bytes 3145732
  13.0 19.7 %slice-start = ((s8[16777216]{0:T(1024)(128)(4,1)}), s8[4194304]{0:T(1024)(128)(4,1)S(1)}, s32[]{:S(2)}) async-start(s8[16777216]{0:T(1024)(128)(4,1)} %bitcast), calls=%async_computation | async-start | bytes 8388608
  13.0 19.7 %slice-start.1 = ((s8[16777216]{0:T(1024)(128)(4,1)}), s8[4194304]{0:T(1024)(128)(4,1)S(1)}, s32[]{:S(2)}) async-start(s8[16777216]{0:T(1024)(128)(4,1)} %bitcast), calls=%async_computation.1 | async-start | bytes 8388608
  13.7 19.0 %slice-start.2 = ((s8[16777216]{0:T(1024)(128)(4,1)}), s8[4194304]{0:T(1024)(128)(4,1)S(1)}, s32[]{:S(2)}) async-start(s8[16777216]{0:T(1024)(128)(4,1)} %bitcast), calls=%async_computation.2 | async-start | bytes 8388608
  14.3 3.1 %collective-permute-start.7 = (bf16[32,128]{1,0:T(8,128)(2,1)S(1)}, bf16[32,128]{1,0:T(8,128)(2,1)S(1)}, u32[]{:S(2)}, u32[]{:S(2)}) collective-permute-start(bf16[32,128]{1,0:T(8,128)(2,1)S(1)} %shard_map.79), channel_id=1, source_target_pairs={{0,9},{1,8},{2,11},{3,10},{4,13},{5,12},{6,15},{7,14},{8,1},{9,0},... | collective-permute-start | bytes 24584 | tf_op jit(solution)/shard_map/ppermute | solution.py:47
  15.7 1.7 %collective-permute-start.6 = (bf16[32,128]{1,0:T(8,128)(2,1)S(1)}, bf16[32,128]{1,0:T(8,128)(2,1)S(1)}, u32[]{:S(2)}, u32[]{:S(2)}) collective-permute-start(bf16[32,128]{1,0:T(8,128)(2,1)S(1)} %shard_map.79), channel_id=1, source_target_pairs={{0,8},{1,9},{2,10},{3,11},{4,12},{5,13},{6,14},{7,15},{8,0},{9,1},... | collective-permute-start | bytes 24584 | tf_op jit(solution)/shard_map/ppermute | solution.py:47
  17.4 15.2 %slice-start.3 = ((s8[16777216]{0:T(1024)(128)(4,1)}), s8[4194304]{0:T(1024)(128)(4,1)S(1)}, s32[]{:S(2)}) async-start(s8[16777216]{0:T(1024)(128)(4,1)} %bitcast), calls=%async_computation.3 | async-start | bytes 8388608
  17.4 4.1 %collective-permute-start.8 = (bf16[2,32,128]{2,1,0:T(8,128)(2,1)S(1)}, bf16[2,32,128]{2,1,0:T(8,128)(2,1)S(1)}, u32[]{:S(2)}, u32[]{:S(2)}) collective-permute-start(bf16[2,32,128]{2,1,0:T(8,128)(2,1)S(1)} %shard_map.80), channel_id=1, source_target_pairs={{0,12},{1,13},{2,14},{3,15},{4,8},{5,9},{6,10},{7,11},{8,4},{9,5},... | collective-permute-start | bytes 49160 | tf_op jit(solution)/shard_map/ppermute | solution.py:47
  17.8 5.0 %collective-permute-start.10 = (bf16[2,32,128]{2,1,0:T(8,128)(2,1)S(1)}, bf16[2,32,128]{2,1,0:T(8,128)(2,1)S(1)}, u32[]{:S(2)}, u32[]{:S(2)}) collective-permute-start(bf16[2,32,128]{2,1,0:T(8,128)(2,1)S(1)} %shard_map.80), channel_id=1, source_target_pairs={{0,14},{1,15},{2,12},{3,13},{4,10},{5,11},{6,8},{7,9},{8,6},{9,7},... | collective-permute-start | bytes 49160 | tf_op jit(solution)/shard_map/ppermute | solution.py:47
  19.4 5.7 %collective-permute-start.12 = (bf16[2,32,128]{2,1,0:T(8,128)(2,1)S(1)}, bf16[2,32,128]{2,1,0:T(8,128)(2,1)S(1)}, u32[]{:S(2)}, u32[]{:S(2)}) collective-permute-start(bf16[2,32,128]{2,1,0:T(8,128)(2,1)S(1)} %shard_map.80), channel_id=1, source_target_pairs={{0,10},{1,11},{2,8},{3,9},{4,14},{5,15},{6,12},{7,13},{8,2},{9,3},... | collective-permute-start | bytes 49160 | tf_op jit(solution)/shard_map/ppermute | solution.py:47
  20.5 6.3 %collective-permute-start.14 = (bf16[2,32,128]{2,1,0:T(8,128)(2,1)S(1)}, bf16[2,32,128]{2,1,0:T(8,128)(2,1)S(1)}, u32[]{:S(2)}, u32[]{:S(2)}) collective-permute-start(bf16[2,32,128]{2,1,0:T(8,128)(2,1)S(1)} %shard_map.80), channel_id=1, source_target_pairs={{0,8},{1,9},{2,10},{3,11},{4,12},{5,13},{6,14},{7,15},{8,0},{9,1},... | collective-permute-start | bytes 49160 | tf_op jit(solution)/shard_map/ppermute | solution.py:47
  22.2 5.4 %collective-permute-start.9 = (bf16[2,40,128]{2,1,0:T(8,128)(2,1)S(1)}, bf16[2,40,128]{2,1,0:T(8,128)(2,1)S(1)}, u32[]{:S(2)}, u32[]{:S(2)}) collective-permute-start(bf16[2,40,128]{2,1,0:T(8,128)(2,1)S(1)} %shard_map.81), channel_id=1, source_target_pairs={{0,12},{1,13},{2,14},{3,15},{4,8},{5,9},{6,10},{7,11},{8,4},{9,5},... | collective-permute-start | bytes 61448 | tf_op jit(solution)/shard_map/ppermute | solution.py:47
  23.4 5.1 %collective-permute-start.11 = (bf16[2,40,128]{2,1,0:T(8,128)(2,1)S(1)}, bf16[2,40,128]{2,1,0:T(8,128)(2,1)S(1)}, u32[]{:S(2)}, u32[]{:S(2)}) collective-permute-start(bf16[2,40,128]{2,1,0:T(8,128)(2,1)S(1)} %shard_map.82), channel_id=1, source_target_pairs={{0,14},{1,15},{2,12},{3,13},{4,10},{5,11},{6,8},{7,9},{8,6},{9,7},... | collective-permute-start | bytes 61448 | tf_op jit(solution)/shard_map/ppermute | solution.py:47
  25.6 3.3 %collective-permute-start.13 = (bf16[2,40,128]{2,1,0:T(8,128)(2,1)S(1)}, bf16[2,40,128]{2,1,0:T(8,128)(2,1)S(1)}, u32[]{:S(2)}, u32[]{:S(2)}) collective-permute-start(bf16[2,40,128]{2,1,0:T(8,128)(2,1)S(1)} %shard_map.83), channel_id=1, source_target_pairs={{0,10},{1,11},{2,8},{3,9},{4,14},{5,15},{6,12},{7,13},{8,2},{9,3},... | collective-permute-start | bytes 61448 | tf_op jit(solution)/shard_map/ppermute | solution.py:47
  27.4 1.5 %collective-permute-start.15 = (bf16[2,40,128]{2,1,0:T(8,128)(2,1)S(1)}, bf16[2,40,128]{2,1,0:T(8,128)(2,1)S(1)}, u32[]{:S(2)}, u32[]{:S(2)}) collective-permute-start(bf16[2,40,128]{2,1,0:T(8,128)(2,1)S(1)} %shard_map.84), channel_id=1, source_target_pairs={{0,8},{1,9},{2,10},{3,11},{4,12},{5,13},{6,14},{7,15},{8,0},{9,1},... | collective-permute-start | bytes 61448 | tf_op jit(solution)/shard_map/ppermute | solution.py:47
  28.9 1.8 %collective-permute-start.16 = (bf16[4,40,128]{2,1,0:T(8,128)(2,1)S(1)}, bf16[4,40,128]{2,1,0:T(8,128)(2,1)S(1)}, u32[]{:S(2)}, u32[]{:S(2)}) collective-permute-start(bf16[4,40,128]{2,1,0:T(8,128)(2,1)S(1)} %get-tuple-element.11), channel_id=1, source_target_pairs={{0,8},{1,9},{2,10},{3,11},{4,12},{5,13},{6,14},{7,15},{8,0},{9,1},... | collective-permute-start | bytes 122888 | tf_op jit(solution)/shard_map/ppermute | solution.py:47
  29.2 3.4 %collective-permute-start.17 = (bf16[4,40,128]{2,1,0:T(8,128)(2,1)S(1)}, bf16[4,40,128]{2,1,0:T(8,128)(2,1)S(1)}, u32[]{:S(2)}, u32[]{:S(2)}) collective-permute-start(bf16[4,40,128]{2,1,0:T(8,128)(2,1)S(1)} %get-tuple-element.12), channel_id=1, source_target_pairs={{0,9},{1,8},{2,11},{3,10},{4,13},{5,12},{6,15},{7,14},{8,1},{9,0},... | collective-permute-start | bytes 122888 | tf_op jit(solution)/shard_map/ppermute | solution.py:47
  33.6 5.6 %collective-permute-start.18 = (bf16[2,4,1024]{2,1,0:T(4,128)(2,1)S(1)}, bf16[2,4,1024]{2,1,0:T(4,128)(2,1)S(1)}, u32[]{:S(2)}, u32[]{:S(2)}) collective-permute-start(bf16[2,4,1024]{2,1,0:T(4,128)(2,1)S(1)} %get-tuple-element.13), channel_id=1, source_target_pairs={{0,12},{1,13},{2,14},{3,15},{4,8},{5,9},{6,10},{7,11},{8,4},{9,5},... | collective-permute-start | bytes 49160 | tf_op jit(solution)/shard_map/ppermute | solution.py:47
  35.5 5.0 %collective-permute-start.19 = (bf16[2,4,1024]{2,1,0:T(4,128)(2,1)S(1)}, bf16[2,4,1024]{2,1,0:T(4,128)(2,1)S(1)}, u32[]{:S(2)}, u32[]{:S(2)}) collective-permute-start(bf16[2,4,1024]{2,1,0:T(4,128)(2,1)S(1)} %shard_map.88), channel_id=1, source_target_pairs={{0,14},{1,15},{2,12},{3,13},{4,10},{5,11},{6,8},{7,9},{8,6},{9,7},... | collective-permute-start | bytes 49160 | tf_op jit(solution)/shard_map/ppermute | solution.py:47
  38.4 3.2 %collective-permute-start.20 = (bf16[2,4,1024]{2,1,0:T(4,128)(2,1)S(1)}, bf16[2,4,1024]{2,1,0:T(4,128)(2,1)S(1)}, u32[]{:S(2)}, u32[]{:S(2)}) collective-permute-start(bf16[2,4,1024]{2,1,0:T(4,128)(2,1)S(1)} %shard_map.90), channel_id=1, source_target_pairs={{0,10},{1,11},{2,8},{3,9},{4,14},{5,15},{6,12},{7,13},{8,2},{9,3},... | collective-permute-start | bytes 49160 | tf_op jit(solution)/shard_map/ppermute | solution.py:47
  39.0 2.5 %collective-permute-start.21 = (bf16[2,4,1024]{2,1,0:T(4,128)(2,1)S(1)}, bf16[2,4,1024]{2,1,0:T(4,128)(2,1)S(1)}, u32[]{:S(2)}, u32[]{:S(2)}) collective-permute-start(bf16[2,4,1024]{2,1,0:T(4,128)(2,1)S(1)} %shard_map.92), channel_id=1, source_target_pairs={{0,8},{1,9},{2,10},{3,11},{4,12},{5,13},{6,14},{7,15},{8,0},{9,1},... | collective-permute-start | bytes 49160 | tf_op jit(solution)/shard_map/ppermute | solution.py:47
  41.6 3.3 %collective-permute-start.22 = (f32[4,1024]{1,0:T(4,128)S(1)}, f32[4,1024]{1,0:T(4,128)S(1)}, u32[]{:S(2)}, u32[]{:S(2)}) collective-permute-start(f32[4,1024]{1,0:T(4,128)S(1)} %get-tuple-element.15), channel_id=1, source_target_pairs={{0,8},{1,9},{2,10},{3,11},{4,12},{5,13},{6,14},{7,15},{8,0},{9,1},... | collective-permute-start | bytes 49160 | tf_op jit(solution)/shard_map/ppermute | solution.py:47
  41.8 3.1 %collective-permute-start.23 = (bf16[4,1024]{1,0:T(4,128)(2,1)S(1)}, bf16[4,1024]{1,0:T(4,128)(2,1)S(1)}, u32[]{:S(2)}, u32[]{:S(2)}) collective-permute-start(bf16[4,1024]{1,0:T(4,128)(2,1)S(1)} %get-tuple-element.16), channel_id=1, source_target_pairs={{0,9},{1,8},{2,11},{3,10},{4,13},{5,12},{6,15},{7,14},{8,1},{9,0},... | collective-permute-start | bytes 24584 | tf_op jit(solution)/shard_map/ppermute | solution.py:47

commit v12 on v11

--- a/solution.py
+++ b/solution.py
@@ -19,7 +19,7 @@
 BOTH = ("section", "tensor")
 SPLIT_OUTPUT = False
 ORDER = (4, 6, 2)
-MIDDLE = (4, 6, 2)
+MIDDLE = (2, 6, 4)
 LIMIT = 10**7
 BACK = (4, 6, 2)
 ADD = 23000000

time: 45.7 us -> 45.5 us (level)
  transfers between devices with their start and end apart: 24 -> 24, of which waited for: 12 -> 11; matrix products, arithmetic and copies ran while one was open for 0% -> 0% of each run, Pallas kernels for 15% -> 15%
where the time goes in v12:
time: 45.5 us; the launch traced here: 45.3 us
  starting transfers between devices  23.3 us (51%)
  waiting for transfers between devices  12 us (26%)
  Pallas kernels  9.13 us (20%)
  local copies, waits for them, and re-layouts  0.73 us (2%)
    ppermute x24, starting transfers between devices, flip(): lax.ppermute(x, BOTH, [(i, (i // n ^ 1) * n + (i % n ^ apart)) for i in r...  23.3 us
    ppermute x24, waiting for transfers between devices, flip(): lax.ppermute(x, BOTH, [(i, (i // n ^ 1) * n + (i % n ^ apart)) for i in r...  12 us
    pallas_call x22, Pallas kernels, call(): pl.pallas_call(kernel, in_specs=specs or [VMEM] * len(args), out_specs=ou...  9.13 us
  transfers between devices with their start and end apart: 24, of which 11 were waited for; matrix products, arithmetic and copies ran while one was open for 0% of the time, Pallas kernels for 15%

profile of v12, /device:TPU:0, one launch (start us, length us, event | category | flops | bytes accessed | tf_op | source)
XLA Modules:
  0.0 45.3 jit_solution(13610303773497140309)
XLA Ops:
  0.0 0.7 %copy-done.3 = bf16[4,1024]{1,0:T(4,128)(2,1)S(1)} copy-done((bf16[4,1024]{1,0:T(4,128)(2,1)S(1)}, bf16[4,1024]{1,0:T(4,128)(2,1)}, u32[]{:S(2)}) %copy-start.3) | copy-done | bytes 8216
  0.7 2.5 %collective-permute-start.1 = (bf16[4,1024]{1,0:T(4,128)(2,1)S(1)}, bf16[4,1024]{1,0:T(4,128)(2,1)S(1)}, u32[]{:S(2)}, u32[]{:S(2)}) collective-permute-start(bf16[4,1024]{1,0:T(4,128)(2,1)S(1)} %shard_map.74), channel_id=1, source_target_pairs={{0,9},{1,8},{2,11},{3,10},{4,13},{5,12},{6,15},{7,14},{8,1},{9,0},... | collective-permute-start | bytes 24584 | tf_op jit(solution)/shard_map/ppermute | solution.py:47
  3.2 0.7 %collective-permute-start = (bf16[4,1024]{1,0:T(4,128)(2,1)S(1)}, bf16[4,1024]{1,0:T(4,128)(2,1)S(1)}, u32[]{:S(2)}, u32[]{:S(2)}) collective-permute-start(bf16[4,1024]{1,0:T(4,128)(2,1)S(1)} %shard_map.74), channel_id=1, source_target_pairs={{0,8},{1,9},{2,10},{3,11},{4,12},{5,13},{6,14},{7,15},{8,0},{9,1},... | collective-permute-start | bytes 24584 | tf_op jit(solution)/shard_map/ppermute | solution.py:47
  3.9 0.0 copy-done.5
  3.9 0.6 %shard_map.73._.limit_ref = s32[2,64]{1,0:T(2,128)S(1)} custom-call(s32[4]{0:T(128)S(1)} %copy-done.4, s32[4]{0:T(128)S(1)} %copy-done.5), custom_call_target="tpu_custom_call" | custom-call | flops 10000000 | tf_op jit(solution)/shard_map/pallas_call | solution.py:56
  4.4 0.1 collective-permute-done.1.y_ref
  4.5 0.1 collective-permute-done.x_ref
  4.7 0.5 %collective-permute-start.5 = (bf16[2,4,1024]{2,1,0:T(4,128)(2,1)S(1)}, bf16[2,4,1024]{2,1,0:T(4,128)(2,1)S(1)}, u32[]{:S(2)}, u32[]{:S(2)}) collective-permute-start(bf16[2,4,1024]{2,1,0:T(4,128)(2,1)S(1)} %shard_map.75), channel_id=1, source_target_pairs={{0,8},{1,9},{2,10},{3,11},{4,12},{5,13},{6,14},{7,15},{8,0},{9,1},... | collective-permute-start | bytes 49160 | tf_op jit(solution)/shard_map/ppermute | solution.py:47
  5.2 2.8 %collective-permute-start.4 = (bf16[2,4,1024]{2,1,0:T(4,128)(2,1)S(1)}, bf16[2,4,1024]{2,1,0:T(4,128)(2,1)S(1)}, u32[]{:S(2)}, u32[]{:S(2)}) collective-permute-start(bf16[2,4,1024]{2,1,0:T(4,128)(2,1)S(1)} %shard_map.75), channel_id=1, source_target_pairs={{0,12},{1,13},{2,14},{3,15},{4,8},{5,9},{6,10},{7,11},{8,4},{9,5},... | collective-permute-start | bytes 49160 | tf_op jit(solution)/shard_map/ppermute | solution.py:47
  8.0 1.1 %collective-permute-start.3 = (bf16[2,4,1024]{2,1,0:T(4,128)(2,1)S(1)}, bf16[2,4,1024]{2,1,0:T(4,128)(2,1)S(1)}, u32[]{:S(2)}, u32[]{:S(2)}) collective-permute-start(bf16[2,4,1024]{2,1,0:T(4,128)(2,1)S(1)} %shard_map.75), channel_id=1, source_target_pairs={{0,14},{1,15},{2,12},{3,13},{4,10},{5,11},{6,8},{7,9},{8,6},{9,7},... | collective-permute-start | bytes 49160 | tf_op jit(solution)/shard_map/ppermute | solution.py:47
  9.1 0.2 collective-permute-start.2
  9.4 0.0 collective-permute-done.5.x_ref
  9.4 0.7 %shard_map.76.old_ref = f32[4,1024]{1,0:T(4,128)S(1)} custom-call(bf16[2,4,1024]{2,1,0:T(4,128)(2,1)S(1)} %collective-permute-done.5.x_ref, bf16[8192,1024]{1,0:T(8,128)(2,1)S(1)} %copy-done), custom_call_target="tpu_custom_call" | custom-call | tf_op jit(solution)/shard_map/pallas_call | solution.py:56
  10.0 0.0 collective-permute-done.4.x_ref
  10.0 0.7 %shard_map.77.old_ref = f32[4,1024]{1,0:T(4,128)S(1)} custom-call(bf16[2,4,1024]{2,1,0:T(4,128)(2,1)S(1)} %collective-permute-done.4.x_ref, bf16[8192,1024]{1,0:T(8,128)(2,1)S(1)} %copy-done, f32[4,1024]{1,0:T(4,128)S(1)} %shard_map.76.old_ref), custom_call_target="tpu_custom_call" | custom-call | flops 10000000000 | tf_op jit(solution)/shard_map/pallas_call | solution.py:56
  10.7 2.3 %collective-permute-done.3.x_ref = bf16[2,4,1024]{2,1,0:T(4,128)(2,1)S(1)} collective-permute-done((bf16[2,4,1024]{2,1,0:T(4,128)(2,1)S(1)}, bf16[2,4,1024]{2,1,0:T(4,128)(2,1)S(1)}, u32[]{:S(2)}, u32[]{:S(2)}) %collective-permute-start.3) | collective-permute-done | bytes 16416 | tf_op jit(solution)/shard_map/ppermute | solution.py:47
  13.0 0.7 %shard_map.78.old_ref = f32[4,1024]{1,0:T(4,128)S(1)} custom-call(bf16[2,4,1024]{2,1,0:T(4,128)(2,1)S(1)} %collective-permute-done.3.x_ref, bf16[8192,1024]{1,0:T(8,128)(2,1)S(1)} %copy-done, f32[4,1024]{1,0:T(4,128)S(1)} %shard_map.77.old_ref), custom_call_target="tpu_custom_call" | custom-call | tf_op jit(solution)/shard_map/pallas_call | solution.py:56
  13.7 0.0 collective-permute-done.2.x_ref
  13.7 0.7 %shard_map.79 = bf16[32,128]{1,0:T(8,128)(2,1)S(1)} custom-call(bf16[2,4,1024]{2,1,0:T(4,128)(2,1)S(1)} %collective-permute-done.2.x_ref, bf16[8192,1024]{1,0:T(8,128)(2,1)S(1)} %copy-done, f32[4,1024]{1,0:T(4,128)S(1)} %shard_map.78.old_ref), custom_call_target="tpu_custom_call" | custom-call | tf_op jit(solution)/shard_map/pallas_call | solution.py:56
  14.3 1.4 %collective-permute-start.7 = (bf16[32,128]{1,0:T(8,128)(2,1)S(1)}, bf16[32,128]{1,0:T(8,128)(2,1)S(1)}, u32[]{:S(2)}, u32[]{:S(2)}) collective-permute-start(bf16[32,128]{1,0:T(8,128)(2,1)S(1)} %shard_map.79), channel_id=1, source_target_pairs={{0,9},{1,8},{2,11},{3,10},{4,13},{5,12},{6,15},{7,14},{8,1},{9,0},... | collective-permute-start | bytes 24584 | tf_op jit(solution)/shard_map/ppermute | solution.py:47
  15.7 0.3 collective-permute-start.6
  16.1 1.4 %collective-permute-done.7.y_ref = bf16[32,128]{1,0:T(8,128)(2,1)S(1)} collective-permute-done((bf16[32,128]{1,0:T(8,128)(2,1)S(1)}, bf16[32,128]{1,0:T(8,128)(2,1)S(1)}, u32[]{:S(2)}, u32[]{:S(2)}) %collective-permute-start.7) | collective-permute-done | bytes 8224 | tf_op jit(solution)/shard_map/ppermute | solution.py:47
  17.4 0.0 collective-permute-done.6.x_ref
  17.4 0.1 collective-permute-start.8
  17.5 1.7 %collective-permute-start.10 = (bf16[2,32,128]{2,1,0:T(8,128)(2,1)S(1)}, bf16[2,32,128]{2,1,0:T(8,128)(2,1)S(1)}, u32[]{:S(2)}, u32[]{:S(2)}) collective-permute-start(bf16[2,32,128]{2,1,0:T(8,128)(2,1)S(1)} %shard_map.80), channel_id=1, source_target_pairs={{0,14},{1,15},{2,12},{3,13},{4,10},{5,11},{6,8},{7,9},{8,6},{9,7},... | collective-permute-start | bytes 49160 | tf_op jit(solution)/shard_map/ppermute | solution.py:47
  19.2 1.3 %collective-permute-start.12 = (bf16[2,32,128]{2,1,0:T(8,128)(2,1)S(1)}, bf16[2,32,128]{2,1,0:T(8,128)(2,1)S(1)}, u32[]{:S(2)}, u32[]{:S(2)}) collective-permute-start(bf16[2,32,128]{2,1,0:T(8,128)(2,1)S(1)} %shard_map.80), channel_id=1, source_target_pairs={{0,12},{1,13},{2,14},{3,15},{4,8},{5,9},{6,10},{7,11},{8,4},{9,5},... | collective-permute-start | bytes 49160 | tf_op jit(solution)/shard_map/ppermute | solution.py:47
  20.5 0.3 collective-permute-start.14
  20.8 0.0 collective-permute-done.8.q_ref
  20.8 0.6 %shard_map.81 = bf16[2,40,128]{2,1,0:T(8,128)(2,1)S(1)} custom-call(s32[2,64]{1,0:T(2,128)S(1)} %shard_map.73._.limit_ref, bf16[2,32,128]{2,1,0:T(8,128)(2,1)S(1)} %collective-permute-done.8.q_ref, bf16[4,128,2048]{2,1,0:T(8,128)(2,1)S(1)} %copy-done.1, bf16[4,64,2048]{2,1,0:T(8,128)(2,1)S(1)} %copy-done.2), custom_call_target="tpu_custom_call" | custom-call | flops 11500000 | tf_op jit(solution)/shard_map/pallas_call | solution.py:56
  21.5 1.0 %collective-permute-start.9 = (bf16[2,40,128]{2,1,0:T(8,128)(2,1)S(1)}, bf16[2,40,128]{2,1,0:T(8,128)(2,1)S(1)}, u32[]{:S(2)}, u32[]{:S(2)}) collective-permute-start(bf16[2,40,128]{2,1,0:T(8,128)(2,1)S(1)} %shard_map.81), channel_id=1, source_target_pairs={{0,10},{1,11},{2,8},{3,9},{4,14},{5,15},{6,12},{7,13},{8,2},{9,3},... | collective-permute-start | bytes 61448 | tf_op jit(solution)/shard_map/ppermute | solution.py:47
  22.5 0.1 collective-permute-done.10.q_ref
  22.6 0.6 %shard_map.82 = bf16[2,40,128]{2,1,0:T(8,128)(2,1)S(1)} custom-call(s32[2,64]{1,0:T(2,128)S(1)} %shard_map.73._.limit_ref, bf16[2,32,128]{2,1,0:T(8,128)(2,1)S(1)} %collective-permute-done.10.q_ref, bf16[4,128,2048]{2,1,0:T(8,128)(2,1)S(1)} %copy-done.1, bf16[4,64,2048]{2,1,0:T(8,128)(2,1)S(1)} %copy-done.2), custom_call_target="tpu_custom_call" | custom-call | flops 11500000 | tf_op jit(solution)/shard_map/pallas_call | solution.py:56
  23.2 1.6 %collective-permute-start.11 = (bf16[2,40,128]{2,1,0:T(8,128)(2,1)S(1)}, bf16[2,40,128]{2,1,0:T(8,128)(2,1)S(1)}, u32[]{:S(2)}, u32[]{:S(2)}) collective-permute-start(bf16[2,40,128]{2,1,0:T(8,128)(2,1)S(1)} %shard_map.82), channel_id=1, source_target_pairs={{0,14},{1,15},{2,12},{3,13},{4,10},{5,11},{6,8},{7,9},{8,6},{9,7},... | collective-permute-start | bytes 61448 | tf_op jit(solution)/shard_map/ppermute | solution.py:47
  24.8 0.0 collective-permute-done.12.q_ref
  24.8 0.6 %shard_map.83 = bf16[2,40,128]{2,1,0:T(8,128)(2,1)S(1)} custom-call(s32[2,64]{1,0:T(2,128)S(1)} %shard_map.73._.limit_ref, bf16[2,32,128]{2,1,0:T(8,128)(2,1)S(1)} %collective-permute-done.12.q_ref, bf16[4,128,2048]{2,1,0:T(8,128)(2,1)S(1)} %copy-done.1, bf16[4,64,2048]{2,1,0:T(8,128)(2,1)S(1)} %copy-done.2), custom_call_target="tpu_custom_call" | custom-call | flops 11500000 | tf_op jit(solution)/shard_map/pallas_call | solution.py:56
  25.4 0.4 collective-permute-start.13
  25.9 0.0 collective-permute-done.14.q_ref
  25.9 0.6 %shard_map.84 = bf16[2,40,128]{2,1,0:T(8,128)(2,1)S(1)} custom-call(s32[2,64]{1,0:T(2,128)S(1)} %shard_map.73._.limit_ref, bf16[2,32,128]{2,1,0:T(8,128)(2,1)S(1)} %collective-permute-done.14.q_ref, bf16[4,128,2048]{2,1,0:T(8,128)(2,1)S(1)} %copy-done.1, bf16[4,64,2048]{2,1,0:T(8,128)(2,1)S(1)} %copy-done.2), custom_call_target="tpu_custom_call" | custom-call | flops 11500000 | tf_op jit(solution)/shard_map/pallas_call | solution.py:56
  26.5 0.4 collective-permute-start.15
  26.9 0.0 collective-permute-done.9.a_ref
  26.9 1.4 %collective-permute-done.11.b_ref = bf16[2,40,128]{2,1,0:T(8,128)(2,1)S(1)} collective-permute-done((bf16[2,40,128]{2,1,0:T(8,128)(2,1)S(1)}, bf16[2,40,128]{2,1,0:T(8,128)(2,1)S(1)}, u32[]{:S(2)}, u32[]{:S(2)}) %collective-permute-start.11) | collective-permute-done | bytes 20512 | tf_op jit(solution)/shard_map/ppermute | solution.py:47
  28.3 1.3 %collective-permute-done.13.c_ref = bf16[2,40,128]{2,1,0:T(8,128)(2,1)S(1)} collective-permute-done((bf16[2,40,128]{2,1,0:T(8,128)(2,1)S(1)}, bf16[2,40,128]{2,1,0:T(8,128)(2,1)S(1)}, u32[]{:S(2)}, u32[]{:S(2)}) %collective-permute-start.13) | collective-permute-done | bytes 20512 | tf_op jit(solution)/shard_map/ppermute | solution.py:47
  29.6 0.0 collective-permute-done.15.d_ref
  29.6 0.2 collective-permute-start.16
  29.9 1.5 %collective-permute-start.17 = (bf16[4,40,128]{2,1,0:T(8,128)(2,1)S(1)}, bf16[4,40,128]{2,1,0:T(8,128)(2,1)S(1)}, u32[]{:S(2)}, u32[]{:S(2)}) collective-permute-start(bf16[4,40,128]{2,1,0:T(8,128)(2,1)S(1)} %get-tuple-element.12), channel_id=1, source_target_pairs={{0,9},{1,8},{2,11},{3,10},{4,13},{5,12},{6,15},{7,14},{8,1},{9,0},... | collective-permute-start | bytes 122888 | tf_op jit(solution)/shard_map/ppermute | solution.py:47
  31.4 0.0 collective-permute-done.16.a_ref
  31.4 1.9 %collective-permute-done.17.b_ref = bf16[4,40,128]{2,1,0:T(8,128)(2,1)S(1)} collective-permute-done((bf16[4,40,128]{2,1,0:T(8,128)(2,1)S(1)}, bf16[4,40,128]{2,1,0:T(8,128)(2,1)S(1)}, u32[]{:S(2)}, u32[]{:S(2)}) %collective-permute-start.17) | collective-permute-done | bytes 40992 | tf_op jit(solution)/shard_map/ppermute | solution.py:47
  33.3 0.9 %shard_map.86 = (bf16[2,4,1024]{2,1,0:T(4,128)(2,1)S(1)}, bf16[4,1024]{1,0:T(4,128)(2,1)S(1)}) custom-call(bf16[4,40,128]{2,1,0:T(8,128)(2,1)S(1)} %collective-permute-done.16.a_ref, bf16[4,40,128]{2,1,0:T(8,128)(2,1)S(1)} %collective-permute-done.17.b_ref, bf16[1024,8192]{1,0:T(8,128)(2,1)S(1)} %bitcast.1), custom_call_target="tpu_custom_call" | custom-call | flops 11500000 | tf_op jit(solution)/shard_map/pallas_call | solution.py:56
  34.2 0.5 %collective-permute-start.18 = (bf16[2,4,1024]{2,1,0:T(4,128)(2,1)S(1)}, bf16[2,4,1024]{2,1,0:T(4,128)(2,1)S(1)}, u32[]{:S(2)}, u32[]{:S(2)}) collective-permute-start(bf16[2,4,1024]{2,1,0:T(4,128)(2,1)S(1)} %get-tuple-element.13), channel_id=1, source_target_pairs={{0,12},{1,13},{2,14},{3,15},{4,8},{5,9},{6,10},{7,11},{8,4},{9,5},... | collective-permute-start | bytes 49160 | tf_op jit(solution)/shard_map/ppermute | solution.py:47
  34.8 0.7 %shard_map.88 = bf16[2,4,1024]{2,1,0:T(4,128)(2,1)S(1)} custom-call(bf16[4,1024]{1,0:T(4,128)(2,1)S(1)} %get-tuple-element.14.context_ref, bf16[1024,8192]{1,0:T(8,128)(2,1)S(1)} %bitcast.1), custom_call_target="tpu_custom_call" | custom-call | flops 11500000 | tf_op jit(solution)/shard_map/pallas_call | solution.py:56
  35.4 1.9 %collective-permute-start.19 = (bf16[2,4,1024]{2,1,0:T(4,128)(2,1)S(1)}, bf16[2,4,1024]{2,1,0:T(4,128)(2,1)S(1)}, u32[]{:S(2)}, u32[]{:S(2)}) collective-permute-start(bf16[2,4,1024]{2,1,0:T(4,128)(2,1)S(1)} %shard_map.88), channel_id=1, source_target_pairs={{0,14},{1,15},{2,12},{3,13},{4,10},{5,11},{6,8},{7,9},{8,6},{9,7},... | collective-permute-start | bytes 49160 | tf_op jit(solution)/shard_map/ppermute | solution.py:47
  37.3 0.7 %shard_map.90 = bf16[2,4,1024]{2,1,0:T(4,128)(2,1)S(1)} custom-call(bf16[4,1024]{1,0:T(4,128)(2,1)S(1)} %get-tuple-element.14.context_ref, bf16[1024,8192]{1,0:T(8,128)(2,1)S(1)} %bitcast.1), custom_call_target="tpu_custom_call" | custom-call | flops 11500000 | tf_op jit(solution)/shard_map/pallas_call | solution.py:56
  38.0 0.8 %collective-permute-start.20 = (bf16[2,4,1024]{2,1,0:T(4,128)(2,1)S(1)}, bf16[2,4,1024]{2,1,0:T(4,128)(2,1)S(1)}, u32[]{:S(2)}, u32[]{:S(2)}) collective-permute-start(bf16[2,4,1024]{2,1,0:T(4,128)(2,1)S(1)} %shard_map.90), channel_id=1, source_target_pairs={{0,10},{1,11},{2,8},{3,9},{4,14},{5,15},{6,12},{7,13},{8,2},{9,3},... | collective-permute-start | bytes 49160 | tf_op jit(solution)/shard_map/ppermute | solution.py:47
  38.7 0.7 %shard_map.92 = bf16[2,4,1024]{2,1,0:T(4,128)(2,1)S(1)} custom-call(bf16[4,1024]{1,0:T(4,128)(2,1)S(1)} %get-tuple-element.14.context_ref, bf16[1024,8192]{1,0:T(8,128)(2,1)S(1)} %bitcast.1), custom_call_target="tpu_custom_call" | custom-call | flops 11500000 | tf_op jit(solution)/shard_map/pallas_call | solution.py:56
  39.4 0.2 collective-permute-start.21
  39.6 0.0 collective-permute-done.18.x_ref
  39.6 0.8 %collective-permute-done.19.y_ref = bf16[2,4,1024]{2,1,0:T(4,128)(2,1)S(1)} collective-permute-done((bf16[2,4,1024]{2,1,0:T(4,128)(2,1)S(1)}, bf16[2,4,1024]{2,1,0:T(4,128)(2,1)S(1)}, u32[]{:S(2)}, u32[]{:S(2)}) %collective-permute-start.19) | collective-permute-done | bytes 16416 | tf_op jit(solution)/shard_map/ppermute | solution.py:47
  40.4 0.7 %collective-permute-done.20.y_ref = bf16[2,4,1024]{2,1,0:T(4,128)(2,1)S(1)} collective-permute-done((bf16[2,4,1024]{2,1,0:T(4,128)(2,1)S(1)}, bf16[2,4,1024]{2,1,0:T(4,128)(2,1)S(1)}, u32[]{:S(2)}, u32[]{:S(2)}) %collective-permute-start.20) | collective-permute-done | bytes 16416 | tf_op jit(solution)/shard_map/ppermute | solution.py:47
  41.2 0.0 collective-permute-done.21.y_ref
  41.2 0.4 collective-permute-start.22
  41.6 1.4 %collective-permute-start.23 = (bf16[4,1024]{1,0:T(4,128)(2,1)S(1)}, bf16[4,1024]{1,0:T(4,128)(2,1)S(1)}, u32[]{:S(2)}, u32[]{:S(2)}) collective-permute-start(bf16[4,1024]{1,0:T(4,128)(2,1)S(1)} %get-tuple-element.16), channel_id=1, source_target_pairs={{0,9},{1,8},{2,11},{3,10},{4,13},{5,12},{6,15},{7,14},{8,1},{9,0},... | collective-permute-start | bytes 24584 | tf_op jit(solution)/shard_map/ppermute | solution.py:47
  42.9 1.7 %collective-permute-done.23.y_ref = bf16[4,1024]{1,0:T(4,128)(2,1)S(1)} collective-permute-done((bf16[4,1024]{1,0:T(4,128)(2,1)S(1)}, bf16[4,1024]{1,0:T(4,128)(2,1)S(1)}, u32[]{:S(2)}, u32[]{:S(2)}) %collective-permute-start.23) | collective-permute-done | bytes 8224 | tf_op jit(solution)/shard_map/ppermute | solution.py:47
  44.7 0.0 collective-permute-done.22.x_ref
  44.7 0.6 %shard_map.94 = bf16[4,1024]{1,0:T(4,128)(2,1)} custom-call(f32[4,1024]{1,0:T(4,128)S(1)} %collective-permute-done.22.x_ref, bf16[4,1024]{1,0:T(4,128)(2,1)S(1)} %collective-permute-done.23.y_ref), custom_call_target="tpu_custom_call" | custom-call | tf_op jit(solution)/shard_map/pallas_call | solution.py:56
  (27 shorter events, 0.1 us)
Async XLA Ops:
  0.0 0.7 %copy-start.3 = (bf16[4,1024]{1,0:T(4,128)(2,1)S(1)}, bf16[4,1024]{1,0:T(4,128)(2,1)}, u32[]{:S(2)}) copy-start(bf16[4,1024]{1,0:T(4,128)(2,1)} %x_ref.1) | copy-start | bytes 24580
  0.7 3.2 %copy-start.4 = (s32[4]{0:T(128)S(1)}, s32[4]{0:T(128)}, u32[]{:S(2)}) copy-start(s32[4]{0:T(128)} %clen_ref.1) | copy-start | bytes 52
  0.7 3.2 %copy-start.5 = (s32[4]{0:T(128)S(1)}, s32[4]{0:T(128)}, u32[]{:S(2)}) copy-start(s32[4]{0:T(128)} %nlen_ref.1) | copy-start | bytes 52
  0.7 8.7 %copy-start = (bf16[8192,1024]{1,0:T(8,128)(2,1)S(1)}, bf16[8192,1024]{1,0:T(8,128)(2,1)}, u32[]{:S(2)}) copy-start(bf16[8192,1024]{1,0:T(8,128)(2,1)} %w_ref.11) | copy-start | bytes 50331652
  0.7 3.8 %collective-permute-start.1 = (bf16[4,1024]{1,0:T(4,128)(2,1)S(1)}, bf16[4,1024]{1,0:T(4,128)(2,1)S(1)}, u32[]{:S(2)}, u32[]{:S(2)}) collective-permute-start(bf16[4,1024]{1,0:T(4,128)(2,1)S(1)} %shard_map.74), channel_id=1, source_target_pairs={{0,9},{1,8},{2,11},{3,10},{4,13},{5,12},{6,15},{7,14},{8,1},{9,0},... | collective-permute-start | bytes 24584 | tf_op jit(solution)/shard_map/ppermute | solution.py:47
  3.2 1.5 %collective-permute-start = (bf16[4,1024]{1,0:T(4,128)(2,1)S(1)}, bf16[4,1024]{1,0:T(4,128)(2,1)S(1)}, u32[]{:S(2)}, u32[]{:S(2)}) collective-permute-start(bf16[4,1024]{1,0:T(4,128)(2,1)S(1)} %shard_map.74), channel_id=1, source_target_pairs={{0,8},{1,9},{2,10},{3,11},{4,12},{5,13},{6,14},{7,15},{8,0},{9,1},... | collective-permute-start | bytes 24584 | tf_op jit(solution)/shard_map/ppermute | solution.py:47
  4.7 4.7 %collective-permute-start.5 = (bf16[2,4,1024]{2,1,0:T(4,128)(2,1)S(1)}, bf16[2,4,1024]{2,1,0:T(4,128)(2,1)S(1)}, u32[]{:S(2)}, u32[]{:S(2)}) collective-permute-start(bf16[2,4,1024]{2,1,0:T(4,128)(2,1)S(1)} %shard_map.75), channel_id=1, source_target_pairs={{0,8},{1,9},{2,10},{3,11},{4,12},{5,13},{6,14},{7,15},{8,0},{9,1},... | collective-permute-start | bytes 49160 | tf_op jit(solution)/shard_map/ppermute | solution.py:47
  5.2 4.8 %collective-permute-start.4 = (bf16[2,4,1024]{2,1,0:T(4,128)(2,1)S(1)}, bf16[2,4,1024]{2,1,0:T(4,128)(2,1)S(1)}, u32[]{:S(2)}, u32[]{:S(2)}) collective-permute-start(bf16[2,4,1024]{2,1,0:T(4,128)(2,1)S(1)} %shard_map.75), channel_id=1, source_target_pairs={{0,12},{1,13},{2,14},{3,15},{4,8},{5,9},{6,10},{7,11},{8,4},{9,5},... | collective-permute-start | bytes 49160 | tf_op jit(solution)/shard_map/ppermute | solution.py:47
  8.0 5.0 %collective-permute-start.3 = (bf16[2,4,1024]{2,1,0:T(4,128)(2,1)S(1)}, bf16[2,4,1024]{2,1,0:T(4,128)(2,1)S(1)}, u32[]{:S(2)}, u32[]{:S(2)}) collective-permute-start(bf16[2,4,1024]{2,1,0:T(4,128)(2,1)S(1)} %shard_map.75), channel_id=1, source_target_pairs={{0,14},{1,15},{2,12},{3,13},{4,10},{5,11},{6,8},{7,9},{8,6},{9,7},... | collective-permute-start | bytes 49160 | tf_op jit(solution)/shard_map/ppermute | solution.py:47
  9.1 4.5 %collective-permute-start.2 = (bf16[2,4,1024]{2,1,0:T(4,128)(2,1)S(1)}, bf16[2,4,1024]{2,1,0:T(4,128)(2,1)S(1)}, u32[]{:S(2)}, u32[]{:S(2)}) collective-permute-start(bf16[2,4,1024]{2,1,0:T(4,128)(2,1)S(1)} %shard_map.75), channel_id=1, source_target_pairs={{0,10},{1,11},{2,8},{3,9},{4,14},{5,15},{6,12},{7,13},{8,2},{9,3},... | collective-permute-start | bytes 49160 | tf_op jit(solution)/shard_map/ppermute | solution.py:47
  10.7 10.2 %copy-start.1 = (bf16[4,128,2048]{2,1,0:T(8,128)(2,1)S(1)}, bf16[4,128,2048]{2,1,0:T(8,128)(2,1)}, u32[]{:S(2)}) copy-start(bf16[4,128,2048]{2,1,0:T(8,128)(2,1)} %cache_ref.7) | copy-start | bytes 6291460
  10.7 10.2 %copy-start.2 = (bf16[4,64,2048]{2,1,0:T(8,128)(2,1)S(1)}, bf16[4,64,2048]{2,1,0:T(8,128)(2,1)}, u32[]{:S(2)}) copy-start(bf16[4,64,2048]{2,1,0:T(8,128)(2,1)} %fresh_ref.7) | copy-start | bytes 3145732
  13.0 20.3 %slice-start = ((s8[16777216]{0:T(1024)(128)(4,1)}), s8[4194304]{0:T(1024)(128)(4,1)S(1)}, s32[]{:S(2)}) async-start(s8[16777216]{0:T(1024)(128)(4,1)} %bitcast), calls=%async_computation | async-start | bytes 8388608
  13.0 20.3 %slice-start.1 = ((s8[16777216]{0:T(1024)(128)(4,1)}), s8[4194304]{0:T(1024)(128)(4,1)S(1)}, s32[]{:S(2)}) async-start(s8[16777216]{0:T(1024)(128)(4,1)} %bitcast), calls=%async_computation.1 | async-start | bytes 8388608
  13.7 19.6 %slice-start.2 = ((s8[16777216]{0:T(1024)(128)(4,1)}), s8[4194304]{0:T(1024)(128)(4,1)S(1)}, s32[]{:S(2)}) async-start(s8[16777216]{0:T(1024)(128)(4,1)} %bitcast), calls=%async_computation.2 | async-start | bytes 8388608
  14.3 3.1 %collective-permute-start.7 = (bf16[32,128]{1,0:T(8,128)(2,1)S(1)}, bf16[32,128]{1,0:T(8,128)(2,1)S(1)}, u32[]{:S(2)}, u32[]{:S(2)}) collective-permute-start(bf16[32,128]{1,0:T(8,128)(2,1)S(1)} %shard_map.79), channel_id=1, source_target_pairs={{0,9},{1,8},{2,11},{3,10},{4,13},{5,12},{6,15},{7,14},{8,1},{9,0},... | collective-permute-start | bytes 24584 | tf_op jit(solution)/shard_map/ppermute | solution.py:47
  15.7 1.7 %collective-permute-start.6 = (bf16[32,128]{1,0:T(8,128)(2,1)S(1)}, bf16[32,128]{1,0:T(8,128)(2,1)S(1)}, u32[]{:S(2)}, u32[]{:S(2)}) collective-permute-start(bf16[32,128]{1,0:T(8,128)(2,1)S(1)} %shard_map.79), channel_id=1, source_target_pairs={{0,8},{1,9},{2,10},{3,11},{4,12},{5,13},{6,14},{7,15},{8,0},{9,1},... | collective-permute-start | bytes 24584 | tf_op jit(solution)/shard_map/ppermute | solution.py:47
  17.4 15.9 %slice-start.3 = ((s8[16777216]{0:T(1024)(128)(4,1)}), s8[4194304]{0:T(1024)(128)(4,1)S(1)}, s32[]{:S(2)}) async-start(s8[16777216]{0:T(1024)(128)(4,1)} %bitcast), calls=%async_computation.3 | async-start | bytes 8388608
  17.4 3.4 %collective-permute-start.8 = (bf16[2,32,128]{2,1,0:T(8,128)(2,1)S(1)}, bf16[2,32,128]{2,1,0:T(8,128)(2,1)S(1)}, u32[]{:S(2)}, u32[]{:S(2)}) collective-permute-start(bf16[2,32,128]{2,1,0:T(8,128)(2,1)S(1)} %shard_map.80), channel_id=1, source_target_pairs={{0,10},{1,11},{2,8},{3,9},{4,14},{5,15},{6,12},{7,13},{8,2},{9,3},... | collective-permute-start | bytes 49160 | tf_op jit(solution)/shard_map/ppermute | solution.py:47
  17.5 5.1 %collective-permute-start.10 = (bf16[2,32,128]{2,1,0:T(8,128)(2,1)S(1)}, bf16[2,32,128]{2,1,0:T(8,128)(2,1)S(1)}, u32[]{:S(2)}, u32[]{:S(2)}) collective-permute-start(bf16[2,32,128]{2,1,0:T(8,128)(2,1)S(1)} %shard_map.80), channel_id=1, source_target_pairs={{0,14},{1,15},{2,12},{3,13},{4,10},{5,11},{6,8},{7,9},{8,6},{9,7},... | collective-permute-start | bytes 49160 | tf_op jit(solution)/shard_map/ppermute | solution.py:47
  19.2 5.6 %collective-permute-start.12 = (bf16[2,32,128]{2,1,0:T(8,128)(2,1)S(1)}, bf16[2,32,128]{2,1,0:T(8,128)(2,1)S(1)}, u32[]{:S(2)}, u32[]{:S(2)}) collective-permute-start(bf16[2,32,128]{2,1,0:T(8,128)(2,1)S(1)} %shard_map.80), channel_id=1, source_target_pairs={{0,12},{1,13},{2,14},{3,15},{4,8},{5,9},{6,10},{7,11},{8,4},{9,5},... | collective-permute-start | bytes 49160 | tf_op jit(solution)/shard_map/ppermute | solution.py:47
  20.5 5.4 %collective-permute-start.14 = (bf16[2,32,128]{2,1,0:T(8,128)(2,1)S(1)}, bf16[2,32,128]{2,1,0:T(8,128)(2,1)S(1)}, u32[]{:S(2)}, u32[]{:S(2)}) collective-permute-start(bf16[2,32,128]{2,1,0:T(8,128)(2,1)S(1)} %shard_map.80), channel_id=1, source_target_pairs={{0,8},{1,9},{2,10},{3,11},{4,12},{5,13},{6,14},{7,15},{8,0},{9,1},... | collective-permute-start | bytes 49160 | tf_op jit(solution)/shard_map/ppermute | solution.py:47
  21.5 5.4 %collective-permute-start.9 = (bf16[2,40,128]{2,1,0:T(8,128)(2,1)S(1)}, bf16[2,40,128]{2,1,0:T(8,128)(2,1)S(1)}, u32[]{:S(2)}, u32[]{:S(2)}) collective-permute-start(bf16[2,40,128]{2,1,0:T(8,128)(2,1)S(1)} %shard_map.81), channel_id=1, source_target_pairs={{0,10},{1,11},{2,8},{3,9},{4,14},{5,15},{6,12},{7,13},{8,2},{9,3},... | collective-permute-start | bytes 61448 | tf_op jit(solution)/shard_map/ppermute | solution.py:47
  23.2 5.1 %collective-permute-start.11 = (bf16[2,40,128]{2,1,0:T(8,128)(2,1)S(1)}, bf16[2,40,128]{2,1,0:T(8,128)(2,1)S(1)}, u32[]{:S(2)}, u32[]{:S(2)}) collective-permute-start(bf16[2,40,128]{2,1,0:T(8,128)(2,1)S(1)} %shard_map.82), channel_id=1, source_target_pairs={{0,14},{1,15},{2,12},{3,13},{4,10},{5,11},{6,8},{7,9},{8,6},{9,7},... | collective-permute-start | bytes 61448 | tf_op jit(solution)/shard_map/ppermute | solution.py:47
  25.4 4.2 %collective-permute-start.13 = (bf16[2,40,128]{2,1,0:T(8,128)(2,1)S(1)}, bf16[2,40,128]{2,1,0:T(8,128)(2,1)S(1)}, u32[]{:S(2)}, u32[]{:S(2)}) collective-permute-start(bf16[2,40,128]{2,1,0:T(8,128)(2,1)S(1)} %shard_map.83), channel_id=1, source_target_pairs={{0,12},{1,13},{2,14},{3,15},{4,8},{5,9},{6,10},{7,11},{8,4},{9,5},... | collective-permute-start | bytes 61448 | tf_op jit(solution)/shard_map/ppermute | solution.py:47
  26.5 3.1 %collective-permute-start.15 = (bf16[2,40,128]{2,1,0:T(8,128)(2,1)S(1)}, bf16[2,40,128]{2,1,0:T(8,128)(2,1)S(1)}, u32[]{:S(2)}, u32[]{:S(2)}) collective-permute-start(bf16[2,40,128]{2,1,0:T(8,128)(2,1)S(1)} %shard_map.84), channel_id=1, source_target_pairs={{0,8},{1,9},{2,10},{3,11},{4,12},{5,13},{6,14},{7,15},{8,0},{9,1},... | collective-permute-start | bytes 61448 | tf_op jit(solution)/shard_map/ppermute | solution.py:47
  29.6 1.8 %collective-permute-start.16 = (bf16[4,40,128]{2,1,0:T(8,128)(2,1)S(1)}, bf16[4,40,128]{2,1,0:T(8,128)(2,1)S(1)}, u32[]{:S(2)}, u32[]{:S(2)}) collective-permute-start(bf16[4,40,128]{2,1,0:T(8,128)(2,1)S(1)} %get-tuple-element.11), channel_id=1, source_target_pairs={{0,8},{1,9},{2,10},{3,11},{4,12},{5,13},{6,14},{7,15},{8,0},{9,1},... | collective-permute-start | bytes 122888 | tf_op jit(solution)/shard_map/ppermute | solution.py:47
  29.9 3.4 %collective-permute-start.17 = (bf16[4,40,128]{2,1,0:T(8,128)(2,1)S(1)}, bf16[4,40,128]{2,1,0:T(8,128)(2,1)S(1)}, u32[]{:S(2)}, u32[]{:S(2)}) collective-permute-start(bf16[4,40,128]{2,1,0:T(8,128)(2,1)S(1)} %get-tuple-element.12), channel_id=1, source_target_pairs={{0,9},{1,8},{2,11},{3,10},{4,13},{5,12},{6,15},{7,14},{8,1},{9,0},... | collective-permute-start | bytes 122888 | tf_op jit(solution)/shard_map/ppermute | solution.py:47
  34.2 5.3 %collective-permute-start.18 = (bf16[2,4,1024]{2,1,0:T(4,128)(2,1)S(1)}, bf16[2,4,1024]{2,1,0:T(4,128)(2,1)S(1)}, u32[]{:S(2)}, u32[]{:S(2)}) collective-permute-start(bf16[2,4,1024]{2,1,0:T(4,128)(2,1)S(1)} %get-tuple-element.13), channel_id=1, source_target_pairs={{0,12},{1,13},{2,14},{3,15},{4,8},{5,9},{6,10},{7,11},{8,4},{9,5},... | collective-permute-start | bytes 49160 | tf_op jit(solution)/shard_map/ppermute | solution.py:47
  35.4 5.0 %collective-permute-start.19 = (bf16[2,4,1024]{2,1,0:T(4,128)(2,1)S(1)}, bf16[2,4,1024]{2,1,0:T(4,128)(2,1)S(1)}, u32[]{:S(2)}, u32[]{:S(2)}) collective-permute-start(bf16[2,4,1024]{2,1,0:T(4,128)(2,1)S(1)} %shard_map.88), channel_id=1, source_target_pairs={{0,14},{1,15},{2,12},{3,13},{4,10},{5,11},{6,8},{7,9},{8,6},{9,7},... | collective-permute-start | bytes 49160 | tf_op jit(solution)/shard_map/ppermute | solution.py:47
  38.0 3.2 %collective-permute-start.20 = (bf16[2,4,1024]{2,1,0:T(4,128)(2,1)S(1)}, bf16[2,4,1024]{2,1,0:T(4,128)(2,1)S(1)}, u32[]{:S(2)}, u32[]{:S(2)}) collective-permute-start(bf16[2,4,1024]{2,1,0:T(4,128)(2,1)S(1)} %shard_map.90), channel_id=1, source_target_pairs={{0,10},{1,11},{2,8},{3,9},{4,14},{5,15},{6,12},{7,13},{8,2},{9,3},... | collective-permute-start | bytes 49160 | tf_op jit(solution)/shard_map/ppermute | solution.py:47
  39.4 1.8 %collective-permute-start.21 = (bf16[2,4,1024]{2,1,0:T(4,128)(2,1)S(1)}, bf16[2,4,1024]{2,1,0:T(4,128)(2,1)S(1)}, u32[]{:S(2)}, u32[]{:S(2)}) collective-permute-start(bf16[2,4,1024]{2,1,0:T(4,128)(2,1)S(1)} %shard_map.92), channel_id=1, source_target_pairs={{0,8},{1,9},{2,10},{3,11},{4,12},{5,13},{6,14},{7,15},{8,0},{9,1},... | collective-permute-start | bytes 49160 | tf_op jit(solution)/shard_map/ppermute | solution.py:47
  41.2 3.5 %collective-permute-start.22 = (f32[4,1024]{1,0:T(4,128)S(1)}, f32[4,1024]{1,0:T(4,128)S(1)}, u32[]{:S(2)}, u32[]{:S(2)}) collective-permute-start(f32[4,1024]{1,0:T(4,128)S(1)} %get-tuple-element.15), channel_id=1, source_target_pairs={{0,8},{1,9},{2,10},{3,11},{4,12},{5,13},{6,14},{7,15},{8,0},{9,1},... | collective-permute-start | bytes 49160 | tf_op jit(solution)/shard_map/ppermute | solution.py:47
  41.6 3.1 %collective-permute-start.23 = (bf16[4,1024]{1,0:T(4,128)(2,1)S(1)}, bf16[4,1024]{1,0:T(4,128)(2,1)S(1)}, u32[]{:S(2)}, u32[]{:S(2)}) collective-permute-start(bf16[4,1024]{1,0:T(4,128)(2,1)S(1)} %get-tuple-element.16), channel_id=1, source_target_pairs={{0,9},{1,8},{2,11},{3,10},{4,13},{5,12},{6,15},{7,14},{8,1},{9,0},... | collective-permute-start | bytes 24584 | tf_op jit(solution)/shard_map/ppermute | solution.py:47

commit v13 on v12

--- a/solution.py
+++ b/solution.py
@@ -18,7 +18,7 @@
 SMEM = pl.BlockSpec(memory_space=pltpu.SMEM)
 BOTH = ("section", "tensor")
 SPLIT_OUTPUT = False
-ORDER = (4, 6, 2)
+ORDER = (2, 6, 4)
 MIDDLE = (2, 6, 4)
 LIMIT = 10**7
 BACK = (4, 6, 2)

time: 45.5 us -> 45.6 us (level)
  transfers between devices with their start and end apart: 24 -> 24, of which waited for: 11 -> 12; matrix products, arithmetic and copies ran while one was open for 0% -> 0% of each run, Pallas kernels for 15% -> 15%
where the time goes in v13:
time: 45.6 us; the launch traced here: 45.4 us
  starting transfers between devices  23.4 us (51%)
  waiting for transfers between devices  12.1 us (27%)
  Pallas kernels  9.12 us (20%)
  local copies, waits for them, and re-layouts  0.73 us (2%)
    ppermute x24, starting transfers between devices, flip(): lax.ppermute(x, BOTH, [(i, (i // n ^ 1) * n + (i % n ^ apart)) for i in r...  23.4 us
    ppermute x24, waiting for transfers between devices, flip(): lax.ppermute(x, BOTH, [(i, (i // n ^ 1) * n + (i % n ^ apart)) for i in r...  12.1 us
    pallas_call x22, Pallas kernels, call(): pl.pallas_call(kernel, in_specs=specs or [VMEM] * len(args), out_specs=ou...  9.12 us
  transfers between devices with their start and end apart: 24, of which 12 were waited for; matrix products, arithmetic and copies ran while one was open for 0% of the time, Pallas kernels for 15%

profile of v13, /device:TPU:0, one launch (start us, length us, event | category | flops | bytes accessed | tf_op | source)
XLA Modules:
  0.0 45.4 jit_solution(13809087372167949805)
XLA Ops:
  0.0 0.7 %copy-done.3 = bf16[4,1024]{1,0:T(4,128)(2,1)S(1)} copy-done((bf16[4,1024]{1,0:T(4,128)(2,1)S(1)}, bf16[4,1024]{1,0:T(4,128)(2,1)}, u32[]{:S(2)}) %copy-start.3) | copy-done | bytes 8216
  0.7 2.5 %collective-permute-start.1 = (bf16[4,1024]{1,0:T(4,128)(2,1)S(1)}, bf16[4,1024]{1,0:T(4,128)(2,1)S(1)}, u32[]{:S(2)}, u32[]{:S(2)}) collective-permute-start(bf16[4,1024]{1,0:T(4,128)(2,1)S(1)} %shard_map.74), channel_id=1, source_target_pairs={{0,9},{1,8},{2,11},{3,10},{4,13},{5,12},{6,15},{7,14},{8,1},{9,0},... | collective-permute-start | bytes 24584 | tf_op jit(solution)/shard_map/ppermute | solution.py:47
  3.2 0.7 %collective-permute-start = (bf16[4,1024]{1,0:T(4,128)(2,1)S(1)}, bf16[4,1024]{1,0:T(4,128)(2,1)S(1)}, u32[]{:S(2)}, u32[]{:S(2)}) collective-permute-start(bf16[4,1024]{1,0:T(4,128)(2,1)S(1)} %shard_map.74), channel_id=1, source_target_pairs={{0,8},{1,9},{2,10},{3,11},{4,12},{5,13},{6,14},{7,15},{8,0},{9,1},... | collective-permute-start | bytes 24584 | tf_op jit(solution)/shard_map/ppermute | solution.py:47
  3.9 0.6 %shard_map.73._.limit_ref = s32[2,64]{1,0:T(2,128)S(1)} custom-call(s32[4]{0:T(128)S(1)} %copy-done.4, s32[4]{0:T(128)S(1)} %copy-done.5), custom_call_target="tpu_custom_call" | custom-call | flops 10000000 | tf_op jit(solution)/shard_map/pallas_call | solution.py:56
  4.4 0.1 collective-permute-done.1.y_ref
  4.5 0.1 collective-permute-done.x_ref
  4.7 0.5 %collective-permute-start.5 = (bf16[2,4,1024]{2,1,0:T(4,128)(2,1)S(1)}, bf16[2,4,1024]{2,1,0:T(4,128)(2,1)S(1)}, u32[]{:S(2)}, u32[]{:S(2)}) collective-permute-start(bf16[2,4,1024]{2,1,0:T(4,128)(2,1)S(1)} %shard_map.75), channel_id=1, source_target_pairs={{0,8},{1,9},{2,10},{3,11},{4,12},{5,13},{6,14},{7,15},{8,0},{9,1},... | collective-permute-start | bytes 49160 | tf_op jit(solution)/shard_map/ppermute | solution.py:47
  5.2 1.8 %collective-permute-start.4 = (bf16[2,4,1024]{2,1,0:T(4,128)(2,1)S(1)}, bf16[2,4,1024]{2,1,0:T(4,128)(2,1)S(1)}, u32[]{:S(2)}, u32[]{:S(2)}) collective-permute-start(bf16[2,4,1024]{2,1,0:T(4,128)(2,1)S(1)} %shard_map.75), channel_id=1, source_target_pairs={{0,10},{1,11},{2,8},{3,9},{4,14},{5,15},{6,12},{7,13},{8,2},{9,3},... | collective-permute-start | bytes 49160 | tf_op jit(solution)/shard_map/ppermute | solution.py:47
  7.0 2.2 %collective-permute-start.3 = (bf16[2,4,1024]{2,1,0:T(4,128)(2,1)S(1)}, bf16[2,4,1024]{2,1,0:T(4,128)(2,1)S(1)}, u32[]{:S(2)}, u32[]{:S(2)}) collective-permute-start(bf16[2,4,1024]{2,1,0:T(4,128)(2,1)S(1)} %shard_map.75), channel_id=1, source_target_pairs={{0,14},{1,15},{2,12},{3,13},{4,10},{5,11},{6,8},{7,9},{8,6},{9,7},... | collective-permute-start | bytes 49160 | tf_op jit(solution)/shard_map/ppermute | solution.py:47
  9.2 0.1 collective-permute-start.2
  9.4 0.0 collective-permute-done.5.x_ref
  9.4 0.0 copy-done
  9.4 0.7 %shard_map.76.old_ref = f32[4,1024]{1,0:T(4,128)S(1)} custom-call(bf16[2,4,1024]{2,1,0:T(4,128)(2,1)S(1)} %collective-permute-done.5.x_ref, bf16[8192,1024]{1,0:T(8,128)(2,1)S(1)} %copy-done), custom_call_target="tpu_custom_call" | custom-call | tf_op jit(solution)/shard_map/pallas_call | solution.py:56
  10.0 0.0 collective-permute-done.4.x_ref
  10.0 0.7 %shard_map.77.old_ref = f32[4,1024]{1,0:T(4,128)S(1)} custom-call(bf16[2,4,1024]{2,1,0:T(4,128)(2,1)S(1)} %collective-permute-done.4.x_ref, bf16[8192,1024]{1,0:T(8,128)(2,1)S(1)} %copy-done, f32[4,1024]{1,0:T(4,128)S(1)} %shard_map.76.old_ref), custom_call_target="tpu_custom_call" | custom-call | flops 10000000000 | tf_op jit(solution)/shard_map/pallas_call | solution.py:56
  10.7 1.3 %collective-permute-done.3.x_ref = bf16[2,4,1024]{2,1,0:T(4,128)(2,1)S(1)} collective-permute-done((bf16[2,4,1024]{2,1,0:T(4,128)(2,1)S(1)}, bf16[2,4,1024]{2,1,0:T(4,128)(2,1)S(1)}, u32[]{:S(2)}, u32[]{:S(2)}) %collective-permute-start.3) | collective-permute-done | bytes 16416 | tf_op jit(solution)/shard_map/ppermute | solution.py:47
  12.0 0.7 %shard_map.78.old_ref = f32[4,1024]{1,0:T(4,128)S(1)} custom-call(bf16[2,4,1024]{2,1,0:T(4,128)(2,1)S(1)} %collective-permute-done.3.x_ref, bf16[8192,1024]{1,0:T(8,128)(2,1)S(1)} %copy-done, f32[4,1024]{1,0:T(4,128)S(1)} %shard_map.77.old_ref), custom_call_target="tpu_custom_call" | custom-call | tf_op jit(solution)/shard_map/pallas_call | solution.py:56
  12.6 0.7 %collective-permute-done.2.x_ref = bf16[2,4,1024]{2,1,0:T(4,128)(2,1)S(1)} collective-permute-done((bf16[2,4,1024]{2,1,0:T(4,128)(2,1)S(1)}, bf16[2,4,1024]{2,1,0:T(4,128)(2,1)S(1)}, u32[]{:S(2)}, u32[]{:S(2)}) %collective-permute-start.2) | collective-permute-done | bytes 16416 | tf_op jit(solution)/shard_map/ppermute | solution.py:47
  13.3 0.7 %shard_map.79 = bf16[32,128]{1,0:T(8,128)(2,1)S(1)} custom-call(bf16[2,4,1024]{2,1,0:T(4,128)(2,1)S(1)} %collective-permute-done.2.x_ref, bf16[8192,1024]{1,0:T(8,128)(2,1)S(1)} %copy-done, f32[4,1024]{1,0:T(4,128)S(1)} %shard_map.78.old_ref), custom_call_target="tpu_custom_call" | custom-call | tf_op jit(solution)/shard_map/pallas_call | solution.py:56
  14.0 1.7 %collective-permute-start.7 = (bf16[32,128]{1,0:T(8,128)(2,1)S(1)}, bf16[32,128]{1,0:T(8,128)(2,1)S(1)}, u32[]{:S(2)}, u32[]{:S(2)}) collective-permute-start(bf16[32,128]{1,0:T(8,128)(2,1)S(1)} %shard_map.79), channel_id=1, source_target_pairs={{0,9},{1,8},{2,11},{3,10},{4,13},{5,12},{6,15},{7,14},{8,1},{9,0},... | collective-permute-start | bytes 24584 | tf_op jit(solution)/shard_map/ppermute | solution.py:47
  15.7 0.0 collective-permute-start.6
  15.7 1.4 %collective-permute-done.7.y_ref = bf16[32,128]{1,0:T(8,128)(2,1)S(1)} collective-permute-done((bf16[32,128]{1,0:T(8,128)(2,1)S(1)}, bf16[32,128]{1,0:T(8,128)(2,1)S(1)}, u32[]{:S(2)}, u32[]{:S(2)}) %collective-permute-start.7) | collective-permute-done | bytes 8224 | tf_op jit(solution)/shard_map/ppermute | solution.py:47
  17.1 0.0 collective-permute-done.6.x_ref
  17.1 0.7 %collective-permute-start.8 = (bf16[2,32,128]{2,1,0:T(8,128)(2,1)S(1)}, bf16[2,32,128]{2,1,0:T(8,128)(2,1)S(1)}, u32[]{:S(2)}, u32[]{:S(2)}) collective-permute-start(bf16[2,32,128]{2,1,0:T(8,128)(2,1)S(1)} %shard_map.80), channel_id=1, source_target_pairs={{0,10},{1,11},{2,8},{3,9},{4,14},{5,15},{6,12},{7,13},{8,2},{9,3},... | collective-permute-start | bytes 49160 | tf_op jit(solution)/shard_map/ppermute | solution.py:47
  17.8 1.4 %collective-permute-start.10 = (bf16[2,32,128]{2,1,0:T(8,128)(2,1)S(1)}, bf16[2,32,128]{2,1,0:T(8,128)(2,1)S(1)}, u32[]{:S(2)}, u32[]{:S(2)}) collective-permute-start(bf16[2,32,128]{2,1,0:T(8,128)(2,1)S(1)} %shard_map.80), channel_id=1, source_target_pairs={{0,14},{1,15},{2,12},{3,13},{4,10},{5,11},{6,8},{7,9},{8,6},{9,7},... | collective-permute-start | bytes 49160 | tf_op jit(solution)/shard_map/ppermute | solution.py:47
  19.2 1.3 %collective-permute-start.12 = (bf16[2,32,128]{2,1,0:T(8,128)(2,1)S(1)}, bf16[2,32,128]{2,1,0:T(8,128)(2,1)S(1)}, u32[]{:S(2)}, u32[]{:S(2)}) collective-permute-start(bf16[2,32,128]{2,1,0:T(8,128)(2,1)S(1)} %shard_map.80), channel_id=1, source_target_pairs={{0,12},{1,13},{2,14},{3,15},{4,8},{5,9},{6,10},{7,11},{8,4},{9,5},... | collective-permute-start | bytes 49160 | tf_op jit(solution)/shard_map/ppermute | solution.py:47
  20.5 0.0 collective-permute-start.14
  20.5 0.0 collective-permute-done.8.q_ref
  20.5 0.6 %shard_map.81 = bf16[2,40,128]{2,1,0:T(8,128)(2,1)S(1)} custom-call(s32[2,64]{1,0:T(2,128)S(1)} %shard_map.73._.limit_ref, bf16[2,32,128]{2,1,0:T(8,128)(2,1)S(1)} %collective-permute-done.8.q_ref, bf16[4,128,2048]{2,1,0:T(8,128)(2,1)S(1)} %copy-done.1, bf16[4,64,2048]{2,1,0:T(8,128)(2,1)S(1)} %copy-done.2), custom_call_target="tpu_custom_call" | custom-call | flops 11500000 | tf_op jit(solution)/shard_map/pallas_call | solution.py:56
  21.1 1.6 %collective-permute-start.9 = (bf16[2,40,128]{2,1,0:T(8,128)(2,1)S(1)}, bf16[2,40,128]{2,1,0:T(8,128)(2,1)S(1)}, u32[]{:S(2)}, u32[]{:S(2)}) collective-permute-start(bf16[2,40,128]{2,1,0:T(8,128)(2,1)S(1)} %shard_map.81), channel_id=1, source_target_pairs={{0,10},{1,11},{2,8},{3,9},{4,14},{5,15},{6,12},{7,13},{8,2},{9,3},... | collective-permute-start | bytes 61448 | tf_op jit(solution)/shard_map/ppermute | solution.py:47
  22.7 0.1 collective-permute-done.10.q_ref
  22.7 0.6 %shard_map.82 = bf16[2,40,128]{2,1,0:T(8,128)(2,1)S(1)} custom-call(s32[2,64]{1,0:T(2,128)S(1)} %shard_map.73._.limit_ref, bf16[2,32,128]{2,1,0:T(8,128)(2,1)S(1)} %collective-permute-done.10.q_ref, bf16[4,128,2048]{2,1,0:T(8,128)(2,1)S(1)} %copy-done.1, bf16[4,64,2048]{2,1,0:T(8,128)(2,1)S(1)} %copy-done.2), custom_call_target="tpu_custom_call" | custom-call | flops 11500000 | tf_op jit(solution)/shard_map/pallas_call | solution.py:56
  23.3 1.5 %collective-permute-start.11 = (bf16[2,40,128]{2,1,0:T(8,128)(2,1)S(1)}, bf16[2,40,128]{2,1,0:T(8,128)(2,1)S(1)}, u32[]{:S(2)}, u32[]{:S(2)}) collective-permute-start(bf16[2,40,128]{2,1,0:T(8,128)(2,1)S(1)} %shard_map.82), channel_id=1, source_target_pairs={{0,14},{1,15},{2,12},{3,13},{4,10},{5,11},{6,8},{7,9},{8,6},{9,7},... | collective-permute-start | bytes 61448 | tf_op jit(solution)/shard_map/ppermute | solution.py:47
  24.8 0.0 collective-permute-done.12.q_ref
  24.8 0.6 %shard_map.83 = bf16[2,40,128]{2,1,0:T(8,128)(2,1)S(1)} custom-call(s32[2,64]{1,0:T(2,128)S(1)} %shard_map.73._.limit_ref, bf16[2,32,128]{2,1,0:T(8,128)(2,1)S(1)} %collective-permute-done.12.q_ref, bf16[4,128,2048]{2,1,0:T(8,128)(2,1)S(1)} %copy-done.1, bf16[4,64,2048]{2,1,0:T(8,128)(2,1)S(1)} %copy-done.2), custom_call_target="tpu_custom_call" | custom-call | flops 11500000 | tf_op jit(solution)/shard_map/pallas_call | solution.py:56
  25.4 0.4 collective-permute-start.13
  25.8 0.0 collective-permute-done.14.q_ref
  25.8 0.6 %shard_map.84 = bf16[2,40,128]{2,1,0:T(8,128)(2,1)S(1)} custom-call(s32[2,64]{1,0:T(2,128)S(1)} %shard_map.73._.limit_ref, bf16[2,32,128]{2,1,0:T(8,128)(2,1)S(1)} %collective-permute-done.14.q_ref, bf16[4,128,2048]{2,1,0:T(8,128)(2,1)S(1)} %copy-done.1, bf16[4,64,2048]{2,1,0:T(8,128)(2,1)S(1)} %copy-done.2), custom_call_target="tpu_custom_call" | custom-call | flops 11500000 | tf_op jit(solution)/shard_map/pallas_call | solution.py:56
  26.5 0.1 collective-permute-start.15
  26.5 0.0 collective-permute-done.9.a_ref
  26.5 1.9 %collective-permute-done.11.b_ref = bf16[2,40,128]{2,1,0:T(8,128)(2,1)S(1)} collective-permute-done((bf16[2,40,128]{2,1,0:T(8,128)(2,1)S(1)}, bf16[2,40,128]{2,1,0:T(8,128)(2,1)S(1)}, u32[]{:S(2)}, u32[]{:S(2)}) %collective-permute-start.11) | collective-permute-done | bytes 20512 | tf_op jit(solution)/shard_map/ppermute | solution.py:47
  28.4 1.3 %collective-permute-done.13.c_ref = bf16[2,40,128]{2,1,0:T(8,128)(2,1)S(1)} collective-permute-done((bf16[2,40,128]{2,1,0:T(8,128)(2,1)S(1)}, bf16[2,40,128]{2,1,0:T(8,128)(2,1)S(1)}, u32[]{:S(2)}, u32[]{:S(2)}) %collective-permute-start.13) | collective-permute-done | bytes 20512 | tf_op jit(solution)/shard_map/ppermute | solution.py:47
  29.7 0.0 collective-permute-done.15.d_ref
  29.7 0.2 collective-permute-start.16
  29.9 1.6 %collective-permute-start.17 = (bf16[4,40,128]{2,1,0:T(8,128)(2,1)S(1)}, bf16[4,40,128]{2,1,0:T(8,128)(2,1)S(1)}, u32[]{:S(2)}, u32[]{:S(2)}) collective-permute-start(bf16[4,40,128]{2,1,0:T(8,128)(2,1)S(1)} %get-tuple-element.12), channel_id=1, source_target_pairs={{0,9},{1,8},{2,11},{3,10},{4,13},{5,12},{6,15},{7,14},{8,1},{9,0},... | collective-permute-start | bytes 122888 | tf_op jit(solution)/shard_map/ppermute | solution.py:47
  31.5 0.0 collective-permute-done.16.a_ref
  31.5 1.9 %collective-permute-done.17.b_ref = bf16[4,40,128]{2,1,0:T(8,128)(2,1)S(1)} collective-permute-done((bf16[4,40,128]{2,1,0:T(8,128)(2,1)S(1)}, bf16[4,40,128]{2,1,0:T(8,128)(2,1)S(1)}, u32[]{:S(2)}, u32[]{:S(2)}) %collective-permute-start.17) | collective-permute-done | bytes 40992 | tf_op jit(solution)/shard_map/ppermute | solution.py:47
  33.4 0.9 %shard_map.86 = (bf16[2,4,1024]{2,1,0:T(4,128)(2,1)S(1)}, bf16[4,1024]{1,0:T(4,128)(2,1)S(1)}) custom-call(bf16[4,40,128]{2,1,0:T(8,128)(2,1)S(1)} %collective-permute-done.16.a_ref, bf16[4,40,128]{2,1,0:T(8,128)(2,1)S(1)} %collective-permute-done.17.b_ref, bf16[1024,8192]{1,0:T(8,128)(2,1)S(1)} %bitcast.1), custom_call_target="tpu_custom_call" | custom-call | flops 11500000 | tf_op jit(solution)/shard_map/pallas_call | solution.py:56
  34.3 0.4 collective-permute-start.18
  34.7 0.7 %shard_map.88 = bf16[2,4,1024]{2,1,0:T(4,128)(2,1)S(1)} custom-call(bf16[4,1024]{1,0:T(4,128)(2,1)S(1)} %get-tuple-element.14.context_ref, bf16[1024,8192]{1,0:T(8,128)(2,1)S(1)} %bitcast.1), custom_call_target="tpu_custom_call" | custom-call | flops 11500000 | tf_op jit(solution)/shard_map/pallas_call | solution.py:56
  35.4 2.1 %collective-permute-start.19 = (bf16[2,4,1024]{2,1,0:T(4,128)(2,1)S(1)}, bf16[2,4,1024]{2,1,0:T(4,128)(2,1)S(1)}, u32[]{:S(2)}, u32[]{:S(2)}) collective-permute-start(bf16[2,4,1024]{2,1,0:T(4,128)(2,1)S(1)} %shard_map.88), channel_id=1, source_target_pairs={{0,14},{1,15},{2,12},{3,13},{4,10},{5,11},{6,8},{7,9},{8,6},{9,7},... | collective-permute-start | bytes 49160 | tf_op jit(solution)/shard_map/ppermute | solution.py:47
  37.5 0.7 %shard_map.90 = bf16[2,4,1024]{2,1,0:T(4,128)(2,1)S(1)} custom-call(bf16[4,1024]{1,0:T(4,128)(2,1)S(1)} %get-tuple-element.14.context_ref, bf16[1024,8192]{1,0:T(8,128)(2,1)S(1)} %bitcast.1), custom_call_target="tpu_custom_call" | custom-call | flops 11500000 | tf_op jit(solution)/shard_map/pallas_call | solution.py:56
  38.2 0.7 %collective-permute-start.20 = (bf16[2,4,1024]{2,1,0:T(4,128)(2,1)S(1)}, bf16[2,4,1024]{2,1,0:T(4,128)(2,1)S(1)}, u32[]{:S(2)}, u32[]{:S(2)}) collective-permute-start(bf16[2,4,1024]{2,1,0:T(4,128)(2,1)S(1)} %shard_map.90), channel_id=1, source_target_pairs={{0,10},{1,11},{2,8},{3,9},{4,14},{5,15},{6,12},{7,13},{8,2},{9,3},... | collective-permute-start | bytes 49160 | tf_op jit(solution)/shard_map/ppermute | solution.py:47
  38.9 0.7 %shard_map.92 = bf16[2,4,1024]{2,1,0:T(4,128)(2,1)S(1)} custom-call(bf16[4,1024]{1,0:T(4,128)(2,1)S(1)} %get-tuple-element.14.context_ref, bf16[1024,8192]{1,0:T(8,128)(2,1)S(1)} %bitcast.1), custom_call_target="tpu_custom_call" | custom-call | flops 11500000 | tf_op jit(solution)/shard_map/pallas_call | solution.py:56
  39.5 0.2 collective-permute-start.21
  39.7 0.0 collective-permute-done.18.x_ref
  39.7 0.8 %collective-permute-done.19.y_ref = bf16[2,4,1024]{2,1,0:T(4,128)(2,1)S(1)} collective-permute-done((bf16[2,4,1024]{2,1,0:T(4,128)(2,1)S(1)}, bf16[2,4,1024]{2,1,0:T(4,128)(2,1)S(1)}, u32[]{:S(2)}, u32[]{:S(2)}) %collective-permute-start.19) | collective-permute-done | bytes 16416 | tf_op jit(solution)/shard_map/ppermute | solution.py:47
  40.5 0.8 %collective-permute-done.20.y_ref = bf16[2,4,1024]{2,1,0:T(4,128)(2,1)S(1)} collective-permute-done((bf16[2,4,1024]{2,1,0:T(4,128)(2,1)S(1)}, bf16[2,4,1024]{2,1,0:T(4,128)(2,1)S(1)}, u32[]{:S(2)}, u32[]{:S(2)}) %collective-permute-start.20) | collective-permute-done | bytes 16416 | tf_op jit(solution)/shard_map/ppermute | solution.py:47
  41.3 0.0 collective-permute-done.21.y_ref
  41.4 0.3 collective-permute-start.22
  41.7 1.4 %collective-permute-start.23 = (bf16[4,1024]{1,0:T(4,128)(2,1)S(1)}, bf16[4,1024]{1,0:T(4,128)(2,1)S(1)}, u32[]{:S(2)}, u32[]{:S(2)}) collective-permute-start(bf16[4,1024]{1,0:T(4,128)(2,1)S(1)} %get-tuple-element.16), channel_id=1, source_target_pairs={{0,9},{1,8},{2,11},{3,10},{4,13},{5,12},{6,15},{7,14},{8,1},{9,0},... | collective-permute-start | bytes 24584 | tf_op jit(solution)/shard_map/ppermute | solution.py:47
  43.1 1.7 %collective-permute-done.23.y_ref = bf16[4,1024]{1,0:T(4,128)(2,1)S(1)} collective-permute-done((bf16[4,1024]{1,0:T(4,128)(2,1)S(1)}, bf16[4,1024]{1,0:T(4,128)(2,1)S(1)}, u32[]{:S(2)}, u32[]{:S(2)}) %collective-permute-start.23) | collective-permute-done | bytes 8224 | tf_op jit(solution)/shard_map/ppermute | solution.py:47
  44.8 0.0 collective-permute-done.22.x_ref
  44.8 0.6 %shard_map.94 = bf16[4,1024]{1,0:T(4,128)(2,1)} custom-call(f32[4,1024]{1,0:T(4,128)S(1)} %collective-permute-done.22.x_ref, bf16[4,1024]{1,0:T(4,128)(2,1)S(1)} %collective-permute-done.23.y_ref), custom_call_target="tpu_custom_call" | custom-call | tf_op jit(solution)/shard_map/pallas_call | solution.py:56
  (27 shorter events, 0.1 us)
Async XLA Ops:
  0.0 0.7 %copy-start.3 = (bf16[4,1024]{1,0:T(4,128)(2,1)S(1)}, bf16[4,1024]{1,0:T(4,128)(2,1)}, u32[]{:S(2)}) copy-start(bf16[4,1024]{1,0:T(4,128)(2,1)} %x_ref.1) | copy-start | bytes 24580
  0.7 3.2 %copy-start.4 = (s32[4]{0:T(128)S(1)}, s32[4]{0:T(128)}, u32[]{:S(2)}) copy-start(s32[4]{0:T(128)} %clen_ref.1) | copy-start | bytes 52
  0.7 3.2 %copy-start.5 = (s32[4]{0:T(128)S(1)}, s32[4]{0:T(128)}, u32[]{:S(2)}) copy-start(s32[4]{0:T(128)} %nlen_ref.1) | copy-start | bytes 52
  0.7 8.7 %copy-start = (bf16[8192,1024]{1,0:T(8,128)(2,1)S(1)}, bf16[8192,1024]{1,0:T(8,128)(2,1)}, u32[]{:S(2)}) copy-start(bf16[8192,1024]{1,0:T(8,128)(2,1)} %w_ref.11) | copy-start | bytes 50331652
  0.7 3.8 %collective-permute-start.1 = (bf16[4,1024]{1,0:T(4,128)(2,1)S(1)}, bf16[4,1024]{1,0:T(4,128)(2,1)S(1)}, u32[]{:S(2)}, u32[]{:S(2)}) collective-permute-start(bf16[4,1024]{1,0:T(4,128)(2,1)S(1)} %shard_map.74), channel_id=1, source_target_pairs={{0,9},{1,8},{2,11},{3,10},{4,13},{5,12},{6,15},{7,14},{8,1},{9,0},... | collective-permute-start | bytes 24584 | tf_op jit(solution)/shard_map/ppermute | solution.py:47
  3.2 1.5 %collective-permute-start = (bf16[4,1024]{1,0:T(4,128)(2,1)S(1)}, bf16[4,1024]{1,0:T(4,128)(2,1)S(1)}, u32[]{:S(2)}, u32[]{:S(2)}) collective-permute-start(bf16[4,1024]{1,0:T(4,128)(2,1)S(1)} %shard_map.74), channel_id=1, source_target_pairs={{0,8},{1,9},{2,10},{3,11},{4,12},{5,13},{6,14},{7,15},{8,0},{9,1},... | collective-permute-start | bytes 24584 | tf_op jit(solution)/shard_map/ppermute | solution.py:47
  4.7 4.7 %collective-permute-start.5 = (bf16[2,4,1024]{2,1,0:T(4,128)(2,1)S(1)}, bf16[2,4,1024]{2,1,0:T(4,128)(2,1)S(1)}, u32[]{:S(2)}, u32[]{:S(2)}) collective-permute-start(bf16[2,4,1024]{2,1,0:T(4,128)(2,1)S(1)} %shard_map.75), channel_id=1, source_target_pairs={{0,8},{1,9},{2,10},{3,11},{4,12},{5,13},{6,14},{7,15},{8,0},{9,1},... | collective-permute-start | bytes 49160 | tf_op jit(solution)/shard_map/ppermute | solution.py:47
  5.2 4.8 %collective-permute-start.4 = (bf16[2,4,1024]{2,1,0:T(4,128)(2,1)S(1)}, bf16[2,4,1024]{2,1,0:T(4,128)(2,1)S(1)}, u32[]{:S(2)}, u32[]{:S(2)}) collective-permute-start(bf16[2,4,1024]{2,1,0:T(4,128)(2,1)S(1)} %shard_map.75), channel_id=1, source_target_pairs={{0,10},{1,11},{2,8},{3,9},{4,14},{5,15},{6,12},{7,13},{8,2},{9,3},... | collective-permute-start | bytes 49160 | tf_op jit(solution)/shard_map/ppermute | solution.py:47
  7.0 5.0 %collective-permute-start.3 = (bf16[2,4,1024]{2,1,0:T(4,128)(2,1)S(1)}, bf16[2,4,1024]{2,1,0:T(4,128)(2,1)S(1)}, u32[]{:S(2)}, u32[]{:S(2)}) collective-permute-start(bf16[2,4,1024]{2,1,0:T(4,128)(2,1)S(1)} %shard_map.75), channel_id=1, source_target_pairs={{0,14},{1,15},{2,12},{3,13},{4,10},{5,11},{6,8},{7,9},{8,6},{9,7},... | collective-permute-start | bytes 49160 | tf_op jit(solution)/shard_map/ppermute | solution.py:47
  9.2 4.1 %collective-permute-start.2 = (bf16[2,4,1024]{2,1,0:T(4,128)(2,1)S(1)}, bf16[2,4,1024]{2,1,0:T(4,128)(2,1)S(1)}, u32[]{:S(2)}, u32[]{:S(2)}) collective-permute-start(bf16[2,4,1024]{2,1,0:T(4,128)(2,1)S(1)} %shard_map.75), channel_id=1, source_target_pairs={{0,12},{1,13},{2,14},{3,15},{4,8},{5,9},{6,10},{7,11},{8,4},{9,5},... | collective-permute-start | bytes 49160 | tf_op jit(solution)/shard_map/ppermute | solution.py:47
  10.7 9.8 %copy-start.1 = (bf16[4,128,2048]{2,1,0:T(8,128)(2,1)S(1)}, bf16[4,128,2048]{2,1,0:T(8,128)(2,1)}, u32[]{:S(2)}) copy-start(bf16[4,128,2048]{2,1,0:T(8,128)(2,1)} %cache_ref.7) | copy-start | bytes 6291460
  10.7 9.8 %copy-start.2 = (bf16[4,64,2048]{2,1,0:T(8,128)(2,1)S(1)}, bf16[4,64,2048]{2,1,0:T(8,128)(2,1)}, u32[]{:S(2)}) copy-start(bf16[4,64,2048]{2,1,0:T(8,128)(2,1)} %fresh_ref.7) | copy-start | bytes 3145732
  12.0 21.4 %slice-start = ((s8[16777216]{0:T(1024)(128)(4,1)}), s8[4194304]{0:T(1024)(128)(4,1)S(1)}, s32[]{:S(2)}) async-start(s8[16777216]{0:T(1024)(128)(4,1)} %bitcast), calls=%async_computation | async-start | bytes 8388608
  12.0 21.4 %slice-start.1 = ((s8[16777216]{0:T(1024)(128)(4,1)}), s8[4194304]{0:T(1024)(128)(4,1)S(1)}, s32[]{:S(2)}) async-start(s8[16777216]{0:T(1024)(128)(4,1)} %bitcast), calls=%async_computation.1 | async-start | bytes 8388608
  12.6 20.8 %slice-start.2 = ((s8[16777216]{0:T(1024)(128)(4,1)}), s8[4194304]{0:T(1024)(128)(4,1)S(1)}, s32[]{:S(2)}) async-start(s8[16777216]{0:T(1024)(128)(4,1)} %bitcast), calls=%async_computation.2 | async-start | bytes 8388608
  14.0 3.1 %collective-permute-start.7 = (bf16[32,128]{1,0:T(8,128)(2,1)S(1)}, bf16[32,128]{1,0:T(8,128)(2,1)S(1)}, u32[]{:S(2)}, u32[]{:S(2)}) collective-permute-start(bf16[32,128]{1,0:T(8,128)(2,1)S(1)} %shard_map.79), channel_id=1, source_target_pairs={{0,9},{1,8},{2,11},{3,10},{4,13},{5,12},{6,15},{7,14},{8,1},{9,0},... | collective-permute-start | bytes 24584 | tf_op jit(solution)/shard_map/ppermute | solution.py:47
  15.7 1.4 %collective-permute-start.6 = (bf16[32,128]{1,0:T(8,128)(2,1)S(1)}, bf16[32,128]{1,0:T(8,128)(2,1)S(1)}, u32[]{:S(2)}, u32[]{:S(2)}) collective-permute-start(bf16[32,128]{1,0:T(8,128)(2,1)S(1)} %shard_map.79), channel_id=1, source_target_pairs={{0,8},{1,9},{2,10},{3,11},{4,12},{5,13},{6,14},{7,15},{8,0},{9,1},... | collective-permute-start | bytes 24584 | tf_op jit(solution)/shard_map/ppermute | solution.py:47
  17.1 16.3 %slice-start.3 = ((s8[16777216]{0:T(1024)(128)(4,1)}), s8[4194304]{0:T(1024)(128)(4,1)S(1)}, s32[]{:S(2)}) async-start(s8[16777216]{0:T(1024)(128)(4,1)} %bitcast), calls=%async_computation.3 | async-start | bytes 8388608
  17.1 3.4 %collective-permute-start.8 = (bf16[2,32,128]{2,1,0:T(8,128)(2,1)S(1)}, bf16[2,32,128]{2,1,0:T(8,128)(2,1)S(1)}, u32[]{:S(2)}, u32[]{:S(2)}) collective-permute-start(bf16[2,32,128]{2,1,0:T(8,128)(2,1)S(1)} %shard_map.80), channel_id=1, source_target_pairs={{0,10},{1,11},{2,8},{3,9},{4,14},{5,15},{6,12},{7,13},{8,2},{9,3},... | collective-permute-start | bytes 49160 | tf_op jit(solution)/shard_map/ppermute | solution.py:47
  17.8 5.0 %collective-permute-start.10 = (bf16[2,32,128]{2,1,0:T(8,128)(2,1)S(1)}, bf16[2,32,128]{2,1,0:T(8,128)(2,1)S(1)}, u32[]{:S(2)}, u32[]{:S(2)}) collective-permute-start(bf16[2,32,128]{2,1,0:T(8,128)(2,1)S(1)} %shard_map.80), channel_id=1, source_target_pairs={{0,14},{1,15},{2,12},{3,13},{4,10},{5,11},{6,8},{7,9},{8,6},{9,7},... | collective-permute-start | bytes 49160 | tf_op jit(solution)/shard_map/ppermute | solution.py:47
  19.2 5.6 %collective-permute-start.12 = (bf16[2,32,128]{2,1,0:T(8,128)(2,1)S(1)}, bf16[2,32,128]{2,1,0:T(8,128)(2,1)S(1)}, u32[]{:S(2)}, u32[]{:S(2)}) collective-permute-start(bf16[2,32,128]{2,1,0:T(8,128)(2,1)S(1)} %shard_map.80), channel_id=1, source_target_pairs={{0,12},{1,13},{2,14},{3,15},{4,8},{5,9},{6,10},{7,11},{8,4},{9,5},... | collective-permute-start | bytes 49160 | tf_op jit(solution)/shard_map/ppermute | solution.py:47
  20.5 5.4 %collective-permute-start.14 = (bf16[2,32,128]{2,1,0:T(8,128)(2,1)S(1)}, bf16[2,32,128]{2,1,0:T(8,128)(2,1)S(1)}, u32[]{:S(2)}, u32[]{:S(2)}) collective-permute-start(bf16[2,32,128]{2,1,0:T(8,128)(2,1)S(1)} %shard_map.80), channel_id=1, source_target_pairs={{0,8},{1,9},{2,10},{3,11},{4,12},{5,13},{6,14},{7,15},{8,0},{9,1},... | collective-permute-start | bytes 49160 | tf_op jit(solution)/shard_map/ppermute | solution.py:47
  21.1 5.4 %collective-permute-start.9 = (bf16[2,40,128]{2,1,0:T(8,128)(2,1)S(1)}, bf16[2,40,128]{2,1,0:T(8,128)(2,1)S(1)}, u32[]{:S(2)}, u32[]{:S(2)}) collective-permute-start(bf16[2,40,128]{2,1,0:T(8,128)(2,1)S(1)} %shard_map.81), channel_id=1, source_target_pairs={{0,10},{1,11},{2,8},{3,9},{4,14},{5,15},{6,12},{7,13},{8,2},{9,3},... | collective-permute-start | bytes 61448 | tf_op jit(solution)/shard_map/ppermute | solution.py:47
  23.3 5.1 %collective-permute-start.11 = (bf16[2,40,128]{2,1,0:T(8,128)(2,1)S(1)}, bf16[2,40,128]{2,1,0:T(8,128)(2,1)S(1)}, u32[]{:S(2)}, u32[]{:S(2)}) collective-permute-start(bf16[2,40,128]{2,1,0:T(8,128)(2,1)S(1)} %shard_map.82), channel_id=1, source_target_pairs={{0,14},{1,15},{2,12},{3,13},{4,10},{5,11},{6,8},{7,9},{8,6},{9,7},... | collective-permute-start | bytes 61448 | tf_op jit(solution)/shard_map/ppermute | solution.py:47
  25.4 4.3 %collective-permute-start.13 = (bf16[2,40,128]{2,1,0:T(8,128)(2,1)S(1)}, bf16[2,40,128]{2,1,0:T(8,128)(2,1)S(1)}, u32[]{:S(2)}, u32[]{:S(2)}) collective-permute-start(bf16[2,40,128]{2,1,0:T(8,128)(2,1)S(1)} %shard_map.83), channel_id=1, source_target_pairs={{0,12},{1,13},{2,14},{3,15},{4,8},{5,9},{6,10},{7,11},{8,4},{9,5},... | collective-permute-start | bytes 61448 | tf_op jit(solution)/shard_map/ppermute | solution.py:47
  26.5 3.3 %collective-permute-start.15 = (bf16[2,40,128]{2,1,0:T(8,128)(2,1)S(1)}, bf16[2,40,128]{2,1,0:T(8,128)(2,1)S(1)}, u32[]{:S(2)}, u32[]{:S(2)}) collective-permute-start(bf16[2,40,128]{2,1,0:T(8,128)(2,1)S(1)} %shard_map.84), channel_id=1, source_target_pairs={{0,8},{1,9},{2,10},{3,11},{4,12},{5,13},{6,14},{7,15},{8,0},{9,1},... | collective-permute-start | bytes 61448 | tf_op jit(solution)/shard_map/ppermute | solution.py:47
  29.7 1.8 %collective-permute-start.16 = (bf16[4,40,128]{2,1,0:T(8,128)(2,1)S(1)}, bf16[4,40,128]{2,1,0:T(8,128)(2,1)S(1)}, u32[]{:S(2)}, u32[]{:S(2)}) collective-permute-start(bf16[4,40,128]{2,1,0:T(8,128)(2,1)S(1)} %get-tuple-element.11), channel_id=1, source_target_pairs={{0,8},{1,9},{2,10},{3,11},{4,12},{5,13},{6,14},{7,15},{8,0},{9,1},... | collective-permute-start | bytes 122888 | tf_op jit(solution)/shard_map/ppermute | solution.py:47
  29.9 3.5 %collective-permute-start.17 = (bf16[4,40,128]{2,1,0:T(8,128)(2,1)S(1)}, bf16[4,40,128]{2,1,0:T(8,128)(2,1)S(1)}, u32[]{:S(2)}, u32[]{:S(2)}) collective-permute-start(bf16[4,40,128]{2,1,0:T(8,128)(2,1)S(1)} %get-tuple-element.12), channel_id=1, source_target_pairs={{0,9},{1,8},{2,11},{3,10},{4,13},{5,12},{6,15},{7,14},{8,1},{9,0},... | collective-permute-start | bytes 122888 | tf_op jit(solution)/shard_map/ppermute | solution.py:47
  34.3 5.4 %collective-permute-start.18 = (bf16[2,4,1024]{2,1,0:T(4,128)(2,1)S(1)}, bf16[2,4,1024]{2,1,0:T(4,128)(2,1)S(1)}, u32[]{:S(2)}, u32[]{:S(2)}) collective-permute-start(bf16[2,4,1024]{2,1,0:T(4,128)(2,1)S(1)} %get-tuple-element.13), channel_id=1, source_target_pairs={{0,12},{1,13},{2,14},{3,15},{4,8},{5,9},{6,10},{7,11},{8,4},{9,5},... | collective-permute-start | bytes 49160 | tf_op jit(solution)/shard_map/ppermute | solution.py:47
  35.4 5.1 %collective-permute-start.19 = (bf16[2,4,1024]{2,1,0:T(4,128)(2,1)S(1)}, bf16[2,4,1024]{2,1,0:T(4,128)(2,1)S(1)}, u32[]{:S(2)}, u32[]{:S(2)}) collective-permute-start(bf16[2,4,1024]{2,1,0:T(4,128)(2,1)S(1)} %shard_map.88), channel_id=1, source_target_pairs={{0,14},{1,15},{2,12},{3,13},{4,10},{5,11},{6,8},{7,9},{8,6},{9,7},... | collective-permute-start | bytes 49160 | tf_op jit(solution)/shard_map/ppermute | solution.py:47
  38.2 3.2 %collective-permute-start.20 = (bf16[2,4,1024]{2,1,0:T(4,128)(2,1)S(1)}, bf16[2,4,1024]{2,1,0:T(4,128)(2,1)S(1)}, u32[]{:S(2)}, u32[]{:S(2)}) collective-permute-start(bf16[2,4,1024]{2,1,0:T(4,128)(2,1)S(1)} %shard_map.90), channel_id=1, source_target_pairs={{0,10},{1,11},{2,8},{3,9},{4,14},{5,15},{6,12},{7,13},{8,2},{9,3},... | collective-permute-start | bytes 49160 | tf_op jit(solution)/shard_map/ppermute | solution.py:47
  39.5 1.8 %collective-permute-start.21 = (bf16[2,4,1024]{2,1,0:T(4,128)(2,1)S(1)}, bf16[2,4,1024]{2,1,0:T(4,128)(2,1)S(1)}, u32[]{:S(2)}, u32[]{:S(2)}) collective-permute-start(bf16[2,4,1024]{2,1,0:T(4,128)(2,1)S(1)} %shard_map.92), channel_id=1, source_target_pairs={{0,8},{1,9},{2,10},{3,11},{4,12},{5,13},{6,14},{7,15},{8,0},{9,1},... | collective-permute-start | bytes 49160 | tf_op jit(solution)/shard_map/ppermute | solution.py:47
  41.4 3.4 %collective-permute-start.22 = (f32[4,1024]{1,0:T(4,128)S(1)}, f32[4,1024]{1,0:T(4,128)S(1)}, u32[]{:S(2)}, u32[]{:S(2)}) collective-permute-start(f32[4,1024]{1,0:T(4,128)S(1)} %get-tuple-element.15), channel_id=1, source_target_pairs={{0,8},{1,9},{2,10},{3,11},{4,12},{5,13},{6,14},{7,15},{8,0},{9,1},... | collective-permute-start | bytes 49160 | tf_op jit(solution)/shard_map/ppermute | solution.py:47
  41.7 3.1 %collective-permute-start.23 = (bf16[4,1024]{1,0:T(4,128)(2,1)S(1)}, bf16[4,1024]{1,0:T(4,128)(2,1)S(1)}, u32[]{:S(2)}, u32[]{:S(2)}) collective-permute-start(bf16[4,1024]{1,0:T(4,128)(2,1)S(1)} %get-tuple-element.16), channel_id=1, source_target_pairs={{0,9},{1,8},{2,11},{3,10},{4,13},{5,12},{6,15},{7,14},{8,1},{9,0},... | collective-permute-start | bytes 24584 | tf_op jit(solution)/shard_map/ppermute | solution.py:47
